TPU v7x, 32 devices: a whole 2x2x4 slice. The times are simulated.
32 devices in a mesh: groups: 2 (over y), members: 4 (over z), segment: 2 (over x), rows: 2 (over core).
Axes of the slice: x: 2, y: 2, z: 4, core: 2. Of those that a mesh axis runs over, the one named last changes fastest.
Arguments:
- init_state: bfloat16 [4, 2, 77, 128], P(('groups', 'segment'), 'rows'), parts along dimension 0, may hold values from -6 to 6
- forcing_slots: bfloat16 [4, 4, 2, 2, 4, 128], P('members', ('groups', 'segment'), None, 'rows'), parts along dimension 1, may hold values from -6 to 6
- atmos_owner: int32 [4, 2], P(('groups', 'segment')), parts along dimension 0, may hold values from 0 to 3
- land_mask: int32 [4, 128], P(('groups', 'rows')), parts along dimension 0, may hold values 0 or 1
- param_index: int32 [8], P(('groups', 'members')), parts along dimension 0, may hold values from 0 to 63
- settings: float32 [64, 16], replicated, may hold values from -5 to 5
- scale_weight: float32 [16, 256], replicated, may hold values from -0.75 to 0.75
- shift_weight: float32 [16, 256], replicated, may hold values from -0.75 to 0.75
- encode_weight: bfloat16 [256, 81], replicated, may hold values from -0.625 to 0.625
- conv_weight: bfloat16 [2, 256, 2304], P('segment'), may hold values from -0.125 to 0.125
- point_weight: bfloat16 [2, 256, 256], P('segment'), may hold values from -0.375 to 0.375
- norm_gain: bfloat16 [2, 256], P('segment'), may hold values from 0.099609375 to 1.8984375
- decode_weight: bfloat16 [77, 256], replicated, may hold values from -0.1875 to 0.1875
Outputs:
- final_state: bfloat16 [4, 4, 2, 77, 128], P('members', ('groups', 'segment'), 'rows'), parts along dimension 1
- ensemble_mean: float32 [4, 2, 77, 128], P(('groups', 'segment'), 'rows'), parts along dimension 0
There are 2 independent parts, one for each index of `groups`. A program takes and returns all parts, laid end to end along the dimension named above; an argument that names none is the same for every part. Nothing has to cross between parts.
Inputs may be any that keep to these rules, and one draw needn't show every extreme that they name: `atmos_owner`: a member index of the same group. `param_index`: a row of settings.
All inputs are finite; a program needn't handle non-finite values. No bound on the sum of `land_mask` on one device may be relied on, other than what follows from the above.
Results may differ from a plain program's by a relative error of at most 0.018.
Values may be sent and summed in bfloat16 or wider, within the bound.
No kernel may reach another device: no remote copies, remote signals or barrier semaphores. Data moves between devices by JAX's collectives and lax.ppermute only.
A program may use at most 64 MiB of HBM per device.

v0:
```python
import jax
import jax.numpy as jnp
from jax import lax
from jax.sharding import PartitionSpec as P

STEPS = 2


def padded_2(array, sides, width):
    for axis, dim in sides:
        size, length = (lax.axis_size(axis), array.shape[dim])
        up = [(i, (i + 1) % size) for i in range(size - 1)]
        down = [(j, i) for i, j in up]
        last = lax.slice_in_dim(array, length - width, length, axis=dim)
        initial = lax.slice_in_dim(array, 0, width, axis=dim)
        before = lax.ppermute(last, axis, up)
        after = lax.ppermute(initial, axis, down)
        array = jnp.concatenate([before, array, after], axis=dim)
    return array


def from_root(array, axis, root):
    mine = lax.axis_index(axis) == root
    return lax.psum(jnp.where(mine, array, jnp.zeros_like(array)), axis)


def passed_along(block, axis, distance):
    devices = range(lax.axis_size(axis))
    route = [((i - distance) % len(devices), i) for i in devices]
    return lax.ppermute(block, axis, route)


def build_taps(rimmed, spacing):
    lat_cells = rimmed.shape[0] - 2
    lon_cells = rimmed.shape[2]
    padded = jnp.pad(rimmed, ((0, 0), (0, 0), (4, 4)))
    pieces = []
    for lat_off in range(3):
        lat_band = padded[lat_off : lat_off + lat_cells]
        for lon_off in (-1, 0, 1):
            pieces.append(lax.dynamic_slice_in_dim(lat_band, 4 + lon_off * spacing, lon_cells, 2))
    return jnp.concatenate(pieces, axis=1)


def with_rim(hidden):
    return padded_2(hidden, (("rows", 0),), 1)


def local_section(rimmed, conv_here, point_here, gain_here, spacing, land_cells):
    hidden = rimmed[1:-1]
    taps = build_taps(rimmed, spacing)
    conv_out = jnp.einsum("ok,lkx->lox", conv_here, taps, preferred_element_type=jnp.float32)
    chan_mean = jnp.mean(conv_out, axis=1, keepdims=True)
    centred = conv_out - chan_mean
    spread = jnp.mean(centred * centred, axis=1, keepdims=True)
    normed = centred * lax.rsqrt(spread + 1e-05) * gain_here.astype(jnp.float32)[None, :, None]
    activated = jax.nn.gelu(normed).astype(jnp.bfloat16)
    mixed = jnp.einsum("ok,lkx->lox", point_here, activated, preferred_element_type=jnp.float32)
    return (land_cells * (hidden.astype(jnp.float32) + mixed)).astype(jnp.bfloat16)


def encode(ocean_state, forcing_now, encode_weight, cond_scale, cond_shift, land_cells):
    inputs = jnp.concatenate([ocean_state, forcing_now], axis=1)
    lifted = jnp.einsum("ok,lkx->lox", encode_weight, inputs, preferred_element_type=jnp.float32)
    return (land_cells * (lifted * cond_scale[None, :, None] + cond_shift[None, :, None])).astype(
        jnp.bfloat16
    )


def decode(ocean_state, hidden, decode_weight, land_cells):
    change = jnp.einsum("ok,lkx->lox", decode_weight, hidden, preferred_element_type=jnp.float32)
    return (ocean_state.astype(jnp.float32) + land_cells * change).astype(jnp.bfloat16)


def per_device(
    init_state,
    forcing_slots,
    atmos_owner,
    land_mask,
    param_index,
    settings,
    scale_weight,
    shift_weight,
    encode_weight,
    conv_weight,
    point_weight,
    norm_gain,
    decode_weight,
):
    land_cells = land_mask.astype(jnp.float32)[:, None, :]
    choose_row = (jnp.arange(settings.shape[0]) == param_index[0]).astype(jnp.float32)
    setting_row = jnp.dot(choose_row, settings, precision=lax.Precision.HIGHEST)
    cond_scale = 1.0 + jnp.dot(setting_row, scale_weight, precision=lax.Precision.HIGHEST)
    cond_shift = jnp.dot(setting_row, shift_weight, precision=lax.Precision.HIGHEST)
    own_slots = forcing_slots[0, 0]
    received = []
    for step_no in range(STEPS):
        received.append(from_root(own_slots[step_no], "members", atmos_owner[0, step_no]))
    forcing = jnp.stack(received, axis=0)
    ocean_state = init_state[0]
    segments = lax.axis_size("segment")
    position = lax.axis_index("segment")
    spacing = jnp.left_shift(jnp.int32(1), position % 3)
    conv_here = conv_weight[0]
    point_here = point_weight[0]
    gain_here = norm_gain[0]
    lap_ticks = segments * STEPS
    at_head = position == 0

    def tick(tick_no, carry):
        hidden, state_now, forcing_now = carry
        decoded = decode(state_now, hidden, decode_weight, land_cells)
        state_now = jnp.where(at_head & (tick_no >= segments), decoded, state_now)
        step_force = lax.dynamic_index_in_dim(
            forcing_now, jnp.minimum(tick_no // segments, STEPS - 1), 0, keepdims=False
        )
        encoded = encode(state_now, step_force, encode_weight, cond_scale, cond_shift, land_cells)
        hidden = jnp.where(at_head & (tick_no < lap_ticks), encoded, hidden)
        rimmed = with_rim(hidden)
        active = (tick_no >= position) & (tick_no - position < lap_ticks)

        def run_block():
            return local_section(rimmed, conv_here, point_here, gain_here, spacing, land_cells)

        def keep_block():
            return hidden

        hidden = lax.cond(active, run_block, keep_block)
        return passed_along((hidden, state_now, forcing_now), "segment", 1)

    start_hidden = jnp.zeros(
        (ocean_state.shape[0], conv_weight.shape[1], ocean_state.shape[2]), jnp.bfloat16
    )
    ended = lax.fori_loop(0, segments * (STEPS + 1), tick, (start_hidden, ocean_state, forcing))
    ocean_state = ended[1]
    members = lax.axis_size("members")
    ens_total = lax.psum(ocean_state.astype(jnp.float32).astype(jnp.bfloat16), "members").astype(
        jnp.float32
    )
    return (ocean_state[None, None], (ens_total / members)[None])


def solution(mesh):
    in_specs = (
        P(("groups", "segment"), "rows", None, None),
        P("members", ("groups", "segment"), None, "rows", None, None),
        P(("groups", "segment"), None),
        P(("groups", "rows"), None),
        P(("groups", "members")),
        P(),
        P(),
        P(),
        P(),
        P("segment", None, None),
        P("segment", None, None),
        P("segment", None),
        P(),
    )
    out_specs = (
        P("members", ("groups", "segment"), "rows", None, None),
        P(("groups", "segment"), "rows", None, None),
    )
    return jax.shard_map(
        per_device, mesh=mesh, in_specs=in_specs, out_specs=out_specs, check_vma=False
    )
```

profile of v0, /device:TPU:0, one launch (start us, length us, event | category | flops | bytes accessed | tf_op | source)
XLA Modules:
  0.0 127.6 jit_solution(12876457175498616522)
XLA Ops:
  1.4 1.3 %fusion.45 = (s32[1,1]{1,0:T(1,128)}, s32[1,1]{1,0:T(1,128)}) fusion(s32[1,2]{1,0:T(1,128)} %param.19), kind=kLoop, calls=%fused_computation.74 | loop fusion | bytes 16 | tf_op jit(solution)/shard_map/slice | solution.py:98
  4.7 13.4 %all-reduce.1 = (bf16[1,1,4,128]{3,2,1,0:T(4,128)(2,1)S(1)}, bf16[1,1,4,128]{3,2,1,0:T(4,128)(2,1)S(1)}) all-reduce(bf16[1,1,4,128]{3,2,1,0:T(4,128)(2,1)S(1)} %get-tuple-element.433, bf16[1,1,4,128]{3,2,1,0:T(4,128)(2,1)S(1)} %get-tuple-element.432), channel_id=1, replica_groups=mesh['groups'=2,'members'=4,'segment'=2,'rows'=2] {'members'}, use_global_device_ids=true, to_apply=%region_1.2 | all-reduce | flops 1024 | bytes 4096 | tf_op jit(solution)/shard_map/psum | solution.py:24
  22.0 88.1 %while.19 = (s32[]{:T(128)}, bf16[1,256,128]{1,2,0:T(8,128)(2,1)S(1)}, bf16[1,77,128]{2,1,0:T(8,128)(2,1)S(1)}, bf16[2,1,4,128]{3,2,1,0:T(4,128)(2,1)S(1)}, s32[...) while((s32[]{:T(128)}, ...), condition=%wide.region_7.8_spmd, body=%wide.region_2.7_spmd.sunk | while | flops 179233824 | bytes 11268149 | solution.py:134
  22.1 0.9 fusion.65
  23.0 1.0 fusion.66
  24.0 1.3 %collective-permute-start = (bf16[1,256,128]{1,2,0:T(8,128)(2,1)S(1)}, bf16[1,256,128]{1,2,0:T(8,128)(2,1)S(1)}, u32[]{:S(2)}, u32[]{:S(2)}) collective-permute-start(bf16[1,256,128]{1,2,0:T(8,128)(2,1)S(1)} %fusion.66), channel_id=1, source_target_pairs={{1,0},{3,2},{5,4},{7,6},{9,8},{11,10},{13,12},{15,14},{17,16},{19,... | collective-permute-start | bytes 196616 | tf_op jit(solution)/shard_map/while/body/eval_jaxpr/ppermute | solution.py:17
  25.3 3.0 %collective-permute-start.1 = (bf16[1,256,128]{1,2,0:T(8,128)(2,1)S(1)}, bf16[1,256,128]{1,2,0:T(8,128)(2,1)S(1)}, u32[]{:S(2)}, u32[]{:S(2)}) collective-permute-start(bf16[1,256,128]{1,2,0:T(8,128)(2,1)S(1)} %fusion.66), channel_id=1, source_target_pairs={{0,1},{2,3},{4,5},{6,7},{8,9},{10,11},{12,13},{14,15},{16,17},{18,... | collective-permute-start | bytes 196616 | tf_op jit(solution)/shard_map/while/body/eval_jaxpr/ppermute | solution.py:16
  28.4 0.9 collective-permute-done.1
  29.3 2.4 %conditional.2 = (bf16[1,256,128]{1,2,0:T(8,128)(2,1)S(1)}) conditional(s32[]{:T(128)} %convert_element_type.92, bf16[1,256,128]{1,2,0:T(8,128)(2,1)S(1)} %fusion.66, (f32[1,1,128]{2,1,0:T(1,128)S(1)}, bf16[1,256,128]{1,2,0:T(8,128)(2,1)S(1)}, bf16[3,256,128]{1,2,0:T(8,128)(2,1)S(1)}, s32[]{:T(128)}, bf16[256,2304]{1,0:T(8,128)(2,1)}, ...), branch_computations={%region_3.3_spmd, %region_4.6_spmd} | conditional | flops 168427920 | bytes 9653952 | solution.py:128
  31.8 2.0 %collective-permute-start.3 = (bf16[1,77,128]{2,1,0:T(8,128)(2,1)S(1)}, bf16[1,77,128]{2,1,0:T(8,128)(2,1)S(1)}, u32[]{:S(2)}, u32[]{:S(2)}) collective-permute-start(bf16[1,77,128]{2,1,0:T(8,128)(2,1)S(1)} %fusion.65), channel_id=1, source_target_pairs={{2,0},{0,2},{3,1},{1,3},{6,4},{4,6},{7,5},{5,7},{10,8},{8,10},{11,... | collective-permute-start | bytes 59144 | tf_op jit(solution)/shard_map/while/body/eval_jaxpr/ppermute | solution.py:30
  33.9 3.5 %collective-permute-done.4 = bf16[2,1,4,128]{3,2,1,0:T(4,128)(2,1)S(1)} collective-permute-done((bf16[2,1,4,128]{3,2,1,0:T(4,128)(2,1)S(1)}, bf16[2,1,4,128]{3,2,1,0:T(4,128)(2,1)S(1)}, u32[]{:S(2)}, u32[]{:S(2)}) %collective-permute-start.4) | collective-permute-done | bytes 2080 | tf_op jit(solution)/shard_map/while/body/eval_jaxpr/ppermute | solution.py:30
  37.4 0.9 fusion.65
  38.4 1.0 fusion.66
  39.4 1.3 %collective-permute-start = (bf16[1,256,128]{1,2,0:T(8,128)(2,1)S(1)}, bf16[1,256,128]{1,2,0:T(8,128)(2,1)S(1)}, u32[]{:S(2)}, u32[]{:S(2)}) collective-permute-start(bf16[1,256,128]{1,2,0:T(8,128)(2,1)S(1)} %fusion.66), channel_id=1, source_target_pairs={{1,0},{3,2},{5,4},{7,6},{9,8},{11,10},{13,12},{15,14},{17,16},{19,... | collective-permute-start | bytes 196616 | tf_op jit(solution)/shard_map/while/body/eval_jaxpr/ppermute | solution.py:17
  40.7 3.0 %collective-permute-start.1 = (bf16[1,256,128]{1,2,0:T(8,128)(2,1)S(1)}, bf16[1,256,128]{1,2,0:T(8,128)(2,1)S(1)}, u32[]{:S(2)}, u32[]{:S(2)}) collective-permute-start(bf16[1,256,128]{1,2,0:T(8,128)(2,1)S(1)} %fusion.66), channel_id=1, source_target_pairs={{0,1},{2,3},{4,5},{6,7},{8,9},{10,11},{12,13},{14,15},{16,17},{18,... | collective-permute-start | bytes 196616 | tf_op jit(solution)/shard_map/while/body/eval_jaxpr/ppermute | solution.py:16
  43.7 0.9 collective-permute-done.1
  44.6 2.4 %conditional.2 = (bf16[1,256,128]{1,2,0:T(8,128)(2,1)S(1)}) conditional(s32[]{:T(128)} %convert_element_type.92, bf16[1,256,128]{1,2,0:T(8,128)(2,1)S(1)} %fusion.66, (f32[1,1,128]{2,1,0:T(1,128)S(1)}, bf16[1,256,128]{1,2,0:T(8,128)(2,1)S(1)}, bf16[3,256,128]{1,2,0:T(8,128)(2,1)S(1)}, s32[]{:T(128)}, bf16[256,2304]{1,0:T(8,128)(2,1)}, ...), branch_computations={%region_3.3_spmd, %region_4.6_spmd} | conditional | flops 168427920 | bytes 9653952 | solution.py:128
  47.3 1.8 %collective-permute-start.3 = (bf16[1,77,128]{2,1,0:T(8,128)(2,1)S(1)}, bf16[1,77,128]{2,1,0:T(8,128)(2,1)S(1)}, u32[]{:S(2)}, u32[]{:S(2)}) collective-permute-start(bf16[1,77,128]{2,1,0:T(8,128)(2,1)S(1)} %fusion.65), channel_id=1, source_target_pairs={{2,0},{0,2},{3,1},{1,3},{6,4},{4,6},{7,5},{5,7},{10,8},{8,10},{11,... | collective-permute-start | bytes 59144 | tf_op jit(solution)/shard_map/while/body/eval_jaxpr/ppermute | solution.py:30
  49.3 3.4 %collective-permute-done.4 = bf16[2,1,4,128]{3,2,1,0:T(4,128)(2,1)S(1)} collective-permute-done((bf16[2,1,4,128]{3,2,1,0:T(4,128)(2,1)S(1)}, bf16[2,1,4,128]{3,2,1,0:T(4,128)(2,1)S(1)}, u32[]{:S(2)}, u32[]{:S(2)}) %collective-permute-start.4) | collective-permute-done | bytes 2080 | tf_op jit(solution)/shard_map/while/body/eval_jaxpr/ppermute | solution.py:30
  52.8 0.9 fusion.65
  53.7 1.0 fusion.66
  54.7 1.3 %collective-permute-start = (bf16[1,256,128]{1,2,0:T(8,128)(2,1)S(1)}, bf16[1,256,128]{1,2,0:T(8,128)(2,1)S(1)}, u32[]{:S(2)}, u32[]{:S(2)}) collective-permute-start(bf16[1,256,128]{1,2,0:T(8,128)(2,1)S(1)} %fusion.66), channel_id=1, source_target_pairs={{1,0},{3,2},{5,4},{7,6},{9,8},{11,10},{13,12},{15,14},{17,16},{19,... | collective-permute-start | bytes 196616 | tf_op jit(solution)/shard_map/while/body/eval_jaxpr/ppermute | solution.py:17
  56.0 3.0 %collective-permute-start.1 = (bf16[1,256,128]{1,2,0:T(8,128)(2,1)S(1)}, bf16[1,256,128]{1,2,0:T(8,128)(2,1)S(1)}, u32[]{:S(2)}, u32[]{:S(2)}) collective-permute-start(bf16[1,256,128]{1,2,0:T(8,128)(2,1)S(1)} %fusion.66), channel_id=1, source_target_pairs={{0,1},{2,3},{4,5},{6,7},{8,9},{10,11},{12,13},{14,15},{16,17},{18,... | collective-permute-start | bytes 196616 | tf_op jit(solution)/shard_map/while/body/eval_jaxpr/ppermute | solution.py:16
  60.0 2.4 %conditional.2 = (bf16[1,256,128]{1,2,0:T(8,128)(2,1)S(1)}) conditional(s32[]{:T(128)} %convert_element_type.92, bf16[1,256,128]{1,2,0:T(8,128)(2,1)S(1)} %fusion.66, (f32[1,1,128]{2,1,0:T(1,128)S(1)}, bf16[1,256,128]{1,2,0:T(8,128)(2,1)S(1)}, bf16[3,256,128]{1,2,0:T(8,128)(2,1)S(1)}, s32[]{:T(128)}, bf16[256,2304]{1,0:T(8,128)(2,1)}, ...), branch_computations={%region_3.3_spmd, %region_4.6_spmd} | conditional | flops 168427920 | bytes 9653952 | solution.py:128
  62.7 1.8 %collective-permute-start.3 = (bf16[1,77,128]{2,1,0:T(8,128)(2,1)S(1)}, bf16[1,77,128]{2,1,0:T(8,128)(2,1)S(1)}, u32[]{:S(2)}, u32[]{:S(2)}) collective-permute-start(bf16[1,77,128]{2,1,0:T(8,128)(2,1)S(1)} %fusion.65), channel_id=1, source_target_pairs={{2,0},{0,2},{3,1},{1,3},{6,4},{4,6},{7,5},{5,7},{10,8},{8,10},{11,... | collective-permute-start | bytes 59144 | tf_op jit(solution)/shard_map/while/body/eval_jaxpr/ppermute | solution.py:30
  64.7 3.4 %collective-permute-done.4 = bf16[2,1,4,128]{3,2,1,0:T(4,128)(2,1)S(1)} collective-permute-done((bf16[2,1,4,128]{3,2,1,0:T(4,128)(2,1)S(1)}, bf16[2,1,4,128]{3,2,1,0:T(4,128)(2,1)S(1)}, u32[]{:S(2)}, u32[]{:S(2)}) %collective-permute-start.4) | collective-permute-done | bytes 2080 | tf_op jit(solution)/shard_map/while/body/eval_jaxpr/ppermute | solution.py:30
  68.1 0.9 fusion.65
  69.0 1.0 fusion.66
  70.0 1.3 %collective-permute-start = (bf16[1,256,128]{1,2,0:T(8,128)(2,1)S(1)}, bf16[1,256,128]{1,2,0:T(8,128)(2,1)S(1)}, u32[]{:S(2)}, u32[]{:S(2)}) collective-permute-start(bf16[1,256,128]{1,2,0:T(8,128)(2,1)S(1)} %fusion.66), channel_id=1, source_target_pairs={{1,0},{3,2},{5,4},{7,6},{9,8},{11,10},{13,12},{15,14},{17,16},{19,... | collective-permute-start | bytes 196616 | tf_op jit(solution)/shard_map/while/body/eval_jaxpr/ppermute | solution.py:17
  71.3 3.0 %collective-permute-start.1 = (bf16[1,256,128]{1,2,0:T(8,128)(2,1)S(1)}, bf16[1,256,128]{1,2,0:T(8,128)(2,1)S(1)}, u32[]{:S(2)}, u32[]{:S(2)}) collective-permute-start(bf16[1,256,128]{1,2,0:T(8,128)(2,1)S(1)} %fusion.66), channel_id=1, source_target_pairs={{0,1},{2,3},{4,5},{6,7},{8,9},{10,11},{12,13},{14,15},{16,17},{18,... | collective-permute-start | bytes 196616 | tf_op jit(solution)/shard_map/while/body/eval_jaxpr/ppermute | solution.py:16
  75.3 2.4 %conditional.2 = (bf16[1,256,128]{1,2,0:T(8,128)(2,1)S(1)}) conditional(s32[]{:T(128)} %convert_element_type.92, bf16[1,256,128]{1,2,0:T(8,128)(2,1)S(1)} %fusion.66, (f32[1,1,128]{2,1,0:T(1,128)S(1)}, bf16[1,256,128]{1,2,0:T(8,128)(2,1)S(1)}, bf16[3,256,128]{1,2,0:T(8,128)(2,1)S(1)}, s32[]{:T(128)}, bf16[256,2304]{1,0:T(8,128)(2,1)}, ...), branch_computations={%region_3.3_spmd, %region_4.6_spmd} | conditional | flops 168427920 | bytes 9653952 | solution.py:128
  78.0 1.8 %collective-permute-start.3 = (bf16[1,77,128]{2,1,0:T(8,128)(2,1)S(1)}, bf16[1,77,128]{2,1,0:T(8,128)(2,1)S(1)}, u32[]{:S(2)}, u32[]{:S(2)}) collective-permute-start(bf16[1,77,128]{2,1,0:T(8,128)(2,1)S(1)} %fusion.65), channel_id=1, source_target_pairs={{2,0},{0,2},{3,1},{1,3},{6,4},{4,6},{7,5},{5,7},{10,8},{8,10},{11,... | collective-permute-start | bytes 59144 | tf_op jit(solution)/shard_map/while/body/eval_jaxpr/ppermute | solution.py:30
  80.0 3.4 %collective-permute-done.4 = bf16[2,1,4,128]{3,2,1,0:T(4,128)(2,1)S(1)} collective-permute-done((bf16[2,1,4,128]{3,2,1,0:T(4,128)(2,1)S(1)}, bf16[2,1,4,128]{3,2,1,0:T(4,128)(2,1)S(1)}, u32[]{:S(2)}, u32[]{:S(2)}) %collective-permute-start.4) | collective-permute-done | bytes 2080 | tf_op jit(solution)/shard_map/while/body/eval_jaxpr/ppermute | solution.py:30
  83.4 0.9 fusion.65
  84.4 1.0 fusion.66
  85.4 1.3 %collective-permute-start = (bf16[1,256,128]{1,2,0:T(8,128)(2,1)S(1)}, bf16[1,256,128]{1,2,0:T(8,128)(2,1)S(1)}, u32[]{:S(2)}, u32[]{:S(2)}) collective-permute-start(bf16[1,256,128]{1,2,0:T(8,128)(2,1)S(1)} %fusion.66), channel_id=1, source_target_pairs={{1,0},{3,2},{5,4},{7,6},{9,8},{11,10},{13,12},{15,14},{17,16},{19,... | collective-permute-start | bytes 196616 | tf_op jit(solution)/shard_map/while/body/eval_jaxpr/ppermute | solution.py:17
  86.7 3.0 %collective-permute-start.1 = (bf16[1,256,128]{1,2,0:T(8,128)(2,1)S(1)}, bf16[1,256,128]{1,2,0:T(8,128)(2,1)S(1)}, u32[]{:S(2)}, u32[]{:S(2)}) collective-permute-start(bf16[1,256,128]{1,2,0:T(8,128)(2,1)S(1)} %fusion.66), channel_id=1, source_target_pairs={{0,1},{2,3},{4,5},{6,7},{8,9},{10,11},{12,13},{14,15},{16,17},{18,... | collective-permute-start | bytes 196616 | tf_op jit(solution)/shard_map/while/body/eval_jaxpr/ppermute | solution.py:16
  90.7 2.7 %collective-permute-start.2 = (bf16[1,256,128]{1,2,0:T(8,128)(2,1)S(1)}, bf16[1,256,128]{1,2,0:T(8,128)(2,1)S(1)}, u32[]{:S(2)}, u32[]{:S(2)}) collective-permute-start(bf16[1,256,128]{1,2,0:T(8,128)(2,1)S(1)} %get-tuple-element.591), channel_id=1, source_target_pairs={{2,0},{0,2},{3,1},{1,3},{6,4},{4,6},{7,5},{5,7},{10,8},{8,10},{11,... | collective-permute-start | bytes 196616 | tf_op jit(solution)/shard_map/while/body/eval_jaxpr/ppermute | solution.py:30
  93.4 1.9 %collective-permute-start.4 = (bf16[2,1,4,128]{3,2,1,0:T(4,128)(2,1)S(1)}, bf16[2,1,4,128]{3,2,1,0:T(4,128)(2,1)S(1)}, u32[]{:S(2)}, u32[]{:S(2)}) collective-permute-start(bf16[2,1,4,128]{3,2,1,0:T(4,128)(2,1)S(1)} %copy.34), channel_id=1, source_target_pairs={{2,0},{0,2},{3,1},{1,3},{6,4},{4,6},{7,5},{5,7},{10,8},{8,10},{11,... | collective-permute-start | bytes 6152 | tf_op jit(solution)/shard_map/while/body/eval_jaxpr/ppermute | solution.py:30
  95.4 1.8 %collective-permute-done.4 = bf16[2,1,4,128]{3,2,1,0:T(4,128)(2,1)S(1)} collective-permute-done((bf16[2,1,4,128]{3,2,1,0:T(4,128)(2,1)S(1)}, bf16[2,1,4,128]{3,2,1,0:T(4,128)(2,1)S(1)}, u32[]{:S(2)}, u32[]{:S(2)}) %collective-permute-start.4) | collective-permute-done | bytes 2080 | tf_op jit(solution)/shard_map/while/body/eval_jaxpr/ppermute | solution.py:30
  97.2 0.9 fusion.65
  98.1 1.0 fusion.66
  99.1 1.3 %collective-permute-start = (bf16[1,256,128]{1,2,0:T(8,128)(2,1)S(1)}, bf16[1,256,128]{1,2,0:T(8,128)(2,1)S(1)}, u32[]{:S(2)}, u32[]{:S(2)}) collective-permute-start(bf16[1,256,128]{1,2,0:T(8,128)(2,1)S(1)} %fusion.66), channel_id=1, source_target_pairs={{1,0},{3,2},{5,4},{7,6},{9,8},{11,10},{13,12},{15,14},{17,16},{19,... | collective-permute-start | bytes 196616 | tf_op jit(solution)/shard_map/while/body/eval_jaxpr/ppermute | solution.py:17
  100.4 3.0 %collective-permute-start.1 = (bf16[1,256,128]{1,2,0:T(8,128)(2,1)S(1)}, bf16[1,256,128]{1,2,0:T(8,128)(2,1)S(1)}, u32[]{:S(2)}, u32[]{:S(2)}) collective-permute-start(bf16[1,256,128]{1,2,0:T(8,128)(2,1)S(1)} %fusion.66), channel_id=1, source_target_pairs={{0,1},{2,3},{4,5},{6,7},{8,9},{10,11},{12,13},{14,15},{16,17},{18,... | collective-permute-start | bytes 196616 | tf_op jit(solution)/shard_map/while/body/eval_jaxpr/ppermute | solution.py:16
  104.4 1.9 %collective-permute-start.2 = (bf16[1,256,128]{1,2,0:T(8,128)(2,1)S(1)}, bf16[1,256,128]{1,2,0:T(8,128)(2,1)S(1)}, u32[]{:S(2)}, u32[]{:S(2)}) collective-permute-start(bf16[1,256,128]{1,2,0:T(8,128)(2,1)S(1)} %get-tuple-element.591), channel_id=1, source_target_pairs={{2,0},{0,2},{3,1},{1,3},{6,4},{4,6},{7,5},{5,7},{10,8},{8,10},{11,... | collective-permute-start | bytes 196616 | tf_op jit(solution)/shard_map/while/body/eval_jaxpr/ppermute | solution.py:30
  106.5 1.8 %collective-permute-start.4 = (bf16[2,1,4,128]{3,2,1,0:T(4,128)(2,1)S(1)}, bf16[2,1,4,128]{3,2,1,0:T(4,128)(2,1)S(1)}, u32[]{:S(2)}, u32[]{:S(2)}) collective-permute-start(bf16[2,1,4,128]{3,2,1,0:T(4,128)(2,1)S(1)} %copy.34), channel_id=1, source_target_pairs={{2,0},{0,2},{3,1},{1,3},{6,4},{4,6},{7,5},{5,7},{10,8},{8,10},{11,... | collective-permute-start | bytes 6152 | tf_op jit(solution)/shard_map/while/body/eval_jaxpr/ppermute | solution.py:30
  108.3 1.8 %collective-permute-done.4 = bf16[2,1,4,128]{3,2,1,0:T(4,128)(2,1)S(1)} collective-permute-done((bf16[2,1,4,128]{3,2,1,0:T(4,128)(2,1)S(1)}, bf16[2,1,4,128]{3,2,1,0:T(4,128)(2,1)S(1)}, u32[]{:S(2)}, u32[]{:S(2)}) %collective-permute-start.4) | collective-permute-done | bytes 2080 | tf_op jit(solution)/shard_map/while/body/eval_jaxpr/ppermute | solution.py:30
  110.1 16.2 %psum.23 = bf16[1,77,128]{2,0,1:T(2,128)(2,1)S(1)} all-reduce(bf16[1,77,128]{2,0,1:T(2,128)(2,1)S(1)} %copy.16), channel_id=1, replica_groups=mesh['groups'=2,'members'=4,'segment'=2,'rows'=2] {'members'}, use_global_device_ids=true, to_apply=%region_8.9 | all-reduce | flops 9856 | bytes 39424 | tf_op jit(solution)/shard_map/psum | solution.py:137
  (151 shorter events, 20.7 us)
Async XLA Ops:
  0.6 19.0 %copy-start = (f32[16,256]{1,0:T(8,128)S(1)}, f32[16,256]{1,0:T(8,128)}, u32[]{:S(2)}) copy-start(f32[16,256]{1,0:T(8,128)} %param.23) | copy-start | bytes 49156
  24.0 4.4 %collective-permute-start = (bf16[1,256,128]{1,2,0:T(8,128)(2,1)S(1)}, bf16[1,256,128]{1,2,0:T(8,128)(2,1)S(1)}, u32[]{:S(2)}, u32[]{:S(2)}) collective-permute-start(bf16[1,256,128]{1,2,0:T(8,128)(2,1)S(1)} %fusion.66), channel_id=1, source_target_pairs={{1,0},{3,2},{5,4},{7,6},{9,8},{11,10},{13,12},{15,14},{17,16},{19,... | collective-permute-start | bytes 196616 | tf_op jit(solution)/shard_map/while/body/eval_jaxpr/ppermute | solution.py:17
  25.3 3.9 %collective-permute-start.1 = (bf16[1,256,128]{1,2,0:T(8,128)(2,1)S(1)}, bf16[1,256,128]{1,2,0:T(8,128)(2,1)S(1)}, u32[]{:S(2)}, u32[]{:S(2)}) collective-permute-start(bf16[1,256,128]{1,2,0:T(8,128)(2,1)S(1)} %fusion.66), channel_id=1, source_target_pairs={{0,1},{2,3},{4,5},{6,7},{8,9},{10,11},{12,13},{14,15},{16,17},{18,... | collective-permute-start | bytes 196616 | tf_op jit(solution)/shard_map/while/body/eval_jaxpr/ppermute | solution.py:16
  29.3 1.3 copy-start.1
  30.3 1.1 copy-start.2
  31.7 5.7 %collective-permute-start.2 = (bf16[1,256,128]{1,2,0:T(8,128)(2,1)S(1)}, bf16[1,256,128]{1,2,0:T(8,128)(2,1)S(1)}, u32[]{:S(2)}, u32[]{:S(2)}) collective-permute-start(bf16[1,256,128]{1,2,0:T(8,128)(2,1)S(1)} %get-tuple-element.591), channel_id=1, source_target_pairs={{2,0},{0,2},{3,1},{1,3},{6,4},{4,6},{7,5},{5,7},{10,8},{8,10},{11,... | collective-permute-start | bytes 196616 | tf_op jit(solution)/shard_map/while/body/eval_jaxpr/ppermute | solution.py:30
  31.8 5.6 %collective-permute-start.3 = (bf16[1,77,128]{2,1,0:T(8,128)(2,1)S(1)}, bf16[1,77,128]{2,1,0:T(8,128)(2,1)S(1)}, u32[]{:S(2)}, u32[]{:S(2)}) collective-permute-start(bf16[1,77,128]{2,1,0:T(8,128)(2,1)S(1)} %fusion.65), channel_id=1, source_target_pairs={{2,0},{0,2},{3,1},{1,3},{6,4},{4,6},{7,5},{5,7},{10,8},{8,10},{11,... | collective-permute-start | bytes 59144 | tf_op jit(solution)/shard_map/while/body/eval_jaxpr/ppermute | solution.py:30
  33.8 3.6 %collective-permute-start.4 = (bf16[2,1,4,128]{3,2,1,0:T(4,128)(2,1)S(1)}, bf16[2,1,4,128]{3,2,1,0:T(4,128)(2,1)S(1)}, u32[]{:S(2)}, u32[]{:S(2)}) collective-permute-start(bf16[2,1,4,128]{3,2,1,0:T(4,128)(2,1)S(1)} %copy.34), channel_id=1, source_target_pairs={{2,0},{0,2},{3,1},{1,3},{6,4},{4,6},{7,5},{5,7},{10,8},{8,10},{11,... | collective-permute-start | bytes 6152 | tf_op jit(solution)/shard_map/while/body/eval_jaxpr/ppermute | solution.py:30
  39.4 4.4 %collective-permute-start = (bf16[1,256,128]{1,2,0:T(8,128)(2,1)S(1)}, bf16[1,256,128]{1,2,0:T(8,128)(2,1)S(1)}, u32[]{:S(2)}, u32[]{:S(2)}) collective-permute-start(bf16[1,256,128]{1,2,0:T(8,128)(2,1)S(1)} %fusion.66), channel_id=1, source_target_pairs={{1,0},{3,2},{5,4},{7,6},{9,8},{11,10},{13,12},{15,14},{17,16},{19,... | collective-permute-start | bytes 196616 | tf_op jit(solution)/shard_map/while/body/eval_jaxpr/ppermute | solution.py:17
  40.7 3.9 %collective-permute-start.1 = (bf16[1,256,128]{1,2,0:T(8,128)(2,1)S(1)}, bf16[1,256,128]{1,2,0:T(8,128)(2,1)S(1)}, u32[]{:S(2)}, u32[]{:S(2)}) collective-permute-start(bf16[1,256,128]{1,2,0:T(8,128)(2,1)S(1)} %fusion.66), channel_id=1, source_target_pairs={{0,1},{2,3},{4,5},{6,7},{8,9},{10,11},{12,13},{14,15},{16,17},{18,... | collective-permute-start | bytes 196616 | tf_op jit(solution)/shard_map/while/body/eval_jaxpr/ppermute | solution.py:16
  44.6 1.3 copy-start.1
  45.6 1.1 copy-start.2
  47.0 5.7 %collective-permute-start.2 = (bf16[1,256,128]{1,2,0:T(8,128)(2,1)S(1)}, bf16[1,256,128]{1,2,0:T(8,128)(2,1)S(1)}, u32[]{:S(2)}, u32[]{:S(2)}) collective-permute-start(bf16[1,256,128]{1,2,0:T(8,128)(2,1)S(1)} %get-tuple-element.591), channel_id=1, source_target_pairs={{2,0},{0,2},{3,1},{1,3},{6,4},{4,6},{7,5},{5,7},{10,8},{8,10},{11,... | collective-permute-start | bytes 196616 | tf_op jit(solution)/shard_map/while/body/eval_jaxpr/ppermute | solution.py:30
  47.3 5.4 %collective-permute-start.3 = (bf16[1,77,128]{2,1,0:T(8,128)(2,1)S(1)}, bf16[1,77,128]{2,1,0:T(8,128)(2,1)S(1)}, u32[]{:S(2)}, u32[]{:S(2)}) collective-permute-start(bf16[1,77,128]{2,1,0:T(8,128)(2,1)S(1)} %fusion.65), channel_id=1, source_target_pairs={{2,0},{0,2},{3,1},{1,3},{6,4},{4,6},{7,5},{5,7},{10,8},{8,10},{11,... | collective-permute-start | bytes 59144 | tf_op jit(solution)/shard_map/while/body/eval_jaxpr/ppermute | solution.py:30
  49.1 3.6 %collective-permute-start.4 = (bf16[2,1,4,128]{3,2,1,0:T(4,128)(2,1)S(1)}, bf16[2,1,4,128]{3,2,1,0:T(4,128)(2,1)S(1)}, u32[]{:S(2)}, u32[]{:S(2)}) collective-permute-start(bf16[2,1,4,128]{3,2,1,0:T(4,128)(2,1)S(1)} %copy.34), channel_id=1, source_target_pairs={{2,0},{0,2},{3,1},{1,3},{6,4},{4,6},{7,5},{5,7},{10,8},{8,10},{11,... | collective-permute-start | bytes 6152 | tf_op jit(solution)/shard_map/while/body/eval_jaxpr/ppermute | solution.py:30
  54.7 4.4 %collective-permute-start = (bf16[1,256,128]{1,2,0:T(8,128)(2,1)S(1)}, bf16[1,256,128]{1,2,0:T(8,128)(2,1)S(1)}, u32[]{:S(2)}, u32[]{:S(2)}) collective-permute-start(bf16[1,256,128]{1,2,0:T(8,128)(2,1)S(1)} %fusion.66), channel_id=1, source_target_pairs={{1,0},{3,2},{5,4},{7,6},{9,8},{11,10},{13,12},{15,14},{17,16},{19,... | collective-permute-start | bytes 196616 | tf_op jit(solution)/shard_map/while/body/eval_jaxpr/ppermute | solution.py:17
  56.0 3.9 %collective-permute-start.1 = (bf16[1,256,128]{1,2,0:T(8,128)(2,1)S(1)}, bf16[1,256,128]{1,2,0:T(8,128)(2,1)S(1)}, u32[]{:S(2)}, u32[]{:S(2)}) collective-permute-start(bf16[1,256,128]{1,2,0:T(8,128)(2,1)S(1)} %fusion.66), channel_id=1, source_target_pairs={{0,1},{2,3},{4,5},{6,7},{8,9},{10,11},{12,13},{14,15},{16,17},{18,... | collective-permute-start | bytes 196616 | tf_op jit(solution)/shard_map/while/body/eval_jaxpr/ppermute | solution.py:16
  60.0 1.3 copy-start.1
  61.0 1.1 copy-start.2
  62.4 5.7 %collective-permute-start.2 = (bf16[1,256,128]{1,2,0:T(8,128)(2,1)S(1)}, bf16[1,256,128]{1,2,0:T(8,128)(2,1)S(1)}, u32[]{:S(2)}, u32[]{:S(2)}) collective-permute-start(bf16[1,256,128]{1,2,0:T(8,128)(2,1)S(1)} %get-tuple-element.591), channel_id=1, source_target_pairs={{2,0},{0,2},{3,1},{1,3},{6,4},{4,6},{7,5},{5,7},{10,8},{8,10},{11,... | collective-permute-start | bytes 196616 | tf_op jit(solution)/shard_map/while/body/eval_jaxpr/ppermute | solution.py:30
  62.7 5.4 %collective-permute-start.3 = (bf16[1,77,128]{2,1,0:T(8,128)(2,1)S(1)}, bf16[1,77,128]{2,1,0:T(8,128)(2,1)S(1)}, u32[]{:S(2)}, u32[]{:S(2)}) collective-permute-start(bf16[1,77,128]{2,1,0:T(8,128)(2,1)S(1)} %fusion.65), channel_id=1, source_target_pairs={{2,0},{0,2},{3,1},{1,3},{6,4},{4,6},{7,5},{5,7},{10,8},{8,10},{11,... | collective-permute-start | bytes 59144 | tf_op jit(solution)/shard_map/while/body/eval_jaxpr/ppermute | solution.py:30
  64.5 3.6 %collective-permute-start.4 = (bf16[2,1,4,128]{3,2,1,0:T(4,128)(2,1)S(1)}, bf16[2,1,4,128]{3,2,1,0:T(4,128)(2,1)S(1)}, u32[]{:S(2)}, u32[]{:S(2)}) collective-permute-start(bf16[2,1,4,128]{3,2,1,0:T(4,128)(2,1)S(1)} %copy.34), channel_id=1, source_target_pairs={{2,0},{0,2},{3,1},{1,3},{6,4},{4,6},{7,5},{5,7},{10,8},{8,10},{11,... | collective-permute-start | bytes 6152 | tf_op jit(solution)/shard_map/while/body/eval_jaxpr/ppermute | solution.py:30
  70.0 4.4 %collective-permute-start = (bf16[1,256,128]{1,2,0:T(8,128)(2,1)S(1)}, bf16[1,256,128]{1,2,0:T(8,128)(2,1)S(1)}, u32[]{:S(2)}, u32[]{:S(2)}) collective-permute-start(bf16[1,256,128]{1,2,0:T(8,128)(2,1)S(1)} %fusion.66), channel_id=1, source_target_pairs={{1,0},{3,2},{5,4},{7,6},{9,8},{11,10},{13,12},{15,14},{17,16},{19,... | collective-permute-start | bytes 196616 | tf_op jit(solution)/shard_map/while/body/eval_jaxpr/ppermute | solution.py:17
  71.3 3.9 %collective-permute-start.1 = (bf16[1,256,128]{1,2,0:T(8,128)(2,1)S(1)}, bf16[1,256,128]{1,2,0:T(8,128)(2,1)S(1)}, u32[]{:S(2)}, u32[]{:S(2)}) collective-permute-start(bf16[1,256,128]{1,2,0:T(8,128)(2,1)S(1)} %fusion.66), channel_id=1, source_target_pairs={{0,1},{2,3},{4,5},{6,7},{8,9},{10,11},{12,13},{14,15},{16,17},{18,... | collective-permute-start | bytes 196616 | tf_op jit(solution)/shard_map/while/body/eval_jaxpr/ppermute | solution.py:16
  75.3 1.3 copy-start.1
  76.3 1.1 copy-start.2
  77.7 5.7 %collective-permute-start.2 = (bf16[1,256,128]{1,2,0:T(8,128)(2,1)S(1)}, bf16[1,256,128]{1,2,0:T(8,128)(2,1)S(1)}, u32[]{:S(2)}, u32[]{:S(2)}) collective-permute-start(bf16[1,256,128]{1,2,0:T(8,128)(2,1)S(1)} %get-tuple-element.591), channel_id=1, source_target_pairs={{2,0},{0,2},{3,1},{1,3},{6,4},{4,6},{7,5},{5,7},{10,8},{8,10},{11,... | collective-permute-start | bytes 196616 | tf_op jit(solution)/shard_map/while/body/eval_jaxpr/ppermute | solution.py:30
  78.0 5.4 %collective-permute-start.3 = (bf16[1,77,128]{2,1,0:T(8,128)(2,1)S(1)}, bf16[1,77,128]{2,1,0:T(8,128)(2,1)S(1)}, u32[]{:S(2)}, u32[]{:S(2)}) collective-permute-start(bf16[1,77,128]{2,1,0:T(8,128)(2,1)S(1)} %fusion.65), channel_id=1, source_target_pairs={{2,0},{0,2},{3,1},{1,3},{6,4},{4,6},{7,5},{5,7},{10,8},{8,10},{11,... | collective-permute-start | bytes 59144 | tf_op jit(solution)/shard_map/while/body/eval_jaxpr/ppermute | solution.py:30
  79.8 3.6 %collective-permute-start.4 = (bf16[2,1,4,128]{3,2,1,0:T(4,128)(2,1)S(1)}, bf16[2,1,4,128]{3,2,1,0:T(4,128)(2,1)S(1)}, u32[]{:S(2)}, u32[]{:S(2)}) collective-permute-start(bf16[2,1,4,128]{3,2,1,0:T(4,128)(2,1)S(1)} %copy.34), channel_id=1, source_target_pairs={{2,0},{0,2},{3,1},{1,3},{6,4},{4,6},{7,5},{5,7},{10,8},{8,10},{11,... | collective-permute-start | bytes 6152 | tf_op jit(solution)/shard_map/while/body/eval_jaxpr/ppermute | solution.py:30
  85.4 4.4 %collective-permute-start = (bf16[1,256,128]{1,2,0:T(8,128)(2,1)S(1)}, bf16[1,256,128]{1,2,0:T(8,128)(2,1)S(1)}, u32[]{:S(2)}, u32[]{:S(2)}) collective-permute-start(bf16[1,256,128]{1,2,0:T(8,128)(2,1)S(1)} %fusion.66), channel_id=1, source_target_pairs={{1,0},{3,2},{5,4},{7,6},{9,8},{11,10},{13,12},{15,14},{17,16},{19,... | collective-permute-start | bytes 196616 | tf_op jit(solution)/shard_map/while/body/eval_jaxpr/ppermute | solution.py:17
  86.7 3.9 %collective-permute-start.1 = (bf16[1,256,128]{1,2,0:T(8,128)(2,1)S(1)}, bf16[1,256,128]{1,2,0:T(8,128)(2,1)S(1)}, u32[]{:S(2)}, u32[]{:S(2)}) collective-permute-start(bf16[1,256,128]{1,2,0:T(8,128)(2,1)S(1)} %fusion.66), channel_id=1, source_target_pairs={{0,1},{2,3},{4,5},{6,7},{8,9},{10,11},{12,13},{14,15},{16,17},{18,... | collective-permute-start | bytes 196616 | tf_op jit(solution)/shard_map/while/body/eval_jaxpr/ppermute | solution.py:16
  90.7 6.5 %collective-permute-start.2 = (bf16[1,256,128]{1,2,0:T(8,128)(2,1)S(1)}, bf16[1,256,128]{1,2,0:T(8,128)(2,1)S(1)}, u32[]{:S(2)}, u32[]{:S(2)}) collective-permute-start(bf16[1,256,128]{1,2,0:T(8,128)(2,1)S(1)} %get-tuple-element.591), channel_id=1, source_target_pairs={{2,0},{0,2},{3,1},{1,3},{6,4},{4,6},{7,5},{5,7},{10,8},{8,10},{11,... | collective-permute-start | bytes 196616 | tf_op jit(solution)/shard_map/while/body/eval_jaxpr/ppermute | solution.py:30
  93.3 3.8 %collective-permute-start.3 = (bf16[1,77,128]{2,1,0:T(8,128)(2,1)S(1)}, bf16[1,77,128]{2,1,0:T(8,128)(2,1)S(1)}, u32[]{:S(2)}, u32[]{:S(2)}) collective-permute-start(bf16[1,77,128]{2,1,0:T(8,128)(2,1)S(1)} %fusion.65), channel_id=1, source_target_pairs={{2,0},{0,2},{3,1},{1,3},{6,4},{4,6},{7,5},{5,7},{10,8},{8,10},{11,... | collective-permute-start | bytes 59144 | tf_op jit(solution)/shard_map/while/body/eval_jaxpr/ppermute | solution.py:30
  93.4 3.7 %collective-permute-start.4 = (bf16[2,1,4,128]{3,2,1,0:T(4,128)(2,1)S(1)}, bf16[2,1,4,128]{3,2,1,0:T(4,128)(2,1)S(1)}, u32[]{:S(2)}, u32[]{:S(2)}) collective-permute-start(bf16[2,1,4,128]{3,2,1,0:T(4,128)(2,1)S(1)} %copy.34), channel_id=1, source_target_pairs={{2,0},{0,2},{3,1},{1,3},{6,4},{4,6},{7,5},{5,7},{10,8},{8,10},{11,... | collective-permute-start | bytes 6152 | tf_op jit(solution)/shard_map/while/body/eval_jaxpr/ppermute | solution.py:30
  99.1 4.4 %collective-permute-start = (bf16[1,256,128]{1,2,0:T(8,128)(2,1)S(1)}, bf16[1,256,128]{1,2,0:T(8,128)(2,1)S(1)}, u32[]{:S(2)}, u32[]{:S(2)}) collective-permute-start(bf16[1,256,128]{1,2,0:T(8,128)(2,1)S(1)} %fusion.66), channel_id=1, source_target_pairs={{1,0},{3,2},{5,4},{7,6},{9,8},{11,10},{13,12},{15,14},{17,16},{19,... | collective-permute-start | bytes 196616 | tf_op jit(solution)/shard_map/while/body/eval_jaxpr/ppermute | solution.py:17
  100.4 3.9 %collective-permute-start.1 = (bf16[1,256,128]{1,2,0:T(8,128)(2,1)S(1)}, bf16[1,256,128]{1,2,0:T(8,128)(2,1)S(1)}, u32[]{:S(2)}, u32[]{:S(2)}) collective-permute-start(bf16[1,256,128]{1,2,0:T(8,128)(2,1)S(1)} %fusion.66), channel_id=1, source_target_pairs={{0,1},{2,3},{4,5},{6,7},{8,9},{10,11},{12,13},{14,15},{16,17},{18,... | collective-permute-start | bytes 196616 | tf_op jit(solution)/shard_map/while/body/eval_jaxpr/ppermute | solution.py:16
  104.4 5.7 %collective-permute-start.2 = (bf16[1,256,128]{1,2,0:T(8,128)(2,1)S(1)}, bf16[1,256,128]{1,2,0:T(8,128)(2,1)S(1)}, u32[]{:S(2)}, u32[]{:S(2)}) collective-permute-start(bf16[1,256,128]{1,2,0:T(8,128)(2,1)S(1)} %get-tuple-element.591), channel_id=1, source_target_pairs={{2,0},{0,2},{3,1},{1,3},{6,4},{4,6},{7,5},{5,7},{10,8},{8,10},{11,... | collective-permute-start | bytes 196616 | tf_op jit(solution)/shard_map/while/body/eval_jaxpr/ppermute | solution.py:30
  106.3 3.8 %collective-permute-start.3 = (bf16[1,77,128]{2,1,0:T(8,128)(2,1)S(1)}, bf16[1,77,128]{2,1,0:T(8,128)(2,1)S(1)}, u32[]{:S(2)}, u32[]{:S(2)}) collective-permute-start(bf16[1,77,128]{2,1,0:T(8,128)(2,1)S(1)} %fusion.65), channel_id=1, source_target_pairs={{2,0},{0,2},{3,1},{1,3},{6,4},{4,6},{7,5},{5,7},{10,8},{8,10},{11,... | collective-permute-start | bytes 59144 | tf_op jit(solution)/shard_map/while/body/eval_jaxpr/ppermute | solution.py:30
  106.5 3.6 %collective-permute-start.4 = (bf16[2,1,4,128]{3,2,1,0:T(4,128)(2,1)S(1)}, bf16[2,1,4,128]{3,2,1,0:T(4,128)(2,1)S(1)}, u32[]{:S(2)}, u32[]{:S(2)}) collective-permute-start(bf16[2,1,4,128]{3,2,1,0:T(4,128)(2,1)S(1)} %copy.34), channel_id=1, source_target_pairs={{2,0},{0,2},{3,1},{1,3},{6,4},{4,6},{7,5},{5,7},{10,8},{8,10},{11,... | collective-permute-start | bytes 6152 | tf_op jit(solution)/shard_map/while/body/eval_jaxpr/ppermute | solution.py:30
where the time goes:
time: 129 us; the launch traced here: 128 us
  starting transfers between devices  43.7 us (34%)
  blocking collectives  29.7 us (23%)
  waiting for transfers between devices  22.4 us (17%)
  matrix products  17 us (13%)
  local copies, waits for them, and re-layouts  7.54 us (6%)
  other arithmetic  3.66 us (3%)
  between operations  2.62 us (2%)
    ppermute x6, starting transfers between devices, padded_2(): before = lax.ppermute(last, axis, up)  18.2 us
    ppermute x18, starting transfers between devices, passed_along(): return lax.ppermute(block, axis, route)  17.8 us
    ppermute x18, waiting for transfers between devices, passed_along(): return lax.ppermute(block, axis, route)  17.2 us
    psum x1, blocking collectives, per_device(): lax.psum(ocean_state.astype(jnp.float32).astype(jnp.bfloat16), 'members')  16.2 us
    psum x1, blocking collectives, from_root(): return lax.psum(jnp.where(mine, array, jnp.zeros_like(array)), axis)  13.4 us
    ppermute x6, starting transfers between devices, padded_2(): after = lax.ppermute(initial, axis, down)  7.75 us
    dot_general x6, matrix products, encode(): jnp.einsum('ok,lkx->lox', encode_weight, inputs, preferred_element_type=j...  5.99 us
    dot_general x6, matrix products, decode(): jnp.einsum('ok,lkx->lox', decode_weight, hidden, preferred_element_type=j...  5.64 us
  transfers between devices with their start and end apart: 30, of which 12 were waited for; matrix products, arithmetic and copies ran while one was open for 0% of the time, Pallas kernels for 0%

commit v1 on v0

v1 whole, which is shorter than its diff:
```python
import functools

import jax
import jax.numpy as jnp
from jax import lax
from jax.experimental import pallas as pl
from jax.experimental.pallas import tpu as pltpu
from jax.sharding import PartitionSpec as P

BF16_ROWS = 16


def padded_rows(count):
    return -(-count // BF16_ROWS) * BF16_ROWS


def passed_along(block, axis, distance):
    size = lax.axis_size(axis)
    return lax.ppermute(block, axis, [(i, (i + distance) % size) for i in range(size)])


def all_along(block, axis):
    return [block] + [passed_along(block, axis, k) for k in range(1, lax.axis_size(axis))]


def in_order(parts, axis):
    size, here = lax.axis_size(axis), lax.axis_index(axis)
    ordered = []
    for place in range(size):
        chosen = parts[0]
        for k in range(1, size):
            chosen = jnp.where((here - k) % size == place, parts[k], chosen)
        ordered.append(chosen)
    return ordered


def window_kernel(dims, place_ref, field_ref, scale_ref, shift_ref, gain_ref, enc_ref, dec_ref, *rest):
    steps, layers, bands, lat, members, lon, chans, vp, fp = dims
    blocks = rest[: 2 + (layers - 1) * bands]
    final_ref, mean_ref, weights, taps, hidden, conv, act, inputs, total, sems = rest[len(blocks):]
    here, band = place_ref[0], place_ref[1]
    taps_wide = 9 * chans
    part = chans // bands

    pltpu.make_async_copy(blocks[0], weights.at[here, :, pl.ds(0, taps_wide)], sems.at[here]).start()
    pltpu.make_async_copy(blocks[1], weights.at[here, :, pl.ds(taps_wide, chans)], sems.at[here]).start()
    for k in range(1, layers):
        slot = lax.rem(here - k + layers, layers)
        for j in range(bands):
            first = pl.multiple_of(lax.rem(band - j + bands, bands) * part, part)
            pltpu.make_async_copy(
                blocks[2 + (k - 1) * bands + j], weights.at[slot, pl.ds(first, part), :], sems.at[slot]
            ).start()

    def columns(m):
        return slice(m * lon, (m + 1) * lon)

    lane = lax.broadcasted_iota(jnp.int32, (chans, lon), 1)
    land = [field_ref[i, vp + fp * steps : vp + fp * steps + 1, :].astype(jnp.float32) for i in range(lat)]

    def encode(step, turn):
        enc = enc_ref[...]
        for i in range(lat):
            force = field_ref[i, vp + fp * step : vp + fp * (step + 1), :]
            if step == 0:
                fed = jnp.concatenate([field_ref[i, 0:vp, :], force], axis=0)
                shared = jnp.dot(enc, fed, preferred_element_type=jnp.float32)
            else:
                for m in range(members):
                    inputs[i, vp : vp + fp, columns(m)] = force
                lifted = jnp.dot(enc, inputs[i], preferred_element_type=jnp.float32)
            for m in range(members):
                value = shared if step == 0 else lifted[:, columns(m)]
                value = land[i] * (value * scale_ref[turn, :, m : m + 1] + shift_ref[turn, :, m : m + 1])
                hidden[i, :, columns(m)] = value.astype(jnp.bfloat16)

    def block(layer, not_yet):
        spacing = 2 ** (layer % 3)
        for i in range(lat):
            for m in range(members):
                value = hidden[i, :, columns(m)]
                base = 3 * chans * i
                zero = jnp.zeros_like(value)
                before = jnp.where(lane >= spacing, pltpu.roll(value, spacing, 1), zero)
                after = jnp.where(lane < lon - spacing, pltpu.roll(value, lon - spacing, 1), zero)
                taps[base : base + chans, columns(m)] = before
                taps[base + chans : base + 2 * chans, columns(m)] = value
                taps[base + 2 * chans : base + 3 * chans, columns(m)] = after
        if not_yet is not None:
            @pl.when(not_yet)
            def _():
                pltpu.make_async_copy(weights.at[layer], weights.at[layer], sems.at[layer]).wait()
        wide = 3 * chans
        for i in range(lat):
            low, high = max(i - 1, 0), min(i + 1, lat - 1)
            conv[i] = jnp.dot(
                weights[layer, :, (low - i + 1) * wide : (high - i + 2) * wide],
                taps[low * wide : (high + 1) * wide, :],
                preferred_element_type=jnp.float32,
            )
        gain = gain_ref[:, layer : layer + 1]
        for i in range(lat):
            for m in range(members):
                value = conv[i, :, columns(m)]
                centred = value - jnp.mean(value, axis=0, keepdims=True)
                spread = jnp.mean(centred * centred, axis=0, keepdims=True)
                normed = centred * lax.rsqrt(spread + 1e-05) * gain
                act[i, :, columns(m)] = jax.nn.gelu(normed).astype(jnp.bfloat16)
        for i in range(lat):
            mixed = jnp.dot(
                weights[layer, :, taps_wide:], act[i], preferred_element_type=jnp.float32
            )
            for m in range(members):
                kept = hidden[i, :, columns(m)].astype(jnp.float32)
                hidden[i, :, columns(m)] = (land[i] * (kept + mixed[:, columns(m)])).astype(jnp.bfloat16)

    varied = final_ref.shape[1]
    local = final_ref.shape[0]

    def window(turn, first):
        for step in range(steps):
            encode(step, turn)
            for layer in range(layers):
                block(layer, first if step == 0 else None)
            for i in range(lat):
                change = jnp.dot(dec_ref[...], hidden[i], preferred_element_type=jnp.float32)
                for m in range(members):
                    old = field_ref[i, 0:vp, :] if step == 0 else inputs[i, 0:vp, columns(m)]
                    new = old.astype(jnp.float32) + land[i] * change[:, columns(m)]
                    inputs[i, 0:vp, columns(m)] = new.astype(jnp.bfloat16)
        for i in range(local):
            row = band * local + i
            summed = inputs[row, 0:vp, columns(0)].astype(jnp.float32)
            for m in range(1, members):
                summed = summed + inputs[row, 0:vp, columns(m)].astype(jnp.float32)
            if turns == 1:
                total[i] = summed
            else:
                total[i] = jnp.where(first, summed, total[i] + summed)

            @pl.when(first)
            def _():
                final_ref[i] = inputs[row, 0:varied, columns(0)]

    turns = scale_ref.shape[0]
    if turns == 1:
        window(0, True)
    else:
        lax.fori_loop(0, turns, lambda turn, _: window(turn, turn == 0), None)
    for i in range(local):
        mean_ref[i] = total[i, 0:varied] * (1.0 / (members * turns))


def per_device(
    init_state,
    forcing_slots,
    atmos_owner,
    land_mask,
    param_index,
    settings,
    scale_weight,
    shift_weight,
    encode_weight,
    conv_weight,
    point_weight,
    norm_gain,
    decode_weight,
):
    members, layers, bands = (lax.axis_size(a) for a in ("members", "segment", "rows"))
    here, band = lax.axis_index("segment"), lax.axis_index("rows")
    _, local, varied, lon = init_state.shape
    steps, forced = forcing_slots.shape[2], forcing_slots.shape[4]
    chans = conv_weight.shape[1]
    lat = local * bands
    vp, fp = padded_rows(varied), padded_rows(forced)
    part = chans // bands

    mine = jnp.concatenate([conv_weight[0], point_weight[0]], axis=1)
    mine = lax.dynamic_slice_in_dim(mine, band * part, part, 0)
    sections = all_along(mine, "segment")[1:]
    gains = in_order(all_along(norm_gain.astype(jnp.float32), "segment"), "segment")
    gain = jnp.concatenate(gains, axis=0).T

    slots = forcing_slots[0, 0].astype(jnp.float32).reshape(-1, lon)
    index_row = jnp.broadcast_to(param_index.astype(jnp.float32)[:, None], (1, lon))
    group = all_along(jnp.concatenate([slots, index_row], axis=0), "members")
    member = lax.axis_index("members")
    forcing = jnp.zeros((steps, slots.shape[0] // steps, lon), jnp.float32)
    for k in range(members):
        owned = (atmos_owner[0] == (member - k) % members)[:, None, None]
        forcing = jnp.where(owned, group[k][:-1].reshape(forcing.shape), forcing)
    forcing = forcing.reshape(steps, local, forced, lon).astype(jnp.bfloat16)

    picked = jnp.stack([g[-1, 0] for g in group])
    choose = (jnp.arange(settings.shape[0], dtype=jnp.float32)[None] == picked[:, None]).astype(jnp.float32)
    rows = jnp.dot(choose, settings, precision=lax.Precision.HIGHEST)
    scale = 1.0 + jnp.dot(scale_weight.T, rows.T, precision=lax.Precision.HIGHEST)
    shift = jnp.dot(shift_weight.T, rows.T, precision=lax.Precision.HIGHEST)

    rim = ((0, 0), (0, fp - forced), (0, 0))
    field = [jnp.pad(init_state[0], ((0, 0), (0, vp - varied), (0, 0)))]
    field += [jnp.pad(forcing[t], rim) for t in range(steps)]
    field += [jnp.broadcast_to(land_mask.astype(jnp.bfloat16)[:, None, :], (local, BF16_ROWS, lon))]
    field = jnp.concatenate(field, axis=1)
    field = jnp.concatenate(in_order(all_along(field, "rows"), "rows"), axis=0)

    enc = jnp.pad(encode_weight[:, :varied], ((0, 0), (0, vp - varied)))
    enc = jnp.concatenate([enc, jnp.pad(encode_weight[:, varied:], ((0, 0), (0, fp - forced)))], axis=1)
    dec = jnp.pad(decode_weight, ((0, vp - varied), (0, 0)))

    blocks = [conv_weight[0], point_weight[0]]
    for section in sections:
        blocks += all_along(section, "rows")

    place = jnp.stack([here, band]).astype(jnp.int32)
    at_once = next(n for n in (4, 2, 1) if members % n == 0)
    scale, shift = (a.reshape(chans, -1, at_once).swapaxes(0, 1) for a in (scale, shift))
    dims = (steps, layers, bands, lat, at_once, lon, chans, vp, fp)
    wide = at_once * lon
    vmem = pl.BlockSpec(memory_space=pltpu.VMEM)
    final, mean = pl.pallas_call(
        functools.partial(window_kernel, dims),
        out_shape=(
            jax.ShapeDtypeStruct((local, varied, lon), jnp.bfloat16),
            jax.ShapeDtypeStruct((local, varied, lon), jnp.float32),
        ),
        in_specs=[pl.BlockSpec(memory_space=pltpu.SMEM)]
        + [vmem] * 6
        + [pl.BlockSpec(memory_space=pl.ANY)] * len(blocks),
        out_specs=(vmem, vmem),
        scratch_shapes=[
            pltpu.VMEM((layers, chans, 10 * chans), jnp.bfloat16),
            pltpu.VMEM((lat * 3 * chans, wide), jnp.bfloat16),
            pltpu.VMEM((lat, chans, wide), jnp.bfloat16),
            pltpu.VMEM((lat, chans, wide), jnp.float32),
            pltpu.VMEM((lat, chans, wide), jnp.bfloat16),
            pltpu.VMEM((lat, vp + fp, wide), jnp.bfloat16),
            pltpu.VMEM((local, vp, lon), jnp.float32),
            pltpu.SemaphoreType.DMA((layers,)),
        ],
        compiler_params=pltpu.CompilerParams(vmem_limit_bytes=40 * 1024 * 1024),
    )(place, field, scale, shift, gain, enc, dec, *blocks)
    return final[None, None], mean[None]


def solution(mesh):
    in_specs = (
        P(("groups", "segment"), "rows", None, None),
        P("members", ("groups", "segment"), None, "rows", None, None),
        P(("groups", "segment"), None),
        P(("groups", "rows"), None),
        P(("groups", "members")),
        P(),
        P(),
        P(),
        P(),
        P("segment", None, None),
        P("segment", None, None),
        P("segment", None),
        P(),
    )
    out_specs = (
        P("members", ("groups", "segment"), "rows", None, None),
        P(("groups", "segment"), "rows", None, None),
    )
    return jax.shard_map(
        per_device, mesh=mesh, in_specs=in_specs, out_specs=out_specs, check_vma=False
    )
```

time: 129 us -> 41.8 us (0.32)
  starting transfers between devices: 43.7 us -> 9.13 us
  blocking collectives: 29.7 us -> 0 us
  matrix products: 17 us -> 0.98 us
  waiting for transfers between devices: 22.4 us -> 11.1 us
  Pallas kernels: 0 us -> 10.9 us
  local copies, waits for them, and re-layouts: 7.54 us -> 2.76 us
    ppermute x30 -> x7, starting transfers between devices: 43.7 us -> 9.13 us  [passed_along(): lax.ppermute(block, axis, [(i, (i + distance) % size) for i in range(size)])]
    psum x2 -> x0, blocking collectives: 29.7 us -> none  [the longest x1 16.2 us: per_device(): lax.psum(ocean_state.astype(jnp.float32).astype(jnp.bfloat16), 'members')]
    dot_general x23 -> x3, matrix products: 17 us -> 0.98 us  [the longest x1 0.4 us: per_device(): jnp.dot(scale_weight.T, rows.T, precision=lax.Precision.HIGHEST)]
    ppermute x30 -> x7, waiting for transfers between devices: 22.4 us -> 11.1 us  [passed_along(): lax.ppermute(block, axis, [(i, (i + distance) % size) for i in range(size)])]
    pallas_call x0 -> x1, Pallas kernels: none -> 10.9 us  [per_device(): pl.pallas_call(functools.partial(window_kernel, dims), out_shape=(jax.Sha...]
    cond x48 -> x0, local copies, waits for them, and re-layouts: 2.91 us -> none
    convert_element_type x4 -> x3, other arithmetic: 0.01 us -> 1.45 us  [the longest x1 0.69 us: per_device(): slots = forcing_slots[0, 0].astype(jnp.float32).reshape(-1, lon)]
    another operation x2, other arithmetic: 0.72 us -> 2.12 us  [the longest x1 2.04 us: per_device(): picked = jnp.stack([g[-1, 0] for g in group])]
  transfers between devices with their start and end apart: 30 -> 7, of which waited for: 12 -> 2; matrix products, arithmetic and copies ran while one was open for 0% -> 17% of each run, Pallas kernels for 0% -> 0%
where the time goes in v1:
time: 41.8 us; the launch traced here: 41.6 us
  waiting for transfers between devices  11.1 us (27%)
  Pallas kernels  10.9 us (26%)
  starting transfers between devices  9.13 us (22%)
  other arithmetic  4.9 us (12%)
  local copies, waits for them, and re-layouts  2.76 us (7%)
  between operations  1.72 us (4%)
  matrix products  0.98 us (2%)
    ppermute x7, waiting for transfers between devices, passed_along(): lax.ppermute(block, axis, [(i, (i + distance) % size) for i in range(size)])  11.1 us
    pallas_call x1, Pallas kernels, per_device(): pl.pallas_call(functools.partial(window_kernel, dims), out_shape=(jax.Sha...  10.9 us
    ppermute x7, starting transfers between devices, passed_along(): lax.ppermute(block, axis, [(i, (i + distance) % size) for i in range(size)])  9.13 us
    another operation x1, other arithmetic, per_device(): picked = jnp.stack([g[-1, 0] for g in group])  2.04 us
    slice x3, local copies, waits for them, and re-layouts, per_device(): picked = jnp.stack([g[-1, 0] for g in group])  1.6 us
    concatenate x1, other arithmetic, per_device(): mine = jnp.concatenate([conv_weight[0], point_weight[0]], axis=1)  1.16 us
    unnamed x29, local copies, waits for them, and re-layouts  0.99 us
  transfers between devices with their start and end apart: 7, of which 2 were waited for; matrix products, arithmetic and copies ran while one was open for 17% of the time, Pallas kernels for 0%

profile of v1, /device:TPU:0, one launch (start us, length us, event | category | flops | bytes accessed | tf_op | source)
XLA Modules:
  0.0 41.6 jit_solution(7150526747270116612)
XLA Ops:
  0.6 0.0 copy-start
  0.6 0.0 copy-start.3
  0.7 0.0 slice-start
  0.7 0.0 copy-start.12
  1.3 0.7 %bitcast_convert_fusion = f32[1,1,2,1,4,128]{5,4,2,3,1,0:T(4,128)S(1)} fusion(bf16[1,1,2,1,4,128]{5,4,3,2,1,0:T(4,128)(2,1)} %param.14), kind=kLoop, calls=%fused_computation.32 | loop fusion | flops 1024 | bytes 6144 | tf_op jit(solution)/shard_map/convert_element_type | solution.py:184
  2.0 3.0 %collective-permute-start.2 = (f32[9,128]{1,0:T(8,128)S(1)}, f32[9,128]{1,0:T(8,128)S(1)}, u32[]{:S(2)}, u32[]{:S(2)}) collective-permute-start(f32[9,128]{1,0:T(8,128)S(1)} %concatenate.18), channel_id=1, source_target_pairs={{0,4},{4,8},{8,12},{12,0},{1,5},{5,9},{9,13},{13,1},{2,6},{6,10},{... | collective-permute-start | bytes 13832 | tf_op jit(solution)/shard_map/ppermute | solution.py:19
  5.1 2.6 %collective-permute-start.1 = (f32[9,128]{1,0:T(8,128)S(1)}, f32[9,128]{1,0:T(8,128)S(1)}, u32[]{:S(2)}, u32[]{:S(2)}) collective-permute-start(f32[9,128]{1,0:T(8,128)S(1)} %concatenate.18), channel_id=1, source_target_pairs={{0,8},{4,12},{8,0},{12,4},{1,9},{5,13},{9,1},{13,5},{2,10},{6,14},... | collective-permute-start | bytes 13832 | tf_op jit(solution)/shard_map/ppermute | solution.py:19
  7.6 1.3 %collective-permute-start = (f32[9,128]{1,0:T(8,128)S(1)}, f32[9,128]{1,0:T(8,128)S(1)}, u32[]{:S(2)}, u32[]{:S(2)}) collective-permute-start(f32[9,128]{1,0:T(8,128)S(1)} %concatenate.18), channel_id=1, source_target_pairs={{0,12},{4,0},{8,4},{12,8},{1,13},{5,1},{9,5},{13,9},{2,14},{6,2},{... | collective-permute-start | bytes 13832 | tf_op jit(solution)/shard_map/ppermute | solution.py:19
  9.0 0.7 %convert_element_type.61 = f32[1,256]{1,0:T(1,128)S(1)} convert(bf16[1,256]{1,0:T(2,128)(2,1)} %param.24) | non-fusion elementwise | flops 256 | bytes 1536 | tf_op jit(solution)/shard_map/convert_element_type | solution.py:181
  9.7 1.5 %collective-permute-start.4 = (f32[1,256]{1,0:T(1,128)S(1)}, f32[1,256]{1,0:T(1,128)S(1)}, u32[]{:S(2)}, u32[]{:S(2)}) collective-permute-start(f32[1,256]{1,0:T(1,128)S(1)} %convert_element_type.61), channel_id=1, source_target_pairs={{0,2},{2,0},{1,3},{3,1},{4,6},{6,4},{5,7},{7,5},{8,10},{10,8},{9,1... | collective-permute-start | bytes 3080 | tf_op jit(solution)/shard_map/ppermute | solution.py:19
  11.2 0.0 copy-start.7
  11.2 0.0 copy-start.4
  11.2 0.0 copy-start.11
  11.2 0.0 copy-start.6
  11.2 1.2 %fusion.1 = bf16[128,2560]{1,0:T(8,128)(2,1)S(1)} fusion(s32[]{:T(128)S(6)} %select_n.121, bf16[256,2304]{1,0:T(8,128)(2,1)} %bitcast.57, bf16[256,256]{1,0:T(8,128)(2,1)} %bitcast.59), kind=kLoop, calls=%fused_computation.5 | loop fusion | flops 1310720 | bytes 1966084 | tf_op jit(solution)/shard_map/concatenate | solution.py:178
  12.4 0.0 copy-start.1
  12.4 0.0 copy-start.2
  12.4 0.6 %collective-permute-start.5 = (bf16[128,2560]{1,0:T(8,128)(2,1)S(1)}, bf16[128,2560]{1,0:T(8,128)(2,1)S(1)}, u32[]{:S(2)}, u32[]{:S(2)}) collective-permute-start(bf16[128,2560]{1,0:T(8,128)(2,1)S(1)} %fusion.1), channel_id=1, source_target_pairs={{0,2},{2,0},{1,3},{3,1},{4,6},{6,4},{5,7},{7,5},{8,10},{10,8},{9,1... | collective-permute-start | bytes 1966088 | tf_op jit(solution)/shard_map/ppermute | solution.py:19
  13.0 0.0 copy-done.3
  13.0 0.0 copy-done.12
  13.1 0.1 copy.41
  13.2 0.1 copy.42
  13.4 0.1 pad_add_fusion.place_ref
  13.5 0.1 fusion.3.enc_ref
  13.6 0.0 copy-done.5
  13.6 0.0 collective-permute-done.4
  13.6 0.0 copy-done.8
  13.7 0.1 copy.35
  13.8 0.0 collective-permute-done.2
  13.8 0.0 collective-permute-done.1
  13.9 0.0 collective-permute-done
  13.9 0.0 copy-done.7
  13.9 0.1 fusion.15
  14.0 0.1 collective-permute-start.3
  14.1 0.6 %slice.47 = f32[1,1]{1,0:T(1,128)} slice(f32[9,128]{1,0:T(8,128)S(1)} %collective-permute-done.2), slice={[8:9], [0:1]} | slice | bytes 8 | tf_op jit(solution)/shard_map/slice | solution.py:194
  14.7 0.5 %slice.48 = f32[1,1]{1,0:T(1,128)} slice(f32[9,128]{1,0:T(8,128)S(1)} %collective-permute-done.1), slice={[8:9], [0:1]} | slice | bytes 8 | tf_op jit(solution)/shard_map/slice | solution.py:194
  15.2 0.5 %slice.49 = f32[1,1]{1,0:T(1,128)} slice(f32[9,128]{1,0:T(8,128)S(1)} %collective-permute-done), slice={[8:9], [0:1]} | slice | bytes 8 | tf_op jit(solution)/shard_map/slice | solution.py:194
  15.7 2.0 %pad_maximum_fusion.2 = f32[4]{0:T(128)S(1)} fusion(f32[1]{0:T(128)} %bitcast.19, f32[1]{0:T(128)} %bitcast.18, f32[1]{0:T(128)} %bitcast.17, f32[1]{0:T(128)} %convert_element_type.56), kind=kLoop, calls=%fused_computation.45 | loop fusion | flops 12 | bytes 32 | tf_op jit(solution)/shard_map/stack | solution.py:194
  17.8 10.1 %collective-permute-done.5.rest_2_ = bf16[128,2560]{1,0:T(8,128)(2,1)S(1)} collective-permute-done((bf16[128,2560]{1,0:T(8,128)(2,1)S(1)}, bf16[128,2560]{1,0:T(8,128)(2,1)S(1)}, u32[]{:S(2)}, u32[]{:S(2)}) %collective-permute-start.5) | collective-permute-done | bytes 655392 | tf_op jit(solution)/shard_map/ppermute | solution.py:19
  27.8 0.0 collective-permute-start.6
  27.8 0.2 fusion.16
  28.0 0.4 fusion.scale_ref
  28.5 0.4 convolution_bitcast_fusion.shift_ref
  28.8 0.0 collective-permute-done.3
  28.9 1.0 %collective-permute-done.6.rest_3_ = bf16[128,2560]{1,0:T(8,128)(2,1)S(1)} collective-permute-done((bf16[128,2560]{1,0:T(8,128)(2,1)S(1)}, bf16[128,2560]{1,0:T(8,128)(2,1)S(1)}, u32[]{:S(2)}, u32[]{:S(2)}) %collective-permute-start.6) | collective-permute-done | bytes 655392 | tf_op jit(solution)/shard_map/ppermute | solution.py:19
  29.9 0.0 copy-done.2
  29.9 10.9 %shard_map.140 = (bf16[1,77,128]{2,1,0:T(8,128)(2,1)}, f32[1,77,128]{2,1,0:T(8,128)S(1)}) custom-call(s32[2]{0:T(128)S(1)} %pad_add_fusion.place_ref, bf16[2,128,128]{2,1,0:T(8,128)(2,1)S(1)} %pad_maximum_fusion.field_ref, f32[1,256,4]{2,1,0:T(8,128)S(1)} %fusion.scale_ref, f32[1,256,4]{2,1,0:T(8,128)S(1)} %convolution_bitcast_fusion.shift_ref, ...), custom_call_target="tpu_custom_call" | custom-call | tf_op jit(solution)/shard_map/pallas_call | solution.py:221
  40.9 0.7 %copy.38 = f32[1,1,77,128]{3,1,2,0:T(1,128)} copy(f32[1,1,77,128]{3,2,1,0:T(8,128)S(1)} %bitcast.62) | data formatting | bytes 78848
  (28 shorter events, 0.1 us)
Async XLA Ops:
  0.6 27.4 %copy-start = (f32[16,256]{1,0:T(8,128)S(1)}, f32[16,256]{1,0:T(8,128)}, u32[]{:S(2)}) copy-start(f32[16,256]{1,0:T(8,128)} %param.19) | copy-start | bytes 49156
  0.6 12.4 %copy-start.3 = (bf16[256,81]{0,1:T(8,128)(2,1)S(1)}, bf16[256,81]{0,1:T(8,128)(2,1)}, u32[]{:S(2)}) copy-start(bf16[256,81]{0,1:T(8,128)(2,1)} %param.21) | copy-start | bytes 124420
  0.7 12.4 %slice-start = ((bf16[256,81]{0,1:T(8,128)(2,1)}), bf16[256,80]{0,1:T(8,128)(2,1)S(1)}, s32[]{:S(2)}) async-start(bf16[256,81]{0,1:T(8,128)(2,1)} %param.21), calls=%async_computation | async-start | bytes 81920 | tf_op jit(solution)/shard_map/slice
  0.7 12.4 %copy-start.12 = (s32[1,128]{1,0:T(1,128)S(1)}, s32[1,128]{1,0:T(1,128)}, u32[]{:S(2)}) copy-start(s32[1,128]{1,0:T(1,128)} %param.16) | copy-start | bytes 1540
  2.0 11.8 %collective-permute-start.2 = (f32[9,128]{1,0:T(8,128)S(1)}, f32[9,128]{1,0:T(8,128)S(1)}, u32[]{:S(2)}, u32[]{:S(2)}) collective-permute-start(f32[9,128]{1,0:T(8,128)S(1)} %concatenate.18), channel_id=1, source_target_pairs={{0,4},{4,8},{8,12},{12,0},{1,5},{5,9},{9,13},{13,1},{2,6},{6,10},{... | collective-permute-start | bytes 13832 | tf_op jit(solution)/shard_map/ppermute | solution.py:19
  5.1 8.8 %collective-permute-start.1 = (f32[9,128]{1,0:T(8,128)S(1)}, f32[9,128]{1,0:T(8,128)S(1)}, u32[]{:S(2)}, u32[]{:S(2)}) collective-permute-start(f32[9,128]{1,0:T(8,128)S(1)} %concatenate.18), channel_id=1, source_target_pairs={{0,8},{4,12},{8,0},{12,4},{1,9},{5,13},{9,1},{13,5},{2,10},{6,14},... | collective-permute-start | bytes 13832 | tf_op jit(solution)/shard_map/ppermute | solution.py:19
  7.6 6.2 %collective-permute-start = (f32[9,128]{1,0:T(8,128)S(1)}, f32[9,128]{1,0:T(8,128)S(1)}, u32[]{:S(2)}, u32[]{:S(2)}) collective-permute-start(f32[9,128]{1,0:T(8,128)S(1)} %concatenate.18), channel_id=1, source_target_pairs={{0,12},{4,0},{8,4},{12,8},{1,13},{5,1},{9,5},{13,9},{2,14},{6,2},{... | collective-permute-start | bytes 13832 | tf_op jit(solution)/shard_map/ppermute | solution.py:19
  9.7 4.0 %collective-permute-start.4 = (f32[1,256]{1,0:T(1,128)S(1)}, f32[1,256]{1,0:T(1,128)S(1)}, u32[]{:S(2)}, u32[]{:S(2)}) collective-permute-start(f32[1,256]{1,0:T(1,128)S(1)} %convert_element_type.61), channel_id=1, source_target_pairs={{0,2},{2,0},{1,3},{3,1},{4,6},{6,4},{5,7},{7,5},{8,10},{10,8},{9,1... | collective-permute-start | bytes 3080 | tf_op jit(solution)/shard_map/ppermute | solution.py:19
  11.2 2.3 %copy-start.9 = (pred[80]{0:T(512)(128)(4,1)S(1)}, pred[80]{0:T(512)(128)(4,1)}, u32[]{:S(2)}) copy-start(pred[80]{0:T(512)(128)(4,1)} %constant.74.clone.1) | copy-start | bytes 244
  11.2 2.4 %copy-start.10 = (s32[1,2]{1,0:T(1,128)S(1)}, s32[1,2]{1,0:T(1,128)}, u32[]{:S(2)}) copy-start(s32[1,2]{1,0:T(1,128)} %param.15) | copy-start | bytes 28
  11.2 2.4 %copy-start.5 = (bf16[77,256]{1,0:T(8,128)(2,1)S(1)}, bf16[77,256]{1,0:T(8,128)(2,1)}, u32[]{:S(2)}) copy-start(bf16[77,256]{1,0:T(8,128)(2,1)} %param.25) | copy-start | bytes 118276
  11.2 2.5 %copy-start.8 = (bf16[1,256]{1,0:T(2,128)(2,1)S(1)}, bf16[1,256]{1,0:T(2,128)(2,1)}, u32[]{:S(2)}) copy-start(bf16[1,256]{1,0:T(2,128)(2,1)} %param.24) | copy-start | bytes 1540
  11.2 2.7 %copy-start.7 = (bf16[1,1,2,1,4,128]{5,4,3,2,1,0:T(4,128)(2,1)S(1)}, bf16[1,1,2,1,4,128]{5,4,3,2,1,0:T(4,128)(2,1)}, u32[]{:S(2)}) copy-start(bf16[1,1,2,1,4,128]{5,4,3,2,1,0:T(4,128)(2,1)} %param.14) | copy-start | bytes 6148
  11.2 2.8 %copy-start.4 = (bf16[1,1,77,128]{3,2,1,0:T(8,128)(2,1)S(1)}, bf16[1,1,77,128]{3,2,1,0:T(8,128)(2,1)}, u32[]{:S(2)}) copy-start(bf16[1,1,77,128]{3,2,1,0:T(8,128)(2,1)} %param.13) | copy-start | bytes 59140
  11.2 16.6 %copy-start.11 = (f32[64,16]{0,1:T(8,128)S(1)}, f32[64,16]{0,1:T(8,128)}, u32[]{:S(2)}) copy-start(f32[64,16]{0,1:T(8,128)} %param.18) | copy-start | bytes 12292
  11.2 17.2 %copy-start.6 = (f32[16,256]{1,0:T(8,128)S(1)}, f32[16,256]{1,0:T(8,128)}, u32[]{:S(2)}) copy-start(f32[16,256]{1,0:T(8,128)} %param.20) | copy-start | bytes 49156
  12.4 17.5 %copy-start.1 = (bf16[1,256,2304]{2,1,0:T(8,128)(2,1)S(1)}, bf16[1,256,2304]{2,1,0:T(8,128)(2,1)}, u32[]{:S(2)}) copy-start(bf16[1,256,2304]{2,1,0:T(8,128)(2,1)} %param.22) | copy-start | bytes 3538948
  12.4 17.5 %copy-start.2 = (bf16[1,256,256]{2,1,0:T(8,128)(2,1)S(1)}, bf16[1,256,256]{2,1,0:T(8,128)(2,1)}, u32[]{:S(2)}) copy-start(bf16[1,256,256]{2,1,0:T(8,128)(2,1)} %param.23) | copy-start | bytes 393220
  12.4 15.4 %collective-permute-start.5 = (bf16[128,2560]{1,0:T(8,128)(2,1)S(1)}, bf16[128,2560]{1,0:T(8,128)(2,1)S(1)}, u32[]{:S(2)}, u32[]{:S(2)}) collective-permute-start(bf16[128,2560]{1,0:T(8,128)(2,1)S(1)} %fusion.1), channel_id=1, source_target_pairs={{0,2},{2,0},{1,3},{3,1},{4,6},{6,4},{5,7},{7,5},{8,10},{10,8},{9,1... | collective-permute-start | bytes 1966088 | tf_op jit(solution)/shard_map/ppermute | solution.py:19
  14.0 14.8 %collective-permute-start.3 = (bf16[1,128,128]{2,1,0:T(8,128)(2,1)S(1)}, bf16[1,128,128]{2,1,0:T(8,128)(2,1)S(1)}, u32[]{:S(2)}, u32[]{:S(2)}) collective-permute-start(bf16[1,128,128]{2,1,0:T(8,128)(2,1)S(1)} %fusion.10), channel_id=1, source_target_pairs={{0,1},{1,0},{2,3},{3,2},{4,5},{5,4},{6,7},{7,6},{8,9},{9,8},{10,11... | collective-permute-start | bytes 98312 | tf_op jit(solution)/shard_map/ppermute | solution.py:19
  27.8 2.1 %collective-permute-start.6 = (bf16[128,2560]{1,0:T(8,128)(2,1)S(1)}, bf16[128,2560]{1,0:T(8,128)(2,1)S(1)}, u32[]{:S(2)}, u32[]{:S(2)}) collective-permute-start(bf16[128,2560]{1,0:T(8,128)(2,1)S(1)} %collective-permute-done.5.rest_2_), channel_id=1, source_target_pairs={{0,1},{1,0},{2,3},{3,2},{4,5},{5,4},{6,7},{7,6},{8,9},{9,8},{10,11... | collective-permute-start | bytes 1966088 | tf_op jit(solution)/shard_map/ppermute | solution.py:19

commit v2 on v1

v2 whole, which is shorter than its diff:
```python
import functools

import jax
import jax.numpy as jnp
from jax import lax
from jax.experimental import pallas as pl
from jax.experimental.pallas import tpu as pltpu
from jax.sharding import PartitionSpec as P

BF16_ROWS = 16
VMEM_BYTES = 28 * 1024 * 1024


def padded_rows(count):
    return -(-count // BF16_ROWS) * BF16_ROWS


def passed_along(block, axis, distance):
    size = lax.axis_size(axis)
    return lax.ppermute(block, axis, [(i, (i + distance) % size) for i in range(size)])


def all_along(block, axis):
    return [block] + [passed_along(block, axis, k) for k in range(1, lax.axis_size(axis))]


def from_place(parts, here, place):
    chosen = parts[0]
    for k in range(1, len(parts)):
        chosen = jnp.where(lax.rem(here - k + len(parts), len(parts)) == place, parts[k], chosen)
    return chosen


def field_kernel(dims, scalar_ref, state_ref, land_ref, *rest):
    steps, members, local, forced, vp, fp = dims
    group, out_ref = rest[:members], rest[members]
    varied, lon = state_ref.shape[1:]
    for i in range(local):
        out_ref[i] = jnp.zeros(out_ref.shape[1:], jnp.bfloat16)
        out_ref[i, 0:varied] = state_ref[i]
        for t in range(steps):
            first = (t * local + i) * forced
            force = group[0][first : first + forced, :]
            for k in range(1, members):
                source = lax.rem(scalar_ref[2] - k + members, members)
                force = jnp.where(scalar_ref[3 + t] == source, group[k][first : first + forced, :], force)
            out_ref[i, vp + fp * t : vp + fp * t + forced, :] = force.astype(jnp.bfloat16)
        out_ref[i, vp + fp * steps : vp + fp * steps + 1, :] = land_ref[i : i + 1, :].astype(jnp.bfloat16)


def put_taps(taps, value, row, cols, spacing):
    chans, lon = value.shape
    lane = lax.broadcasted_iota(jnp.int32, (chans, lon), 1)
    zero = jnp.zeros_like(value)
    base = 3 * chans * row
    taps[base : base + chans, cols] = jnp.where(lane >= spacing, pltpu.roll(value, spacing, 1), zero)
    taps[base + chans : base + 2 * chans, cols] = value
    taps[base + 2 * chans : base + 3 * chans, cols] = jnp.where(
        lane < lon - spacing, pltpu.roll(value, lon - spacing, 1), zero
    )


def first_kernel(dims, scalar_ref, enc_ref, settings_ref, scale_w_ref, shift_w_ref, *rest):
    steps, layers, bands, local, members, lon, chans, vp, fp, turns = dims
    fields, rest = rest[:bands], rest[bands:]
    group, rest = rest[: members * turns], rest[members * turns :]
    gains, rest = rest[:layers], rest[layers:]
    field_ref, scale_ref, shift_ref, gain_ref, hidden_ref, taps_ref = rest
    here, band = scalar_ref[0], scalar_ref[1]
    for b in range(bands):
        field_ref[b * local : (b + 1) * local] = from_place([f[...] for f in fields], band, b)

    eye = lax.broadcasted_iota(jnp.int32, (chans, chans), 0) == lax.broadcasted_iota(jnp.int32, (chans, chans), 1)
    for layer in range(layers):
        row = from_place([g[...] for g in gains], here, layer)
        column = jnp.sum(jnp.where(eye, row, 0.0), axis=1, keepdims=True)
        gain_ref[layer] = jnp.broadcast_to(column, (chans, lon))

    settings = settings_ref[...]
    numbers = lax.broadcasted_iota(jnp.int32, settings.shape, 0).astype(jnp.float32)
    for m, entry in enumerate(group):
        chosen = entry[entry.shape[0] - 1 : entry.shape[0], 0 : settings.shape[1]]
        row = jnp.sum(jnp.where(numbers == chosen, settings, 0.0), axis=0, keepdims=True)
        cols = slice((m % members) * lon, (m % members + 1) * lon)
        scale = 1.0 + jnp.sum(scale_w_ref[...] * row, axis=1, keepdims=True)
        shift = jnp.sum(shift_w_ref[...] * row, axis=1, keepdims=True)
        scale_ref[m // members, :, cols] = jnp.broadcast_to(scale, (chans, lon))
        shift_ref[m // members, :, cols] = jnp.broadcast_to(shift, (chans, lon))

    if turns == 1:
        for i in range(bands * local):
            land = field_ref[i, vp + fp * steps : vp + fp * steps + 1, :].astype(jnp.float32)
            lifted = jnp.dot(enc_ref[...], field_ref[i, 0 : vp + fp, :], preferred_element_type=jnp.float32)
            for m in range(members):
                cols = slice(m * lon, (m + 1) * lon)
                value = land * (lifted * scale_ref[0, :, cols] + shift_ref[0, :, cols])
                value = value.astype(jnp.bfloat16)
                hidden_ref[i, :, cols] = value
                put_taps(taps_ref, value, i, cols, 1)


def after_kernel(section_ref, earlier_ref, out_ref):
    pass


def after(section, earlier):
    whole = pl.BlockSpec(memory_space=pl.ANY)
    return pl.pallas_call(
        after_kernel,
        out_shape=jax.ShapeDtypeStruct(section.shape, section.dtype),
        in_specs=[whole, whole],
        out_specs=whole,
        input_output_aliases={0: 0},
        cost_estimate=pl.CostEstimate(flops=0, bytes_accessed=0, transcendentals=0),
    )(section, earlier)


def window_kernel(dims, scalar_ref, field_ref, scale_ref, shift_ref, gain_ref, enc_ref, dec_ref, *rest):
    steps, layers, bands, local, members, lon, chans, vp, fp, turns = dims
    lat = bands * local
    hidden, taps = rest[:2]
    blocks, rest = rest[2 : 4 + (layers - 1) * bands], rest[4 + (layers - 1) * bands :]
    final_ref, mean_ref, weights, conv, act, inputs, total, sems = rest[:8]
    here, band = scalar_ref[0], scalar_ref[1]
    taps_wide, wide = 9 * chans, 3 * chans
    part = chans // bands

    pltpu.make_async_copy(blocks[0], weights.at[here, :, pl.ds(0, taps_wide)], sems.at[here]).start()
    pltpu.make_async_copy(blocks[1], weights.at[here, :, pl.ds(taps_wide, chans)], sems.at[here]).start()
    for k in range(1, layers):
        slot = lax.rem(here - k + layers, layers)
        for j in range(bands):
            first = pl.multiple_of(lax.rem(band - j + bands, bands) * part, part)
            pltpu.make_async_copy(
                blocks[2 + (k - 1) * bands + j], weights.at[slot, pl.ds(first, part), :], sems.at[slot]
            ).start()

    if turns > 1:
        hidden, taps = rest[8:]

    def columns(m):
        return slice(m * lon, (m + 1) * lon)

    land = [field_ref[i, vp + fp * steps : vp + fp * steps + 1, :].astype(jnp.float32) for i in range(lat)]

    def put_hidden(i, m, value, layer):
        value = value.astype(jnp.bfloat16)
        hidden[i, :, columns(m)] = value
        if layer is not None:
            put_taps(taps, value, i, columns(m), 2 ** (layer % 3))

    def encode(step, turn):
        for i in range(lat):
            force = field_ref[i, vp + fp * step : vp + fp * (step + 1), :]
            for m in range(members):
                inputs[i, vp : vp + fp, columns(m)] = force
                if step == 0:
                    inputs[i, 0:vp, columns(m)] = field_ref[i, 0:vp, :]
            lifted = jnp.dot(enc_ref[...], inputs[i], preferred_element_type=jnp.float32)
            for m in range(members):
                value = lifted[:, columns(m)] * scale_ref[turn, :, columns(m)] + shift_ref[turn, :, columns(m)]
                put_hidden(i, m, land[i] * value, 0)

    def activate(value, layer):
        centred = value - jnp.sum(value, axis=0, keepdims=True) * (1.0 / chans)
        spread = jnp.sum(centred * centred, axis=0, keepdims=True) * (1.0 / chans)
        normed = (centred * lax.rsqrt(spread + 1e-05)).astype(jnp.bfloat16) * gain_ref[layer].astype(jnp.bfloat16)
        inner = normed * (normed * normed * 0.0356774081 + 0.7978845608)
        half = normed * 0.5
        return half + half * jnp.tanh(inner)

    def block(layer, not_yet):
        if not_yet is True:
            pltpu.make_async_copy(weights.at[layer], weights.at[layer], sems.at[layer]).wait()
        elif not_yet is not None:

            @pl.when(not_yet)
            def _():
                pltpu.make_async_copy(weights.at[layer], weights.at[layer], sems.at[layer]).wait()

        for i in range(lat):
            low, high = max(i - 1, 0), min(i + 1, lat - 1)
            conv[i] = jnp.dot(
                weights[layer, :, (low - i + 1) * wide : (high - i + 2) * wide],
                taps[low * wide : (high + 1) * wide, :],
                preferred_element_type=jnp.float32,
            )
        for i in range(lat):
            for m in range(members):
                act[i, :, columns(m)] = activate(conv[i, :, columns(m)], layer)
        for i in range(lat):
            mixed = jnp.dot(weights[layer, :, taps_wide:], act[i], preferred_element_type=jnp.float32)
            for m in range(members):
                kept = hidden[i, :, columns(m)].astype(jnp.float32)
                later = layer + 1 if layer + 1 < layers else None
                put_hidden(i, m, land[i] * (kept + mixed[:, columns(m)]), later)

    varied = final_ref.shape[1]

    def window(turn, first):
        for step in range(steps):
            if step > 0 or turns > 1:
                encode(step, turn)
            for layer in range(layers):
                block(layer, first if step == 0 else None)
            for i in range(lat):
                change = jnp.dot(dec_ref[...], hidden[i], preferred_element_type=jnp.float32)
                for m in range(members):
                    old = field_ref[i, 0:vp, :] if step == 0 else inputs[i, 0:vp, columns(m)]
                    new = old.astype(jnp.float32) + land[i] * change[:, columns(m)]
                    inputs[i, 0:vp, columns(m)] = new.astype(jnp.bfloat16)
        for i in range(local):
            row = band * local + i
            summed = inputs[row, 0:vp, columns(0)].astype(jnp.float32)
            for m in range(1, members):
                summed = summed + inputs[row, 0:vp, columns(m)].astype(jnp.float32)
            if turns == 1:
                mean_ref[:, i, :] = summed[0:varied] * (1.0 / members)
                final_ref[i] = inputs[row, 0:varied, columns(0)]
            else:
                total[i] = jnp.where(first, summed, total[i] + summed)
                mean_ref[:, i, :] = total[i, 0:varied] * (1.0 / (members * turns))

                @pl.when(first)
                def _():
                    final_ref[i] = inputs[row, 0:varied, columns(0)]

    if turns == 1:
        window(0, True)
    else:
        lax.fori_loop(0, turns, lambda turn, _: window(turn, turn == 0), None)


def per_device(
    init_state,
    forcing_slots,
    atmos_owner,
    land_mask,
    param_index,
    settings,
    scale_weight,
    shift_weight,
    encode_weight,
    conv_weight,
    point_weight,
    norm_gain,
    decode_weight,
):
    members, layers, bands = (lax.axis_size(a) for a in ("members", "segment", "rows"))
    here, band = lax.axis_index("segment"), lax.axis_index("rows")
    _, local, varied, lon = init_state.shape
    steps, forced = forcing_slots.shape[2], forcing_slots.shape[4]
    chans = conv_weight.shape[1]
    lat = local * bands
    vp, fp = padded_rows(varied), padded_rows(forced)
    part = chans // bands
    at_once = next(n for n in (4, 2, 1) if members % n == 0)
    turns, wide = members // at_once, at_once * lon
    smem, vmem, whole = (pl.BlockSpec(memory_space=s) for s in (pltpu.SMEM, pltpu.VMEM, pl.ANY))
    params = pltpu.CompilerParams(vmem_limit_bytes=VMEM_BYTES)
    free = pl.CostEstimate(flops=0, bytes_accessed=0, transcendentals=0)

    mine = jnp.concatenate([conv_weight[0], point_weight[0]], axis=1)
    mine = lax.dynamic_slice_in_dim(mine, band * part, part, 0)
    sections = all_along(mine, "segment")[1:]

    slots = forcing_slots[0, 0].astype(jnp.float32).reshape(-1, lon)
    index_row = jnp.broadcast_to(param_index.astype(jnp.float32)[:, None], (1, lon))
    group = all_along(jnp.concatenate([slots, index_row], axis=0), "members")
    gains = all_along(norm_gain.astype(jnp.float32), "segment")
    scalars = jnp.concatenate(
        [jnp.stack([here, band, lax.axis_index("members")]).astype(jnp.int32), atmos_owner[0]]
    )
    field = pl.pallas_call(
        functools.partial(field_kernel, (steps, members, local, forced, vp, fp)),
        out_shape=jax.ShapeDtypeStruct((local, vp + fp * steps + BF16_ROWS, lon), jnp.bfloat16),
        in_specs=[smem] + [vmem] * (2 + members),
        out_specs=vmem,
        compiler_params=params,
        cost_estimate=free,
    )(scalars, init_state[0], land_mask, *group)
    fields = all_along(field, "rows")

    enc = jnp.pad(encode_weight[:, :varied], ((0, 0), (0, vp - varied)))
    enc = jnp.concatenate([enc, jnp.pad(encode_weight[:, varied:], ((0, 0), (0, fp - forced)))], axis=1)
    dec = jnp.pad(decode_weight, ((0, vp - varied), (0, 0)))
    dims = (steps, layers, bands, local, at_once, lon, chans, vp, fp, turns)
    field, scale, shift, gain, hidden, taps = pl.pallas_call(
        functools.partial(first_kernel, dims),
        out_shape=(
            jax.ShapeDtypeStruct((lat, vp + fp * steps + BF16_ROWS, lon), jnp.bfloat16),
            jax.ShapeDtypeStruct((turns, chans, wide), jnp.float32),
            jax.ShapeDtypeStruct((turns, chans, wide), jnp.float32),
            jax.ShapeDtypeStruct((layers, chans, lon), jnp.float32),
            jax.ShapeDtypeStruct((lat, chans, wide), jnp.bfloat16),
            jax.ShapeDtypeStruct((lat * 3 * chans, wide), jnp.bfloat16),
        ),
        in_specs=[smem] + [vmem] * (4 + bands + members + layers),
        out_specs=(vmem,) * 6,
        compiler_params=params,
        cost_estimate=free,
    )(scalars, enc, settings, scale_weight.T, shift_weight.T, *fields, *group, *gains)

    blocks = [conv_weight[0], point_weight[0]]
    for section in sections:
        blocks += all_along(after(section, taps), "rows")

    scratch = [
        pltpu.VMEM((layers, chans, 10 * chans), jnp.bfloat16),
        pltpu.VMEM((lat, chans, wide), jnp.float32),
        pltpu.VMEM((lat, chans, wide), jnp.bfloat16),
        pltpu.VMEM((lat, vp + fp, wide), jnp.bfloat16),
        pltpu.VMEM((local, vp, lon), jnp.float32),
        pltpu.SemaphoreType.DMA((layers,)),
    ]
    if turns > 1:
        scratch += [pltpu.VMEM(hidden.shape, jnp.bfloat16), pltpu.VMEM(taps.shape, jnp.bfloat16)]
    final, mean = pl.pallas_call(
        functools.partial(window_kernel, dims),
        out_shape=(
            jax.ShapeDtypeStruct((local, varied, lon), jnp.bfloat16),
            jax.ShapeDtypeStruct((varied, local, lon), jnp.float32),
        ),
        in_specs=[smem] + [vmem] * 8 + [whole] * len(blocks),
        out_specs=(vmem, vmem),
        scratch_shapes=scratch,
        compiler_params=params,
        cost_estimate=free,
    )(scalars, field, scale, shift, gain, enc, dec, hidden, taps, *blocks)
    return final[None, None], jnp.swapaxes(mean, 0, 1)[None]
def solution(mesh):
    in_specs = (
        P(("groups", "segment"), "rows", None, None),
        P("members", ("groups", "segment"), None, "rows", None, None),
        P(("groups", "segment"), None),
        P(("groups", "rows"), None),
        P(("groups", "members")),
        P(),
        P(),
        P(),
        P(),
        P("segment", None, None),
        P("segment", None, None),
        P("segment", None),
        P(),
    )
    out_specs = (
        P("members", ("groups", "segment"), "rows", None, None),
        P(("groups", "segment"), "rows", None, None),
    )
    return jax.shard_map(
        per_device, mesh=mesh, in_specs=in_specs, out_specs=out_specs, check_vma=False
    )
```

time: 41.8 us -> 43.9 us (1.050)
  local copies, waits for them, and re-layouts: 2.76 us -> 12.7 us
  other arithmetic: 4.9 us -> 1.36 us
  waiting for transfers between devices: 11.1 us -> 8.82 us
  matrix products: 0.98 us -> 0 us
  starting transfers between devices: 9.13 us -> 8.28 us
    unnamed x29 -> x53, local copies, waits for them, and re-layouts: 0.99 us -> 11.8 us
    ppermute x7, waiting for transfers between devices: 11.1 us -> 8.82 us  [passed_along(): lax.ppermute(block, axis, [(i, (i + distance) % size) for i in range(size)])]
    another operation x2 -> x0, other arithmetic: 2.12 us -> none  [the longest x1 2.04 us: per_device(): picked = jnp.stack([g[-1, 0] for g in group])]
    pallas_call x1, Pallas kernels: 10.9 us -> 8.85 us  [per_device(): pl.pallas_call(functools.partial(window_kernel, dims), out_shape=(jax.Sha...]
    pallas_call x0 -> x3, Pallas kernels: none -> 2 us  [the longest x1 1.44 us: per_device(): pl.pallas_call(functools.partial(first_kernel, dims), out_shape=(jax.Shap...]
    slice x8 -> x2, local copies, waits for them, and re-layouts: 1.61 us -> 0.01 us  [the longest x3 1.6 us: per_device(): picked = jnp.stack([g[-1, 0] for g in group])]
    convert_element_type x3 -> x1, other arithmetic: 1.45 us -> 0.01 us  [per_device(): gains = all_along(norm_gain.astype(jnp.float32), 'segment')]
    dot_general x3 -> x0, matrix products: 0.98 us -> none  [the longest x1 0.4 us: per_device(): jnp.dot(scale_weight.T, rows.T, precision=lax.Precision.HIGHEST)]
  transfers between devices with their start and end apart: 7 -> 7, of which waited for: 2 -> 4; matrix products, arithmetic and copies ran while one was open for 17% -> 4% of each run, Pallas kernels for 0% -> 5%
where the time goes in v2:
time: 43.9 us; the launch traced here: 43.5 us
  local copies, waits for them, and re-layouts  12.7 us (29%)
  Pallas kernels  10.9 us (25%)
  waiting for transfers between devices  8.82 us (20%)
  starting transfers between devices  8.28 us (19%)
  between operations  1.51 us (3%)
  other arithmetic  1.36 us (3%)
    unnamed x53, local copies, waits for them, and re-layouts  11.8 us
    pallas_call x1, Pallas kernels, per_device(): pl.pallas_call(functools.partial(window_kernel, dims), out_shape=(jax.Sha...  8.85 us
    ppermute x7, waiting for transfers between devices, passed_along(): lax.ppermute(block, axis, [(i, (i + distance) % size) for i in range(size)])  8.82 us
    ppermute x7, starting transfers between devices, passed_along(): lax.ppermute(block, axis, [(i, (i + distance) % size) for i in range(size)])  8.28 us
    pallas_call x1, Pallas kernels, per_device(): pl.pallas_call(functools.partial(first_kernel, dims), out_shape=(jax.Shap...  1.44 us
    concatenate x1, other arithmetic, per_device(): mine = jnp.concatenate([conv_weight[0], point_weight[0]], axis=1)  1.18 us
    pad x1, local copies, waits for them, and re-layouts, per_device(): dec = jnp.pad(decode_weight, ((0, vp - varied), (0, 0)))  0.94 us
  transfers between devices with their start and end apart: 7, of which 4 were waited for; matrix products, arithmetic and copies ran while one was open for 4% of the time, Pallas kernels for 5%

profile of v2, /device:TPU:0, one launch (start us, length us, event | category | flops | bytes accessed | tf_op | source)
XLA Modules:
  0.0 43.5 jit_solution(16434549972295848355)
XLA Ops:
  0.6 0.0 copy-start.22
  0.6 0.0 copy-start.20
  0.7 0.0 slice-start
  0.7 0.0 copy-start.19
  0.7 0.0 copy-start.17
  0.7 0.0 copy-start.18
  0.8 1.2 %fusion = bf16[128,2560]{1,0:T(8,128)(2,1)S(1)} fusion(s32[]{:T(128)S(6)} %select_n.3, bf16[256,2304]{1,0:T(8,128)(2,1)} %bitcast.16, bf16[256,256]{1,0:T(8,128)(2,1)} %bitcast.18), kind=kLoop, calls=%fused_computation.2 | loop fusion | flops 1310720 | bytes 1966084 | tf_op jit(solution)/shard_map/concatenate | solution.py:263
  1.9 3.0 %collective-permute-start.5 = (bf16[128,2560]{1,0:T(8,128)(2,1)S(1)}, bf16[128,2560]{1,0:T(8,128)(2,1)S(1)}, u32[]{:S(2)}, u32[]{:S(2)}) collective-permute-start(bf16[128,2560]{1,0:T(8,128)(2,1)S(1)} %fusion), channel_id=1, source_target_pairs={{0,2},{2,0},{1,3},{3,1},{4,6},{6,4},{5,7},{7,5},{8,10},{10,8},{9,1... | collective-permute-start | bytes 1966088 | tf_op jit(solution)/shard_map/ppermute | solution.py:20
  5.6 3.7 %collective-permute-start.2 = (f32[9,128]{1,0:T(8,128)S(1)}, f32[9,128]{1,0:T(8,128)S(1)}, u32[]{:S(2)}, u32[]{:S(2)}) collective-permute-start(f32[9,128]{1,0:T(8,128)S(1)} %concatenate.14.rest_0_.rest_2_), channel_id=1, source_target_pairs={{0,12},{4,0},{8,4},{12,8},{1,13},{5,1},{9,5},{13,9},{2,14},{6,2},{... | collective-permute-start | bytes 13832 | tf_op jit(solution)/shard_map/ppermute | solution.py:20
  9.3 0.0 collective-permute-start.1
  9.3 1.0 %collective-permute-start = (f32[9,128]{1,0:T(8,128)S(1)}, f32[9,128]{1,0:T(8,128)S(1)}, u32[]{:S(2)}, u32[]{:S(2)}) collective-permute-start(f32[9,128]{1,0:T(8,128)S(1)} %concatenate.14.rest_0_.rest_2_), channel_id=1, source_target_pairs={{0,4},{4,8},{8,12},{12,0},{1,5},{5,9},{9,13},{13,1},{2,6},{6,10},{... | collective-permute-start | bytes 13832 | tf_op jit(solution)/shard_map/ppermute | solution.py:20
  10.3 0.5 %collective-permute-start.4 = (f32[1,256]{1,0:T(1,128)S(1)}, f32[1,256]{1,0:T(1,128)S(1)}, u32[]{:S(2)}, u32[]{:S(2)}) collective-permute-start(f32[1,256]{1,0:T(1,128)S(1)} %convert_element_type.24.rest_6_), channel_id=1, source_target_pairs={{0,2},{2,0},{1,3},{3,1},{4,6},{6,4},{5,7},{7,5},{8,10},{10,8},{9,1... | collective-permute-start | bytes 3080 | tf_op jit(solution)/shard_map/ppermute | solution.py:20
  10.8 0.0 slice-done
  10.8 0.1 copy.22
  11.0 0.1 pad_add_fusion.scalar_ref
  11.1 0.1 copy.23
  11.2 0.0 collective-permute-done.2.rest_3_.rest_5_
  11.2 2.6 %collective-permute-done.1.rest_2_.rest_4_ = f32[9,128]{1,0:T(8,128)S(1)} collective-permute-done((f32[9,128]{1,0:T(8,128)S(1)}, f32[9,128]{1,0:T(8,128)S(1)}, u32[]{:S(2)}, u32[]{:S(2)}) %collective-permute-start.1) | collective-permute-done | bytes 4640 | tf_op jit(solution)/shard_map/ppermute | solution.py:20
  13.8 0.9 %collective-permute-done.rest_1_.rest_3_ = f32[9,128]{1,0:T(8,128)S(1)} collective-permute-done((f32[9,128]{1,0:T(8,128)S(1)}, f32[9,128]{1,0:T(8,128)S(1)}, u32[]{:S(2)}, u32[]{:S(2)}) %collective-permute-start) | collective-permute-done | bytes 4640 | tf_op jit(solution)/shard_map/ppermute | solution.py:20
  14.7 0.0 copy-done.14
  14.7 0.6 %shard_map.140.rest_0_ = bf16[1,128,128]{2,1,0:T(8,128)(2,1)S(1)} custom-call(s32[5]{0:T(128)S(1)} %pad_add_fusion.scalar_ref, bf16[1,77,128]{2,1,0:T(8,128)(2,1)S(1)} %bitcast.22, s32[1,128]{1,0:T(1,128)S(1)} %copy-done.15, f32[9,128]{1,0:T(8,128)S(1)} %concatenate.14.rest_0_.rest_2_, f32[9,128]{1,0:T(8,128)S(1)} %collective-permute-done.rest_1_.rest_3_, ...), custom_call_target="tpu_custom_call" | custom-call | tf_op jit(solution)/shard_map/pallas_call | solution.py:274
  15.3 0.1 collective-permute-start.3
  15.4 0.1 fusion.2.enc_ref
  15.5 0.0 copy-done.19
  15.5 0.1 copy.20.settings_ref
  15.6 0.0 copy-done.17
  15.6 0.1 copy.18
  15.7 0.1 copy.19
  15.8 4.0 %collective-permute-done.4.rest_7_ = f32[1,256]{1,0:T(1,128)S(1)} collective-permute-done((f32[1,256]{1,0:T(1,128)S(1)}, f32[1,256]{1,0:T(1,128)S(1)}, u32[]{:S(2)}, u32[]{:S(2)}) %collective-permute-start.4) | collective-permute-done | bytes 1056 | tf_op jit(solution)/shard_map/ppermute | solution.py:20
  19.7 0.0 collective-permute-done.3.rest_1_
  19.7 1.4 %shard_map.141 = (bf16[2,128,128]{2,1,0:T(8,128)(2,1)S(1)}, f32[1,256,512]{2,1,0:T(8,128)S(1)}, f32[1,256,512]{2,1,0:T(8,128)S(1)}, f32[2,256,128]{2,1,0:T(8,128...) custom-call(s32[5]{0:T(128)S(1)} %pad_add_fusion.scalar_ref, bf16[256,96]{1,0:T(8,128)(2,1)S(1)} %fusion.2.enc_ref, ...), custom_call_target="tpu_custom_call" | custom-call | tf_op jit(solution)/shard_map/pallas_call | solution.py:288
  21.2 1.2 %copy-done = bf16[1536,512]{1,0:T(8,128)(2,1)} copy-done((bf16[1536,512]{1,0:T(8,128)(2,1)}, bf16[1536,512]{1,0:T(8,128)(2,1)S(1)}, u32[]{:S(2)}) %copy-start) | copy-done | bytes 1572888
  22.4 0.8 %copy-done.5 = f32[1,256,512]{2,1,0:T(8,128)} copy-done((f32[1,256,512]{2,1,0:T(8,128)}, f32[1,256,512]{2,1,0:T(8,128)S(1)}, u32[]{:S(2)}) %copy-start.5) | copy-done | bytes 524312
  23.2 0.8 %copy-done.7 = f32[1,256,512]{2,1,0:T(8,128)} copy-done((f32[1,256,512]{2,1,0:T(8,128)}, f32[1,256,512]{2,1,0:T(8,128)S(1)}, u32[]{:S(2)}) %copy-start.7) | copy-done | bytes 524312
  24.0 0.8 %copy-done.9 = bf16[2,256,512]{2,1,0:T(8,128)(2,1)} copy-done((bf16[2,256,512]{2,1,0:T(8,128)(2,1)}, bf16[2,256,512]{2,1,0:T(8,128)(2,1)S(1)}, u32[]{:S(2)}) %copy-start.9) | copy-done | bytes 524312
  24.8 0.7 %copy-done.12 = f32[2,256,128]{2,1,0:T(8,128)} copy-done((f32[2,256,128]{2,1,0:T(8,128)}, f32[2,256,128]{2,1,0:T(8,128)S(1)}, u32[]{:S(2)}) %copy-start.12) | copy-done | bytes 262168
  25.4 0.0 collective-permute-done.5.section_ref
  25.5 0.8 %copy-done.3 = bf16[128,2560]{1,0:T(8,128)(2,1)} copy-done((bf16[128,2560]{1,0:T(8,128)(2,1)}, bf16[128,2560]{1,0:T(8,128)(2,1)S(1)}, u32[]{:S(2)}) %copy-start.3) | copy-done | bytes 655384
  26.3 0.0 collective-permute-start.6
  26.3 0.9 %pad.15.dec_ref = bf16[80,256]{1,0:T(8,128)(2,1)S(1)} pad(bf16[77,256]{1,0:T(8,128)(2,1)} %param.25, bf16[]{:T(256)} %constant.17.clone.1), padding=0_3x0_0 | pad | bytes 80386 | tf_op jit(solution)/shard_map/jit(_pad)/pad | solution.py:286
  27.2 1.4 %collective-permute-done.6.rest_5_ = bf16[128,2560]{1,0:T(8,128)(2,1)S(1)} collective-permute-done((bf16[128,2560]{1,0:T(8,128)(2,1)}, bf16[128,2560]{1,0:T(8,128)(2,1)S(1)}, u32[]{:S(2)}, u32[]{:S(2)}) %collective-permute-start.6) | collective-permute-done | bytes 655392 | tf_op jit(solution)/shard_map/ppermute | solution.py:20
  28.6 1.1 %copy-done.4 = bf16[128,2560]{1,0:T(8,128)(2,1)S(1)} copy-done((bf16[128,2560]{1,0:T(8,128)(2,1)S(1)}, bf16[128,2560]{1,0:T(8,128)(2,1)}, u32[]{:S(2)}) %copy-start.4) | copy-done | bytes 655384
  29.7 1.0 %copy-done.6 = f32[1,256,512]{2,1,0:T(8,128)S(1)} copy-done((f32[1,256,512]{2,1,0:T(8,128)S(1)}, f32[1,256,512]{2,1,0:T(8,128)}, u32[]{:S(2)}) %copy-start.6) | copy-done | bytes 524312
  30.8 1.0 %copy-done.8 = f32[1,256,512]{2,1,0:T(8,128)S(1)} copy-done((f32[1,256,512]{2,1,0:T(8,128)S(1)}, f32[1,256,512]{2,1,0:T(8,128)}, u32[]{:S(2)}) %copy-start.8) | copy-done | bytes 524312
  31.8 1.0 %copy-done.10 = bf16[2,256,512]{2,1,0:T(8,128)(2,1)S(1)} copy-done((bf16[2,256,512]{2,1,0:T(8,128)(2,1)S(1)}, bf16[2,256,512]{2,1,0:T(8,128)(2,1)}, u32[]{:S(2)}) %copy-start.10) | copy-done | bytes 524312
  32.8 0.9 %copy-done.11 = bf16[1,256,256]{2,1,0:T(8,128)(2,1)S(1)} copy-done((bf16[1,256,256]{2,1,0:T(8,128)(2,1)S(1)}, bf16[1,256,256]{2,1,0:T(8,128)(2,1)}, u32[]{:S(2)}) %copy-start.11) | copy-done | bytes 131096
  33.7 0.9 %copy-done.13 = f32[2,256,128]{2,1,0:T(8,128)S(1)} copy-done((f32[2,256,128]{2,1,0:T(8,128)S(1)}, f32[2,256,128]{2,1,0:T(8,128)}, u32[]{:S(2)}) %copy-start.13) | copy-done | bytes 262168
  34.7 8.9 %shard_map.143 = (bf16[1,77,128]{2,1,0:T(8,128)(2,1)}, f32[77,1,128]{2,1,0:T(1,128)}) custom-call(s32[5]{0:T(128)S(1)} %pad_add_fusion.scalar_ref, bf16[2,128,128]{2,1,0:T(8,128)(2,1)S(1)} %get-tuple-element.10.field_ref, f32[1,256,512]{2,1,0:T(8,128)S(1)} %copy-done.6, f32[1,256,512]{2,1,0:T(8,128)S(1)} %copy-done.8, f32[2,256,128]{2,1,0:T(8,128)S(1)} %copy-done.13, ...), custom_call_target="tpu_custom_call" | custom-call | tf_op jit(solution)/shard_map/pallas_call | solution.py:318
  (33 shorter events, 0.1 us)
Async XLA Ops:
  0.6 10.3 %copy-start.22 = (pred[80]{0:T(512)(128)(4,1)S(1)}, pred[80]{0:T(512)(128)(4,1)}, u32[]{:S(2)}) copy-start(pred[80]{0:T(512)(128)(4,1)} %constant.16.clone.1) | copy-start | bytes 244
  0.6 4.9 %copy-start.20 = (bf16[1,1,2,1,4,128]{5,4,3,2,1,0:T(4,128)(2,1)S(1)}, bf16[1,1,2,1,4,128]{5,4,3,2,1,0:T(4,128)(2,1)}, u32[]{:S(2)}) copy-start(bf16[1,1,2,1,4,128]{5,4,3,2,1,0:T(4,128)(2,1)} %param.14) | copy-start | bytes 6148
  0.7 9.6 %copy-start.21 = (bf16[1,256]{1,0:T(2,128)(2,1)S(1)}, bf16[1,256]{1,0:T(2,128)(2,1)}, u32[]{:S(2)}) copy-start(bf16[1,256]{1,0:T(2,128)(2,1)} %param.24) | copy-start | bytes 1540
  0.7 10.2 %slice-start = ((bf16[256,81]{0,1:T(8,128)(2,1)}), bf16[256,80]{0,1:T(8,128)(2,1)S(1)}, s32[]{:S(2)}) async-start(bf16[256,81]{0,1:T(8,128)(2,1)} %param.21), calls=%async_computation | async-start | bytes 81920 | tf_op jit(solution)/shard_map/slice
  0.7 10.4 %copy-start.16 = (bf16[256,81]{0,1:T(8,128)(2,1)S(1)}, bf16[256,81]{0,1:T(8,128)(2,1)}, u32[]{:S(2)}) copy-start(bf16[256,81]{0,1:T(8,128)(2,1)} %param.21) | copy-start | bytes 124420
  0.7 10.3 %copy-start.23 = (s32[1,2]{1,0:T(1,128)S(1)}, s32[1,2]{1,0:T(1,128)}, u32[]{:S(2)}) copy-start(s32[1,2]{1,0:T(1,128)} %param.15) | copy-start | bytes 28
  0.7 14.0 %copy-start.15 = (s32[1,128]{1,0:T(1,128)S(1)}, s32[1,128]{1,0:T(1,128)}, u32[]{:S(2)}) copy-start(s32[1,128]{1,0:T(1,128)} %land_ref.1) | copy-start | bytes 1540
  0.7 14.0 %copy-start.14 = (bf16[1,1,77,128]{3,2,1,0:T(8,128)(2,1)S(1)}, bf16[1,1,77,128]{3,2,1,0:T(8,128)(2,1)}, u32[]{:S(2)}) copy-start(bf16[1,1,77,128]{3,2,1,0:T(8,128)(2,1)} %param.13) | copy-start | bytes 59140
  0.7 14.7 %copy-start.19 = (f32[64,16]{0,1:T(8,128)S(1)}, f32[64,16]{0,1:T(8,128)}, u32[]{:S(2)}) copy-start(f32[64,16]{0,1:T(8,128)} %param.18) | copy-start | bytes 12292
  0.7 14.8 %copy-start.17 = (f32[16,256]{1,0:T(8,128)S(1)}, f32[16,256]{1,0:T(8,128)}, u32[]{:S(2)}) copy-start(f32[16,256]{1,0:T(8,128)} %param.19) | copy-start | bytes 49156
  0.7 14.9 %copy-start.18 = (f32[16,256]{1,0:T(8,128)S(1)}, f32[16,256]{1,0:T(8,128)}, u32[]{:S(2)}) copy-start(f32[16,256]{1,0:T(8,128)} %param.20) | copy-start | bytes 49156
  1.9 23.5 %collective-permute-start.5 = (bf16[128,2560]{1,0:T(8,128)(2,1)S(1)}, bf16[128,2560]{1,0:T(8,128)(2,1)S(1)}, u32[]{:S(2)}, u32[]{:S(2)}) collective-permute-start(bf16[128,2560]{1,0:T(8,128)(2,1)S(1)} %fusion), channel_id=1, source_target_pairs={{0,2},{2,0},{1,3},{3,1},{4,6},{6,4},{5,7},{7,5},{8,10},{10,8},{9,1... | collective-permute-start | bytes 1966088 | tf_op jit(solution)/shard_map/ppermute | solution.py:20
  5.6 5.6 %collective-permute-start.2 = (f32[9,128]{1,0:T(8,128)S(1)}, f32[9,128]{1,0:T(8,128)S(1)}, u32[]{:S(2)}, u32[]{:S(2)}) collective-permute-start(f32[9,128]{1,0:T(8,128)S(1)} %concatenate.14.rest_0_.rest_2_), channel_id=1, source_target_pairs={{0,12},{4,0},{8,4},{12,8},{1,13},{5,1},{9,5},{13,9},{2,14},{6,2},{... | collective-permute-start | bytes 13832 | tf_op jit(solution)/shard_map/ppermute | solution.py:20
  9.3 4.5 %collective-permute-start.1 = (f32[9,128]{1,0:T(8,128)S(1)}, f32[9,128]{1,0:T(8,128)S(1)}, u32[]{:S(2)}, u32[]{:S(2)}) collective-permute-start(f32[9,128]{1,0:T(8,128)S(1)} %concatenate.14.rest_0_.rest_2_), channel_id=1, source_target_pairs={{0,8},{4,12},{8,0},{12,4},{1,9},{5,13},{9,1},{13,5},{2,10},{6,14},... | collective-permute-start | bytes 13832 | tf_op jit(solution)/shard_map/ppermute | solution.py:20
  9.3 5.4 %collective-permute-start = (f32[9,128]{1,0:T(8,128)S(1)}, f32[9,128]{1,0:T(8,128)S(1)}, u32[]{:S(2)}, u32[]{:S(2)}) collective-permute-start(f32[9,128]{1,0:T(8,128)S(1)} %concatenate.14.rest_0_.rest_2_), channel_id=1, source_target_pairs={{0,4},{4,8},{8,12},{12,0},{1,5},{5,9},{9,13},{13,1},{2,6},{6,10},{... | collective-permute-start | bytes 13832 | tf_op jit(solution)/shard_map/ppermute | solution.py:20
  10.3 9.4 %collective-permute-start.4 = (f32[1,256]{1,0:T(1,128)S(1)}, f32[1,256]{1,0:T(1,128)S(1)}, u32[]{:S(2)}, u32[]{:S(2)}) collective-permute-start(f32[1,256]{1,0:T(1,128)S(1)} %convert_element_type.24.rest_6_), channel_id=1, source_target_pairs={{0,2},{2,0},{1,3},{3,1},{4,6},{6,4},{5,7},{7,5},{8,10},{10,8},{9,1... | collective-permute-start | bytes 3080 | tf_op jit(solution)/shard_map/ppermute | solution.py:20
  15.3 4.4 %collective-permute-start.3 = (bf16[1,128,128]{2,1,0:T(8,128)(2,1)S(1)}, bf16[1,128,128]{2,1,0:T(8,128)(2,1)S(1)}, u32[]{:S(2)}, u32[]{:S(2)}) collective-permute-start(bf16[1,128,128]{2,1,0:T(8,128)(2,1)S(1)} %shard_map.140.rest_0_), channel_id=1, source_target_pairs={{0,1},{1,0},{2,3},{3,2},{4,5},{5,4},{6,7},{7,6},{8,9},{9,8},{10,11... | collective-permute-start | bytes 98312 | tf_op jit(solution)/shard_map/ppermute | solution.py:20
  21.2 1.2 %copy-start = (bf16[1536,512]{1,0:T(8,128)(2,1)}, bf16[1536,512]{1,0:T(8,128)(2,1)S(1)}, u32[]{:S(2)}) copy-start(bf16[1536,512]{1,0:T(8,128)(2,1)S(1)} %get-tuple-element.15.earlier_ref.rest_1_) | copy-start | bytes 4718596
  22.4 0.8 %copy-start.5 = (f32[1,256,512]{2,1,0:T(8,128)}, f32[1,256,512]{2,1,0:T(8,128)S(1)}, u32[]{:S(2)}) copy-start(f32[1,256,512]{2,1,0:T(8,128)S(1)} %get-tuple-element.11.scale_ref) | copy-start | bytes 1572868
  23.2 0.8 %copy-start.7 = (f32[1,256,512]{2,1,0:T(8,128)}, f32[1,256,512]{2,1,0:T(8,128)S(1)}, u32[]{:S(2)}) copy-start(f32[1,256,512]{2,1,0:T(8,128)S(1)} %get-tuple-element.12.shift_ref) | copy-start | bytes 1572868
  24.0 0.8 %copy-start.9 = (bf16[2,256,512]{2,1,0:T(8,128)(2,1)}, bf16[2,256,512]{2,1,0:T(8,128)(2,1)S(1)}, u32[]{:S(2)}) copy-start(bf16[2,256,512]{2,1,0:T(8,128)(2,1)S(1)} %get-tuple-element.14.rest_0_) | copy-start | bytes 1572868
  24.8 0.7 %copy-start.12 = (f32[2,256,128]{2,1,0:T(8,128)}, f32[2,256,128]{2,1,0:T(8,128)S(1)}, u32[]{:S(2)}) copy-start(f32[2,256,128]{2,1,0:T(8,128)S(1)} %get-tuple-element.13.gain_ref) | copy-start | bytes 786436
  25.5 0.8 %copy-start.3 = (bf16[128,2560]{1,0:T(8,128)(2,1)}, bf16[128,2560]{1,0:T(8,128)(2,1)S(1)}, u32[]{:S(2)}) copy-start(bf16[128,2560]{1,0:T(8,128)(2,1)S(1)} %collective-permute-done.5.section_ref) | copy-start | bytes 1966084
  26.3 2.3 %copy-start.1 = (bf16[1536,512]{1,0:T(8,128)(2,1)S(1)}, bf16[1536,512]{1,0:T(8,128)(2,1)}, u32[]{:S(2)}) copy-start(bf16[1536,512]{1,0:T(8,128)(2,1)} %copy-done) | copy-start | bytes 4718596
  26.3 2.3 %copy-start.2 = (bf16[1,256,2304]{2,1,0:T(8,128)(2,1)S(1)}, bf16[1,256,2304]{2,1,0:T(8,128)(2,1)}, u32[]{:S(2)}) copy-start(bf16[1,256,2304]{2,1,0:T(8,128)(2,1)} %param.22) | copy-start | bytes 3538948
  26.3 2.3 %collective-permute-start.6 = (bf16[128,2560]{1,0:T(8,128)(2,1)}, bf16[128,2560]{1,0:T(8,128)(2,1)S(1)}, u32[]{:S(2)}, u32[]{:S(2)}) collective-permute-start(bf16[128,2560]{1,0:T(8,128)(2,1)} %shard_map.142.rest_4_), channel_id=1, source_target_pairs={{0,1},{1,0},{2,3},{3,2},{4,5},{5,4},{6,7},{7,6},{8,9},{9,8},{10,11... | collective-permute-start | bytes 1966088 | tf_op jit(solution)/shard_map/ppermute | solution.py:20
  28.6 1.1 %copy-start.4 = (bf16[128,2560]{1,0:T(8,128)(2,1)S(1)}, bf16[128,2560]{1,0:T(8,128)(2,1)}, u32[]{:S(2)}) copy-start(bf16[128,2560]{1,0:T(8,128)(2,1)} %shard_map.142.rest_4_) | copy-start | bytes 1966084
  29.7 1.0 %copy-start.6 = (f32[1,256,512]{2,1,0:T(8,128)S(1)}, f32[1,256,512]{2,1,0:T(8,128)}, u32[]{:S(2)}) copy-start(f32[1,256,512]{2,1,0:T(8,128)} %copy-done.5) | copy-start | bytes 1572868
  30.8 1.0 %copy-start.8 = (f32[1,256,512]{2,1,0:T(8,128)S(1)}, f32[1,256,512]{2,1,0:T(8,128)}, u32[]{:S(2)}) copy-start(f32[1,256,512]{2,1,0:T(8,128)} %copy-done.7) | copy-start | bytes 1572868
  31.8 1.0 %copy-start.10 = (bf16[2,256,512]{2,1,0:T(8,128)(2,1)S(1)}, bf16[2,256,512]{2,1,0:T(8,128)(2,1)}, u32[]{:S(2)}) copy-start(bf16[2,256,512]{2,1,0:T(8,128)(2,1)} %copy-done.9) | copy-start | bytes 1572868
  32.8 0.9 %copy-start.11 = (bf16[1,256,256]{2,1,0:T(8,128)(2,1)S(1)}, bf16[1,256,256]{2,1,0:T(8,128)(2,1)}, u32[]{:S(2)}) copy-start(bf16[1,256,256]{2,1,0:T(8,128)(2,1)} %param.23) | copy-start | bytes 393220
  33.7 0.9 %copy-start.13 = (f32[2,256,128]{2,1,0:T(8,128)S(1)}, f32[2,256,128]{2,1,0:T(8,128)}, u32[]{:S(2)}) copy-start(f32[2,256,128]{2,1,0:T(8,128)} %copy-done.12) | copy-start | bytes 786436

commit v3 on v2

--- a/solution.py
+++ b/solution.py
@@ -8,7 +8,7 @@
 from jax.sharding import PartitionSpec as P
 
 BF16_ROWS = 16
-VMEM_BYTES = 28 * 1024 * 1024
+MIB = 1024 * 1024
 
 
 def padded_rows(count):
@@ -64,17 +64,10 @@
     steps, layers, bands, local, members, lon, chans, vp, fp, turns = dims
     fields, rest = rest[:bands], rest[bands:]
     group, rest = rest[: members * turns], rest[members * turns :]
-    gains, rest = rest[:layers], rest[layers:]
-    field_ref, scale_ref, shift_ref, gain_ref, hidden_ref, taps_ref = rest
-    here, band = scalar_ref[0], scalar_ref[1]
+    field_ref, scale_ref, shift_ref, hidden_ref, taps_ref = rest
+    band = scalar_ref[1]
     for b in range(bands):
         field_ref[b * local : (b + 1) * local] = from_place([f[...] for f in fields], band, b)
-
-    eye = lax.broadcasted_iota(jnp.int32, (chans, chans), 0) == lax.broadcasted_iota(jnp.int32, (chans, chans), 1)
-    for layer in range(layers):
-        row = from_place([g[...] for g in gains], here, layer)
-        column = jnp.sum(jnp.where(eye, row, 0.0), axis=1, keepdims=True)
-        gain_ref[layer] = jnp.broadcast_to(column, (chans, lon))
 
     settings = settings_ref[...]
     numbers = lax.broadcasted_iota(jnp.int32, settings.shape, 0).astype(jnp.float32)
@@ -111,16 +104,18 @@
         in_specs=[whole, whole],
         out_specs=whole,
         input_output_aliases={0: 0},
+        compiler_params=pltpu.CompilerParams(vmem_limit_bytes=MIB),
         cost_estimate=pl.CostEstimate(flops=0, bytes_accessed=0, transcendentals=0),
     )(section, earlier)
 
 
-def window_kernel(dims, scalar_ref, field_ref, scale_ref, shift_ref, gain_ref, enc_ref, dec_ref, *rest):
+def window_kernel(dims, scalar_ref, field_ref, scale_ref, shift_ref, enc_ref, dec_ref, *rest):
     steps, layers, bands, local, members, lon, chans, vp, fp, turns = dims
     lat = bands * local
+    gains, rest = rest[:layers], rest[layers:]
     hidden, taps = rest[:2]
     blocks, rest = rest[2 : 4 + (layers - 1) * bands], rest[4 + (layers - 1) * bands :]
-    final_ref, mean_ref, weights, conv, act, inputs, total, sems = rest[:8]
+    final_ref, mean_ref, weights, gain_ref, conv, act, inputs, total, sems = rest[:9]
     here, band = scalar_ref[0], scalar_ref[1]
     taps_wide, wide = 9 * chans, 3 * chans
     part = chans // bands
@@ -136,7 +131,13 @@
             ).start()
 
     if turns > 1:
-        hidden, taps = rest[8:]
+        hidden, taps = rest[9:]
+
+    eye = lax.broadcasted_iota(jnp.int32, (chans, chans), 0) == lax.broadcasted_iota(jnp.int32, (chans, chans), 1)
+    for layer in range(layers):
+        row = from_place([g[...] for g in gains], here, layer)
+        column = jnp.sum(jnp.where(eye, row, 0.0), axis=1, keepdims=True)
+        gain_ref[layer] = jnp.broadcast_to(column, (chans, lon)).astype(jnp.bfloat16)
 
     def columns(m):
         return slice(m * lon, (m + 1) * lon)
@@ -164,7 +165,7 @@
     def activate(value, layer):
         centred = value - jnp.sum(value, axis=0, keepdims=True) * (1.0 / chans)
         spread = jnp.sum(centred * centred, axis=0, keepdims=True) * (1.0 / chans)
-        normed = (centred * lax.rsqrt(spread + 1e-05)).astype(jnp.bfloat16) * gain_ref[layer].astype(jnp.bfloat16)
+        normed = (centred * lax.rsqrt(spread + 1e-05)).astype(jnp.bfloat16) * gain_ref[layer]
         inner = normed * (normed * normed * 0.0356774081 + 0.7978845608)
         half = normed * 0.5
         return half + half * jnp.tanh(inner)
@@ -257,7 +258,7 @@
     at_once = next(n for n in (4, 2, 1) if members % n == 0)
     turns, wide = members // at_once, at_once * lon
     smem, vmem, whole = (pl.BlockSpec(memory_space=s) for s in (pltpu.SMEM, pltpu.VMEM, pl.ANY))
-    params = pltpu.CompilerParams(vmem_limit_bytes=VMEM_BYTES)
+    small, large = (pltpu.CompilerParams(vmem_limit_bytes=n * MIB) for n in (8, 16 + 2 * layers))
     free = pl.CostEstimate(flops=0, bytes_accessed=0, transcendentals=0)
 
     mine = jnp.concatenate([conv_weight[0], point_weight[0]], axis=1)
@@ -276,7 +277,7 @@
         out_shape=jax.ShapeDtypeStruct((local, vp + fp * steps + BF16_ROWS, lon), jnp.bfloat16),
         in_specs=[smem] + [vmem] * (2 + members),
         out_specs=vmem,
-        compiler_params=params,
+        compiler_params=small,
         cost_estimate=free,
     )(scalars, init_state[0], land_mask, *group)
     fields = all_along(field, "rows")
@@ -285,21 +286,20 @@
     enc = jnp.concatenate([enc, jnp.pad(encode_weight[:, varied:], ((0, 0), (0, fp - forced)))], axis=1)
     dec = jnp.pad(decode_weight, ((0, vp - varied), (0, 0)))
     dims = (steps, layers, bands, local, at_once, lon, chans, vp, fp, turns)
-    field, scale, shift, gain, hidden, taps = pl.pallas_call(
+    field, scale, shift, hidden, taps = pl.pallas_call(
         functools.partial(first_kernel, dims),
         out_shape=(
             jax.ShapeDtypeStruct((lat, vp + fp * steps + BF16_ROWS, lon), jnp.bfloat16),
             jax.ShapeDtypeStruct((turns, chans, wide), jnp.float32),
             jax.ShapeDtypeStruct((turns, chans, wide), jnp.float32),
-            jax.ShapeDtypeStruct((layers, chans, lon), jnp.float32),
             jax.ShapeDtypeStruct((lat, chans, wide), jnp.bfloat16),
             jax.ShapeDtypeStruct((lat * 3 * chans, wide), jnp.bfloat16),
         ),
-        in_specs=[smem] + [vmem] * (4 + bands + members + layers),
-        out_specs=(vmem,) * 6,
-        compiler_params=params,
+        in_specs=[smem] + [vmem] * (4 + bands + members),
+        out_specs=(vmem,) * 5,
+        compiler_params=small,
         cost_estimate=free,
-    )(scalars, enc, settings, scale_weight.T, shift_weight.T, *fields, *group, *gains)
+    )(scalars, enc, settings, scale_weight.T, shift_weight.T, *fields, *group)
 
     blocks = [conv_weight[0], point_weight[0]]
     for section in sections:
@@ -307,6 +307,7 @@
 
     scratch = [
         pltpu.VMEM((layers, chans, 10 * chans), jnp.bfloat16),
+        pltpu.VMEM((layers, chans, lon), jnp.bfloat16),
         pltpu.VMEM((lat, chans, wide), jnp.float32),
         pltpu.VMEM((lat, chans, wide), jnp.bfloat16),
         pltpu.VMEM((lat, vp + fp, wide), jnp.bfloat16),
@@ -321,12 +322,12 @@
             jax.ShapeDtypeStruct((local, varied, lon), jnp.bfloat16),
             jax.ShapeDtypeStruct((varied, local, lon), jnp.float32),
         ),
-        in_specs=[smem] + [vmem] * 8 + [whole] * len(blocks),
+        in_specs=[smem] + [vmem] * (7 + layers) + [whole] * len(blocks),
         out_specs=(vmem, vmem),
         scratch_shapes=scratch,
-        compiler_params=params,
+        compiler_params=large,
         cost_estimate=free,
-    )(scalars, field, scale, shift, gain, enc, dec, hidden, taps, *blocks)
+    )(scalars, field, scale, shift, enc, dec, *gains, hidden, taps, *blocks)
     return final[None, None], jnp.swapaxes(mean, 0, 1)[None]
 def solution(mesh):
     in_specs = (

time: 43.9 us -> 33.2 us (0.76)
  local copies, waits for them, and re-layouts: 12.7 us -> 1.19 us
  starting transfers between devices: 8.28 us -> 9.55 us
  waiting for transfers between devices: 8.82 us -> 8.38 us
    unnamed x53 -> x31, local copies, waits for them, and re-layouts: 11.8 us -> 1.17 us
    ppermute x7, starting transfers between devices: 8.28 us -> 9.55 us  [passed_along(): lax.ppermute(block, axis, [(i, (i + distance) % size) for i in range(size)])]
    pad x1, local copies, waits for them, and re-layouts: 0.94 us -> 0.01 us  [per_device(): dec = jnp.pad(decode_weight, ((0, vp - varied), (0, 0)))]
  transfers between devices with their start and end apart: 7 -> 7, of which waited for: 4 -> 5; matrix products, arithmetic and copies ran while one was open for 4% -> 2% of each run, Pallas kernels for 5% -> 6%
where the time goes in v3:
time: 33.2 us; the launch traced here: 33.1 us
  Pallas kernels  11.1 us (33%)
  starting transfers between devices  9.55 us (29%)
  waiting for transfers between devices  8.38 us (25%)
  between operations  1.5 us (5%)
  other arithmetic  1.36 us (4%)
  local copies, waits for them, and re-layouts  1.19 us (4%)
    ppermute x7, starting transfers between devices, passed_along(): lax.ppermute(block, axis, [(i, (i + distance) % size) for i in range(size)])  9.55 us
    pallas_call x1, Pallas kernels, per_device(): pl.pallas_call(functools.partial(window_kernel, dims), out_shape=(jax.Sha...  9.16 us
    ppermute x7, waiting for transfers between devices, passed_along(): lax.ppermute(block, axis, [(i, (i + distance) % size) for i in range(size)])  8.38 us
    pallas_call x1, Pallas kernels, per_device(): pl.pallas_call(functools.partial(first_kernel, dims), out_shape=(jax.Shap...  1.37 us
    unnamed x31, local copies, waits for them, and re-layouts  1.17 us
    concatenate x1, other arithmetic, per_device(): mine = jnp.concatenate([conv_weight[0], point_weight[0]], axis=1)  1.17 us
  transfers between devices with their start and end apart: 7, of which 5 were waited for; matrix products, arithmetic and copies ran while one was open for 2% of the time, Pallas kernels for 6%

profile of v3, /device:TPU:0, one launch (start us, length us, event | category | flops | bytes accessed | tf_op | source)
XLA Modules:
  0.0 33.1 jit_solution(15900435928614010621)
XLA Ops:
  0.6 0.0 copy-start.11
  0.6 0.0 copy-start.9
  0.7 0.0 slice-start
  0.7 0.0 copy-start.4
  0.7 0.0 copy-start.12
  0.7 0.0 copy-start.3
  0.7 0.0 copy-start.2
  0.7 0.0 copy-start.8
  0.7 0.0 copy-start.6
  0.7 0.0 copy-start.7
  0.7 1.2 %fusion = bf16[128,2560]{1,0:T(8,128)(2,1)S(1)} fusion(s32[]{:T(128)S(6)} %select_n.3, bf16[256,2304]{1,0:T(8,128)(2,1)} %bitcast.16, bf16[256,256]{1,0:T(8,128)(2,1)} %bitcast.18), kind=kLoop, calls=%fused_computation.2 | loop fusion | flops 1310720 | bytes 1966084 | tf_op jit(solution)/shard_map/concatenate | solution.py:264
  1.9 3.0 %collective-permute-start.5 = (bf16[128,2560]{1,0:T(8,128)(2,1)S(1)}, bf16[128,2560]{1,0:T(8,128)(2,1)S(1)}, u32[]{:S(2)}, u32[]{:S(2)}) collective-permute-start(bf16[128,2560]{1,0:T(8,128)(2,1)S(1)} %fusion), channel_id=1, source_target_pairs={{0,2},{2,0},{1,3},{3,1},{4,6},{6,4},{5,7},{7,5},{8,10},{10,8},{9,1... | collective-permute-start | bytes 1966088 | tf_op jit(solution)/shard_map/ppermute | solution.py:20
  5.6 0.0 copy-done.9
  5.6 3.7 %collective-permute-start.2 = (f32[9,128]{1,0:T(8,128)S(1)}, f32[9,128]{1,0:T(8,128)S(1)}, u32[]{:S(2)}, u32[]{:S(2)}) collective-permute-start(f32[9,128]{1,0:T(8,128)S(1)} %concatenate.14.rest_0_.rest_2_), channel_id=1, source_target_pairs={{0,12},{4,0},{8,4},{12,8},{1,13},{5,1},{9,5},{13,9},{2,14},{6,2},{... | collective-permute-start | bytes 13832 | tf_op jit(solution)/shard_map/ppermute | solution.py:20
  9.2 0.0 collective-permute-start.1
  9.2 1.0 %collective-permute-start = (f32[9,128]{1,0:T(8,128)S(1)}, f32[9,128]{1,0:T(8,128)S(1)}, u32[]{:S(2)}, u32[]{:S(2)}) collective-permute-start(f32[9,128]{1,0:T(8,128)S(1)} %concatenate.14.rest_0_.rest_2_), channel_id=1, source_target_pairs={{0,4},{4,8},{8,12},{12,0},{1,5},{5,9},{9,13},{13,1},{2,6},{6,10},{... | collective-permute-start | bytes 13832 | tf_op jit(solution)/shard_map/ppermute | solution.py:20
  10.3 0.0 slice-done
  10.3 0.1 copy.22
  10.4 0.0 copy-done.11
  10.4 0.0 copy-done.12
  10.4 0.1 pad_add_fusion.scalar_ref
  10.5 0.0 copy-done.4
  10.5 0.1 copy.23
  10.7 0.0 collective-permute-done.2.rest_3_.rest_5_
  10.7 3.1 %collective-permute-done.1.rest_2_.rest_4_ = f32[9,128]{1,0:T(8,128)S(1)} collective-permute-done((f32[9,128]{1,0:T(8,128)S(1)}, f32[9,128]{1,0:T(8,128)S(1)}, u32[]{:S(2)}, u32[]{:S(2)}) %collective-permute-start.1) | collective-permute-done | bytes 4640 | tf_op jit(solution)/shard_map/ppermute | solution.py:20
  13.8 0.9 %collective-permute-done.rest_1_.rest_3_ = f32[9,128]{1,0:T(8,128)S(1)} collective-permute-done((f32[9,128]{1,0:T(8,128)S(1)}, f32[9,128]{1,0:T(8,128)S(1)}, u32[]{:S(2)}, u32[]{:S(2)}) %collective-permute-start) | collective-permute-done | bytes 4640 | tf_op jit(solution)/shard_map/ppermute | solution.py:20
  14.7 0.0 copy-done.3
  14.7 0.0 copy-done.2
  14.7 0.6 %shard_map.140.rest_0_ = bf16[1,128,128]{2,1,0:T(8,128)(2,1)S(1)} custom-call(s32[5]{0:T(128)S(1)} %pad_add_fusion.scalar_ref, bf16[1,77,128]{2,1,0:T(8,128)(2,1)S(1)} %bitcast.22, s32[1,128]{1,0:T(1,128)S(1)} %copy-done.3, f32[9,128]{1,0:T(8,128)S(1)} %concatenate.14.rest_0_.rest_2_, f32[9,128]{1,0:T(8,128)S(1)} %collective-permute-done.rest_1_.rest_3_, ...), custom_call_target="tpu_custom_call" | custom-call | tf_op jit(solution)/shard_map/pallas_call | solution.py:275
  15.3 0.1 collective-permute-start.3
  15.3 0.1 fusion.2.enc_ref
  15.4 0.0 copy-done.8
  15.5 0.1 copy.20.settings_ref
  15.5 0.0 copy-done.6
  15.5 0.1 copy.18
  15.6 0.0 copy-done.7
  15.7 0.1 copy.19
  15.8 0.8 %collective-permute-done.3.rest_1_ = bf16[1,128,128]{2,1,0:T(8,128)(2,1)S(1)} collective-permute-done((bf16[1,128,128]{2,1,0:T(8,128)(2,1)S(1)}, bf16[1,128,128]{2,1,0:T(8,128)(2,1)S(1)}, u32[]{:S(2)}, u32[]{:S(2)}) %collective-permute-start.3) | collective-permute-done | bytes 32800 | tf_op jit(solution)/shard_map/ppermute | solution.py:20
  16.5 1.4 %shard_map.141 = (bf16[2,128,128]{2,1,0:T(8,128)(2,1)S(1)}, f32[1,256,512]{2,1,0:T(8,128)S(1)}, f32[1,256,512]{2,1,0:T(8,128)S(1)}, bf16[2,256,512]{2,1,0:T(8,128)(2,1)S(1)}, bf16[1536,512]{1,0:T(8,128)(2,1)S(1)}) custom-call(s32[5]{0:T(128)S(1)} %pad_add_fusion.scalar_ref, bf16[256,96]{1,0:T(8,128)(2,1)S(1)} %fusion.2.enc_ref, ...), custom_call_target="tpu_custom_call" | custom-call | tf_op jit(solution)/shard_map/pallas_call | solution.py:289
  17.9 1.7 %collective-permute-done.5.section_ref = bf16[128,2560]{1,0:T(8,128)(2,1)S(1)} collective-permute-done((bf16[128,2560]{1,0:T(8,128)(2,1)S(1)}, bf16[128,2560]{1,0:T(8,128)(2,1)S(1)}, u32[]{:S(2)}, u32[]{:S(2)}) %collective-permute-start.5) | collective-permute-done | bytes 655392 | tf_op jit(solution)/shard_map/ppermute | solution.py:20
  19.7 0.1 collective-permute-start.6
  19.8 0.6 %copy-done.10 = bf16[1,256]{1,0:T(2,128)(2,1)S(1)} copy-done((bf16[1,256]{1,0:T(2,128)(2,1)S(1)}, bf16[1,256]{1,0:T(2,128)(2,1)}, u32[]{:S(2)}) %copy-start.10) | copy-done | bytes 536
  20.3 1.7 %collective-permute-start.4 = (f32[1,256]{1,0:T(1,128)S(1)}, f32[1,256]{1,0:T(1,128)S(1)}, u32[]{:S(2)}, u32[]{:S(2)}) collective-permute-start(f32[1,256]{1,0:T(1,128)S(1)} %convert_element_type.24.rest_0_), channel_id=1, source_target_pairs={{0,2},{2,0},{1,3},{3,1},{4,6},{6,4},{5,7},{7,5},{8,10},{10,8},{9,1... | collective-permute-start | bytes 3080 | tf_op jit(solution)/shard_map/ppermute | solution.py:20
  22.1 0.0 copy-done.5
  22.1 1.8 %collective-permute-done.4.rest_1_ = f32[1,256]{1,0:T(1,128)S(1)} collective-permute-done((f32[1,256]{1,0:T(1,128)S(1)}, f32[1,256]{1,0:T(1,128)S(1)}, u32[]{:S(2)}, u32[]{:S(2)}) %collective-permute-start.4) | collective-permute-done | bytes 1056 | tf_op jit(solution)/shard_map/ppermute | solution.py:20
  23.9 0.0 collective-permute-done.6.rest_7_
  23.9 0.0 copy-done.1
  23.9 9.2 %shard_map.143 = (bf16[1,77,128]{2,1,0:T(8,128)(2,1)}, f32[77,1,128]{2,1,0:T(1,128)}) custom-call(s32[5]{0:T(128)S(1)} %pad_add_fusion.scalar_ref, bf16[2,128,128]{2,1,0:T(8,128)(2,1)S(1)} %get-tuple-element.9.field_ref, f32[1,256,512]{2,1,0:T(8,128)S(1)} %get-tuple-element.10.scale_ref, f32[1,256,512]{2,1,0:T(8,128)S(1)} %get-tuple-element.11.shift_ref, ...), custom_call_target="tpu_custom_call" | custom-call | tf_op jit(solution)/shard_map/pallas_call | solution.py:319
  (11 shorter events, 0.0 us)
Async XLA Ops:
  0.6 9.7 %copy-start.11 = (pred[80]{0:T(512)(128)(4,1)S(1)}, pred[80]{0:T(512)(128)(4,1)}, u32[]{:S(2)}) copy-start(pred[80]{0:T(512)(128)(4,1)} %constant.16.clone.1) | copy-start | bytes 244
  0.6 4.9 %copy-start.9 = (bf16[1,1,2,1,4,128]{5,4,3,2,1,0:T(4,128)(2,1)S(1)}, bf16[1,1,2,1,4,128]{5,4,3,2,1,0:T(4,128)(2,1)}, u32[]{:S(2)}) copy-start(bf16[1,1,2,1,4,128]{5,4,3,2,1,0:T(4,128)(2,1)} %param.14) | copy-start | bytes 6148
  0.7 9.6 %slice-start = ((bf16[256,81]{0,1:T(8,128)(2,1)}), bf16[256,80]{0,1:T(8,128)(2,1)S(1)}, s32[]{:S(2)}) async-start(bf16[256,81]{0,1:T(8,128)(2,1)} %param.21), calls=%async_computation | async-start | bytes 81920 | tf_op jit(solution)/shard_map/slice
  0.7 9.8 %copy-start.4 = (bf16[256,81]{0,1:T(8,128)(2,1)S(1)}, bf16[256,81]{0,1:T(8,128)(2,1)}, u32[]{:S(2)}) copy-start(bf16[256,81]{0,1:T(8,128)(2,1)} %param.21) | copy-start | bytes 124420
  0.7 9.7 %copy-start.12 = (s32[1,2]{1,0:T(1,128)S(1)}, s32[1,2]{1,0:T(1,128)}, u32[]{:S(2)}) copy-start(s32[1,2]{1,0:T(1,128)} %param.15) | copy-start | bytes 28
  0.7 14.0 %copy-start.3 = (s32[1,128]{1,0:T(1,128)S(1)}, s32[1,128]{1,0:T(1,128)}, u32[]{:S(2)}) copy-start(s32[1,128]{1,0:T(1,128)} %land_ref.1) | copy-start | bytes 1540
  0.7 14.0 %copy-start.2 = (bf16[1,1,77,128]{3,2,1,0:T(8,128)(2,1)S(1)}, bf16[1,1,77,128]{3,2,1,0:T(8,128)(2,1)}, u32[]{:S(2)}) copy-start(bf16[1,1,77,128]{3,2,1,0:T(8,128)(2,1)} %param.13) | copy-start | bytes 59140
  0.7 14.7 %copy-start.8 = (f32[64,16]{0,1:T(8,128)S(1)}, f32[64,16]{0,1:T(8,128)}, u32[]{:S(2)}) copy-start(f32[64,16]{0,1:T(8,128)} %param.18) | copy-start | bytes 12292
  0.7 14.8 %copy-start.6 = (f32[16,256]{1,0:T(8,128)S(1)}, f32[16,256]{1,0:T(8,128)}, u32[]{:S(2)}) copy-start(f32[16,256]{1,0:T(8,128)} %param.19) | copy-start | bytes 49156
  0.7 14.9 %copy-start.7 = (f32[16,256]{1,0:T(8,128)S(1)}, f32[16,256]{1,0:T(8,128)}, u32[]{:S(2)}) copy-start(f32[16,256]{1,0:T(8,128)} %param.20) | copy-start | bytes 49156
  1.9 17.7 %collective-permute-start.5 = (bf16[128,2560]{1,0:T(8,128)(2,1)S(1)}, bf16[128,2560]{1,0:T(8,128)(2,1)S(1)}, u32[]{:S(2)}, u32[]{:S(2)}) collective-permute-start(bf16[128,2560]{1,0:T(8,128)(2,1)S(1)} %fusion), channel_id=1, source_target_pairs={{0,2},{2,0},{1,3},{3,1},{4,6},{6,4},{5,7},{7,5},{8,10},{10,8},{9,1... | collective-permute-start | bytes 1966088 | tf_op jit(solution)/shard_map/ppermute | solution.py:20
  5.6 5.1 %collective-permute-start.2 = (f32[9,128]{1,0:T(8,128)S(1)}, f32[9,128]{1,0:T(8,128)S(1)}, u32[]{:S(2)}, u32[]{:S(2)}) collective-permute-start(f32[9,128]{1,0:T(8,128)S(1)} %concatenate.14.rest_0_.rest_2_), channel_id=1, source_target_pairs={{0,12},{4,0},{8,4},{12,8},{1,13},{5,1},{9,5},{13,9},{2,14},{6,2},{... | collective-permute-start | bytes 13832 | tf_op jit(solution)/shard_map/ppermute | solution.py:20
  9.2 4.5 %collective-permute-start.1 = (f32[9,128]{1,0:T(8,128)S(1)}, f32[9,128]{1,0:T(8,128)S(1)}, u32[]{:S(2)}, u32[]{:S(2)}) collective-permute-start(f32[9,128]{1,0:T(8,128)S(1)} %concatenate.14.rest_0_.rest_2_), channel_id=1, source_target_pairs={{0,8},{4,12},{8,0},{12,4},{1,9},{5,13},{9,1},{13,5},{2,10},{6,14},... | collective-permute-start | bytes 13832 | tf_op jit(solution)/shard_map/ppermute | solution.py:20
  9.2 5.4 %collective-permute-start = (f32[9,128]{1,0:T(8,128)S(1)}, f32[9,128]{1,0:T(8,128)S(1)}, u32[]{:S(2)}, u32[]{:S(2)}) collective-permute-start(f32[9,128]{1,0:T(8,128)S(1)} %concatenate.14.rest_0_.rest_2_), channel_id=1, source_target_pairs={{0,4},{4,8},{8,12},{12,0},{1,5},{5,9},{9,13},{13,1},{2,6},{6,10},{... | collective-permute-start | bytes 13832 | tf_op jit(solution)/shard_map/ppermute | solution.py:20
  15.3 1.3 %collective-permute-start.3 = (bf16[1,128,128]{2,1,0:T(8,128)(2,1)S(1)}, bf16[1,128,128]{2,1,0:T(8,128)(2,1)S(1)}, u32[]{:S(2)}, u32[]{:S(2)}) collective-permute-start(bf16[1,128,128]{2,1,0:T(8,128)(2,1)S(1)} %shard_map.140.rest_0_), channel_id=1, source_target_pairs={{0,1},{1,0},{2,3},{3,2},{4,5},{5,4},{6,7},{7,6},{8,9},{9,8},{10,11... | collective-permute-start | bytes 98312 | tf_op jit(solution)/shard_map/ppermute | solution.py:20
  19.7 0.7 %copy-start.10 = (bf16[1,256]{1,0:T(2,128)(2,1)S(1)}, bf16[1,256]{1,0:T(2,128)(2,1)}, u32[]{:S(2)}) copy-start(bf16[1,256]{1,0:T(2,128)(2,1)} %param.24) | copy-start | bytes 1540
  19.7 2.4 %copy-start.5 = (bf16[77,256]{1,0:T(8,128)(2,1)S(1)}, bf16[77,256]{1,0:T(8,128)(2,1)}, u32[]{:S(2)}) copy-start(bf16[77,256]{1,0:T(8,128)(2,1)} %param.25) | copy-start | bytes 118276
  19.7 4.3 %copy-start = (bf16[1,256,2304]{2,1,0:T(8,128)(2,1)S(1)}, bf16[1,256,2304]{2,1,0:T(8,128)(2,1)}, u32[]{:S(2)}) copy-start(bf16[1,256,2304]{2,1,0:T(8,128)(2,1)} %param.22) | copy-start | bytes 3538948
  19.7 4.3 %copy-start.1 = (bf16[1,256,256]{2,1,0:T(8,128)(2,1)S(1)}, bf16[1,256,256]{2,1,0:T(8,128)(2,1)}, u32[]{:S(2)}) copy-start(bf16[1,256,256]{2,1,0:T(8,128)(2,1)} %param.23) | copy-start | bytes 393220
  19.7 4.2 %collective-permute-start.6 = (bf16[128,2560]{1,0:T(8,128)(2,1)S(1)}, bf16[128,2560]{1,0:T(8,128)(2,1)S(1)}, u32[]{:S(2)}, u32[]{:S(2)}) collective-permute-start(bf16[128,2560]{1,0:T(8,128)(2,1)S(1)} %shard_map.142.rest_6_), channel_id=1, source_target_pairs={{0,1},{1,0},{2,3},{3,2},{4,5},{5,4},{6,7},{7,6},{8,9},{9,8},{10,11... | collective-permute-start | bytes 1966088 | tf_op jit(solution)/shard_map/ppermute | solution.py:20
  20.3 3.6 %collective-permute-start.4 = (f32[1,256]{1,0:T(1,128)S(1)}, f32[1,256]{1,0:T(1,128)S(1)}, u32[]{:S(2)}, u32[]{:S(2)}) collective-permute-start(f32[1,256]{1,0:T(1,128)S(1)} %convert_element_type.24.rest_0_), channel_id=1, source_target_pairs={{0,2},{2,0},{1,3},{3,1},{4,6},{6,4},{5,7},{7,5},{8,10},{10,8},{9,1... | collective-permute-start | bytes 3080 | tf_op jit(solution)/shard_map/ppermute | solution.py:20

commit v4 on v3

--- a/solution.py
+++ b/solution.py
@@ -29,6 +29,19 @@
     for k in range(1, len(parts)):
         chosen = jnp.where(lax.rem(here - k + len(parts), len(parts)) == place, parts[k], chosen)
     return chosen
+
+
+def pack_kernel(bands, scalar_ref, conv_ref, point_ref, out_ref, sems):
+    part, wide = out_ref.shape[0], conv_ref.shape[1]
+    rows = pl.ds(pl.multiple_of(scalar_ref[1] * part, part), part)
+    copies = [
+        pltpu.make_async_copy(conv_ref.at[rows, :], out_ref.at[:, pl.ds(0, wide)], sems.at[0]),
+        pltpu.make_async_copy(point_ref.at[rows, :], out_ref.at[:, pl.ds(wide, point_ref.shape[1])], sems.at[1]),
+    ]
+    for copy in copies:
+        copy.start()
+    for copy in copies:
+        copy.wait()
 
 
 def field_kernel(dims, scalar_ref, state_ref, land_ref, *rest):
@@ -92,21 +105,21 @@
                 put_taps(taps_ref, value, i, cols, 1)
 
 
-def after_kernel(section_ref, earlier_ref, out_ref):
+def after_kernel(*refs):
     pass
 
 
-def after(section, earlier):
+def after(section, *earlier):
     whole = pl.BlockSpec(memory_space=pl.ANY)
     return pl.pallas_call(
         after_kernel,
         out_shape=jax.ShapeDtypeStruct(section.shape, section.dtype),
-        in_specs=[whole, whole],
+        in_specs=[whole] * (1 + len(earlier)),
         out_specs=whole,
         input_output_aliases={0: 0},
         compiler_params=pltpu.CompilerParams(vmem_limit_bytes=MIB),
         cost_estimate=pl.CostEstimate(flops=0, bytes_accessed=0, transcendentals=0),
-    )(section, earlier)
+    )(section, *earlier)
 
 
 def window_kernel(dims, scalar_ref, field_ref, scale_ref, shift_ref, enc_ref, dec_ref, *rest):
@@ -187,14 +200,30 @@
                 preferred_element_type=jnp.float32,
             )
         for i in range(lat):
-            for m in range(members):
-                act[i, :, columns(m)] = activate(conv[i, :, columns(m)], layer)
-        for i in range(lat):
-            mixed = jnp.dot(weights[layer, :, taps_wide:], act[i], preferred_element_type=jnp.float32)
-            for m in range(members):
-                kept = hidden[i, :, columns(m)].astype(jnp.float32)
-                later = layer + 1 if layer + 1 < layers else None
-                put_hidden(i, m, land[i] * (kept + mixed[:, columns(m)]), later)
+            mix(i, i, land[i], layer)
+
+    def mix(i, row, sea, layer):
+        for m in range(members):
+            act[i, :, columns(m)] = activate(conv[i, :, columns(m)], layer)
+        mixed = jnp.dot(weights[layer, :, taps_wide:], act[i], preferred_element_type=jnp.float32)
+        for m in range(members):
+            kept = hidden[row, :, columns(m)].astype(jnp.float32)
+            later = layer + 1 if layer + 1 < layers else None
+            put_hidden(row, m, sea * (kept + mixed[:, columns(m)]), later)
+
+    def decode(row, sea, step):
+        change = jnp.dot(dec_ref[...], hidden[row], preferred_element_type=jnp.float32)
+        for m in range(members):
+            old = field_ref[row, 0:vp, :] if step == 0 else inputs[row, 0:vp, columns(m)]
+            new = old.astype(jnp.float32) + sea * change[:, columns(m)]
+            inputs[row, 0:vp, columns(m)] = new.astype(jnp.bfloat16)
+
+    def last_block(layer):
+        first = pl.multiple_of((1 - band) * wide, wide)
+        conv[0] = jnp.dot(weights[layer, :, pl.ds(first, 2 * wide)], taps[...], preferred_element_type=jnp.float32)
+        sea = field_ref[band, vp + fp * steps : vp + fp * steps + 1, :].astype(jnp.float32)
+        mix(0, band, sea, layer)
+        decode(band, sea, steps - 1)
 
     varied = final_ref.shape[1]
 
@@ -202,14 +231,15 @@
         for step in range(steps):
             if step > 0 or turns > 1:
                 encode(step, turn)
+            own_row = step == steps - 1 and step > 0 and lat == 2 and local == 1
             for layer in range(layers):
-                block(layer, first if step == 0 else None)
-            for i in range(lat):
-                change = jnp.dot(dec_ref[...], hidden[i], preferred_element_type=jnp.float32)
-                for m in range(members):
-                    old = field_ref[i, 0:vp, :] if step == 0 else inputs[i, 0:vp, columns(m)]
-                    new = old.astype(jnp.float32) + land[i] * change[:, columns(m)]
-                    inputs[i, 0:vp, columns(m)] = new.astype(jnp.bfloat16)
+                if own_row and layer == layers - 1:
+                    last_block(layer)
+                else:
+                    block(layer, first if step == 0 else None)
+            if not own_row:
+                for i in range(lat):
+                    decode(i, land[i], step)
         for i in range(local):
             row = band * local + i
             summed = inputs[row, 0:vp, columns(0)].astype(jnp.float32)
@@ -261,17 +291,23 @@
     small, large = (pltpu.CompilerParams(vmem_limit_bytes=n * MIB) for n in (8, 16 + 2 * layers))
     free = pl.CostEstimate(flops=0, bytes_accessed=0, transcendentals=0)
 
-    mine = jnp.concatenate([conv_weight[0], point_weight[0]], axis=1)
-    mine = lax.dynamic_slice_in_dim(mine, band * part, part, 0)
+    places = jnp.stack([here, band, lax.axis_index("members")]).astype(jnp.int32)
+    mine = pl.pallas_call(
+        functools.partial(pack_kernel, bands),
+        out_shape=jax.ShapeDtypeStruct((part, 10 * chans), jnp.bfloat16),
+        in_specs=[smem, whole, whole],
+        out_specs=whole,
+        scratch_shapes=[pltpu.SemaphoreType.DMA((2,))],
+        compiler_params=pltpu.CompilerParams(vmem_limit_bytes=MIB),
+        cost_estimate=free,
+    )(places, conv_weight[0], point_weight[0])
     sections = all_along(mine, "segment")[1:]
 
     slots = forcing_slots[0, 0].astype(jnp.float32).reshape(-1, lon)
     index_row = jnp.broadcast_to(param_index.astype(jnp.float32)[:, None], (1, lon))
     group = all_along(jnp.concatenate([slots, index_row], axis=0), "members")
     gains = all_along(norm_gain.astype(jnp.float32), "segment")
-    scalars = jnp.concatenate(
-        [jnp.stack([here, band, lax.axis_index("members")]).astype(jnp.int32), atmos_owner[0]]
-    )
+    scalars = jnp.concatenate([places, atmos_owner[0]])
     field = pl.pallas_call(
         functools.partial(field_kernel, (steps, members, local, forced, vp, fp)),
         out_shape=jax.ShapeDtypeStruct((local, vp + fp * steps + BF16_ROWS, lon), jnp.bfloat16),
@@ -303,7 +339,7 @@
 
     blocks = [conv_weight[0], point_weight[0]]
     for section in sections:
-        blocks += all_along(after(section, taps), "rows")
+        blocks += all_along(after(section, taps, *gains), "rows")
 
     scratch = [
         pltpu.VMEM((layers, chans, 10 * chans), jnp.bfloat16),

time: 33.2 us -> 32.3 us (0.973)
  local copies, waits for them, and re-layouts: 1.19 us -> 2.8 us
  starting transfers between devices: 9.55 us -> 8.28 us
  other arithmetic: 1.36 us -> 0.27 us
    unnamed x31 -> x35, local copies, waits for them, and re-layouts: 1.17 us -> 2.78 us
    ppermute x7, starting transfers between devices: 9.55 us -> 8.28 us  [passed_along(): lax.ppermute(block, axis, [(i, (i + distance) % size) for i in range(size)])]
    concatenate x2 -> x1, other arithmetic: 1.25 us -> 0.08 us  [per_device(): scalars = jnp.concatenate([places, atmos_owner[0]])]
    pallas_call x0 -> x1, Pallas kernels: none -> 0.62 us  [per_device(): pl.pallas_call(functools.partial(pack_kernel, bands), out_shape=jax.Shape...]
    pallas_call x1, Pallas kernels: 9.16 us -> 8.65 us  [per_device(): pl.pallas_call(functools.partial(window_kernel, dims), out_shape=(jax.Sha...]
where the time goes in v4:
time: 32.3 us; the launch traced here: 32.2 us
  Pallas kernels  11.2 us (35%)
  starting transfers between devices  8.28 us (26%)
  waiting for transfers between devices  8.13 us (25%)
  local copies, waits for them, and re-layouts  2.8 us (9%)
  between operations  1.49 us (5%)
    pallas_call x1, Pallas kernels, per_device(): pl.pallas_call(functools.partial(window_kernel, dims), out_shape=(jax.Sha...  8.65 us
    ppermute x7, starting transfers between devices, passed_along(): lax.ppermute(block, axis, [(i, (i + distance) % size) for i in range(size)])  8.28 us
    ppermute x7, waiting for transfers between devices, passed_along(): lax.ppermute(block, axis, [(i, (i + distance) % size) for i in range(size)])  8.13 us
    unnamed x35, local copies, waits for them, and re-layouts  2.78 us
    pallas_call x1, Pallas kernels, per_device(): pl.pallas_call(functools.partial(first_kernel, dims), out_shape=(jax.Shap...  1.37 us
  transfers between devices with their start and end apart: 7, of which 5 were waited for; matrix products, arithmetic and copies ran while one was open for 2% of the time, Pallas kernels for 6%

profile of v4, /device:TPU:0, one launch (start us, length us, event | category | flops | bytes accessed | tf_op | source)
XLA Modules:
  0.0 32.2 jit_solution(14913454069123094676)
XLA Ops:
  0.6 0.0 copy-start.13
  0.6 0.0 copy-start.11
  0.7 0.0 copy-start.12
  0.7 0.0 copy-start.14
  0.7 0.0 copy-start.5
  0.7 0.0 copy-start.4
  0.7 0.1 pad_add_fusion.1.scalar_ref
  0.8 1.3 %copy-done = bf16[1,256,2304]{2,1,0:T(8,128)(2,1)S(1)} copy-done((bf16[1,256,2304]{2,1,0:T(8,128)(2,1)S(1)}, bf16[1,256,2304]{2,1,0:T(8,128)(2,1)}, u32[]{:S(2)}) %copy-start) | copy-done | bytes 1179672
  2.1 0.9 %copy-done.2 = bf16[1,256,256]{2,1,0:T(8,128)(2,1)S(1)} copy-done((bf16[1,256,256]{2,1,0:T(8,128)(2,1)S(1)}, bf16[1,256,256]{2,1,0:T(8,128)(2,1)}, u32[]{:S(2)}) %copy-start.2) | copy-done | bytes 131096
  3.0 0.0 copy-start.9
  3.0 0.6 %shard_map.142 = bf16[128,2560]{1,0:T(8,128)(2,1)S(1)} custom-call(s32[3]{0:T(128)S(1)} %pad_add_fusion.1.scalar_ref, bf16[256,2304]{1,0:T(8,128)(2,1)S(1)} %bitcast.16, bf16[256,256]{1,0:T(8,128)(2,1)S(1)} %bitcast.18), custom_call_target="tpu_custom_call" | custom-call | tf_op jit(solution)/shard_map/pallas_call | solution.py:295
  3.6 3.0 %collective-permute-start.5 = (bf16[128,2560]{1,0:T(8,128)(2,1)S(1)}, bf16[128,2560]{1,0:T(8,128)(2,1)S(1)}, u32[]{:S(2)}, u32[]{:S(2)}) collective-permute-start(bf16[128,2560]{1,0:T(8,128)(2,1)S(1)} %shard_map.142), channel_id=1, source_target_pairs={{0,2},{2,0},{1,3},{3,1},{4,6},{6,4},{5,7},{7,5},{8,10},{10,8},{9,1... | collective-permute-start | bytes 1966088 | tf_op jit(solution)/shard_map/ppermute | solution.py:20
  7.3 0.0 copy-done.11
  7.3 3.7 %collective-permute-start.2 = (f32[9,128]{1,0:T(8,128)S(1)}, f32[9,128]{1,0:T(8,128)S(1)}, u32[]{:S(2)}, u32[]{:S(2)}) collective-permute-start(f32[9,128]{1,0:T(8,128)S(1)} %concatenate.12.rest_0_.rest_2_), channel_id=1, source_target_pairs={{0,12},{4,0},{8,4},{12,8},{1,13},{5,1},{9,5},{13,9},{2,14},{6,2},{... | collective-permute-start | bytes 13832 | tf_op jit(solution)/shard_map/ppermute | solution.py:20
  10.9 0.0 collective-permute-start.1
  10.9 1.0 %collective-permute-start = (f32[9,128]{1,0:T(8,128)S(1)}, f32[9,128]{1,0:T(8,128)S(1)}, u32[]{:S(2)}, u32[]{:S(2)}) collective-permute-start(f32[9,128]{1,0:T(8,128)S(1)} %concatenate.12.rest_0_.rest_2_), channel_id=1, source_target_pairs={{0,4},{4,8},{8,12},{12,0},{1,5},{5,9},{9,13},{13,1},{2,6},{6,10},{... | collective-permute-start | bytes 13832 | tf_op jit(solution)/shard_map/ppermute | solution.py:20
  11.9 0.0 copy-done.12
  12.0 0.5 %collective-permute-start.4 = (f32[1,256]{1,0:T(1,128)S(1)}, f32[1,256]{1,0:T(1,128)S(1)}, u32[]{:S(2)}, u32[]{:S(2)}) collective-permute-start(f32[1,256]{1,0:T(1,128)S(1)} %convert_element_type.24.refs_2_.rest_0_), channel_id=1, source_target_pairs={{0,2},{2,0},{1,3},{3,1},{4,6},{6,4},{5,7},{7,5},{8,10},{10,8},{9,1... | collective-permute-start | bytes 3080 | tf_op jit(solution)/shard_map/ppermute | solution.py:20
  12.5 0.0 slice-done
  12.5 0.1 copy.22
  12.6 0.0 copy-done.13
  12.6 0.0 copy-done.14
  12.6 0.1 pad_add_fusion.scalar_ref
  12.7 0.0 copy-done.6
  12.7 0.1 copy.23
  12.9 0.0 collective-permute-done.2.rest_3_.rest_5_
  12.9 2.6 %collective-permute-done.1.rest_2_.rest_4_ = f32[9,128]{1,0:T(8,128)S(1)} collective-permute-done((f32[9,128]{1,0:T(8,128)S(1)}, f32[9,128]{1,0:T(8,128)S(1)}, u32[]{:S(2)}, u32[]{:S(2)}) %collective-permute-start.1) | collective-permute-done | bytes 4640 | tf_op jit(solution)/shard_map/ppermute | solution.py:20
  15.5 0.9 %collective-permute-done.rest_1_.rest_3_ = f32[9,128]{1,0:T(8,128)S(1)} collective-permute-done((f32[9,128]{1,0:T(8,128)S(1)}, f32[9,128]{1,0:T(8,128)S(1)}, u32[]{:S(2)}, u32[]{:S(2)}) %collective-permute-start) | collective-permute-done | bytes 4640 | tf_op jit(solution)/shard_map/ppermute | solution.py:20
  16.4 0.0 copy-done.5
  16.4 0.0 copy-done.4
  16.4 0.6 %shard_map.140.rest_0_ = bf16[1,128,128]{2,1,0:T(8,128)(2,1)S(1)} custom-call(s32[5]{0:T(128)S(1)} %pad_add_fusion.scalar_ref, bf16[1,77,128]{2,1,0:T(8,128)(2,1)S(1)} %bitcast.22, s32[1,128]{1,0:T(1,128)S(1)} %copy-done.5, f32[9,128]{1,0:T(8,128)S(1)} %concatenate.12.rest_0_.rest_2_, f32[9,128]{1,0:T(8,128)S(1)} %collective-permute-done.rest_1_.rest_3_, ...), custom_call_target="tpu_custom_call" | custom-call | tf_op jit(solution)/shard_map/pallas_call | solution.py:311
  17.0 0.1 collective-permute-start.3
  17.0 0.1 fusion.1.enc_ref
  17.1 0.0 copy-done.10
  17.1 0.1 copy.20.settings_ref
  17.2 0.0 copy-done.8
  17.2 0.1 copy.18
  17.3 0.0 copy-done.9
  17.3 0.1 copy.19
  17.4 0.8 %collective-permute-done.3.rest_1_ = bf16[1,128,128]{2,1,0:T(8,128)(2,1)S(1)} collective-permute-done((bf16[1,128,128]{2,1,0:T(8,128)(2,1)S(1)}, bf16[1,128,128]{2,1,0:T(8,128)(2,1)S(1)}, u32[]{:S(2)}, u32[]{:S(2)}) %collective-permute-start.3) | collective-permute-done | bytes 32800 | tf_op jit(solution)/shard_map/ppermute | solution.py:20
  18.2 1.4 %shard_map.141 = (bf16[2,128,128]{2,1,0:T(8,128)(2,1)S(1)}, f32[1,256,512]{2,1,0:T(8,128)S(1)}, f32[1,256,512]{2,1,0:T(8,128)S(1)}, bf16[2,256,512]{2,1,0:T(8,128)(2,1)S(1)}, bf16[1536,512]{1,0:T(8,128)(2,1)S(1)}) custom-call(s32[5]{0:T(128)S(1)} %pad_add_fusion.scalar_ref, bf16[256,96]{1,0:T(8,128)(2,1)S(1)} %fusion.1.enc_ref, ...), custom_call_target="tpu_custom_call" | custom-call | tf_op jit(solution)/shard_map/pallas_call | solution.py:325
  19.6 0.0 copy-start.1
  19.6 0.0 copy-start.3
  19.6 1.8 %collective-permute-done.4.refs_3_.rest_1_ = f32[1,256]{1,0:T(1,128)S(1)} collective-permute-done((f32[1,256]{1,0:T(1,128)S(1)}, f32[1,256]{1,0:T(1,128)S(1)}, u32[]{:S(2)}, u32[]{:S(2)}) %collective-permute-start.4) | collective-permute-done | bytes 1056 | tf_op jit(solution)/shard_map/ppermute | solution.py:20
  21.4 0.0 collective-permute-done.5.refs_0_
  21.4 0.0 collective-permute-start.6
  21.4 2.1 %collective-permute-done.6.rest_7_ = bf16[128,2560]{1,0:T(8,128)(2,1)S(1)} collective-permute-done((bf16[128,2560]{1,0:T(8,128)(2,1)S(1)}, bf16[128,2560]{1,0:T(8,128)(2,1)S(1)}, u32[]{:S(2)}, u32[]{:S(2)}) %collective-permute-start.6) | collective-permute-done | bytes 655392 | tf_op jit(solution)/shard_map/ppermute | solution.py:20
  23.5 8.6 %shard_map.144 = (bf16[1,77,128]{2,1,0:T(8,128)(2,1)}, f32[77,1,128]{2,1,0:T(1,128)}) custom-call(s32[5]{0:T(128)S(1)} %pad_add_fusion.scalar_ref, bf16[2,128,128]{2,1,0:T(8,128)(2,1)S(1)} %get-tuple-element.9.field_ref, f32[1,256,512]{2,1,0:T(8,128)S(1)} %get-tuple-element.10.scale_ref, f32[1,256,512]{2,1,0:T(8,128)S(1)} %get-tuple-element.11.shift_ref, ...), custom_call_target="tpu_custom_call" | custom-call | tf_op jit(solution)/shard_map/pallas_call | solution.py:355
  (16 shorter events, 0.0 us)
Async XLA Ops:
  0.6 12.0 %copy-start.13 = (pred[80]{0:T(512)(128)(4,1)S(1)}, pred[80]{0:T(512)(128)(4,1)}, u32[]{:S(2)}) copy-start(pred[80]{0:T(512)(128)(4,1)} %constant.14.clone.1) | copy-start | bytes 244
  0.6 6.6 %copy-start.11 = (bf16[1,1,2,1,4,128]{5,4,3,2,1,0:T(4,128)(2,1)S(1)}, bf16[1,1,2,1,4,128]{5,4,3,2,1,0:T(4,128)(2,1)}, u32[]{:S(2)}) copy-start(bf16[1,1,2,1,4,128]{5,4,3,2,1,0:T(4,128)(2,1)} %param.14) | copy-start | bytes 6148
  0.7 11.3 %copy-start.12 = (bf16[1,256]{1,0:T(2,128)(2,1)S(1)}, bf16[1,256]{1,0:T(2,128)(2,1)}, u32[]{:S(2)}) copy-start(bf16[1,256]{1,0:T(2,128)(2,1)} %param.24) | copy-start | bytes 1540
  0.7 12.0 %copy-start.14 = (s32[1,2]{1,0:T(1,128)S(1)}, s32[1,2]{1,0:T(1,128)}, u32[]{:S(2)}) copy-start(s32[1,2]{1,0:T(1,128)} %param.15) | copy-start | bytes 28
  0.7 15.7 %copy-start.5 = (s32[1,128]{1,0:T(1,128)S(1)}, s32[1,128]{1,0:T(1,128)}, u32[]{:S(2)}) copy-start(s32[1,128]{1,0:T(1,128)} %land_ref.1) | copy-start | bytes 1540
  0.7 15.7 %copy-start.4 = (bf16[1,1,77,128]{3,2,1,0:T(8,128)(2,1)S(1)}, bf16[1,1,77,128]{3,2,1,0:T(8,128)(2,1)}, u32[]{:S(2)}) copy-start(bf16[1,1,77,128]{3,2,1,0:T(8,128)(2,1)} %param.13) | copy-start | bytes 59140
  0.8 1.3 %copy-start = (bf16[1,256,2304]{2,1,0:T(8,128)(2,1)S(1)}, bf16[1,256,2304]{2,1,0:T(8,128)(2,1)}, u32[]{:S(2)}) copy-start(bf16[1,256,2304]{2,1,0:T(8,128)(2,1)} %param.22) | copy-start | bytes 3538948
  2.0 0.9 %copy-start.2 = (bf16[1,256,256]{2,1,0:T(8,128)(2,1)S(1)}, bf16[1,256,256]{2,1,0:T(8,128)(2,1)}, u32[]{:S(2)}) copy-start(bf16[1,256,256]{2,1,0:T(8,128)(2,1)} %param.23) | copy-start | bytes 393220
  3.0 9.5 %slice-start = ((bf16[256,81]{0,1:T(8,128)(2,1)}), bf16[256,80]{0,1:T(8,128)(2,1)S(1)}, s32[]{:S(2)}) async-start(bf16[256,81]{0,1:T(8,128)(2,1)} %param.21), calls=%async_computation | async-start | bytes 81920 | tf_op jit(solution)/shard_map/slice
  3.0 9.8 %copy-start.6 = (bf16[256,81]{0,1:T(8,128)(2,1)S(1)}, bf16[256,81]{0,1:T(8,128)(2,1)}, u32[]{:S(2)}) copy-start(bf16[256,81]{0,1:T(8,128)(2,1)} %param.21) | copy-start | bytes 124420
  3.0 14.2 %copy-start.10 = (f32[64,16]{0,1:T(8,128)S(1)}, f32[64,16]{0,1:T(8,128)}, u32[]{:S(2)}) copy-start(f32[64,16]{0,1:T(8,128)} %param.18) | copy-start | bytes 12292
  3.0 14.3 %copy-start.8 = (f32[16,256]{1,0:T(8,128)S(1)}, f32[16,256]{1,0:T(8,128)}, u32[]{:S(2)}) copy-start(f32[16,256]{1,0:T(8,128)} %param.19) | copy-start | bytes 49156
  3.0 14.4 %copy-start.9 = (f32[16,256]{1,0:T(8,128)S(1)}, f32[16,256]{1,0:T(8,128)}, u32[]{:S(2)}) copy-start(f32[16,256]{1,0:T(8,128)} %param.20) | copy-start | bytes 49156
  3.6 17.8 %collective-permute-start.5 = (bf16[128,2560]{1,0:T(8,128)(2,1)S(1)}, bf16[128,2560]{1,0:T(8,128)(2,1)S(1)}, u32[]{:S(2)}, u32[]{:S(2)}) collective-permute-start(bf16[128,2560]{1,0:T(8,128)(2,1)S(1)} %shard_map.142), channel_id=1, source_target_pairs={{0,2},{2,0},{1,3},{3,1},{4,6},{6,4},{5,7},{7,5},{8,10},{10,8},{9,1... | collective-permute-start | bytes 1966088 | tf_op jit(solution)/shard_map/ppermute | solution.py:20
  7.3 5.6 %collective-permute-start.2 = (f32[9,128]{1,0:T(8,128)S(1)}, f32[9,128]{1,0:T(8,128)S(1)}, u32[]{:S(2)}, u32[]{:S(2)}) collective-permute-start(f32[9,128]{1,0:T(8,128)S(1)} %concatenate.12.rest_0_.rest_2_), channel_id=1, source_target_pairs={{0,12},{4,0},{8,4},{12,8},{1,13},{5,1},{9,5},{13,9},{2,14},{6,2},{... | collective-permute-start | bytes 13832 | tf_op jit(solution)/shard_map/ppermute | solution.py:20
  10.9 4.5 %collective-permute-start.1 = (f32[9,128]{1,0:T(8,128)S(1)}, f32[9,128]{1,0:T(8,128)S(1)}, u32[]{:S(2)}, u32[]{:S(2)}) collective-permute-start(f32[9,128]{1,0:T(8,128)S(1)} %concatenate.12.rest_0_.rest_2_), channel_id=1, source_target_pairs={{0,8},{4,12},{8,0},{12,4},{1,9},{5,13},{9,1},{13,5},{2,10},{6,14},... | collective-permute-start | bytes 13832 | tf_op jit(solution)/shard_map/ppermute | solution.py:20
  10.9 5.4 %collective-permute-start = (f32[9,128]{1,0:T(8,128)S(1)}, f32[9,128]{1,0:T(8,128)S(1)}, u32[]{:S(2)}, u32[]{:S(2)}) collective-permute-start(f32[9,128]{1,0:T(8,128)S(1)} %concatenate.12.rest_0_.rest_2_), channel_id=1, source_target_pairs={{0,4},{4,8},{8,12},{12,0},{1,5},{5,9},{9,13},{13,1},{2,6},{6,10},{... | collective-permute-start | bytes 13832 | tf_op jit(solution)/shard_map/ppermute | solution.py:20
  12.0 9.4 %collective-permute-start.4 = (f32[1,256]{1,0:T(1,128)S(1)}, f32[1,256]{1,0:T(1,128)S(1)}, u32[]{:S(2)}, u32[]{:S(2)}) collective-permute-start(f32[1,256]{1,0:T(1,128)S(1)} %convert_element_type.24.refs_2_.rest_0_), channel_id=1, source_target_pairs={{0,2},{2,0},{1,3},{3,1},{4,6},{6,4},{5,7},{7,5},{8,10},{10,8},{9,1... | collective-permute-start | bytes 3080 | tf_op jit(solution)/shard_map/ppermute | solution.py:20
  17.0 1.3 %collective-permute-start.3 = (bf16[1,128,128]{2,1,0:T(8,128)(2,1)S(1)}, bf16[1,128,128]{2,1,0:T(8,128)(2,1)S(1)}, u32[]{:S(2)}, u32[]{:S(2)}) collective-permute-start(bf16[1,128,128]{2,1,0:T(8,128)(2,1)S(1)} %shard_map.140.rest_0_), channel_id=1, source_target_pairs={{0,1},{1,0},{2,3},{3,2},{4,5},{5,4},{6,7},{7,6},{8,9},{9,8},{10,11... | collective-permute-start | bytes 98312 | tf_op jit(solution)/shard_map/ppermute | solution.py:20
  18.2 3.2 %copy-start.7 = (bf16[77,256]{1,0:T(8,128)(2,1)S(1)}, bf16[77,256]{1,0:T(8,128)(2,1)}, u32[]{:S(2)}) copy-start(bf16[77,256]{1,0:T(8,128)(2,1)} %param.25) | copy-start | bytes 118276
  19.6 3.9 %copy-start.1 = (bf16[1,256,2304]{2,1,0:T(8,128)(2,1)S(1)}, bf16[1,256,2304]{2,1,0:T(8,128)(2,1)}, u32[]{:S(2)}) copy-start(bf16[1,256,2304]{2,1,0:T(8,128)(2,1)} %param.22) | copy-start | bytes 3538948
  19.6 3.9 %copy-start.3 = (bf16[1,256,256]{2,1,0:T(8,128)(2,1)S(1)}, bf16[1,256,256]{2,1,0:T(8,128)(2,1)}, u32[]{:S(2)}) copy-start(bf16[1,256,256]{2,1,0:T(8,128)(2,1)} %param.23) | copy-start | bytes 393220
  21.4 2.1 %collective-permute-start.6 = (bf16[128,2560]{1,0:T(8,128)(2,1)S(1)}, bf16[128,2560]{1,0:T(8,128)(2,1)S(1)}, u32[]{:S(2)}, u32[]{:S(2)}) collective-permute-start(bf16[128,2560]{1,0:T(8,128)(2,1)S(1)} %shard_map.143.rest_6_), channel_id=1, source_target_pairs={{0,1},{1,0},{2,3},{3,2},{4,5},{5,4},{6,7},{7,6},{8,9},{9,8},{10,11... | collective-permute-start | bytes 1966088 | tf_op jit(solution)/shard_map/ppermute | solution.py:20

commit v5 on v4

--- a/solution.py
+++ b/solution.py
@@ -31,12 +31,19 @@
     return chosen
 
 
-def pack_kernel(bands, scalar_ref, conv_ref, point_ref, out_ref, sems):
-    part, wide = out_ref.shape[0], conv_ref.shape[1]
+def pack_kernel(scalar_ref, conv_ref, point_ref, relayed_ref, direct_ref, sems):
+    part, wide, share = direct_ref.shape[0], conv_ref.shape[1], relayed_ref.shape[1]
+    rest = wide + point_ref.shape[1] - direct_ref.shape[1]
     rows = pl.ds(pl.multiple_of(scalar_ref[1] * part, part), part)
+    mine = pl.ds(pl.multiple_of(scalar_ref[3] * share, 128), share)
     copies = [
-        pltpu.make_async_copy(conv_ref.at[rows, :], out_ref.at[:, pl.ds(0, wide)], sems.at[0]),
-        pltpu.make_async_copy(point_ref.at[rows, :], out_ref.at[:, pl.ds(wide, point_ref.shape[1])], sems.at[1]),
+        pltpu.make_async_copy(conv_ref.at[rows, mine], relayed_ref, sems.at[0]),
+        pltpu.make_async_copy(
+            conv_ref.at[rows, pl.ds(rest, wide - rest)], direct_ref.at[:, pl.ds(0, wide - rest)], sems.at[1]
+        ),
+        pltpu.make_async_copy(
+            point_ref.at[rows, :], direct_ref.at[:, pl.ds(wide - rest, point_ref.shape[1])], sems.at[2]
+        ),
     ]
     for copy in copies:
         copy.start()
@@ -56,7 +63,7 @@
             force = group[0][first : first + forced, :]
             for k in range(1, members):
                 source = lax.rem(scalar_ref[2] - k + members, members)
-                force = jnp.where(scalar_ref[3 + t] == source, group[k][first : first + forced, :], force)
+                force = jnp.where(scalar_ref[4 + t] == source, group[k][first : first + forced, :], force)
             out_ref[i, vp + fp * t : vp + fp * t + forced, :] = force.astype(jnp.bfloat16)
         out_ref[i, vp + fp * steps : vp + fp * steps + 1, :] = land_ref[i : i + 1, :].astype(jnp.bfloat16)
 
@@ -123,11 +130,12 @@
 
 
 def window_kernel(dims, scalar_ref, field_ref, scale_ref, shift_ref, enc_ref, dec_ref, *rest):
-    steps, layers, bands, local, members, lon, chans, vp, fp, turns = dims
+    steps, layers, bands, local, members, lon, chans, vp, fp, turns, groups = dims
     lat = bands * local
     gains, rest = rest[:layers], rest[layers:]
     hidden, taps = rest[:2]
-    blocks, rest = rest[2 : 4 + (layers - 1) * bands], rest[4 + (layers - 1) * bands :]
+    pieces = 2 + (layers - 1) * (groups + 1) * bands
+    blocks, rest = rest[2 : 2 + pieces], rest[2 + pieces :]
     final_ref, mean_ref, weights, gain_ref, conv, act, inputs, total, sems = rest[:9]
     here, band = scalar_ref[0], scalar_ref[1]
     taps_wide, wide = 9 * chans, 3 * chans
@@ -135,13 +143,19 @@
 
     pltpu.make_async_copy(blocks[0], weights.at[here, :, pl.ds(0, taps_wide)], sems.at[here]).start()
     pltpu.make_async_copy(blocks[1], weights.at[here, :, pl.ds(taps_wide, chans)], sems.at[here]).start()
+    share = 4 * chans // groups
     for k in range(1, layers):
         slot = lax.rem(here - k + layers, layers)
-        for j in range(bands):
-            first = pl.multiple_of(lax.rem(band - j + bands, bands) * part, part)
-            pltpu.make_async_copy(
-                blocks[2 + (k - 1) * bands + j], weights.at[slot, pl.ds(first, part), :], sems.at[slot]
-            ).start()
+        for g in range(groups + 1):
+            if g < groups:
+                place = lax.rem(scalar_ref[3] - g + groups, groups)
+                cols = pl.ds(pl.multiple_of(place * share, 128), share)
+            else:
+                cols = pl.ds(groups * share, 10 * chans - groups * share)
+            for j in range(bands):
+                rows = pl.ds(pl.multiple_of(lax.rem(band - j + bands, bands) * part, part), part)
+                block = blocks[2 + ((k - 1) * (groups + 1) + g) * bands + j]
+                pltpu.make_async_copy(block, weights.at[slot, rows, cols], sems.at[slot]).start()
 
     if turns > 1:
         hidden, taps = rest[9:]
@@ -291,17 +305,25 @@
     small, large = (pltpu.CompilerParams(vmem_limit_bytes=n * MIB) for n in (8, 16 + 2 * layers))
     free = pl.CostEstimate(flops=0, bytes_accessed=0, transcendentals=0)
 
-    places = jnp.stack([here, band, lax.axis_index("members")]).astype(jnp.int32)
-    mine = pl.pallas_call(
-        functools.partial(pack_kernel, bands),
-        out_shape=jax.ShapeDtypeStruct((part, 10 * chans), jnp.bfloat16),
-        in_specs=[smem, whole, whole],
-        out_specs=whole,
-        scratch_shapes=[pltpu.SemaphoreType.DMA((2,))],
+    groups = lax.axis_size("groups")
+    share = 4 * chans // groups
+    places = [here, band, lax.axis_index("members"), lax.axis_index("groups")]
+    places = jnp.stack(places).astype(jnp.int32)
+    hbm = pl.BlockSpec(memory_space=pltpu.HBM)
+    relayed, direct = pl.pallas_call(
+        pack_kernel,
+        out_shape=(
+            jax.ShapeDtypeStruct((part, share), jnp.bfloat16),
+            jax.ShapeDtypeStruct((part, 10 * chans - groups * share), jnp.bfloat16),
+        ),
+        in_specs=[smem, hbm, hbm],
+        out_specs=(whole, whole),
+        scratch_shapes=[pltpu.SemaphoreType.DMA((3,))],
         compiler_params=pltpu.CompilerParams(vmem_limit_bytes=MIB),
         cost_estimate=free,
     )(places, conv_weight[0], point_weight[0])
-    sections = all_along(mine, "segment")[1:]
+    relayed = all_along(relayed, "segment")[1:]
+    direct = all_along(direct, "segment")[1:]
 
     slots = forcing_slots[0, 0].astype(jnp.float32).reshape(-1, lon)
     index_row = jnp.broadcast_to(param_index.astype(jnp.float32)[:, None], (1, lon))
@@ -338,8 +360,11 @@
     )(scalars, enc, settings, scale_weight.T, shift_weight.T, *fields, *group)
 
     blocks = [conv_weight[0], point_weight[0]]
-    for section in sections:
-        blocks += all_along(after(section, taps, *gains), "rows")
+    for k in range(layers - 1):
+        shares = all_along(relayed[k], "groups")
+        for shared in shares:
+            blocks += all_along(shared, "rows")
+        blocks += all_along(after(direct[k], taps, *gains, *shares[1:]), "rows")
 
     scratch = [
         pltpu.VMEM((layers, chans, 10 * chans), jnp.bfloat16),
@@ -353,7 +378,7 @@
     if turns > 1:
         scratch += [pltpu.VMEM(hidden.shape, jnp.bfloat16), pltpu.VMEM(taps.shape, jnp.bfloat16)]
     final, mean = pl.pallas_call(
-        functools.partial(window_kernel, dims),
+        functools.partial(window_kernel, dims + (groups,)),
         out_shape=(
             jax.ShapeDtypeStruct((local, varied, lon), jnp.bfloat16),
             jax.ShapeDtypeStruct((varied, local, lon), jnp.float32),

time: 32.3 us -> 32.8 us (1.015)
  waiting for transfers between devices: 8.13 us -> 2.19 us
  starting transfers between devices: 8.28 us -> 12.1 us
  local copies, waits for them, and re-layouts: 2.8 us -> 5.02 us
  other arithmetic: 0.27 us -> 0.84 us
    ppermute x7 -> x11, waiting for transfers between devices: 8.13 us -> 2.19 us  [passed_along(): lax.ppermute(block, axis, [(i, (i + distance) % size) for i in range(size)])]
    ppermute x7 -> x11, starting transfers between devices: 8.28 us -> 12.1 us  [passed_along(): lax.ppermute(block, axis, [(i, (i + distance) % size) for i in range(size)])]
    slice x2 -> x1, local copies, waits for them, and re-layouts: 0.01 us -> 0.78 us
    slice x1, local copies, waits for them, and re-layouts: 0.01 us -> 0.7 us  [per_device(): encode_weight[:, varied:]]
    concatenate x1, local copies, waits for them, and re-layouts: 0.01 us -> 0.69 us  [per_device(): group = all_along(jnp.concatenate([slots, index_row], axis=0), 'members')]
    pad x1, other arithmetic: 0.01 us -> 0.66 us  [per_device(): enc = jnp.pad(encode_weight[:, :varied], ((0, 0), (0, vp - varied)))]
    unnamed x35 -> x29, local copies, waits for them, and re-layouts: 2.78 us -> 2.76 us
  transfers between devices with their start and end apart: 7 -> 11, of which waited for: 5 -> 3; matrix products, arithmetic and copies ran while one was open for 2% -> 11% of each run, Pallas kernels for 6% -> 6%
where the time goes in v5:
time: 32.8 us; the launch traced here: 32.5 us
  starting transfers between devices  12.1 us (37%)
  Pallas kernels  10.9 us (33%)
  local copies, waits for them, and re-layouts  5.02 us (15%)
  waiting for transfers between devices  2.19 us (7%)
  between operations  1.47 us (4%)
  other arithmetic  0.84 us (3%)
    ppermute x11, starting transfers between devices, passed_along(): lax.ppermute(block, axis, [(i, (i + distance) % size) for i in range(size)])  12.1 us
    pallas_call x1, Pallas kernels, per_device(): pl.pallas_call(functools.partial(window_kernel, dims + (groups,)), out_sh...  8.36 us
    unnamed x29, local copies, waits for them, and re-layouts  2.76 us
    ppermute x11, waiting for transfers between devices, passed_along(): lax.ppermute(block, axis, [(i, (i + distance) % size) for i in range(size)])  2.19 us
    pallas_call x1, Pallas kernels, per_device(): pl.pallas_call(functools.partial(first_kernel, dims), out_shape=(jax.Shap...  1.37 us
    slice x1, local copies, waits for them, and re-layouts  0.78 us
    slice x1, local copies, waits for them, and re-layouts, per_device(): encode_weight[:, varied:]  0.7 us
    concatenate x1, local copies, waits for them, and re-layouts, per_device(): group = all_along(jnp.concatenate([slots, index_row], axis=0), 'members')  0.69 us
  transfers between devices with their start and end apart: 11, of which 3 were waited for; matrix products, arithmetic and copies ran while one was open for 11% of the time, Pallas kernels for 6%

profile of v5, /device:TPU:0, one launch (start us, length us, event | category | flops | bytes accessed | tf_op | source)
XLA Modules:
  0.0 32.5 jit_solution(11450314079646144978)
XLA Ops:
  0.6 0.0 copy-start.5
  0.6 0.0 copy-start.4
  0.6 0.0 copy-start.7
  0.7 0.1 pad_add_fusion.scalar_ref
  0.7 1.3 %copy-done = bf16[1,256,2304]{2,1,0:T(8,128)(2,1)S(1)} copy-done((bf16[1,256,2304]{2,1,0:T(8,128)(2,1)S(1)}, bf16[1,256,2304]{2,1,0:T(8,128)(2,1)}, u32[]{:S(2)}) %copy-start) | copy-done | bytes 1179672
  2.0 0.9 %copy-done.2 = bf16[1,256,256]{2,1,0:T(8,128)(2,1)S(1)} copy-done((bf16[1,256,256]{2,1,0:T(8,128)(2,1)S(1)}, bf16[1,256,256]{2,1,0:T(8,128)(2,1)}, u32[]{:S(2)}) %copy-start.2) | copy-done | bytes 131096
  2.9 0.6 %shard_map.142 = (bf16[128,512]{1,0:T(8,128)(2,1)S(1)}, bf16[128,1536]{1,0:T(8,128)(2,1)S(1)}) custom-call(s32[4]{0:T(128)S(1)} %pad_add_fusion.scalar_ref, bf16[256,2304]{1,0:T(8,128)(2,1)S(1)} %bitcast.17, bf16[256,256]{1,0:T(8,128)(2,1)S(1)} %bitcast.19), custom_call_target="tpu_custom_call" | custom-call | tf_op jit(solution)/shard_map/pallas_call | solution.py:313
  3.6 3.0 %collective-permute-start.5 = (bf16[128,512]{1,0:T(8,128)(2,1)S(1)}, bf16[128,512]{1,0:T(8,128)(2,1)S(1)}, u32[]{:S(2)}, u32[]{:S(2)}) collective-permute-start(bf16[128,512]{1,0:T(8,128)(2,1)S(1)} %get-tuple-element.16), channel_id=1, source_target_pairs={{0,2},{2,0},{1,3},{3,1},{4,6},{6,4},{5,7},{7,5},{8,10},{10,8},{9,1... | collective-permute-start | bytes 393224 | tf_op jit(solution)/shard_map/ppermute | solution.py:20
  6.6 0.1 collective-permute-start.9
  7.3 0.7 %concatenate.12.rest_0_.rest_2_ = f32[9,128]{1,0:T(8,128)S(1)} pad(bf16[8,128]{1,0:T(8,128)(2,1)} %bitcast.24, f32[]{:T(128)} %bitcast.9), padding=0_1x0_0 | pad | bytes 6660 | tf_op jit(solution)/shard_map/concatenate | solution.py:330
  8.0 4.1 %collective-permute-start.2 = (f32[9,128]{1,0:T(8,128)S(1)}, f32[9,128]{1,0:T(8,128)S(1)}, u32[]{:S(2)}, u32[]{:S(2)}) collective-permute-start(f32[9,128]{1,0:T(8,128)S(1)} %concatenate.12.rest_0_.rest_2_), channel_id=1, source_target_pairs={{0,12},{4,0},{8,4},{12,8},{1,13},{5,1},{9,5},{13,9},{2,14},{6,2},{... | collective-permute-start | bytes 13832 | tf_op jit(solution)/shard_map/ppermute | solution.py:20
  12.0 0.0 collective-permute-start.1
  12.0 1.0 %collective-permute-start = (f32[9,128]{1,0:T(8,128)S(1)}, f32[9,128]{1,0:T(8,128)S(1)}, u32[]{:S(2)}, u32[]{:S(2)}) collective-permute-start(f32[9,128]{1,0:T(8,128)S(1)} %concatenate.12.rest_0_.rest_2_), channel_id=1, source_target_pairs={{0,4},{4,8},{8,12},{12,0},{1,5},{5,9},{9,13},{13,1},{2,6},{6,10},{... | collective-permute-start | bytes 13832 | tf_op jit(solution)/shard_map/ppermute | solution.py:20
  13.1 0.8 %slice.7 = bf16[256,80]{0,1:T(8,128)(2,1)S(1)} slice(bf16[256,81]{0,1:T(8,128)(2,1)} %param.21), slice={[0:256], [0:80]} | slice | bytes 81920 | tf_op jit(solution)/shard_map/slice
  13.8 0.1 copy.22
  14.0 0.0 collective-permute-done.5.rest_6_
  14.0 1.6 %collective-permute-start.7 = (bf16[128,512]{1,0:T(8,128)(2,1)S(1)}, bf16[128,512]{1,0:T(8,128)(2,1)S(1)}, u32[]{:S(2)}, u32[]{:S(2)}) collective-permute-start(bf16[128,512]{1,0:T(8,128)(2,1)S(1)} %collective-permute-done.5.rest_6_), channel_id=1, source_target_pairs={{0,16},{16,0},{1,17},{17,1},{2,18},{18,2},{3,19},{19,3},{4,20},{20... | collective-permute-start | bytes 393224 | tf_op jit(solution)/shard_map/ppermute | solution.py:20
  15.6 0.7 %broadcast_select_fusion = bf16[256,80]{1,0:T(8,128)(2,1)S(1)} fusion(bf16[256,80]{1,0:T(8,128)(2,1)S(1)} %copy.22, pred[80]{0:T(512)(128)(4,1)} %constant.18.clone.1), kind=kLoop, calls=%fused_computation.3 | loop fusion | flops 20480 | bytes 82000 | tf_op jit(solution)/shard_map/jit(_pad)/pad | solution.py:343
  16.2 0.7 %slice.8 = bf16[256,4]{0,1:T(4,128)(2,1)S(1)} slice(bf16[256,81]{0,1:T(8,128)(2,1)} %param.21), slice={[0:256], [77:81]} | slice | bytes 4096 | tf_op jit(solution)/shard_map/slice | solution.py:344
  16.9 0.1 concatenate.10.scalar_ref
  17.0 0.1 copy.23
  17.2 0.0 collective-permute-done.2.rest_3_.rest_5_
  17.2 1.6 %collective-permute-start.4 = (f32[1,256]{1,0:T(1,128)S(1)}, f32[1,256]{1,0:T(1,128)S(1)}, u32[]{:S(2)}, u32[]{:S(2)}) collective-permute-start(f32[1,256]{1,0:T(1,128)S(1)} %convert_element_type.24.refs_2_.rest_0_), channel_id=1, source_target_pairs={{0,2},{2,0},{1,3},{3,1},{4,6},{6,4},{5,7},{7,5},{8,10},{10,8},{9,1... | collective-permute-start | bytes 3080 | tf_op jit(solution)/shard_map/ppermute | solution.py:20
  18.7 0.0 collective-permute-done.1.rest_2_.rest_4_
  18.7 0.0 collective-permute-done.rest_1_.rest_3_
  18.7 0.0 copy-done.5
  18.7 0.0 copy-done.4
  18.7 0.6 %shard_map.140.rest_0_ = bf16[1,128,128]{2,1,0:T(8,128)(2,1)S(1)} custom-call(s32[6]{0:T(128)S(1)} %concatenate.10.scalar_ref, bf16[1,77,128]{2,1,0:T(8,128)(2,1)S(1)} %bitcast.23, s32[1,128]{1,0:T(1,128)S(1)} %copy-done.5, f32[9,128]{1,0:T(8,128)S(1)} %concatenate.12.rest_0_.rest_2_, f32[9,128]{1,0:T(8,128)S(1)} %collective-permute-done.rest_1_.rest_3_, ...), custom_call_target="tpu_custom_call" | custom-call | tf_op jit(solution)/shard_map/pallas_call | solution.py:333
  19.3 0.1 collective-permute-start.3
  19.4 0.1 fusion.1.enc_ref
  19.5 0.1 copy.20.settings_ref
  19.6 0.1 copy.18
  19.7 0.0 copy-start.6
  19.7 0.0 copy-start.1
  19.7 0.0 copy-start.3
  19.7 0.1 copy.19
  19.8 0.8 %collective-permute-done.3.rest_1_ = bf16[1,128,128]{2,1,0:T(8,128)(2,1)S(1)} collective-permute-done((bf16[1,128,128]{2,1,0:T(8,128)(2,1)S(1)}, bf16[1,128,128]{2,1,0:T(8,128)(2,1)S(1)}, u32[]{:S(2)}, u32[]{:S(2)}) %collective-permute-start.3) | collective-permute-done | bytes 32800 | tf_op jit(solution)/shard_map/ppermute | solution.py:20
  20.6 1.4 %shard_map.141 = (bf16[2,128,128]{2,1,0:T(8,128)(2,1)S(1)}, f32[1,256,512]{2,1,0:T(8,128)S(1)}, f32[1,256,512]{2,1,0:T(8,128)S(1)}, bf16[2,256,512]{2,1,0:T(8,128)(2,1)S(1)}, bf16[1536,512]{1,0:T(8,128)(2,1)S(1)}) custom-call(s32[6]{0:T(128)S(1)} %concatenate.10.scalar_ref, bf16[256,96]{1,0:T(8,128)(2,1)S(1)} %fusion.1.enc_ref, ...), custom_call_target="tpu_custom_call" | custom-call | tf_op jit(solution)/shard_map/pallas_call | solution.py:347
  22.0 0.0 collective-permute-done.4.refs_3_.rest_1_
  22.0 0.0 collective-permute-done.7.refs_4_.rest_8_
  22.0 0.0 collective-permute-done.9.refs_0_
  22.0 0.2 collective-permute-start.10
  22.2 0.3 %collective-permute-start.6 = (bf16[128,512]{1,0:T(8,128)(2,1)S(1)}, bf16[128,512]{1,0:T(8,128)(2,1)S(1)}, u32[]{:S(2)}, u32[]{:S(2)}) collective-permute-start(bf16[128,512]{1,0:T(8,128)(2,1)S(1)} %collective-permute-done.5.rest_6_), channel_id=1, source_target_pairs={{0,1},{1,0},{2,3},{3,2},{4,5},{5,4},{6,7},{7,6},{8,9},{9,8},{10,11... | collective-permute-start | bytes 393224 | tf_op jit(solution)/shard_map/ppermute | solution.py:20
  22.6 0.2 collective-permute-start.8
  22.8 1.2 %collective-permute-done.6.rest_7_ = bf16[128,512]{1,0:T(8,128)(2,1)S(1)} collective-permute-done((bf16[128,512]{1,0:T(8,128)(2,1)S(1)}, bf16[128,512]{1,0:T(8,128)(2,1)S(1)}, u32[]{:S(2)}, u32[]{:S(2)}) %collective-permute-start.6) | collective-permute-done | bytes 131104 | tf_op jit(solution)/shard_map/ppermute | solution.py:20
  24.0 0.2 collective-permute-done.8.rest_9_
  24.2 0.0 collective-permute-done.10.rest_11_
  24.2 8.4 %shard_map.144 = (bf16[1,77,128]{2,1,0:T(8,128)(2,1)}, f32[77,1,128]{2,1,0:T(1,128)}) custom-call(s32[6]{0:T(128)S(1)} %concatenate.10.scalar_ref, bf16[2,128,128]{2,1,0:T(8,128)(2,1)S(1)} %get-tuple-element.11.field_ref, f32[1,256,512]{2,1,0:T(8,128)S(1)} %get-tuple-element.12.scale_ref, f32[1,256,512]{2,1,0:T(8,128)S(1)} %get-tuple-element.13.shift_ref, ...), custom_call_target="tpu_custom_call" | custom-call | tf_op jit(solution)/shard_map/pallas_call | solution.py:380
  (17 shorter events, 0.0 us)
Async XLA Ops:
  0.6 18.1 %copy-start.5 = (s32[1,128]{1,0:T(1,128)S(1)}, s32[1,128]{1,0:T(1,128)}, u32[]{:S(2)}) copy-start(s32[1,128]{1,0:T(1,128)} %land_ref.1) | copy-start | bytes 1540
  0.6 18.1 %copy-start.4 = (bf16[1,1,77,128]{3,2,1,0:T(8,128)(2,1)S(1)}, bf16[1,1,77,128]{3,2,1,0:T(8,128)(2,1)}, u32[]{:S(2)}) copy-start(bf16[1,1,77,128]{3,2,1,0:T(8,128)(2,1)} %param.13) | copy-start | bytes 59140
  0.6 18.9 %copy-start.7 = (f32[16,256]{1,0:T(8,128)S(1)}, f32[16,256]{1,0:T(8,128)}, u32[]{:S(2)}) copy-start(f32[16,256]{1,0:T(8,128)} %param.19) | copy-start | bytes 49156
  0.7 1.3 %copy-start = (bf16[1,256,2304]{2,1,0:T(8,128)(2,1)S(1)}, bf16[1,256,2304]{2,1,0:T(8,128)(2,1)}, u32[]{:S(2)}) copy-start(bf16[1,256,2304]{2,1,0:T(8,128)(2,1)} %param.22) | copy-start | bytes 3538948
  2.0 0.9 %copy-start.2 = (bf16[1,256,256]{2,1,0:T(8,128)(2,1)S(1)}, bf16[1,256,256]{2,1,0:T(8,128)(2,1)}, u32[]{:S(2)}) copy-start(bf16[1,256,256]{2,1,0:T(8,128)(2,1)} %param.23) | copy-start | bytes 393220
  2.9 14.0 %copy-start.11 = (s32[1,2]{1,0:T(1,128)S(1)}, s32[1,2]{1,0:T(1,128)}, u32[]{:S(2)}) copy-start(s32[1,2]{1,0:T(1,128)} %param.15) | copy-start | bytes 28
  2.9 14.1 %copy-start.10 = (bf16[1,256]{1,0:T(2,128)(2,1)S(1)}, bf16[1,256]{1,0:T(2,128)(2,1)}, u32[]{:S(2)}) copy-start(bf16[1,256]{1,0:T(2,128)(2,1)} %param.24) | copy-start | bytes 1540
  2.9 16.6 %copy-start.9 = (f32[64,16]{0,1:T(8,128)S(1)}, f32[64,16]{0,1:T(8,128)}, u32[]{:S(2)}) copy-start(f32[64,16]{0,1:T(8,128)} %param.18) | copy-start | bytes 12292
  2.9 16.8 %copy-start.8 = (f32[16,256]{1,0:T(8,128)S(1)}, f32[16,256]{1,0:T(8,128)}, u32[]{:S(2)}) copy-start(f32[16,256]{1,0:T(8,128)} %param.20) | copy-start | bytes 49156
  3.6 10.4 %collective-permute-start.5 = (bf16[128,512]{1,0:T(8,128)(2,1)S(1)}, bf16[128,512]{1,0:T(8,128)(2,1)S(1)}, u32[]{:S(2)}, u32[]{:S(2)}) collective-permute-start(bf16[128,512]{1,0:T(8,128)(2,1)S(1)} %get-tuple-element.16), channel_id=1, source_target_pairs={{0,2},{2,0},{1,3},{3,1},{4,6},{6,4},{5,7},{7,5},{8,10},{10,8},{9,1... | collective-permute-start | bytes 393224 | tf_op jit(solution)/shard_map/ppermute | solution.py:20
  6.6 15.4 %collective-permute-start.9 = (bf16[128,1536]{1,0:T(8,128)(2,1)S(1)}, bf16[128,1536]{1,0:T(8,128)(2,1)S(1)}, u32[]{:S(2)}, u32[]{:S(2)}) collective-permute-start(bf16[128,1536]{1,0:T(8,128)(2,1)S(1)} %get-tuple-element.17), channel_id=1, source_target_pairs={{0,2},{2,0},{1,3},{3,1},{4,6},{6,4},{5,7},{7,5},{8,10},{10,8},{9,1... | collective-permute-start | bytes 1179656 | tf_op jit(solution)/shard_map/ppermute | solution.py:20
  8.0 9.2 %collective-permute-start.2 = (f32[9,128]{1,0:T(8,128)S(1)}, f32[9,128]{1,0:T(8,128)S(1)}, u32[]{:S(2)}, u32[]{:S(2)}) collective-permute-start(f32[9,128]{1,0:T(8,128)S(1)} %concatenate.12.rest_0_.rest_2_), channel_id=1, source_target_pairs={{0,12},{4,0},{8,4},{12,8},{1,13},{5,1},{9,5},{13,9},{2,14},{6,2},{... | collective-permute-start | bytes 13832 | tf_op jit(solution)/shard_map/ppermute | solution.py:20
  12.0 6.7 %collective-permute-start.1 = (f32[9,128]{1,0:T(8,128)S(1)}, f32[9,128]{1,0:T(8,128)S(1)}, u32[]{:S(2)}, u32[]{:S(2)}) collective-permute-start(f32[9,128]{1,0:T(8,128)S(1)} %concatenate.12.rest_0_.rest_2_), channel_id=1, source_target_pairs={{0,8},{4,12},{8,0},{12,4},{1,9},{5,13},{9,1},{13,5},{2,10},{6,14},... | collective-permute-start | bytes 13832 | tf_op jit(solution)/shard_map/ppermute | solution.py:20
  12.0 6.7 %collective-permute-start = (f32[9,128]{1,0:T(8,128)S(1)}, f32[9,128]{1,0:T(8,128)S(1)}, u32[]{:S(2)}, u32[]{:S(2)}) collective-permute-start(f32[9,128]{1,0:T(8,128)S(1)} %concatenate.12.rest_0_.rest_2_), channel_id=1, source_target_pairs={{0,4},{4,8},{8,12},{12,0},{1,5},{5,9},{9,13},{13,1},{2,6},{6,10},{... | collective-permute-start | bytes 13832 | tf_op jit(solution)/shard_map/ppermute | solution.py:20
  14.0 8.0 %collective-permute-start.7 = (bf16[128,512]{1,0:T(8,128)(2,1)S(1)}, bf16[128,512]{1,0:T(8,128)(2,1)S(1)}, u32[]{:S(2)}, u32[]{:S(2)}) collective-permute-start(bf16[128,512]{1,0:T(8,128)(2,1)S(1)} %collective-permute-done.5.rest_6_), channel_id=1, source_target_pairs={{0,16},{16,0},{1,17},{17,1},{2,18},{18,2},{3,19},{19,3},{4,20},{20... | collective-permute-start | bytes 393224 | tf_op jit(solution)/shard_map/ppermute | solution.py:20
  17.2 4.8 %collective-permute-start.4 = (f32[1,256]{1,0:T(1,128)S(1)}, f32[1,256]{1,0:T(1,128)S(1)}, u32[]{:S(2)}, u32[]{:S(2)}) collective-permute-start(f32[1,256]{1,0:T(1,128)S(1)} %convert_element_type.24.refs_2_.rest_0_), channel_id=1, source_target_pairs={{0,2},{2,0},{1,3},{3,1},{4,6},{6,4},{5,7},{7,5},{8,10},{10,8},{9,1... | collective-permute-start | bytes 3080 | tf_op jit(solution)/shard_map/ppermute | solution.py:20
  19.3 1.3 %collective-permute-start.3 = (bf16[1,128,128]{2,1,0:T(8,128)(2,1)S(1)}, bf16[1,128,128]{2,1,0:T(8,128)(2,1)S(1)}, u32[]{:S(2)}, u32[]{:S(2)}) collective-permute-start(bf16[1,128,128]{2,1,0:T(8,128)(2,1)S(1)} %shard_map.140.rest_0_), channel_id=1, source_target_pairs={{0,1},{1,0},{2,3},{3,2},{4,5},{5,4},{6,7},{7,6},{8,9},{9,8},{10,11... | collective-permute-start | bytes 98312 | tf_op jit(solution)/shard_map/ppermute | solution.py:20
  19.7 3.1 %copy-start.6 = (bf16[77,256]{1,0:T(8,128)(2,1)S(1)}, bf16[77,256]{1,0:T(8,128)(2,1)}, u32[]{:S(2)}) copy-start(bf16[77,256]{1,0:T(8,128)(2,1)} %param.25) | copy-start | bytes 118276
  19.7 4.5 %copy-start.1 = (bf16[1,256,2304]{2,1,0:T(8,128)(2,1)S(1)}, bf16[1,256,2304]{2,1,0:T(8,128)(2,1)}, u32[]{:S(2)}) copy-start(bf16[1,256,2304]{2,1,0:T(8,128)(2,1)} %param.22) | copy-start | bytes 3538948
  19.7 4.5 %copy-start.3 = (bf16[1,256,256]{2,1,0:T(8,128)(2,1)S(1)}, bf16[1,256,256]{2,1,0:T(8,128)(2,1)}, u32[]{:S(2)}) copy-start(bf16[1,256,256]{2,1,0:T(8,128)(2,1)} %param.23) | copy-start | bytes 393220
  22.0 2.2 %collective-permute-start.10 = (bf16[128,1536]{1,0:T(8,128)(2,1)S(1)}, bf16[128,1536]{1,0:T(8,128)(2,1)S(1)}, u32[]{:S(2)}, u32[]{:S(2)}) collective-permute-start(bf16[128,1536]{1,0:T(8,128)(2,1)S(1)} %shard_map.143.rest_10_), channel_id=1, source_target_pairs={{0,1},{1,0},{2,3},{3,2},{4,5},{5,4},{6,7},{7,6},{8,9},{9,8},{10,11... | collective-permute-start | bytes 1179656 | tf_op jit(solution)/shard_map/ppermute | solution.py:20
  22.2 1.7 %collective-permute-start.6 = (bf16[128,512]{1,0:T(8,128)(2,1)S(1)}, bf16[128,512]{1,0:T(8,128)(2,1)S(1)}, u32[]{:S(2)}, u32[]{:S(2)}) collective-permute-start(bf16[128,512]{1,0:T(8,128)(2,1)S(1)} %collective-permute-done.5.rest_6_), channel_id=1, source_target_pairs={{0,1},{1,0},{2,3},{3,2},{4,5},{5,4},{6,7},{7,6},{8,9},{9,8},{10,11... | collective-permute-start | bytes 393224 | tf_op jit(solution)/shard_map/ppermute | solution.py:20
  22.6 1.6 %collective-permute-start.8 = (bf16[128,512]{1,0:T(8,128)(2,1)S(1)}, bf16[128,512]{1,0:T(8,128)(2,1)S(1)}, u32[]{:S(2)}, u32[]{:S(2)}) collective-permute-start(bf16[128,512]{1,0:T(8,128)(2,1)S(1)} %collective-permute-done.7.refs_4_.rest_8_), channel_id=1, source_target_pairs={{0,1},{1,0},{2,3},{3,2},{4,5},{5,4},{6,7},{7,6},{8,9},{9,8},{10,11... | collective-permute-start | bytes 393224 | tf_op jit(solution)/shard_map/ppermute | solution.py:20

commit v6 on v5

--- a/solution.py
+++ b/solution.py
@@ -8,6 +8,7 @@
 from jax.sharding import PartitionSpec as P
 
 BF16_ROWS = 16
+LANES = 128
 MIB = 1024 * 1024
 
 
@@ -31,23 +32,48 @@
     return chosen
 
 
-def pack_kernel(scalar_ref, conv_ref, point_ref, relayed_ref, direct_ref, sems):
-    part, wide, share = direct_ref.shape[0], conv_ref.shape[1], relayed_ref.shape[1]
-    rest = wide + point_ref.shape[1] - direct_ref.shape[1]
-    rows = pl.ds(pl.multiple_of(scalar_ref[1] * part, part), part)
-    mine = pl.ds(pl.multiple_of(scalar_ref[3] * share, 128), share)
-    copies = [
-        pltpu.make_async_copy(conv_ref.at[rows, mine], relayed_ref, sems.at[0]),
-        pltpu.make_async_copy(
-            conv_ref.at[rows, pl.ds(rest, wide - rest)], direct_ref.at[:, pl.ds(0, wide - rest)], sems.at[1]
-        ),
-        pltpu.make_async_copy(
-            point_ref.at[rows, :], direct_ref.at[:, pl.ds(wide - rest, point_ref.shape[1])], sems.at[2]
-        ),
-    ]
+def run_copies(*copies):
     for copy in copies:
         copy.start()
     for copy in copies:
+        copy.wait()
+
+
+def pack_kernel(scalar_ref, gain_ref, conv_ref, point_ref, slots_ref, *rest):
+    relayed_ref, middle_ref, direct_ref, spread_ref, group_ref, slots, gain, sems = rest
+    part, share = relayed_ref.shape
+    wide, chans = conv_ref.shape[1], point_ref.shape[1]
+    left = direct_ref.shape[1] - chans - LANES
+    rows = pl.ds(pl.multiple_of(scalar_ref[1] * part, part), part)
+    mine = pl.ds(pl.multiple_of(scalar_ref[3] * share, LANES), share)
+    small = [
+        pltpu.make_async_copy(gain_ref, gain, sems.at[0]),
+        pltpu.make_async_copy(slots_ref, slots, sems.at[1]),
+    ]
+    large = [
+        pltpu.make_async_copy(conv_ref.at[rows, mine], relayed_ref, sems.at[2]),
+        pltpu.make_async_copy(
+            conv_ref.at[rows, pl.ds(wide - left - middle_ref.shape[1], middle_ref.shape[1])], middle_ref, sems.at[6]
+        ),
+        pltpu.make_async_copy(conv_ref.at[rows, pl.ds(wide - left, left)], direct_ref.at[:, pl.ds(0, left)], sems.at[3]),
+        pltpu.make_async_copy(point_ref.at[rows, :], direct_ref.at[:, pl.ds(left, chans)], sems.at[4]),
+    ]
+    for copy in small + large:
+        copy.start()
+    for copy in small:
+        copy.wait()
+    eye = lax.broadcasted_iota(jnp.int32, (chans, chans), 0) == lax.broadcasted_iota(jnp.int32, (chans, chans), 1)
+    column = jnp.sum(jnp.where(eye, gain[...].astype(jnp.float32), 0.0), axis=1, keepdims=True)
+    spread_ref[...] = jnp.broadcast_to(column, (chans, LANES)).astype(jnp.bfloat16)
+    large.append(
+        pltpu.make_async_copy(spread_ref.at[rows, :], direct_ref.at[:, pl.ds(left + chans, LANES)], sems.at[5])
+    )
+    large[-1].start()
+    count = slots.shape[0]
+    group_ref[0:count] = slots[...].astype(jnp.float32)
+    index = jnp.full((1, group_ref.shape[1]), scalar_ref[4], jnp.int32)
+    group_ref[count : count + 1] = index.astype(jnp.float32)
+    for copy in large:
         copy.wait()
 
 
@@ -63,7 +89,7 @@
             force = group[0][first : first + forced, :]
             for k in range(1, members):
                 source = lax.rem(scalar_ref[2] - k + members, members)
-                force = jnp.where(scalar_ref[4 + t] == source, group[k][first : first + forced, :], force)
+                force = jnp.where(scalar_ref[5 + t] == source, group[k][first : first + forced, :], force)
             out_ref[i, vp + fp * t : vp + fp * t + forced, :] = force.astype(jnp.bfloat16)
         out_ref[i, vp + fp * steps : vp + fp * steps + 1, :] = land_ref[i : i + 1, :].astype(jnp.bfloat16)
 
@@ -80,11 +106,18 @@
     )
 
 
-def first_kernel(dims, scalar_ref, enc_ref, settings_ref, scale_w_ref, shift_w_ref, *rest):
+def first_kernel(dims, scalar_ref, enc_w_ref, dec_w_ref, settings_ref, scale_w_ref, shift_w_ref, *rest):
     steps, layers, bands, local, members, lon, chans, vp, fp, turns = dims
     fields, rest = rest[:bands], rest[bands:]
     group, rest = rest[: members * turns], rest[members * turns :]
-    field_ref, scale_ref, shift_ref, hidden_ref, taps_ref = rest
+    field_ref, scale_ref, shift_ref, enc_ref, dec_ref, hidden_ref, taps_ref = rest
+    varied = dec_w_ref.shape[0]
+    forced = enc_w_ref.shape[1] - varied
+    enc_ref[...] = jnp.zeros(enc_ref.shape, enc_ref.dtype)
+    enc_ref[:, 0:varied] = enc_w_ref[:, 0:varied]
+    enc_ref[:, vp : vp + forced] = enc_w_ref[:, varied : varied + forced]
+    dec_ref[...] = jnp.zeros(dec_ref.shape, dec_ref.dtype)
+    dec_ref[0:varied, :] = dec_w_ref[...]
     band = scalar_ref[1]
     for b in range(bands):
         field_ref[b * local : (b + 1) * local] = from_place([f[...] for f in fields], band, b)
@@ -132,39 +165,36 @@
 def window_kernel(dims, scalar_ref, field_ref, scale_ref, shift_ref, enc_ref, dec_ref, *rest):
     steps, layers, bands, local, members, lon, chans, vp, fp, turns, groups = dims
     lat = bands * local
-    gains, rest = rest[:layers], rest[layers:]
     hidden, taps = rest[:2]
-    pieces = 2 + (layers - 1) * (groups + 1) * bands
+    pieces = 3 + (layers - 1) * (groups + 2) * bands
     blocks, rest = rest[2 : 2 + pieces], rest[2 + pieces :]
-    final_ref, mean_ref, weights, gain_ref, conv, act, inputs, total, sems = rest[:9]
+    final_ref, mean_ref, weights, conv, act, inputs, total, sems = rest[:8]
     here, band = scalar_ref[0], scalar_ref[1]
     taps_wide, wide = 9 * chans, 3 * chans
     part = chans // bands
 
     pltpu.make_async_copy(blocks[0], weights.at[here, :, pl.ds(0, taps_wide)], sems.at[here]).start()
     pltpu.make_async_copy(blocks[1], weights.at[here, :, pl.ds(taps_wide, chans)], sems.at[here]).start()
+    pltpu.make_async_copy(blocks[2], weights.at[here, :, pl.ds(10 * chans, LANES)], sems.at[here]).start()
     share = 4 * chans // groups
+    middle = groups * share + blocks[3 + groups * bands].shape[1] if layers > 1 else 0
     for k in range(1, layers):
         slot = lax.rem(here - k + layers, layers)
-        for g in range(groups + 1):
+        for g in range(groups + 2):
             if g < groups:
                 place = lax.rem(scalar_ref[3] - g + groups, groups)
-                cols = pl.ds(pl.multiple_of(place * share, 128), share)
+                cols = pl.ds(pl.multiple_of(place * share, LANES), share)
+            elif g == groups:
+                cols = pl.ds(groups * share, middle - groups * share)
             else:
-                cols = pl.ds(groups * share, 10 * chans - groups * share)
+                cols = pl.ds(middle, 10 * chans + LANES - middle)
             for j in range(bands):
                 rows = pl.ds(pl.multiple_of(lax.rem(band - j + bands, bands) * part, part), part)
-                block = blocks[2 + ((k - 1) * (groups + 1) + g) * bands + j]
+                block = blocks[3 + ((k - 1) * (groups + 2) + g) * bands + j]
                 pltpu.make_async_copy(block, weights.at[slot, rows, cols], sems.at[slot]).start()
 
     if turns > 1:
-        hidden, taps = rest[9:]
-
-    eye = lax.broadcasted_iota(jnp.int32, (chans, chans), 0) == lax.broadcasted_iota(jnp.int32, (chans, chans), 1)
-    for layer in range(layers):
-        row = from_place([g[...] for g in gains], here, layer)
-        column = jnp.sum(jnp.where(eye, row, 0.0), axis=1, keepdims=True)
-        gain_ref[layer] = jnp.broadcast_to(column, (chans, lon)).astype(jnp.bfloat16)
+        hidden, taps = rest[8:]
 
     def columns(m):
         return slice(m * lon, (m + 1) * lon)
@@ -192,7 +222,7 @@
     def activate(value, layer):
         centred = value - jnp.sum(value, axis=0, keepdims=True) * (1.0 / chans)
         spread = jnp.sum(centred * centred, axis=0, keepdims=True) * (1.0 / chans)
-        normed = (centred * lax.rsqrt(spread + 1e-05)).astype(jnp.bfloat16) * gain_ref[layer]
+        normed = (centred * lax.rsqrt(spread + 1e-05)).astype(jnp.bfloat16) * weights[layer, :, 10 * chans :]
         inner = normed * (normed * normed * 0.0356774081 + 0.7978845608)
         half = normed * 0.5
         return half + half * jnp.tanh(inner)
@@ -219,7 +249,7 @@
     def mix(i, row, sea, layer):
         for m in range(members):
             act[i, :, columns(m)] = activate(conv[i, :, columns(m)], layer)
-        mixed = jnp.dot(weights[layer, :, taps_wide:], act[i], preferred_element_type=jnp.float32)
+        mixed = jnp.dot(weights[layer, :, taps_wide : 10 * chans], act[i], preferred_element_type=jnp.float32)
         for m in range(members):
             kept = hidden[row, :, columns(m)].astype(jnp.float32)
             later = layer + 1 if layer + 1 < layers else None
@@ -308,28 +338,31 @@
     groups = lax.axis_size("groups")
     share = 4 * chans // groups
     places = [here, band, lax.axis_index("members"), lax.axis_index("groups")]
-    places = jnp.stack(places).astype(jnp.int32)
-    hbm = pl.BlockSpec(memory_space=pltpu.HBM)
-    relayed, direct = pl.pallas_call(
+    scalars = jnp.concatenate([jnp.stack(places).astype(jnp.int32), param_index, atmos_owner[0]])
+    slots = forcing_slots[0, 0].reshape(-1, lon)
+    crowded = pltpu.CompilerParams(vmem_limit_bytes=60 * MIB)
+    middle = groups * share + (9 * chans - groups * share) * 7 // 10 // LANES * LANES
+    relayed, between, direct, spread, group = pl.pallas_call(
         pack_kernel,
         out_shape=(
             jax.ShapeDtypeStruct((part, share), jnp.bfloat16),
-            jax.ShapeDtypeStruct((part, 10 * chans - groups * share), jnp.bfloat16),
+            jax.ShapeDtypeStruct((part, middle - groups * share), jnp.bfloat16),
+            jax.ShapeDtypeStruct((part, 10 * chans + LANES - middle), jnp.bfloat16),
+            jax.ShapeDtypeStruct((chans, LANES), jnp.bfloat16),
+            jax.ShapeDtypeStruct((slots.shape[0] + 1, lon), jnp.float32),
         ),
-        in_specs=[smem, hbm, hbm],
-        out_specs=(whole, whole),
-        scratch_shapes=[pltpu.SemaphoreType.DMA((3,))],
-        compiler_params=pltpu.CompilerParams(vmem_limit_bytes=MIB),
+        in_specs=[smem] + [whole] * 4,
+        out_specs=(whole, whole, whole, vmem, vmem),
+        scratch_shapes=[
+            pltpu.VMEM(slots.shape, jnp.bfloat16),
+            pltpu.VMEM(norm_gain.shape, jnp.bfloat16),
+            pltpu.SemaphoreType.DMA((7,)),
+        ],
+        compiler_params=crowded,
         cost_estimate=free,
-    )(places, conv_weight[0], point_weight[0])
-    relayed = all_along(relayed, "segment")[1:]
-    direct = all_along(direct, "segment")[1:]
-
-    slots = forcing_slots[0, 0].astype(jnp.float32).reshape(-1, lon)
-    index_row = jnp.broadcast_to(param_index.astype(jnp.float32)[:, None], (1, lon))
-    group = all_along(jnp.concatenate([slots, index_row], axis=0), "members")
-    gains = all_along(norm_gain.astype(jnp.float32), "segment")
-    scalars = jnp.concatenate([places, atmos_owner[0]])
+    )(scalars, norm_gain, conv_weight[0], point_weight[0], slots)
+    relayed, between, direct = (all_along(piece, "segment")[1:] for piece in (relayed, between, direct))
+    group = all_along(group, "members")
     field = pl.pallas_call(
         functools.partial(field_kernel, (steps, members, local, forced, vp, fp)),
         out_shape=jax.ShapeDtypeStruct((local, vp + fp * steps + BF16_ROWS, lon), jnp.bfloat16),
@@ -340,35 +373,36 @@
     )(scalars, init_state[0], land_mask, *group)
     fields = all_along(field, "rows")
 
-    enc = jnp.pad(encode_weight[:, :varied], ((0, 0), (0, vp - varied)))
-    enc = jnp.concatenate([enc, jnp.pad(encode_weight[:, varied:], ((0, 0), (0, fp - forced)))], axis=1)
-    dec = jnp.pad(decode_weight, ((0, vp - varied), (0, 0)))
     dims = (steps, layers, bands, local, at_once, lon, chans, vp, fp, turns)
-    field, scale, shift, hidden, taps = pl.pallas_call(
+    field, scale, shift, enc, dec, hidden, taps = pl.pallas_call(
         functools.partial(first_kernel, dims),
         out_shape=(
             jax.ShapeDtypeStruct((lat, vp + fp * steps + BF16_ROWS, lon), jnp.bfloat16),
             jax.ShapeDtypeStruct((turns, chans, wide), jnp.float32),
             jax.ShapeDtypeStruct((turns, chans, wide), jnp.float32),
+            jax.ShapeDtypeStruct((chans, vp + fp), jnp.bfloat16),
+            jax.ShapeDtypeStruct((vp, chans), jnp.bfloat16),
             jax.ShapeDtypeStruct((lat, chans, wide), jnp.bfloat16),
             jax.ShapeDtypeStruct((lat * 3 * chans, wide), jnp.bfloat16),
         ),
-        in_specs=[smem] + [vmem] * (4 + bands + members),
-        out_specs=(vmem,) * 5,
+        in_specs=[smem] + [vmem] * (5 + bands + members),
+        out_specs=(vmem,) * 7,
         compiler_params=small,
         cost_estimate=free,
-    )(scalars, enc, settings, scale_weight.T, shift_weight.T, *fields, *group)
-
-    blocks = [conv_weight[0], point_weight[0]]
+    )(scalars, encode_weight, decode_weight, settings, scale_weight.T, shift_weight.T, *fields, *group)
+
+    blocks = [conv_weight[0], point_weight[0], spread]
     for k in range(layers - 1):
-        shares = all_along(relayed[k], "groups")
-        for shared in shares:
+        shares = all_along(after(relayed[k], *group[1:]), "groups")
+        early = all_along(shares[0], "rows")
+        blocks += early
+        for shared in shares[1:]:
             blocks += all_along(shared, "rows")
-        blocks += all_along(after(direct[k], taps, *gains, *shares[1:]), "rows")
+        blocks += all_along(after(between[k], taps, *shares[1:]), "rows")
+        blocks += all_along(after(direct[k], taps, *shares[1:], *early[1:]), "rows")
 
     scratch = [
-        pltpu.VMEM((layers, chans, 10 * chans), jnp.bfloat16),
-        pltpu.VMEM((layers, chans, lon), jnp.bfloat16),
+        pltpu.VMEM((layers, chans, 10 * chans + LANES), jnp.bfloat16),
         pltpu.VMEM((lat, chans, wide), jnp.float32),
         pltpu.VMEM((lat, chans, wide), jnp.bfloat16),
         pltpu.VMEM((lat, vp + fp, wide), jnp.bfloat16),
@@ -383,12 +417,12 @@
             jax.ShapeDtypeStruct((local, varied, lon), jnp.bfloat16),
             jax.ShapeDtypeStruct((varied, local, lon), jnp.float32),
         ),
-        in_specs=[smem] + [vmem] * (7 + layers) + [whole] * len(blocks),
+        in_specs=[smem] + [vmem] * 7 + [whole] * len(blocks),
         out_specs=(vmem, vmem),
         scratch_shapes=scratch,
         compiler_params=large,
         cost_estimate=free,
-    )(scalars, field, scale, shift, enc, dec, *gains, hidden, taps, *blocks)
+    )(scalars, field, scale, shift, enc, dec, hidden, taps, *blocks)
     return final[None, None], jnp.swapaxes(mean, 0, 1)[None]
 def solution(mesh):
     in_specs = (

time: 32.8 us -> 54.4 us (1.66)
  Pallas kernels: 10.9 us -> 28.7 us
  waiting for transfers between devices: 2.19 us -> 8.8 us
  local copies, waits for them, and re-layouts: 5.02 us -> 3.12 us
  other arithmetic: 0.84 us -> 0 us
    pallas_call x1, Pallas kernels: 0.62 us -> 18.5 us  [per_device(): pl.pallas_call(pack_kernel, out_shape=(jax.ShapeDtypeStruct((part, share)...]
    ppermute x11 -> x12, waiting for transfers between devices: 2.19 us -> 8.8 us  [passed_along(): lax.ppermute(block, axis, [(i, (i + distance) % size) for i in range(size)])]
    slice x2 -> x0, local copies, waits for them, and re-layouts: 1.48 us -> none
    unnamed x29 -> x30, local copies, waits for them, and re-layouts: 2.76 us -> 1.84 us
    pad x1 -> x0, other arithmetic: 0.66 us -> none  [per_device(): enc = jnp.pad(encode_weight[:, :varied], ((0, 0), (0, vp - varied)))]
    concatenate x2 -> x1, local copies, waits for them, and re-layouts: 0.77 us -> 1.28 us  [per_device(): jnp.concatenate([jnp.stack(places).astype(jnp.int32), param_index, atmos_...]
    ppermute x11 -> x12, starting transfers between devices: 12.1 us -> 11.9 us  [passed_along(): lax.ppermute(block, axis, [(i, (i + distance) % size) for i in range(size)])]
  transfers between devices with their start and end apart: 11 -> 12, of which waited for: 3 -> 5; matrix products, arithmetic and copies ran while one was open for 11% -> 1% of each run, Pallas kernels for 6% -> 4%
where the time goes in v6:
time: 54.4 us; the launch traced here: 54.1 us
  Pallas kernels  28.7 us (53%)
  starting transfers between devices  11.9 us (22%)
  waiting for transfers between devices  8.8 us (16%)
  local copies, waits for them, and re-layouts  3.12 us (6%)
  between operations  1.53 us (3%)
    pallas_call x1, Pallas kernels, per_device(): pl.pallas_call(pack_kernel, out_shape=(jax.ShapeDtypeStruct((part, share)...  18.5 us
    ppermute x12, starting transfers between devices, passed_along(): lax.ppermute(block, axis, [(i, (i + distance) % size) for i in range(size)])  11.9 us
    ppermute x12, waiting for transfers between devices, passed_along(): lax.ppermute(block, axis, [(i, (i + distance) % size) for i in range(size)])  8.8 us
    pallas_call x1, Pallas kernels, per_device(): pl.pallas_call(functools.partial(window_kernel, dims + (groups,)), out_sh...  8.28 us
    unnamed x30, local copies, waits for them, and re-layouts  1.84 us
    pallas_call x1, Pallas kernels, per_device(): pl.pallas_call(functools.partial(first_kernel, dims), out_shape=(jax.Shap...  1.41 us
    concatenate x1, local copies, waits for them, and re-layouts, per_device(): jnp.concatenate([jnp.stack(places).astype(jnp.int32), param_index, atmos_...  1.28 us
  transfers between devices with their start and end apart: 12, of which 5 were waited for; matrix products, arithmetic and copies ran while one was open for 1% of the time, Pallas kernels for 4%

profile of v6, /device:TPU:0, one launch (start us, length us, event | category | flops | bytes accessed | tf_op | source)
XLA Modules:
  0.0 54.1 jit_solution(1705065132562535371)
XLA Ops:
  0.6 0.0 copy-start.8
  0.6 0.0 copy-start.6
  0.7 0.0 copy-start.12
  0.7 0.0 copy-start.9
  0.7 0.0 copy-start.10
  0.7 0.0 copy-start.11
  0.7 0.0 copy-start.3
  1.4 1.3 %concatenate.3.scalar_ref = s32[7]{0:T(128)} concatenate(s32[1]{0:T(128)} %bitcast, s32[1]{0:T(128)} %bitcast.1, s32[1]{0:T(128)} %bitcast.2, s32[1]{0:T(128)} %bitcast.3, s32[1]{0:T(128)S(6)} %copy.26, s32[2]{0:T(128)} %bitcast.23), dimensions={0} | concatenate | bytes 56 | tf_op jit(solution)/shard_map/concatenate | solution.py:341
  2.7 18.5 %shard_map.140 = (bf16[128,512]{1,0:T(8,128)(2,1)}, bf16[128,896]{1,0:T(8,128)(2,1)}, bf16[128,768]{1,0:T(8,128)(2,1)}, bf16[256,128]{1,0:T(8,128)(2,1)}, f32[9,128]{1,0:T(8,128)}) custom-call(s32[7]{0:T(128)} %concatenate.3.scalar_ref, bf16[1,256]{1,0:T(2,128)(2,1)} %gain_ref.1, bf16[256,2304]{1,0:T(8,128)(2,1)} %bitcast.15, bf16[256,256]{1,0:T(8,128)(2,1)} %bitcast.19, ...), custom_call_target="tpu_custom_call" | custom-call | tf_op jit(solution)/shard_map/pallas_call | solution.py:345
  21.2 3.0 %collective-permute-start.4 = (bf16[128,512]{1,0:T(8,128)(2,1)}, bf16[128,512]{1,0:T(8,128)(2,1)S(1)}, u32[]{:S(2)}, u32[]{:S(2)}) collective-permute-start(bf16[128,512]{1,0:T(8,128)(2,1)} %get-tuple-element.25), channel_id=1, source_target_pairs={{0,2},{2,0},{1,3},{3,1},{4,6},{6,4},{5,7},{7,5},{8,10},{10,8},{9,1... | collective-permute-start | bytes 393224 | tf_op jit(solution)/shard_map/ppermute | solution.py:21
  24.2 0.1 collective-permute-start.8
  24.2 1.9 %collective-permute-start.10 = (bf16[128,768]{1,0:T(8,128)(2,1)}, bf16[128,768]{1,0:T(8,128)(2,1)S(1)}, u32[]{:S(2)}, u32[]{:S(2)}) collective-permute-start(bf16[128,768]{1,0:T(8,128)(2,1)} %get-tuple-element.27), channel_id=1, source_target_pairs={{0,2},{2,0},{1,3},{3,1},{4,6},{6,4},{5,7},{7,5},{8,10},{10,8},{9,1... | collective-permute-start | bytes 589832 | tf_op jit(solution)/shard_map/ppermute | solution.py:21
  26.2 3.6 %collective-permute-start.2 = (f32[9,128]{1,0:T(8,128)}, f32[9,128]{1,0:T(8,128)S(1)}, u32[]{:S(2)}, u32[]{:S(2)}) collective-permute-start(f32[9,128]{1,0:T(8,128)} %get-tuple-element.16.rest_0_.rest_2_), channel_id=1, source_target_pairs={{0,12},{4,0},{8,4},{12,8},{1,13},{5,1},{9,5},{13,9},{2,14},{6,2},{... | collective-permute-start | bytes 13832 | tf_op jit(solution)/shard_map/ppermute | solution.py:21
  29.8 0.0 collective-permute-start.1
  29.8 1.6 %collective-permute-done.2.rest_3_.rest_5_.refs_3_ = f32[9,128]{1,0:T(8,128)S(1)} collective-permute-done((f32[9,128]{1,0:T(8,128)}, f32[9,128]{1,0:T(8,128)S(1)}, u32[]{:S(2)}, u32[]{:S(2)}) %collective-permute-start.2) | collective-permute-done | bytes 4640 | tf_op jit(solution)/shard_map/ppermute | solution.py:21
  31.4 0.3 collective-permute-start
  31.6 2.9 %collective-permute-done.1.rest_2_.rest_4_.refs_2_ = f32[9,128]{1,0:T(8,128)S(1)} collective-permute-done((f32[9,128]{1,0:T(8,128)}, f32[9,128]{1,0:T(8,128)S(1)}, u32[]{:S(2)}, u32[]{:S(2)}) %collective-permute-start.1) | collective-permute-done | bytes 4640 | tf_op jit(solution)/shard_map/ppermute | solution.py:21
  34.6 2.7 %collective-permute-done.rest_1_.rest_3_.refs_1_ = f32[9,128]{1,0:T(8,128)S(1)} collective-permute-done((f32[9,128]{1,0:T(8,128)}, f32[9,128]{1,0:T(8,128)S(1)}, u32[]{:S(2)}, u32[]{:S(2)}) %collective-permute-start) | collective-permute-done | bytes 4640 | tf_op jit(solution)/shard_map/ppermute | solution.py:21
  37.3 0.0 collective-permute-done.4.refs_0_
  37.3 1.5 %collective-permute-start.6 = (bf16[128,512]{1,0:T(8,128)(2,1)S(1)}, bf16[128,512]{1,0:T(8,128)(2,1)S(1)}, u32[]{:S(2)}, u32[]{:S(2)}) collective-permute-start(bf16[128,512]{1,0:T(8,128)(2,1)S(1)} %shard_map.143.rest_5_), channel_id=1, source_target_pairs={{0,16},{16,0},{1,17},{17,1},{2,18},{18,2},{3,19},{19,3},{4,20},{20... | collective-permute-start | bytes 393224 | tf_op jit(solution)/shard_map/ppermute | solution.py:21
  38.8 0.0 collective-permute-start.5
  38.8 0.0 copy-done.8
  38.8 0.0 copy-done.6
  38.8 0.0 copy-start.4
  38.9 0.7 %copy-done.4 = f32[9,128]{1,0:T(8,128)S(1)} copy-done((f32[9,128]{1,0:T(8,128)S(1)}, f32[9,128]{1,0:T(8,128)}, u32[]{:S(2)}) %copy-start.4) | copy-done | bytes 4632
  39.5 0.6 %shard_map.141.rest_0_ = bf16[1,128,128]{2,1,0:T(8,128)(2,1)S(1)} custom-call(s32[7]{0:T(128)S(1)} %copy-done.7, bf16[1,77,128]{2,1,0:T(8,128)(2,1)S(1)} %bitcast.21, s32[1,128]{1,0:T(1,128)S(1)} %copy-done.8, f32[9,128]{1,0:T(8,128)S(1)} %copy-done.4, f32[9,128]{1,0:T(8,128)S(1)} %collective-permute-done.rest_1_.rest_3_.refs_1_, ...), custom_call_target="tpu_custom_call" | custom-call | tf_op jit(solution)/shard_map/pallas_call | solution.py:366
  40.1 0.6 %collective-permute-start.3 = (bf16[1,128,128]{2,1,0:T(8,128)(2,1)S(1)}, bf16[1,128,128]{2,1,0:T(8,128)(2,1)S(1)}, u32[]{:S(2)}, u32[]{:S(2)}) collective-permute-start(bf16[1,128,128]{2,1,0:T(8,128)(2,1)S(1)} %shard_map.141.rest_0_), channel_id=1, source_target_pairs={{0,1},{1,0},{2,3},{3,2},{4,5},{5,4},{6,7},{7,6},{8,9},{9,8},{10,11... | collective-permute-start | bytes 98312 | tf_op jit(solution)/shard_map/ppermute | solution.py:21
  40.7 0.1 copy.21.settings_ref
  40.8 0.1 copy.20.enc_w_ref
  40.9 0.1 copy.18
  41.0 0.1 copy.19
  41.1 0.4 collective-permute-done.3.rest_1_
  41.5 0.7 %copy-done.5 = f32[9,128]{1,0:T(8,128)S(1)} copy-done((f32[9,128]{1,0:T(8,128)S(1)}, f32[9,128]{1,0:T(8,128)}, u32[]{:S(2)}) %copy-start.5) | copy-done | bytes 4632
  42.2 1.4 %shard_map.142 = (bf16[2,128,128]{2,1,0:T(8,128)(2,1)S(1)}, f32[1,256,512]{2,1,0:T(8,128)S(1)}, f32[1,256,512]{2,1,0:T(8,128)S(1)}, bf16[256,96]{1,0:T(8,128)(2,...) custom-call(s32[7]{0:T(128)S(1)} %copy-done.7, ...), custom_call_target="tpu_custom_call" | custom-call | tf_op jit(solution)/shard_map/pallas_call | solution.py:377
  43.6 0.0 collective-permute-done.8.refs_0_
  43.7 0.0 collective-permute-done.6.refs_2_.rest_7_
  43.7 0.0 copy-start
  43.7 0.0 copy-start.1
  43.7 0.4 collective-permute-start.9
  44.1 0.0 collective-permute-done.10.refs_0_
  44.1 0.0 collective-permute-done.5.refs_3_.rest_6_
  44.1 0.2 collective-permute-start.11
  44.3 0.3 collective-permute-start.7
  44.6 1.1 %collective-permute-done.7.rest_8_ = bf16[128,512]{1,0:T(8,128)(2,1)S(1)} collective-permute-done((bf16[128,512]{1,0:T(8,128)(2,1)S(1)}, bf16[128,512]{1,0:T(8,128)(2,1)S(1)}, u32[]{:S(2)}, u32[]{:S(2)}) %collective-permute-start.7) | collective-permute-done | bytes 131104 | tf_op jit(solution)/shard_map/ppermute | solution.py:21
  45.8 0.0 collective-permute-done.11.rest_12_
  45.8 0.0 collective-permute-done.9.rest_10_
  45.8 0.0 copy-done
  45.8 8.3 %shard_map.146 = (bf16[1,77,128]{2,1,0:T(8,128)(2,1)}, f32[77,1,128]{2,1,0:T(1,128)}) custom-call(s32[7]{0:T(128)S(1)} %copy-done.7, bf16[2,128,128]{2,1,0:T(8,128)(2,1)S(1)} %get-tuple-element.17.field_ref, f32[1,256,512]{2,1,0:T(8,128)S(1)} %get-tuple-element.18.scale_ref, f32[1,256,512]{2,1,0:T(8,128)S(1)} %get-tuple-element.19.shift_ref, ...), custom_call_target="tpu_custom_call" | custom-call | tf_op jit(solution)/shard_map/pallas_call | solution.py:414
  (14 shorter events, 0.0 us)
Async XLA Ops:
  0.6 38.2 %copy-start.8 = (s32[1,128]{1,0:T(1,128)S(1)}, s32[1,128]{1,0:T(1,128)}, u32[]{:S(2)}) copy-start(s32[1,128]{1,0:T(1,128)} %land_ref.1) | copy-start | bytes 1540
  0.6 38.2 %copy-start.6 = (bf16[1,1,77,128]{3,2,1,0:T(8,128)(2,1)S(1)}, bf16[1,1,77,128]{3,2,1,0:T(8,128)(2,1)}, u32[]{:S(2)}) copy-start(bf16[1,1,77,128]{3,2,1,0:T(8,128)(2,1)} %param.13) | copy-start | bytes 59140
  0.7 40.0 %copy-start.12 = (f32[64,16]{0,1:T(8,128)S(1)}, f32[64,16]{0,1:T(8,128)}, u32[]{:S(2)}) copy-start(f32[64,16]{0,1:T(8,128)} %param.18) | copy-start | bytes 12292
  0.7 40.1 %copy-start.9 = (bf16[256,81]{0,1:T(8,128)(2,1)S(1)}, bf16[256,81]{0,1:T(8,128)(2,1)}, u32[]{:S(2)}) copy-start(bf16[256,81]{0,1:T(8,128)(2,1)} %param.21) | copy-start | bytes 124420
  0.7 40.2 %copy-start.10 = (f32[16,256]{1,0:T(8,128)S(1)}, f32[16,256]{1,0:T(8,128)}, u32[]{:S(2)}) copy-start(f32[16,256]{1,0:T(8,128)} %param.19) | copy-start | bytes 49156
  0.7 40.3 %copy-start.11 = (f32[16,256]{1,0:T(8,128)S(1)}, f32[16,256]{1,0:T(8,128)}, u32[]{:S(2)}) copy-start(f32[16,256]{1,0:T(8,128)} %param.20) | copy-start | bytes 49156
  0.7 40.8 %copy-start.3 = (bf16[77,256]{1,0:T(8,128)(2,1)S(1)}, bf16[77,256]{1,0:T(8,128)(2,1)}, u32[]{:S(2)}) copy-start(bf16[77,256]{1,0:T(8,128)(2,1)} %dec_w_ref.1) | copy-start | bytes 118276
  2.7 36.1 %copy-start.7 = (s32[7]{0:T(128)S(1)}, s32[7]{0:T(128)}, u32[]{:S(2)}) copy-start(s32[7]{0:T(128)} %concatenate.3.scalar_ref) | copy-start | bytes 88
  21.2 16.1 %collective-permute-start.4 = (bf16[128,512]{1,0:T(8,128)(2,1)}, bf16[128,512]{1,0:T(8,128)(2,1)S(1)}, u32[]{:S(2)}, u32[]{:S(2)}) collective-permute-start(bf16[128,512]{1,0:T(8,128)(2,1)} %get-tuple-element.25), channel_id=1, source_target_pairs={{0,2},{2,0},{1,3},{3,1},{4,6},{6,4},{5,7},{7,5},{8,10},{10,8},{9,1... | collective-permute-start | bytes 393224 | tf_op jit(solution)/shard_map/ppermute | solution.py:21
  24.2 19.5 %collective-permute-start.8 = (bf16[128,896]{1,0:T(8,128)(2,1)}, bf16[128,896]{1,0:T(8,128)(2,1)S(1)}, u32[]{:S(2)}, u32[]{:S(2)}) collective-permute-start(bf16[128,896]{1,0:T(8,128)(2,1)} %get-tuple-element.26), channel_id=1, source_target_pairs={{0,2},{2,0},{1,3},{3,1},{4,6},{6,4},{5,7},{7,5},{8,10},{10,8},{9,1... | collective-permute-start | bytes 688136 | tf_op jit(solution)/shard_map/ppermute | solution.py:21
  24.2 19.9 %collective-permute-start.10 = (bf16[128,768]{1,0:T(8,128)(2,1)}, bf16[128,768]{1,0:T(8,128)(2,1)S(1)}, u32[]{:S(2)}, u32[]{:S(2)}) collective-permute-start(bf16[128,768]{1,0:T(8,128)(2,1)} %get-tuple-element.27), channel_id=1, source_target_pairs={{0,2},{2,0},{1,3},{3,1},{4,6},{6,4},{5,7},{7,5},{8,10},{10,8},{9,1... | collective-permute-start | bytes 589832 | tf_op jit(solution)/shard_map/ppermute | solution.py:21
  26.2 5.2 %collective-permute-start.2 = (f32[9,128]{1,0:T(8,128)}, f32[9,128]{1,0:T(8,128)S(1)}, u32[]{:S(2)}, u32[]{:S(2)}) collective-permute-start(f32[9,128]{1,0:T(8,128)} %get-tuple-element.16.rest_0_.rest_2_), channel_id=1, source_target_pairs={{0,12},{4,0},{8,4},{12,8},{1,13},{5,1},{9,5},{13,9},{2,14},{6,2},{... | collective-permute-start | bytes 13832 | tf_op jit(solution)/shard_map/ppermute | solution.py:21
  29.8 4.8 %collective-permute-start.1 = (f32[9,128]{1,0:T(8,128)}, f32[9,128]{1,0:T(8,128)S(1)}, u32[]{:S(2)}, u32[]{:S(2)}) collective-permute-start(f32[9,128]{1,0:T(8,128)} %get-tuple-element.16.rest_0_.rest_2_), channel_id=1, source_target_pairs={{0,8},{4,12},{8,0},{12,4},{1,9},{5,13},{9,1},{13,5},{2,10},{6,14},... | collective-permute-start | bytes 13832 | tf_op jit(solution)/shard_map/ppermute | solution.py:21
  31.4 5.9 %collective-permute-start = (f32[9,128]{1,0:T(8,128)}, f32[9,128]{1,0:T(8,128)S(1)}, u32[]{:S(2)}, u32[]{:S(2)}) collective-permute-start(f32[9,128]{1,0:T(8,128)} %get-tuple-element.16.rest_0_.rest_2_), channel_id=1, source_target_pairs={{0,4},{4,8},{8,12},{12,0},{1,5},{5,9},{9,13},{13,1},{2,6},{6,10},{... | collective-permute-start | bytes 13832 | tf_op jit(solution)/shard_map/ppermute | solution.py:21
  37.3 6.4 %collective-permute-start.6 = (bf16[128,512]{1,0:T(8,128)(2,1)S(1)}, bf16[128,512]{1,0:T(8,128)(2,1)S(1)}, u32[]{:S(2)}, u32[]{:S(2)}) collective-permute-start(bf16[128,512]{1,0:T(8,128)(2,1)S(1)} %shard_map.143.rest_5_), channel_id=1, source_target_pairs={{0,16},{16,0},{1,17},{17,1},{2,18},{18,2},{3,19},{19,3},{4,20},{20... | collective-permute-start | bytes 393224 | tf_op jit(solution)/shard_map/ppermute | solution.py:21
  38.8 5.3 %collective-permute-start.5 = (bf16[128,512]{1,0:T(8,128)(2,1)S(1)}, bf16[128,512]{1,0:T(8,128)(2,1)S(1)}, u32[]{:S(2)}, u32[]{:S(2)}) collective-permute-start(bf16[128,512]{1,0:T(8,128)(2,1)S(1)} %shard_map.143.rest_5_), channel_id=1, source_target_pairs={{0,1},{1,0},{2,3},{3,2},{4,5},{5,4},{6,7},{7,6},{8,9},{9,8},{10,11... | collective-permute-start | bytes 393224 | tf_op jit(solution)/shard_map/ppermute | solution.py:21
  38.8 0.7 %copy-start.4 = (f32[9,128]{1,0:T(8,128)S(1)}, f32[9,128]{1,0:T(8,128)}, u32[]{:S(2)}) copy-start(f32[9,128]{1,0:T(8,128)} %get-tuple-element.16.rest_0_.rest_2_) | copy-start | bytes 13828
  40.1 1.4 %collective-permute-start.3 = (bf16[1,128,128]{2,1,0:T(8,128)(2,1)S(1)}, bf16[1,128,128]{2,1,0:T(8,128)(2,1)S(1)}, u32[]{:S(2)}, u32[]{:S(2)}) collective-permute-start(bf16[1,128,128]{2,1,0:T(8,128)(2,1)S(1)} %shard_map.141.rest_0_), channel_id=1, source_target_pairs={{0,1},{1,0},{2,3},{3,2},{4,5},{5,4},{6,7},{7,6},{8,9},{9,8},{10,11... | collective-permute-start | bytes 98312 | tf_op jit(solution)/shard_map/ppermute | solution.py:21
  41.5 0.7 %copy-start.5 = (f32[9,128]{1,0:T(8,128)S(1)}, f32[9,128]{1,0:T(8,128)}, u32[]{:S(2)}) copy-start(f32[9,128]{1,0:T(8,128)} %get-tuple-element.16.rest_0_.rest_2_) | copy-start | bytes 13828
  43.7 2.1 %copy-start = (bf16[1,256,2304]{2,1,0:T(8,128)(2,1)S(1)}, bf16[1,256,2304]{2,1,0:T(8,128)(2,1)}, u32[]{:S(2)}) copy-start(bf16[1,256,2304]{2,1,0:T(8,128)(2,1)} %param.22) | copy-start | bytes 3538948
  43.7 2.1 %copy-start.1 = (bf16[1,256,256]{2,1,0:T(8,128)(2,1)S(1)}, bf16[1,256,256]{2,1,0:T(8,128)(2,1)}, u32[]{:S(2)}) copy-start(bf16[1,256,256]{2,1,0:T(8,128)(2,1)} %param.23) | copy-start | bytes 393220
  43.7 2.1 %copy-start.2 = (bf16[256,128]{1,0:T(8,128)(2,1)S(1)}, bf16[256,128]{1,0:T(8,128)(2,1)}, u32[]{:S(2)}) copy-start(bf16[256,128]{1,0:T(8,128)(2,1)} %get-tuple-element.24.rest_4_) | copy-start | bytes 196612
  43.7 2.1 %collective-permute-start.9 = (bf16[128,896]{1,0:T(8,128)(2,1)S(1)}, bf16[128,896]{1,0:T(8,128)(2,1)S(1)}, u32[]{:S(2)}, u32[]{:S(2)}) collective-permute-start(bf16[128,896]{1,0:T(8,128)(2,1)S(1)} %shard_map.144.rest_9_), channel_id=1, source_target_pairs={{0,1},{1,0},{2,3},{3,2},{4,5},{5,4},{6,7},{7,6},{8,9},{9,8},{10,11... | collective-permute-start | bytes 688136 | tf_op jit(solution)/shard_map/ppermute | solution.py:21
  44.1 1.6 %collective-permute-start.11 = (bf16[128,768]{1,0:T(8,128)(2,1)S(1)}, bf16[128,768]{1,0:T(8,128)(2,1)S(1)}, u32[]{:S(2)}, u32[]{:S(2)}) collective-permute-start(bf16[128,768]{1,0:T(8,128)(2,1)S(1)} %shard_map.145.rest_11_), channel_id=1, source_target_pairs={{0,1},{1,0},{2,3},{3,2},{4,5},{5,4},{6,7},{7,6},{8,9},{9,8},{10,11... | collective-permute-start | bytes 589832 | tf_op jit(solution)/shard_map/ppermute | solution.py:21
  44.3 1.4 %collective-permute-start.7 = (bf16[128,512]{1,0:T(8,128)(2,1)S(1)}, bf16[128,512]{1,0:T(8,128)(2,1)S(1)}, u32[]{:S(2)}, u32[]{:S(2)}) collective-permute-start(bf16[128,512]{1,0:T(8,128)(2,1)S(1)} %collective-permute-done.6.refs_2_.rest_7_), channel_id=1, source_target_pairs={{0,1},{1,0},{2,3},{3,2},{4,5},{5,4},{6,7},{7,6},{8,9},{9,8},{10,11... | collective-permute-start | bytes 393224 | tf_op jit(solution)/shard_map/ppermute | solution.py:21

commit v7 on v6

--- a/solution.py
+++ b/solution.py
@@ -25,6 +25,15 @@
     return [block] + [passed_along(block, axis, k) for k in range(1, lax.axis_size(axis))]
 
 
+def by_doubling(block, axis):
+    size, reach = lax.axis_size(axis), 1
+    while reach < size:
+        partner = lax.ppermute(block, axis, [(i, i ^ reach) for i in range(size)])
+        block = jnp.concatenate([block, partner], axis=0)
+        reach *= 2
+    return block
+
+
 def from_place(parts, here, place):
     chosen = parts[0]
     for k in range(1, len(parts)):
@@ -32,31 +41,24 @@
     return chosen
 
 
-def run_copies(*copies):
-    for copy in copies:
-        copy.start()
-    for copy in copies:
-        copy.wait()
-
-
-def pack_kernel(scalar_ref, gain_ref, conv_ref, point_ref, slots_ref, *rest):
-    relayed_ref, middle_ref, direct_ref, spread_ref, group_ref, slots, gain, sems = rest
+def pack_kernel(dims, place_ref, gain_ref, conv_ref, point_ref, slots_ref, state_ref, land_ref, *rest):
+    steps, local, forced, vp, fp = dims
+    relayed_ref, direct_ref, spread_ref, field_ref, slots, gain, state, land, sems = rest
     part, share = relayed_ref.shape
     wide, chans = conv_ref.shape[1], point_ref.shape[1]
     left = direct_ref.shape[1] - chans - LANES
-    rows = pl.ds(pl.multiple_of(scalar_ref[1] * part, part), part)
-    mine = pl.ds(pl.multiple_of(scalar_ref[3] * share, LANES), share)
+    rows = pl.ds(pl.multiple_of(place_ref[1] * part, part), part)
+    mine = pl.ds(pl.multiple_of(place_ref[3] * share, LANES), share)
     small = [
         pltpu.make_async_copy(gain_ref, gain, sems.at[0]),
         pltpu.make_async_copy(slots_ref, slots, sems.at[1]),
+        pltpu.make_async_copy(state_ref, state, sems.at[2]),
+        pltpu.make_async_copy(land_ref, land, sems.at[3]),
     ]
     large = [
-        pltpu.make_async_copy(conv_ref.at[rows, mine], relayed_ref, sems.at[2]),
-        pltpu.make_async_copy(
-            conv_ref.at[rows, pl.ds(wide - left - middle_ref.shape[1], middle_ref.shape[1])], middle_ref, sems.at[6]
-        ),
-        pltpu.make_async_copy(conv_ref.at[rows, pl.ds(wide - left, left)], direct_ref.at[:, pl.ds(0, left)], sems.at[3]),
-        pltpu.make_async_copy(point_ref.at[rows, :], direct_ref.at[:, pl.ds(left, chans)], sems.at[4]),
+        pltpu.make_async_copy(conv_ref.at[rows, mine], relayed_ref, sems.at[4]),
+        pltpu.make_async_copy(conv_ref.at[rows, pl.ds(wide - left, left)], direct_ref.at[:, pl.ds(0, left)], sems.at[5]),
+        pltpu.make_async_copy(point_ref.at[rows, :], direct_ref.at[:, pl.ds(left, chans)], sems.at[6]),
     ]
     for copy in small + large:
         copy.start()
@@ -65,33 +67,29 @@
     eye = lax.broadcasted_iota(jnp.int32, (chans, chans), 0) == lax.broadcasted_iota(jnp.int32, (chans, chans), 1)
     column = jnp.sum(jnp.where(eye, gain[...].astype(jnp.float32), 0.0), axis=1, keepdims=True)
     spread_ref[...] = jnp.broadcast_to(column, (chans, LANES)).astype(jnp.bfloat16)
-    large.append(
-        pltpu.make_async_copy(spread_ref.at[rows, :], direct_ref.at[:, pl.ds(left + chans, LANES)], sems.at[5])
-    )
-    large[-1].start()
-    count = slots.shape[0]
-    group_ref[0:count] = slots[...].astype(jnp.float32)
-    index = jnp.full((1, group_ref.shape[1]), scalar_ref[4], jnp.int32)
-    group_ref[count : count + 1] = index.astype(jnp.float32)
+    direct_ref[:, left + chans :] = spread_ref[rows, :]
+    field_ref[...] = jnp.zeros(field_ref.shape, field_ref.dtype)
+    for i in range(local):
+        field_ref[i, 0 : state.shape[1]] = state[i]
+        for t in range(steps):
+            first = (t * local + i) * forced
+            field_ref[i, vp + fp * t : vp + fp * t + forced] = slots[first : first + forced]
+        field_ref[i, vp + fp * steps : vp + fp * steps + 1] = land[i : i + 1].astype(jnp.bfloat16)
     for copy in large:
         copy.wait()
 
 
-def field_kernel(dims, scalar_ref, state_ref, land_ref, *rest):
-    steps, members, local, forced, vp, fp = dims
-    group, out_ref = rest[:members], rest[members]
-    varied, lon = state_ref.shape[1:]
-    for i in range(local):
-        out_ref[i] = jnp.zeros(out_ref.shape[1:], jnp.bfloat16)
-        out_ref[i, 0:varied] = state_ref[i]
-        for t in range(steps):
-            first = (t * local + i) * forced
-            force = group[0][first : first + forced, :]
-            for k in range(1, members):
-                source = lax.rem(scalar_ref[2] - k + members, members)
-                force = jnp.where(scalar_ref[5 + t] == source, group[k][first : first + forced, :], force)
-            out_ref[i, vp + fp * t : vp + fp * t + forced, :] = force.astype(jnp.bfloat16)
-        out_ref[i, vp + fp * steps : vp + fp * steps + 1, :] = land_ref[i : i + 1, :].astype(jnp.bfloat16)
+def group_kernel(dims, place_ref, index_ref, *rest):
+    steps, bands, local, forced, vp, fp = dims
+    fields, group_ref = rest[:bands], rest[bands]
+    for b in range(bands):
+        field = from_place([f[...] for f in fields], place_ref[1], b)
+        for i in range(local):
+            for t in range(steps):
+                first = ((b * local + i) * steps + t) * forced
+                group_ref[first : first + forced] = field[i, vp + fp * t : vp + fp * t + forced].astype(jnp.float32)
+    last = bands * local * steps * forced
+    group_ref[last : last + 1] = jnp.full((1, group_ref.shape[1]), index_ref[0], jnp.int32).astype(jnp.float32)
 
 
 def put_taps(taps, value, row, cols, spacing):
@@ -106,10 +104,13 @@
     )
 
 
-def first_kernel(dims, scalar_ref, enc_w_ref, dec_w_ref, settings_ref, scale_w_ref, shift_w_ref, *rest):
+def first_kernel(dims, scalar_ref, owner_ref, enc_w_ref, dec_w_ref, settings_ref, scale_w_ref, shift_w_ref, *rest):
     steps, layers, bands, local, members, lon, chans, vp, fp, turns = dims
     fields, rest = rest[:bands], rest[bands:]
-    group, rest = rest[: members * turns], rest[members * turns :]
+    everyone, rest = rest[0], rest[1:]
+    forced = enc_w_ref.shape[1] - dec_w_ref.shape[0]
+    used = bands * local * steps * forced
+    group = [everyone.at[k * (used + 8) : (k + 1) * (used + 8)] for k in range(members * turns)]
     field_ref, scale_ref, shift_ref, enc_ref, dec_ref, hidden_ref, taps_ref = rest
     varied = dec_w_ref.shape[0]
     forced = enc_w_ref.shape[1] - varied
@@ -121,11 +122,19 @@
     band = scalar_ref[1]
     for b in range(bands):
         field_ref[b * local : (b + 1) * local] = from_place([f[...] for f in fields], band, b)
+    for i in range(bands * local):
+        for t in range(steps):
+            rows = slice((i * steps + t) * forced, (i * steps + t + 1) * forced)
+            place = scalar_ref[2] ^ owner_ref[t]
+            force = group[0][rows, :]
+            for k in range(1, members * turns):
+                force = jnp.where(place == k, group[k][rows, :], force)
+            field_ref[i, vp + fp * t : vp + fp * t + forced, :] = force.astype(jnp.bfloat16)
 
     settings = settings_ref[...]
     numbers = lax.broadcasted_iota(jnp.int32, settings.shape, 0).astype(jnp.float32)
     for m, entry in enumerate(group):
-        chosen = entry[entry.shape[0] - 1 : entry.shape[0], 0 : settings.shape[1]]
+        chosen = entry[used : used + 1, 0 : settings.shape[1]]
         row = jnp.sum(jnp.where(numbers == chosen, settings, 0.0), axis=0, keepdims=True)
         cols = slice((m % members) * lon, (m % members + 1) * lon)
         scale = 1.0 + jnp.sum(scale_w_ref[...] * row, axis=1, keepdims=True)
@@ -166,7 +175,7 @@
     steps, layers, bands, local, members, lon, chans, vp, fp, turns, groups = dims
     lat = bands * local
     hidden, taps = rest[:2]
-    pieces = 3 + (layers - 1) * (groups + 2) * bands
+    pieces = 3 + (layers - 1) * (groups + 1) * bands
     blocks, rest = rest[2 : 2 + pieces], rest[2 + pieces :]
     final_ref, mean_ref, weights, conv, act, inputs, total, sems = rest[:8]
     here, band = scalar_ref[0], scalar_ref[1]
@@ -176,21 +185,18 @@
     pltpu.make_async_copy(blocks[0], weights.at[here, :, pl.ds(0, taps_wide)], sems.at[here]).start()
     pltpu.make_async_copy(blocks[1], weights.at[here, :, pl.ds(taps_wide, chans)], sems.at[here]).start()
     pltpu.make_async_copy(blocks[2], weights.at[here, :, pl.ds(10 * chans, LANES)], sems.at[here]).start()
-    share = 4 * chans // groups
-    middle = groups * share + blocks[3 + groups * bands].shape[1] if layers > 1 else 0
+    share = 5 * chans // groups
     for k in range(1, layers):
         slot = lax.rem(here - k + layers, layers)
-        for g in range(groups + 2):
+        for g in range(groups + 1):
             if g < groups:
                 place = lax.rem(scalar_ref[3] - g + groups, groups)
                 cols = pl.ds(pl.multiple_of(place * share, LANES), share)
-            elif g == groups:
-                cols = pl.ds(groups * share, middle - groups * share)
             else:
-                cols = pl.ds(middle, 10 * chans + LANES - middle)
+                cols = pl.ds(groups * share, 10 * chans + LANES - groups * share)
             for j in range(bands):
                 rows = pl.ds(pl.multiple_of(lax.rem(band - j + bands, bands) * part, part), part)
-                block = blocks[3 + ((k - 1) * (groups + 2) + g) * bands + j]
+                block = blocks[3 + ((k - 1) * (groups + 1) + g) * bands + j]
                 pltpu.make_async_copy(block, weights.at[slot, rows, cols], sems.at[slot]).start()
 
     if turns > 1:
@@ -336,42 +342,41 @@
     free = pl.CostEstimate(flops=0, bytes_accessed=0, transcendentals=0)
 
     groups = lax.axis_size("groups")
-    share = 4 * chans // groups
+    share = 5 * chans // groups
     places = [here, band, lax.axis_index("members"), lax.axis_index("groups")]
-    scalars = jnp.concatenate([jnp.stack(places).astype(jnp.int32), param_index, atmos_owner[0]])
+    scalars = jnp.stack(places).astype(jnp.int32)
     slots = forcing_slots[0, 0].reshape(-1, lon)
-    crowded = pltpu.CompilerParams(vmem_limit_bytes=60 * MIB)
-    middle = groups * share + (9 * chans - groups * share) * 7 // 10 // LANES * LANES
-    relayed, between, direct, spread, group = pl.pallas_call(
-        pack_kernel,
+    relayed, direct, spread, field = pl.pallas_call(
+        functools.partial(pack_kernel, (steps, local, forced, vp, fp)),
         out_shape=(
             jax.ShapeDtypeStruct((part, share), jnp.bfloat16),
-            jax.ShapeDtypeStruct((part, middle - groups * share), jnp.bfloat16),
-            jax.ShapeDtypeStruct((part, 10 * chans + LANES - middle), jnp.bfloat16),
+            jax.ShapeDtypeStruct((part, 10 * chans + LANES - groups * share), jnp.bfloat16),
             jax.ShapeDtypeStruct((chans, LANES), jnp.bfloat16),
-            jax.ShapeDtypeStruct((slots.shape[0] + 1, lon), jnp.float32),
+            jax.ShapeDtypeStruct((local, vp + fp * steps + BF16_ROWS, lon), jnp.bfloat16),
         ),
-        in_specs=[smem] + [whole] * 4,
-        out_specs=(whole, whole, whole, vmem, vmem),
+        in_specs=[smem] + [whole] * 6,
+        out_specs=(vmem,) * 4,
         scratch_shapes=[
             pltpu.VMEM(slots.shape, jnp.bfloat16),
             pltpu.VMEM(norm_gain.shape, jnp.bfloat16),
+            pltpu.VMEM(init_state.shape[1:], jnp.bfloat16),
+            pltpu.VMEM(land_mask.shape, jnp.int32),
             pltpu.SemaphoreType.DMA((7,)),
         ],
-        compiler_params=crowded,
+        compiler_params=pltpu.CompilerParams(vmem_limit_bytes=60 * MIB),
         cost_estimate=free,
-    )(scalars, norm_gain, conv_weight[0], point_weight[0], slots)
-    relayed, between, direct = (all_along(piece, "segment")[1:] for piece in (relayed, between, direct))
-    group = all_along(group, "members")
-    field = pl.pallas_call(
-        functools.partial(field_kernel, (steps, members, local, forced, vp, fp)),
-        out_shape=jax.ShapeDtypeStruct((local, vp + fp * steps + BF16_ROWS, lon), jnp.bfloat16),
-        in_specs=[smem] + [vmem] * (2 + members),
+    )(scalars, norm_gain, conv_weight[0], point_weight[0], slots, init_state[0], land_mask)
+    relayed, direct = (all_along(piece, "segment")[1:] for piece in (relayed, direct))
+    fields = all_along(field, "rows")
+    group = pl.pallas_call(
+        functools.partial(group_kernel, (steps, bands, local, forced, vp, fp)),
+        out_shape=jax.ShapeDtypeStruct((lat * steps * forced + 8, lon), jnp.float32),
+        in_specs=[smem, smem] + [vmem] * bands,
         out_specs=vmem,
         compiler_params=small,
         cost_estimate=free,
-    )(scalars, init_state[0], land_mask, *group)
-    fields = all_along(field, "rows")
+    )(scalars, param_index, *fields)
+    group = by_doubling(group, "members")
 
     dims = (steps, layers, bands, local, at_once, lon, chans, vp, fp, turns)
     field, scale, shift, enc, dec, hidden, taps = pl.pallas_call(
@@ -385,21 +390,20 @@
             jax.ShapeDtypeStruct((lat, chans, wide), jnp.bfloat16),
             jax.ShapeDtypeStruct((lat * 3 * chans, wide), jnp.bfloat16),
         ),
-        in_specs=[smem] + [vmem] * (5 + bands + members),
+        in_specs=[smem, smem] + [vmem] * (6 + bands),
         out_specs=(vmem,) * 7,
         compiler_params=small,
         cost_estimate=free,
-    )(scalars, encode_weight, decode_weight, settings, scale_weight.T, shift_weight.T, *fields, *group)
+    )(scalars, atmos_owner[0], encode_weight, decode_weight, settings, scale_weight.T, shift_weight.T, *fields, group)
 
     blocks = [conv_weight[0], point_weight[0], spread]
     for k in range(layers - 1):
-        shares = all_along(after(relayed[k], *group[1:]), "groups")
+        shares = all_along(relayed[k], "groups")
         early = all_along(shares[0], "rows")
         blocks += early
         for shared in shares[1:]:
             blocks += all_along(shared, "rows")
-        blocks += all_along(after(between[k], taps, *shares[1:]), "rows")
-        blocks += all_along(after(direct[k], taps, *shares[1:], *early[1:]), "rows")
+        blocks += all_along(after(direct[k], group, *shares[1:], *early[1:]), "rows")
 
     scratch = [
         pltpu.VMEM((layers, chans, 10 * chans + LANES), jnp.bfloat16),

time: 54.4 us -> 31.2 us (0.57)
  Pallas kernels: 28.7 us -> 13 us
  waiting for transfers between devices: 8.8 us -> 2.68 us
  starting transfers between devices: 11.9 us -> 10.4 us
  other arithmetic: 0 us -> 0.66 us
    pallas_call x2, Pallas kernels: 19 us -> 3.34 us  [the longest x1 2.78 us: per_device(): pl.pallas_call(functools.partial(pack_kernel, (steps, local, forced, vp,...]
    ppermute x12 -> x7, waiting for transfers between devices: 8.8 us -> 0.86 us  [passed_along(): lax.ppermute(block, axis, [(i, (i + distance) % size) for i in range(size)])]
    ppermute x12 -> x7, starting transfers between devices: 11.9 us -> 5.34 us  [passed_along(): lax.ppermute(block, axis, [(i, (i + distance) % size) for i in range(size)])]
    ppermute x0 -> x2, starting transfers between devices: none -> 5.06 us  [by_doubling(): partner = lax.ppermute(block, axis, [(i, i ^ reach) for i in range(size)])]
    ppermute x0 -> x2, waiting for transfers between devices: none -> 1.82 us  [by_doubling(): partner = lax.ppermute(block, axis, [(i, i ^ reach) for i in range(size)])]
    concatenate x1 -> x0, local copies, waits for them, and re-layouts: 1.28 us -> none  [per_device(): jnp.concatenate([jnp.stack(places).astype(jnp.int32), param_index, atmos_...]
    unnamed x30 -> x28, local copies, waits for them, and re-layouts: 1.84 us -> 2.65 us
    another operation x0 -> x1, other arithmetic: none -> 0.65 us  [per_device(): scalars = jnp.stack(places).astype(jnp.int32)]
  transfers between devices with their start and end apart: 12 -> 9, of which waited for: 5 -> 3; matrix products, arithmetic and copies ran while one was open for 1% -> 4% of each run, Pallas kernels for 4% -> 6%
where the time goes in v7:
time: 31.2 us; the launch traced here: 30.9 us
  Pallas kernels  13 us (42%)
  starting transfers between devices  10.4 us (33%)
  waiting for transfers between devices  2.68 us (9%)
  local copies, waits for them, and re-layouts  2.65 us (8%)
  between operations  1.45 us (5%)
  other arithmetic  0.66 us (2%)
    pallas_call x1, Pallas kernels, per_device(): pl.pallas_call(functools.partial(window_kernel, dims + (groups,)), out_sh...  8.27 us
    ppermute x7, starting transfers between devices, passed_along(): lax.ppermute(block, axis, [(i, (i + distance) % size) for i in range(size)])  5.34 us
    ppermute x2, starting transfers between devices, by_doubling(): partner = lax.ppermute(block, axis, [(i, i ^ reach) for i in range(size)])  5.06 us
    pallas_call x1, Pallas kernels, per_device(): pl.pallas_call(functools.partial(pack_kernel, (steps, local, forced, vp,...  2.78 us
    unnamed x28, local copies, waits for them, and re-layouts  2.65 us
    ppermute x2, waiting for transfers between devices, by_doubling(): partner = lax.ppermute(block, axis, [(i, i ^ reach) for i in range(size)])  1.82 us
    pallas_call x1, Pallas kernels, per_device(): pl.pallas_call(functools.partial(first_kernel, dims), out_shape=(jax.Shap...  1.41 us
    ppermute x7, waiting for transfers between devices, passed_along(): lax.ppermute(block, axis, [(i, (i + distance) % size) for i in range(size)])  0.86 us
  transfers between devices with their start and end apart: 9, of which 3 were waited for; matrix products, arithmetic and copies ran while one was open for 4% of the time, Pallas kernels for 6%

profile of v7, /device:TPU:0, one launch (start us, length us, event | category | flops | bytes accessed | tf_op | source)
XLA Modules:
  0.0 30.9 jit_solution(3967068991044267879)
XLA Ops:
  0.6 0.0 copy-start.11
  0.6 0.0 copy-start.9
  0.7 0.0 copy-start.5
  0.7 0.0 copy-start.8
  0.7 0.7 %pad_add_fusion.place_ref.scalar_ref = s32[4]{0:T(128)} fusion(s32[1]{0:T(128)} %bitcast.3, s32[1]{0:T(128)} %bitcast.2, s32[1]{0:T(128)} %bitcast.1, s32[1]{0:T(128)} %bitcast), kind=kLoop, calls=%fused_computation.2 | loop fusion | flops 12 | bytes 32 | tf_op jit(solution)/shard_map/stack | solution.py:347
  1.3 0.0 copy-start.7
  1.3 0.0 copy-start
  1.3 0.0 copy-start.1
  1.3 2.8 %shard_map.140 = (bf16[128,640]{1,0:T(8,128)(2,1)}, bf16[128,1408]{1,0:T(8,128)(2,1)}, bf16[256,128]{1,0:T(8,128)(2,1)}, bf16[1,128,128]{2,1,0:T(8,128)(2,1)}) custom-call(s32[4]{0:T(128)} %pad_add_fusion.place_ref.scalar_ref, bf16[1,256]{1,0:T(2,128)(2,1)} %gain_ref.1, bf16[256,2304]{1,0:T(8,128)(2,1)} %bitcast.15, bf16[256,256]{1,0:T(8,128)(2,1)} %bitcast.19, ...), custom_call_target="tpu_custom_call" | custom-call | tf_op jit(solution)/shard_map/pallas_call | solution.py:349
  4.1 3.0 %collective-permute-start.3 = (bf16[128,640]{1,0:T(8,128)(2,1)}, bf16[128,640]{1,0:T(8,128)(2,1)S(1)}, u32[]{:S(2)}, u32[]{:S(2)}) collective-permute-start(bf16[128,640]{1,0:T(8,128)(2,1)} %get-tuple-element.24), channel_id=1, source_target_pairs={{0,2},{2,0},{1,3},{3,1},{4,6},{6,4},{5,7},{7,5},{8,10},{10,8},{9,1... | collective-permute-start | bytes 491528 | tf_op jit(solution)/shard_map/ppermute | solution.py:21
  7.1 0.1 collective-permute-start.7
  7.2 0.0 collective-permute-start
  7.9 0.8 %collective-permute-done.rest_1_ = bf16[1,128,128]{2,1,0:T(8,128)(2,1)S(1)} collective-permute-done((bf16[1,128,128]{2,1,0:T(8,128)(2,1)}, bf16[1,128,128]{2,1,0:T(8,128)(2,1)S(1)}, u32[]{:S(2)}, u32[]{:S(2)}) %collective-permute-start) | collective-permute-done | bytes 32800 | tf_op jit(solution)/shard_map/ppermute | solution.py:21
  8.6 0.0 copy-start.2
  8.6 0.8 %copy-done.2 = bf16[1,128,128]{2,1,0:T(8,128)(2,1)S(1)} copy-done((bf16[1,128,128]{2,1,0:T(8,128)(2,1)S(1)}, bf16[1,128,128]{2,1,0:T(8,128)(2,1)}, u32[]{:S(2)}) %copy-start.2) | copy-done | bytes 32792
  9.4 0.0 copy-start.6
  9.4 0.7 %copy-done.6 = s32[4]{0:T(128)S(1)} copy-done((s32[4]{0:T(128)S(1)}, s32[4]{0:T(128)}, u32[]{:S(2)}) %copy-start.6) | copy-done | bytes 40
  10.1 0.6 %shard_map.141 = f32[24,128]{1,0:T(8,128)S(1)} custom-call(s32[4]{0:T(128)S(1)} %copy-done.6, s32[1]{0:T(128)S(6)} %copy.22.index_ref, bf16[1,128,128]{2,1,0:T(8,128)(2,1)S(1)} %copy-done.2, bf16[1,128,128]{2,1,0:T(8,128)(2,1)S(1)} %collective-permute-done.rest_1_), custom_call_target="tpu_custom_call" | custom-call | tf_op jit(solution)/shard_map/pallas_call | solution.py:371
  10.6 2.1 %collective-permute-start.1 = (f32[24,128]{1,0:T(8,128)S(1)}, f32[24,128]{1,0:T(8,128)S(1)}, u32[]{:S(2)}, u32[]{:S(2)}) collective-permute-start(f32[24,128]{1,0:T(8,128)S(1)} %shard_map.141), channel_id=1, source_target_pairs={{0,4},{4,0},{8,12},{12,8},{1,5},{5,1},{9,13},{13,9},{2,6},{6,2},{1... | collective-permute-start | bytes 36872 | tf_op jit(solution)/shard_map/ppermute | solution.py:31
  12.7 0.0 collective-permute-done.3.rest_5_
  12.7 0.0 collective-permute-start.4
  12.7 1.7 %collective-permute-start.5 = (bf16[128,640]{1,0:T(8,128)(2,1)S(1)}, bf16[128,640]{1,0:T(8,128)(2,1)S(1)}, u32[]{:S(2)}, u32[]{:S(2)}) collective-permute-start(bf16[128,640]{1,0:T(8,128)(2,1)S(1)} %collective-permute-done.3.rest_5_), channel_id=1, source_target_pairs={{0,16},{16,0},{1,17},{17,1},{2,18},{18,2},{3,19},{19,3},{4,20},{20... | collective-permute-start | bytes 491528 | tf_op jit(solution)/shard_map/ppermute | solution.py:21
  14.5 0.0 collective-permute-done.1
  14.5 3.0 %collective-permute-start.2 = (f32[48,128]{1,0:T(8,128)S(1)}, f32[48,128]{1,0:T(8,128)S(1)}, u32[]{:S(2)}, u32[]{:S(2)}) collective-permute-start(f32[48,128]{1,0:T(8,128)S(1)} %pad_maximum_fusion.1), channel_id=1, source_target_pairs={{0,8},{4,12},{8,0},{12,4},{1,9},{5,13},{9,1},{13,5},{2,10},{6,14},... | collective-permute-start | bytes 73736 | tf_op jit(solution)/shard_map/ppermute | solution.py:31
  17.4 1.8 %collective-permute-done.2 = f32[48,128]{1,0:T(8,128)S(1)} collective-permute-done((f32[48,128]{1,0:T(8,128)S(1)}, f32[48,128]{1,0:T(8,128)S(1)}, u32[]{:S(2)}, u32[]{:S(2)}) %collective-permute-start.2) | collective-permute-done | bytes 24608 | tf_op jit(solution)/shard_map/ppermute | solution.py:31
  19.3 0.0 collective-permute-done.4.refs_3_.rest_6_
  19.3 0.1 collective-permute-done.5.refs_2_.rest_7_
  19.3 0.0 collective-permute-done.7.refs_0_
  19.3 0.0 collective-permute-start.8
  19.4 0.5 %collective-permute-start.6 = (bf16[128,640]{1,0:T(8,128)(2,1)S(1)}, bf16[128,640]{1,0:T(8,128)(2,1)S(1)}, u32[]{:S(2)}, u32[]{:S(2)}) collective-permute-start(bf16[128,640]{1,0:T(8,128)(2,1)S(1)} %collective-permute-done.5.refs_2_.rest_7_), channel_id=1, source_target_pairs={{0,1},{1,0},{2,3},{3,2},{4,5},{5,4},{6,7},{7,6},{8,9},{9,8},{10,11... | collective-permute-start | bytes 491528 | tf_op jit(solution)/shard_map/ppermute | solution.py:21
  19.9 0.9 %copy.18.enc_w_ref = bf16[256,81]{1,0:T(8,128)(2,1)S(1)} copy(bf16[256,81]{0,1:T(8,128)(2,1)} %param.21) | data formatting | bytes 82944 | tf_op args[8]
  20.8 0.0 copy-done.11
  20.8 0.1 copy.19.settings_ref
  20.9 0.0 copy-done.9
  20.9 0.1 copy.16
  21.0 0.0 copy-done.10
  21.0 0.1 copy.17
  21.1 0.0 copy-done.5
  21.1 0.0 copy-done.8
  21.1 0.0 copy-done.7
  21.1 0.0 copy-done.3
  21.1 1.4 %shard_map.142 = (bf16[2,128,128]{2,1,0:T(8,128)(2,1)S(1)}, f32[1,256,512]{2,1,0:T(8,128)S(1)}, f32[1,256,512]{2,1,0:T(8,128)S(1)}, bf16[256,96]{1,0:T(8,128)(2,...) custom-call(s32[4]{0:T(128)S(1)} %copy-done.7, ...), custom_call_target="tpu_custom_call" | custom-call | tf_op jit(solution)/shard_map/pallas_call | solution.py:382
  22.5 0.0 collective-permute-done.6.rest_8_
  22.6 0.0 collective-permute-done.8.rest_10_
  22.6 0.0 copy-done
  22.6 0.0 copy-done.1
  22.6 0.0 copy-done.4
  22.6 8.3 %shard_map.144 = (bf16[1,77,128]{2,1,0:T(8,128)(2,1)}, f32[77,1,128]{2,1,0:T(1,128)}) custom-call(s32[4]{0:T(128)S(1)} %copy-done.7, bf16[2,128,128]{2,1,0:T(8,128)(2,1)S(1)} %get-tuple-element.16.field_ref, f32[1,256,512]{2,1,0:T(8,128)S(1)} %get-tuple-element.17.scale_ref, f32[1,256,512]{2,1,0:T(8,128)S(1)} %get-tuple-element.18.shift_ref, ...), custom_call_target="tpu_custom_call" | custom-call | tf_op jit(solution)/shard_map/pallas_call | solution.py:418
  (6 shorter events, 0.0 us)
Async XLA Ops:
  0.6 20.1 %copy-start.11 = (f32[64,16]{0,1:T(8,128)S(1)}, f32[64,16]{0,1:T(8,128)}, u32[]{:S(2)}) copy-start(f32[64,16]{0,1:T(8,128)} %param.18) | copy-start | bytes 12292
  0.6 20.2 %copy-start.9 = (f32[16,256]{1,0:T(8,128)S(1)}, f32[16,256]{1,0:T(8,128)}, u32[]{:S(2)}) copy-start(f32[16,256]{1,0:T(8,128)} %param.19) | copy-start | bytes 49156
  0.7 20.4 %copy-start.5 = (bf16[77,256]{1,0:T(8,128)(2,1)S(1)}, bf16[77,256]{1,0:T(8,128)(2,1)}, u32[]{:S(2)}) copy-start(bf16[77,256]{1,0:T(8,128)(2,1)} %dec_w_ref.1) | copy-start | bytes 118276
  0.7 20.4 %copy-start.8 = (s32[1,2]{1,0:T(1,128)S(1)}, s32[1,2]{1,0:T(1,128)}, u32[]{:S(2)}) copy-start(s32[1,2]{1,0:T(1,128)} %param.15) | copy-start | bytes 28
  1.3 19.8 %copy-start.7 = (s32[4]{0:T(128)S(1)}, s32[4]{0:T(128)}, u32[]{:S(2)}) copy-start(s32[4]{0:T(128)} %pad_add_fusion.place_ref.scalar_ref) | copy-start | bytes 52
  1.3 21.2 %copy-start = (bf16[1,256,2304]{2,1,0:T(8,128)(2,1)S(1)}, bf16[1,256,2304]{2,1,0:T(8,128)(2,1)}, u32[]{:S(2)}) copy-start(bf16[1,256,2304]{2,1,0:T(8,128)(2,1)} %param.22) | copy-start | bytes 3538948
  1.3 21.2 %copy-start.1 = (bf16[1,256,256]{2,1,0:T(8,128)(2,1)S(1)}, bf16[1,256,256]{2,1,0:T(8,128)(2,1)}, u32[]{:S(2)}) copy-start(bf16[1,256,256]{2,1,0:T(8,128)(2,1)} %param.23) | copy-start | bytes 393220
  4.1 8.6 %collective-permute-start.3 = (bf16[128,640]{1,0:T(8,128)(2,1)}, bf16[128,640]{1,0:T(8,128)(2,1)S(1)}, u32[]{:S(2)}, u32[]{:S(2)}) collective-permute-start(bf16[128,640]{1,0:T(8,128)(2,1)} %get-tuple-element.24), channel_id=1, source_target_pairs={{0,2},{2,0},{1,3},{3,1},{4,6},{6,4},{5,7},{7,5},{8,10},{10,8},{9,1... | collective-permute-start | bytes 491528 | tf_op jit(solution)/shard_map/ppermute | solution.py:21
  7.1 12.2 %collective-permute-start.7 = (bf16[128,1408]{1,0:T(8,128)(2,1)}, bf16[128,1408]{1,0:T(8,128)(2,1)S(1)}, u32[]{:S(2)}, u32[]{:S(2)}) collective-permute-start(bf16[128,1408]{1,0:T(8,128)(2,1)} %get-tuple-element.25), channel_id=1, source_target_pairs={{0,2},{2,0},{1,3},{3,1},{4,6},{6,4},{5,7},{7,5},{8,10},{10,8},{9,1... | collective-permute-start | bytes 1081352 | tf_op jit(solution)/shard_map/ppermute | solution.py:21
  7.2 1.4 %collective-permute-start = (bf16[1,128,128]{2,1,0:T(8,128)(2,1)}, bf16[1,128,128]{2,1,0:T(8,128)(2,1)S(1)}, u32[]{:S(2)}, u32[]{:S(2)}) collective-permute-start(bf16[1,128,128]{2,1,0:T(8,128)(2,1)} %get-tuple-element.15.rest_0_), channel_id=1, source_target_pairs={{0,1},{1,0},{2,3},{3,2},{4,5},{5,4},{6,7},{7,6},{8,9},{9,8},{10,11... | collective-permute-start | bytes 98312 | tf_op jit(solution)/shard_map/ppermute | solution.py:21
  8.6 0.8 %copy-start.2 = (bf16[1,128,128]{2,1,0:T(8,128)(2,1)S(1)}, bf16[1,128,128]{2,1,0:T(8,128)(2,1)}, u32[]{:S(2)}) copy-start(bf16[1,128,128]{2,1,0:T(8,128)(2,1)} %get-tuple-element.15.rest_0_) | copy-start | bytes 98308
  9.4 0.7 %copy-start.6 = (s32[4]{0:T(128)S(1)}, s32[4]{0:T(128)}, u32[]{:S(2)}) copy-start(s32[4]{0:T(128)} %pad_add_fusion.place_ref.scalar_ref) | copy-start | bytes 52
  10.1 10.9 %copy-start.10 = (f32[16,256]{1,0:T(8,128)S(1)}, f32[16,256]{1,0:T(8,128)}, u32[]{:S(2)}) copy-start(f32[16,256]{1,0:T(8,128)} %param.20) | copy-start | bytes 49156
  10.1 11.1 %copy-start.3 = (bf16[1,128,128]{2,1,0:T(8,128)(2,1)S(1)}, bf16[1,128,128]{2,1,0:T(8,128)(2,1)}, u32[]{:S(2)}) copy-start(bf16[1,128,128]{2,1,0:T(8,128)(2,1)} %get-tuple-element.15.rest_0_) | copy-start | bytes 98308
  10.1 12.5 %copy-start.4 = (bf16[256,128]{1,0:T(8,128)(2,1)S(1)}, bf16[256,128]{1,0:T(8,128)(2,1)}, u32[]{:S(2)}) copy-start(bf16[256,128]{1,0:T(8,128)(2,1)} %get-tuple-element.23.rest_4_) | copy-start | bytes 196612
  10.6 3.8 %collective-permute-start.1 = (f32[24,128]{1,0:T(8,128)S(1)}, f32[24,128]{1,0:T(8,128)S(1)}, u32[]{:S(2)}, u32[]{:S(2)}) collective-permute-start(f32[24,128]{1,0:T(8,128)S(1)} %shard_map.141), channel_id=1, source_target_pairs={{0,4},{4,0},{8,12},{12,8},{1,5},{5,1},{9,13},{13,9},{2,6},{6,2},{1... | collective-permute-start | bytes 36872 | tf_op jit(solution)/shard_map/ppermute | solution.py:31
  12.7 6.5 %collective-permute-start.4 = (bf16[128,640]{1,0:T(8,128)(2,1)S(1)}, bf16[128,640]{1,0:T(8,128)(2,1)S(1)}, u32[]{:S(2)}, u32[]{:S(2)}) collective-permute-start(bf16[128,640]{1,0:T(8,128)(2,1)S(1)} %collective-permute-done.3.rest_5_), channel_id=1, source_target_pairs={{0,1},{1,0},{2,3},{3,2},{4,5},{5,4},{6,7},{7,6},{8,9},{9,8},{10,11... | collective-permute-start | bytes 491528 | tf_op jit(solution)/shard_map/ppermute | solution.py:21
  12.7 6.6 %collective-permute-start.5 = (bf16[128,640]{1,0:T(8,128)(2,1)S(1)}, bf16[128,640]{1,0:T(8,128)(2,1)S(1)}, u32[]{:S(2)}, u32[]{:S(2)}) collective-permute-start(bf16[128,640]{1,0:T(8,128)(2,1)S(1)} %collective-permute-done.3.rest_5_), channel_id=1, source_target_pairs={{0,16},{16,0},{1,17},{17,1},{2,18},{18,2},{3,19},{19,3},{4,20},{20... | collective-permute-start | bytes 491528 | tf_op jit(solution)/shard_map/ppermute | solution.py:21
  14.5 4.8 %collective-permute-start.2 = (f32[48,128]{1,0:T(8,128)S(1)}, f32[48,128]{1,0:T(8,128)S(1)}, u32[]{:S(2)}, u32[]{:S(2)}) collective-permute-start(f32[48,128]{1,0:T(8,128)S(1)} %pad_maximum_fusion.1), channel_id=1, source_target_pairs={{0,8},{4,12},{8,0},{12,4},{1,9},{5,13},{9,1},{13,5},{2,10},{6,14},... | collective-permute-start | bytes 73736 | tf_op jit(solution)/shard_map/ppermute | solution.py:31
  19.3 3.2 %collective-permute-start.8 = (bf16[128,1408]{1,0:T(8,128)(2,1)S(1)}, bf16[128,1408]{1,0:T(8,128)(2,1)S(1)}, u32[]{:S(2)}, u32[]{:S(2)}) collective-permute-start(bf16[128,1408]{1,0:T(8,128)(2,1)S(1)} %shard_map.143.rest_9_), channel_id=1, source_target_pairs={{0,1},{1,0},{2,3},{3,2},{4,5},{5,4},{6,7},{7,6},{8,9},{9,8},{10,11... | collective-permute-start | bytes 1081352 | tf_op jit(solution)/shard_map/ppermute | solution.py:21
  19.4 3.2 %collective-permute-start.6 = (bf16[128,640]{1,0:T(8,128)(2,1)S(1)}, bf16[128,640]{1,0:T(8,128)(2,1)S(1)}, u32[]{:S(2)}, u32[]{:S(2)}) collective-permute-start(bf16[128,640]{1,0:T(8,128)(2,1)S(1)} %collective-permute-done.5.refs_2_.rest_7_), channel_id=1, source_target_pairs={{0,1},{1,0},{2,3},{3,2},{4,5},{5,4},{6,7},{7,6},{8,9},{9,8},{10,11... | collective-permute-start | bytes 491528 | tf_op jit(solution)/shard_map/ppermute | solution.py:21

commit v8 on v7

--- a/solution.py
+++ b/solution.py
@@ -41,42 +41,19 @@
     return chosen
 
 
-def pack_kernel(dims, place_ref, gain_ref, conv_ref, point_ref, slots_ref, state_ref, land_ref, *rest):
+def pack_kernel(dims, gain_ref, slots_ref, state_ref, land_ref, earlier_ref, spread_ref, field_ref):
     steps, local, forced, vp, fp = dims
-    relayed_ref, direct_ref, spread_ref, field_ref, slots, gain, state, land, sems = rest
-    part, share = relayed_ref.shape
-    wide, chans = conv_ref.shape[1], point_ref.shape[1]
-    left = direct_ref.shape[1] - chans - LANES
-    rows = pl.ds(pl.multiple_of(place_ref[1] * part, part), part)
-    mine = pl.ds(pl.multiple_of(place_ref[3] * share, LANES), share)
-    small = [
-        pltpu.make_async_copy(gain_ref, gain, sems.at[0]),
-        pltpu.make_async_copy(slots_ref, slots, sems.at[1]),
-        pltpu.make_async_copy(state_ref, state, sems.at[2]),
-        pltpu.make_async_copy(land_ref, land, sems.at[3]),
-    ]
-    large = [
-        pltpu.make_async_copy(conv_ref.at[rows, mine], relayed_ref, sems.at[4]),
-        pltpu.make_async_copy(conv_ref.at[rows, pl.ds(wide - left, left)], direct_ref.at[:, pl.ds(0, left)], sems.at[5]),
-        pltpu.make_async_copy(point_ref.at[rows, :], direct_ref.at[:, pl.ds(left, chans)], sems.at[6]),
-    ]
-    for copy in small + large:
-        copy.start()
-    for copy in small:
-        copy.wait()
+    chans = gain_ref.shape[1]
     eye = lax.broadcasted_iota(jnp.int32, (chans, chans), 0) == lax.broadcasted_iota(jnp.int32, (chans, chans), 1)
-    column = jnp.sum(jnp.where(eye, gain[...].astype(jnp.float32), 0.0), axis=1, keepdims=True)
+    column = jnp.sum(jnp.where(eye, gain_ref[...].astype(jnp.float32), 0.0), axis=1, keepdims=True)
     spread_ref[...] = jnp.broadcast_to(column, (chans, LANES)).astype(jnp.bfloat16)
-    direct_ref[:, left + chans :] = spread_ref[rows, :]
     field_ref[...] = jnp.zeros(field_ref.shape, field_ref.dtype)
     for i in range(local):
-        field_ref[i, 0 : state.shape[1]] = state[i]
+        field_ref[i, 0 : state_ref.shape[1]] = state_ref[i]
         for t in range(steps):
             first = (t * local + i) * forced
-            field_ref[i, vp + fp * t : vp + fp * t + forced] = slots[first : first + forced]
-        field_ref[i, vp + fp * steps : vp + fp * steps + 1] = land[i : i + 1].astype(jnp.bfloat16)
-    for copy in large:
-        copy.wait()
+            field_ref[i, vp + fp * t : vp + fp * t + forced] = slots_ref[first : first + forced]
+        field_ref[i, vp + fp * steps : vp + fp * steps + 1] = land_ref[i : i + 1].astype(jnp.bfloat16)
 
 
 def group_kernel(dims, place_ref, index_ref, *rest):
@@ -108,15 +85,15 @@
     steps, layers, bands, local, members, lon, chans, vp, fp, turns = dims
     fields, rest = rest[:bands], rest[bands:]
     everyone, rest = rest[0], rest[1:]
-    forced = enc_w_ref.shape[1] - dec_w_ref.shape[0]
+    forced = enc_w_ref.shape[0] - dec_w_ref.shape[0]
     used = bands * local * steps * forced
     group = [everyone.at[k * (used + 8) : (k + 1) * (used + 8)] for k in range(members * turns)]
-    field_ref, scale_ref, shift_ref, enc_ref, dec_ref, hidden_ref, taps_ref = rest
+    field_ref, scale_ref, shift_ref, enc_ref, dec_ref, hidden_ref, taps_ref, turned = rest
     varied = dec_w_ref.shape[0]
-    forced = enc_w_ref.shape[1] - varied
-    enc_ref[...] = jnp.zeros(enc_ref.shape, enc_ref.dtype)
-    enc_ref[:, 0:varied] = enc_w_ref[:, 0:varied]
-    enc_ref[:, vp : vp + forced] = enc_w_ref[:, varied : varied + forced]
+    turned[...] = jnp.zeros(turned.shape, turned.dtype)
+    turned[0:varied] = enc_w_ref[0:varied].astype(jnp.float32)
+    turned[vp : vp + forced] = enc_w_ref[varied : varied + forced].astype(jnp.float32)
+    enc_ref[...] = turned[...].T.astype(jnp.bfloat16)
     dec_ref[...] = jnp.zeros(dec_ref.shape, dec_ref.dtype)
     dec_ref[0:varied, :] = dec_w_ref[...]
     band = scalar_ref[1]
@@ -346,26 +323,20 @@
     places = [here, band, lax.axis_index("members"), lax.axis_index("groups")]
     scalars = jnp.stack(places).astype(jnp.int32)
     slots = forcing_slots[0, 0].reshape(-1, lon)
-    relayed, direct, spread, field = pl.pallas_call(
+    relayed = lax.dynamic_slice(conv_weight[0], (band * part, places[3] * share), (part, share))
+    spread, field = pl.pallas_call(
         functools.partial(pack_kernel, (steps, local, forced, vp, fp)),
         out_shape=(
-            jax.ShapeDtypeStruct((part, share), jnp.bfloat16),
-            jax.ShapeDtypeStruct((part, 10 * chans + LANES - groups * share), jnp.bfloat16),
             jax.ShapeDtypeStruct((chans, LANES), jnp.bfloat16),
             jax.ShapeDtypeStruct((local, vp + fp * steps + BF16_ROWS, lon), jnp.bfloat16),
         ),
-        in_specs=[smem] + [whole] * 6,
-        out_specs=(vmem,) * 4,
-        scratch_shapes=[
-            pltpu.VMEM(slots.shape, jnp.bfloat16),
-            pltpu.VMEM(norm_gain.shape, jnp.bfloat16),
-            pltpu.VMEM(init_state.shape[1:], jnp.bfloat16),
-            pltpu.VMEM(land_mask.shape, jnp.int32),
-            pltpu.SemaphoreType.DMA((7,)),
-        ],
-        compiler_params=pltpu.CompilerParams(vmem_limit_bytes=60 * MIB),
+        in_specs=[vmem] * 4 + [whole],
+        out_specs=(vmem,) * 2,
+        compiler_params=small,
         cost_estimate=free,
-    )(scalars, norm_gain, conv_weight[0], point_weight[0], slots, init_state[0], land_mask)
+    )(norm_gain, slots, init_state[0], land_mask, relayed)
+    direct = jnp.concatenate([conv_weight[0][:, groups * share :], point_weight[0], spread], axis=1)
+    direct = lax.dynamic_slice_in_dim(direct, band * part, part, 0)
     relayed, direct = (all_along(piece, "segment")[1:] for piece in (relayed, direct))
     fields = all_along(field, "rows")
     group = pl.pallas_call(
@@ -392,9 +363,10 @@
         ),
         in_specs=[smem, smem] + [vmem] * (6 + bands),
         out_specs=(vmem,) * 7,
+        scratch_shapes=[pltpu.VMEM((vp + fp, chans), jnp.float32)],
         compiler_params=small,
         cost_estimate=free,
-    )(scalars, atmos_owner[0], encode_weight, decode_weight, settings, scale_weight.T, shift_weight.T, *fields, group)
+    )(scalars, atmos_owner[0], encode_weight.T, decode_weight, settings, scale_weight.T, shift_weight.T, *fields, group)
 
     blocks = [conv_weight[0], point_weight[0], spread]
     for k in range(layers - 1):

time: 31.2 us -> 30.5 us (0.978)
  Pallas kernels: 13 us -> 10.4 us
  local copies, waits for them, and re-layouts: 2.65 us -> 5.12 us
  other arithmetic: 0.66 us -> 0.12 us
    pallas_call x1, Pallas kernels: 2.78 us -> 0.11 us  [per_device(): pl.pallas_call(functools.partial(pack_kernel, (steps, local, forced, vp,...]
    slice x0 -> x1, local copies, waits for them, and re-layouts: none -> 1.08 us  [per_device(): conv_weight[0][:, groups * share:]]
    dynamic_slice x0 -> x1, local copies, waits for them, and re-layouts: none -> 0.97 us  [per_device(): lax.dynamic_slice(conv_weight[0], (band * part, places[3] * share), (part...]
    another operation x1, other arithmetic: 0.65 us -> 0.08 us  [per_device(): scalars = jnp.stack(places).astype(jnp.int32)]
    unnamed x28 -> x27, local copies, waits for them, and re-layouts: 2.65 us -> 3.07 us
  transfers between devices with their start and end apart: 9 -> 9, of which waited for: 3 -> 4; matrix products, arithmetic and copies ran while one was open for 4% -> 5% of each run, Pallas kernels for 6% -> 7%
where the time goes in v8:
time: 30.5 us; the launch traced here: 30.2 us
  Pallas kernels  10.4 us (34%)
  starting transfers between devices  10.3 us (34%)
  local copies, waits for them, and re-layouts  5.12 us (17%)
  waiting for transfers between devices  2.79 us (9%)
  between operations  1.58 us (5%)
    pallas_call x1, Pallas kernels, per_device(): pl.pallas_call(functools.partial(window_kernel, dims + (groups,)), out_sh...  8.28 us
    ppermute x7, starting transfers between devices, passed_along(): lax.ppermute(block, axis, [(i, (i + distance) % size) for i in range(size)])  5.19 us
    ppermute x2, starting transfers between devices, by_doubling(): partner = lax.ppermute(block, axis, [(i, i ^ reach) for i in range(size)])  5.07 us
    unnamed x27, local copies, waits for them, and re-layouts  3.07 us
    ppermute x2, waiting for transfers between devices, by_doubling(): partner = lax.ppermute(block, axis, [(i, i ^ reach) for i in range(size)])  1.97 us
    pallas_call x1, Pallas kernels, per_device(): pl.pallas_call(functools.partial(first_kernel, dims), out_shape=(jax.Shap...  1.43 us
    slice x1, local copies, waits for them, and re-layouts, per_device(): conv_weight[0][:, groups * share:]  1.08 us
    dynamic_slice x1, local copies, waits for them, and re-layouts, per_device(): lax.dynamic_slice(conv_weight[0], (band * part, places[3] * share), (part...  0.97 us
  transfers between devices with their start and end apart: 9, of which 4 were waited for; matrix products, arithmetic and copies ran while one was open for 5% of the time, Pallas kernels for 7%

profile of v8, /device:TPU:0, one launch (start us, length us, event | category | flops | bytes accessed | tf_op | source)
XLA Modules:
  0.0 30.2 jit_solution(10391140714066050963)
XLA Ops:
  0.6 0.0 copy-start.1
  0.7 1.0 %dynamic-slice_bitcast_fusion.earlier_ref = bf16[128,640]{1,0:T(8,128)(2,1)S(1)} fusion(bf16[1,256,2304]{2,1,0:T(8,128)(2,1)} %param.22, s32[]{:T(128)S(6)} %select_n.7, s32[]{:T(128)S(6)} %select_n.8), kind=kLoop, calls=%fused_computation.5 | loop fusion | bytes 327688 | tf_op jit(solution)/shard_map/dynamic_slice | solution.py:326
  1.6 3.0 %collective-permute-start.3 = (bf16[128,640]{1,0:T(8,128)(2,1)S(1)}, bf16[128,640]{1,0:T(8,128)(2,1)S(1)}, u32[]{:S(2)}, u32[]{:S(2)}) collective-permute-start(bf16[128,640]{1,0:T(8,128)(2,1)S(1)} %dynamic-slice_bitcast_fusion.earlier_ref), channel_id=1, source_target_pairs={{0,2},{2,0},{1,3},{3,1},{4,6},{6,4},{5,7},{7,5},{8,10},{10,8},{9,1... | collective-permute-start | bytes 491528 | tf_op jit(solution)/shard_map/ppermute | solution.py:21
  4.6 0.7 %copy-done.4 = bf16[1,1,77,128]{3,2,1,0:T(8,128)(2,1)S(1)} copy-done((bf16[1,1,77,128]{3,2,1,0:T(8,128)(2,1)S(1)}, bf16[1,1,77,128]{3,2,1,0:T(8,128)(2,1)}, u32[]{:S(2)}) %copy-start.4) | copy-done | bytes 19736
  5.4 0.7 %copy-done.5 = bf16[1,1,2,1,4,128]{5,4,3,2,1,0:T(4,128)(2,1)S(1)} copy-done((bf16[1,1,2,1,4,128]{5,4,3,2,1,0:T(4,128)(2,1)S(1)}, bf16[1,1,2,1,4,128]{5,4,3,2,1,0:T(4,128)(2,1)}, u32[]{:S(2)}) %copy-start.5) | copy-done | bytes 2072
  6.0 0.7 %copy-done.6 = bf16[1,256]{1,0:T(2,128)(2,1)S(1)} copy-done((bf16[1,256]{1,0:T(2,128)(2,1)S(1)}, bf16[1,256]{1,0:T(2,128)(2,1)}, u32[]{:S(2)}) %copy-start.6) | copy-done | bytes 536
  6.7 0.7 %copy-done.7 = s32[1,128]{1,0:T(1,128)S(1)} copy-done((s32[1,128]{1,0:T(1,128)S(1)}, s32[1,128]{1,0:T(1,128)}, u32[]{:S(2)}) %copy-start.7) | copy-done | bytes 536
  7.4 0.1 shard_map.140
  7.5 0.1 collective-permute-start
  7.6 1.1 %slice.4 = bf16[256,1024]{1,0:T(8,128)(2,1)S(1)} slice(bf16[256,2304]{1,0:T(8,128)(2,1)} %bitcast.18), slice={[0:256], [1280:2304]} | slice | bytes 1048576 | tf_op jit(solution)/shard_map/slice | solution.py:338
  8.7 0.0 copy-done.1
  8.7 0.0 copy-start.11
  8.7 0.0 copy-start.9
  8.7 0.0 copy-start.10
  8.7 0.0 copy-start.2
  8.7 0.0 copy-start.3
  8.7 0.0 copy-start.8
  8.8 0.0 copy-start
  8.8 0.1 collective-permute-start.7
  8.9 0.1 pad_add_fusion.place_ref.scalar_ref
  9.7 0.0 collective-permute-done.rest_1_
  9.7 0.6 %shard_map.141 = f32[24,128]{1,0:T(8,128)S(1)} custom-call(s32[4]{0:T(128)S(1)} %pad_add_fusion.place_ref.scalar_ref, s32[1]{0:T(128)S(6)} %copy.21.index_ref, bf16[1,128,128]{2,1,0:T(8,128)(2,1)S(1)} %get-tuple-element.13.rest_0_, bf16[1,128,128]{2,1,0:T(8,128)(2,1)S(1)} %collective-permute-done.rest_1_), custom_call_target="tpu_custom_call" | custom-call | tf_op jit(solution)/shard_map/pallas_call | solution.py:342
  10.3 2.1 %collective-permute-start.1 = (f32[24,128]{1,0:T(8,128)S(1)}, f32[24,128]{1,0:T(8,128)S(1)}, u32[]{:S(2)}, u32[]{:S(2)}) collective-permute-start(f32[24,128]{1,0:T(8,128)S(1)} %shard_map.141), channel_id=1, source_target_pairs={{0,4},{4,0},{8,12},{12,8},{1,5},{5,1},{9,13},{13,9},{2,6},{6,2},{1... | collective-permute-start | bytes 36872 | tf_op jit(solution)/shard_map/ppermute | solution.py:31
  12.3 0.0 collective-permute-done.3.rest_5_
  12.3 0.0 collective-permute-start.4
  12.3 1.5 %collective-permute-start.5 = (bf16[128,640]{1,0:T(8,128)(2,1)S(1)}, bf16[128,640]{1,0:T(8,128)(2,1)S(1)}, u32[]{:S(2)}, u32[]{:S(2)}) collective-permute-start(bf16[128,640]{1,0:T(8,128)(2,1)S(1)} %collective-permute-done.3.rest_5_), channel_id=1, source_target_pairs={{0,16},{16,0},{1,17},{17,1},{2,18},{18,2},{3,19},{19,3},{4,20},{20... | collective-permute-start | bytes 491528 | tf_op jit(solution)/shard_map/ppermute | solution.py:21
  13.9 0.2 collective-permute-done.1
  14.0 3.0 %collective-permute-start.2 = (f32[48,128]{1,0:T(8,128)S(1)}, f32[48,128]{1,0:T(8,128)S(1)}, u32[]{:S(2)}, u32[]{:S(2)}) collective-permute-start(f32[48,128]{1,0:T(8,128)S(1)} %pad_maximum_fusion.1), channel_id=1, source_target_pairs={{0,8},{4,12},{8,0},{12,4},{1,9},{5,13},{9,1},{13,5},{2,10},{6,14},... | collective-permute-start | bytes 73736 | tf_op jit(solution)/shard_map/ppermute | solution.py:31
  17.0 1.8 %collective-permute-done.2 = f32[48,128]{1,0:T(8,128)S(1)} collective-permute-done((f32[48,128]{1,0:T(8,128)S(1)}, f32[48,128]{1,0:T(8,128)S(1)}, u32[]{:S(2)}, u32[]{:S(2)}) %collective-permute-start.2) | collective-permute-done | bytes 24608 | tf_op jit(solution)/shard_map/ppermute | solution.py:31
  18.9 0.0 collective-permute-done.4.refs_3_.rest_6_
  18.9 0.1 collective-permute-done.5.refs_2_.rest_7_
  19.0 0.7 %collective-permute-done.7.refs_0_ = bf16[128,1408]{1,0:T(8,128)(2,1)S(1)} collective-permute-done((bf16[128,1408]{1,0:T(8,128)(2,1)S(1)}, bf16[128,1408]{1,0:T(8,128)(2,1)S(1)}, u32[]{:S(2)}, u32[]{:S(2)}) %collective-permute-start.7) | collective-permute-done | bytes 360480 | tf_op jit(solution)/shard_map/ppermute | solution.py:21
  19.7 0.0 collective-permute-start.8
  19.7 0.5 %collective-permute-start.6 = (bf16[128,640]{1,0:T(8,128)(2,1)S(1)}, bf16[128,640]{1,0:T(8,128)(2,1)S(1)}, u32[]{:S(2)}, u32[]{:S(2)}) collective-permute-start(bf16[128,640]{1,0:T(8,128)(2,1)S(1)} %collective-permute-done.5.refs_2_.rest_7_), channel_id=1, source_target_pairs={{0,1},{1,0},{2,3},{3,2},{4,5},{5,4},{6,7},{7,6},{8,9},{9,8},{10,11... | collective-permute-start | bytes 491528 | tf_op jit(solution)/shard_map/ppermute | solution.py:21
  20.2 0.0 copy-done.11
  20.2 0.1 copy.18.settings_ref
  20.3 0.0 copy-done.9
  20.3 0.1 copy.16
  20.4 0.0 copy-done.10
  20.4 0.1 copy.17
  20.5 0.0 copy-done.2
  20.5 0.0 copy-done.3
  20.5 0.0 copy-done.8
  20.5 1.4 %shard_map.142 = (bf16[2,128,128]{2,1,0:T(8,128)(2,1)S(1)}, f32[1,256,512]{2,1,0:T(8,128)S(1)}, f32[1,256,512]{2,1,0:T(8,128)S(1)}, bf16[256,96]{1,0:T(8,128)(2,...) custom-call(s32[4]{0:T(128)S(1)} %pad_add_fusion.place_ref.scalar_ref, ...), custom_call_target="tpu_custom_call" | custom-call | tf_op jit(solution)/shard_map/pallas_call | solution.py:353
  21.9 0.0 collective-permute-done.6.rest_8_
  21.9 0.0 collective-permute-done.8.rest_10_
  22.0 0.0 copy-done
  22.0 8.3 %shard_map.144 = (bf16[1,77,128]{2,1,0:T(8,128)(2,1)}, f32[77,1,128]{2,1,0:T(1,128)}) custom-call(s32[4]{0:T(128)S(1)} %pad_add_fusion.place_ref.scalar_ref, bf16[2,128,128]{2,1,0:T(8,128)(2,1)S(1)} %get-tuple-element.14.field_ref, f32[1,256,512]{2,1,0:T(8,128)S(1)} %get-tuple-element.15.scale_ref, f32[1,256,512]{2,1,0:T(8,128)S(1)} %get-tuple-element.16.shift_ref, ...), custom_call_target="tpu_custom_call" | custom-call | tf_op jit(solution)/shard_map/pallas_call | solution.py:390
  (8 shorter events, 0.1 us)
Async XLA Ops:
  0.6 8.0 %copy-start.1 = (bf16[1,256,256]{2,1,0:T(8,128)(2,1)S(1)}, bf16[1,256,256]{2,1,0:T(8,128)(2,1)}, u32[]{:S(2)}) copy-start(bf16[1,256,256]{2,1,0:T(8,128)(2,1)} %param.23) | copy-start | bytes 393220
  1.6 10.7 %collective-permute-start.3 = (bf16[128,640]{1,0:T(8,128)(2,1)S(1)}, bf16[128,640]{1,0:T(8,128)(2,1)S(1)}, u32[]{:S(2)}, u32[]{:S(2)}) collective-permute-start(bf16[128,640]{1,0:T(8,128)(2,1)S(1)} %dynamic-slice_bitcast_fusion.earlier_ref), channel_id=1, source_target_pairs={{0,2},{2,0},{1,3},{3,1},{4,6},{6,4},{5,7},{7,5},{8,10},{10,8},{9,1... | collective-permute-start | bytes 491528 | tf_op jit(solution)/shard_map/ppermute | solution.py:21
  4.6 0.7 %copy-start.4 = (bf16[1,1,77,128]{3,2,1,0:T(8,128)(2,1)S(1)}, bf16[1,1,77,128]{3,2,1,0:T(8,128)(2,1)}, u32[]{:S(2)}) copy-start(bf16[1,1,77,128]{3,2,1,0:T(8,128)(2,1)} %param.13) | copy-start | bytes 59140
  5.4 0.7 %copy-start.5 = (bf16[1,1,2,1,4,128]{5,4,3,2,1,0:T(4,128)(2,1)S(1)}, bf16[1,1,2,1,4,128]{5,4,3,2,1,0:T(4,128)(2,1)}, u32[]{:S(2)}) copy-start(bf16[1,1,2,1,4,128]{5,4,3,2,1,0:T(4,128)(2,1)} %param.14) | copy-start | bytes 6148
  6.0 0.7 %copy-start.6 = (bf16[1,256]{1,0:T(2,128)(2,1)S(1)}, bf16[1,256]{1,0:T(2,128)(2,1)}, u32[]{:S(2)}) copy-start(bf16[1,256]{1,0:T(2,128)(2,1)} %gain_ref.1) | copy-start | bytes 1540
  6.7 0.7 %copy-start.7 = (s32[1,128]{1,0:T(1,128)S(1)}, s32[1,128]{1,0:T(1,128)}, u32[]{:S(2)}) copy-start(s32[1,128]{1,0:T(1,128)} %land_ref.1) | copy-start | bytes 1540
  7.5 2.2 %collective-permute-start = (bf16[1,128,128]{2,1,0:T(8,128)(2,1)S(1)}, bf16[1,128,128]{2,1,0:T(8,128)(2,1)S(1)}, u32[]{:S(2)}, u32[]{:S(2)}) collective-permute-start(bf16[1,128,128]{2,1,0:T(8,128)(2,1)S(1)} %get-tuple-element.13.rest_0_), channel_id=1, source_target_pairs={{0,1},{1,0},{2,3},{3,2},{4,5},{5,4},{6,7},{7,6},{8,9},{9,8},{10,11... | collective-permute-start | bytes 98312 | tf_op jit(solution)/shard_map/ppermute | solution.py:21
  8.7 11.5 %copy-start.11 = (f32[64,16]{0,1:T(8,128)S(1)}, f32[64,16]{0,1:T(8,128)}, u32[]{:S(2)}) copy-start(f32[64,16]{0,1:T(8,128)} %param.18) | copy-start | bytes 12292
  8.7 11.6 %copy-start.9 = (f32[16,256]{1,0:T(8,128)S(1)}, f32[16,256]{1,0:T(8,128)}, u32[]{:S(2)}) copy-start(f32[16,256]{1,0:T(8,128)} %param.19) | copy-start | bytes 49156
  8.7 11.7 %copy-start.10 = (f32[16,256]{1,0:T(8,128)S(1)}, f32[16,256]{1,0:T(8,128)}, u32[]{:S(2)}) copy-start(f32[16,256]{1,0:T(8,128)} %param.20) | copy-start | bytes 49156
  8.7 11.8 %copy-start.2 = (bf16[256,81]{0,1:T(8,128)(2,1)S(1)}, bf16[256,81]{0,1:T(8,128)(2,1)}, u32[]{:S(2)}) copy-start(bf16[256,81]{0,1:T(8,128)(2,1)} %param.21) | copy-start | bytes 124420
  8.7 11.8 %copy-start.3 = (bf16[77,256]{1,0:T(8,128)(2,1)S(1)}, bf16[77,256]{1,0:T(8,128)(2,1)}, u32[]{:S(2)}) copy-start(bf16[77,256]{1,0:T(8,128)(2,1)} %dec_w_ref.1) | copy-start | bytes 118276
  8.7 11.8 %copy-start.8 = (s32[1,2]{1,0:T(1,128)S(1)}, s32[1,2]{1,0:T(1,128)}, u32[]{:S(2)}) copy-start(s32[1,2]{1,0:T(1,128)} %param.15) | copy-start | bytes 28
  8.8 13.2 %copy-start = (bf16[1,256,2304]{2,1,0:T(8,128)(2,1)S(1)}, bf16[1,256,2304]{2,1,0:T(8,128)(2,1)}, u32[]{:S(2)}) copy-start(bf16[1,256,2304]{2,1,0:T(8,128)(2,1)} %param.22) | copy-start | bytes 3538948
  8.8 10.9 %collective-permute-start.7 = (bf16[128,1408]{1,0:T(8,128)(2,1)S(1)}, bf16[128,1408]{1,0:T(8,128)(2,1)S(1)}, u32[]{:S(2)}, u32[]{:S(2)}) collective-permute-start(bf16[128,1408]{1,0:T(8,128)(2,1)S(1)} %fusion.1), channel_id=1, source_target_pairs={{0,2},{2,0},{1,3},{3,1},{4,6},{6,4},{5,7},{7,5},{8,10},{10,8},{9,1... | collective-permute-start | bytes 1081352 | tf_op jit(solution)/shard_map/ppermute | solution.py:21
  10.3 3.8 %collective-permute-start.1 = (f32[24,128]{1,0:T(8,128)S(1)}, f32[24,128]{1,0:T(8,128)S(1)}, u32[]{:S(2)}, u32[]{:S(2)}) collective-permute-start(f32[24,128]{1,0:T(8,128)S(1)} %shard_map.141), channel_id=1, source_target_pairs={{0,4},{4,0},{8,12},{12,8},{1,5},{5,1},{9,13},{13,9},{2,6},{6,2},{1... | collective-permute-start | bytes 36872 | tf_op jit(solution)/shard_map/ppermute | solution.py:31
  12.3 6.5 %collective-permute-start.4 = (bf16[128,640]{1,0:T(8,128)(2,1)S(1)}, bf16[128,640]{1,0:T(8,128)(2,1)S(1)}, u32[]{:S(2)}, u32[]{:S(2)}) collective-permute-start(bf16[128,640]{1,0:T(8,128)(2,1)S(1)} %collective-permute-done.3.rest_5_), channel_id=1, source_target_pairs={{0,1},{1,0},{2,3},{3,2},{4,5},{5,4},{6,7},{7,6},{8,9},{9,8},{10,11... | collective-permute-start | bytes 491528 | tf_op jit(solution)/shard_map/ppermute | solution.py:21
  12.3 6.6 %collective-permute-start.5 = (bf16[128,640]{1,0:T(8,128)(2,1)S(1)}, bf16[128,640]{1,0:T(8,128)(2,1)S(1)}, u32[]{:S(2)}, u32[]{:S(2)}) collective-permute-start(bf16[128,640]{1,0:T(8,128)(2,1)S(1)} %collective-permute-done.3.rest_5_), channel_id=1, source_target_pairs={{0,16},{16,0},{1,17},{17,1},{2,18},{18,2},{3,19},{19,3},{4,20},{20... | collective-permute-start | bytes 491528 | tf_op jit(solution)/shard_map/ppermute | solution.py:21
  14.0 4.8 %collective-permute-start.2 = (f32[48,128]{1,0:T(8,128)S(1)}, f32[48,128]{1,0:T(8,128)S(1)}, u32[]{:S(2)}, u32[]{:S(2)}) collective-permute-start(f32[48,128]{1,0:T(8,128)S(1)} %pad_maximum_fusion.1), channel_id=1, source_target_pairs={{0,8},{4,12},{8,0},{12,4},{1,9},{5,13},{9,1},{13,5},{2,10},{6,14},... | collective-permute-start | bytes 73736 | tf_op jit(solution)/shard_map/ppermute | solution.py:31
  19.7 2.3 %collective-permute-start.8 = (bf16[128,1408]{1,0:T(8,128)(2,1)S(1)}, bf16[128,1408]{1,0:T(8,128)(2,1)S(1)}, u32[]{:S(2)}, u32[]{:S(2)}) collective-permute-start(bf16[128,1408]{1,0:T(8,128)(2,1)S(1)} %shard_map.143.rest_9_), channel_id=1, source_target_pairs={{0,1},{1,0},{2,3},{3,2},{4,5},{5,4},{6,7},{7,6},{8,9},{9,8},{10,11... | collective-permute-start | bytes 1081352 | tf_op jit(solution)/shard_map/ppermute | solution.py:21
  19.7 2.3 %collective-permute-start.6 = (bf16[128,640]{1,0:T(8,128)(2,1)S(1)}, bf16[128,640]{1,0:T(8,128)(2,1)S(1)}, u32[]{:S(2)}, u32[]{:S(2)}) collective-permute-start(bf16[128,640]{1,0:T(8,128)(2,1)S(1)} %collective-permute-done.5.refs_2_.rest_7_), channel_id=1, source_target_pairs={{0,1},{1,0},{2,3},{3,2},{4,5},{5,4},{6,7},{7,6},{8,9},{9,8},{10,11... | collective-permute-start | bytes 491528 | tf_op jit(solution)/shard_map/ppermute | solution.py:21

commit v9 on v8

--- a/solution.py
+++ b/solution.py
@@ -41,12 +41,8 @@
     return chosen
 
 
-def pack_kernel(dims, gain_ref, slots_ref, state_ref, land_ref, earlier_ref, spread_ref, field_ref):
+def pack_kernel(dims, slots_ref, state_ref, land_ref, earlier_ref, field_ref):
     steps, local, forced, vp, fp = dims
-    chans = gain_ref.shape[1]
-    eye = lax.broadcasted_iota(jnp.int32, (chans, chans), 0) == lax.broadcasted_iota(jnp.int32, (chans, chans), 1)
-    column = jnp.sum(jnp.where(eye, gain_ref[...].astype(jnp.float32), 0.0), axis=1, keepdims=True)
-    spread_ref[...] = jnp.broadcast_to(column, (chans, LANES)).astype(jnp.bfloat16)
     field_ref[...] = jnp.zeros(field_ref.shape, field_ref.dtype)
     for i in range(local):
         field_ref[i, 0 : state_ref.shape[1]] = state_ref[i]
@@ -323,20 +319,19 @@
     places = [here, band, lax.axis_index("members"), lax.axis_index("groups")]
     scalars = jnp.stack(places).astype(jnp.int32)
     slots = forcing_slots[0, 0].reshape(-1, lon)
-    relayed = lax.dynamic_slice(conv_weight[0], (band * part, places[3] * share), (part, share))
-    spread, field = pl.pallas_call(
+    conv = conv_weight[0]
+    relayed = lax.dynamic_slice(conv, (band * part, places[3] * share), (part, share))
+    spread = jnp.broadcast_to(norm_gain[0][:, None], (chans, LANES))
+    direct = jnp.concatenate([conv[:, groups * share :], point_weight[0], spread], axis=1)
+    direct = lax.dynamic_slice_in_dim(direct, band * part, part, 0)
+    field = pl.pallas_call(
         functools.partial(pack_kernel, (steps, local, forced, vp, fp)),
-        out_shape=(
-            jax.ShapeDtypeStruct((chans, LANES), jnp.bfloat16),
-            jax.ShapeDtypeStruct((local, vp + fp * steps + BF16_ROWS, lon), jnp.bfloat16),
-        ),
-        in_specs=[vmem] * 4 + [whole],
-        out_specs=(vmem,) * 2,
+        out_shape=jax.ShapeDtypeStruct((local, vp + fp * steps + BF16_ROWS, lon), jnp.bfloat16),
+        in_specs=[vmem] * 3 + [whole],
+        out_specs=vmem,
         compiler_params=small,
         cost_estimate=free,
-    )(norm_gain, slots, init_state[0], land_mask, relayed)
-    direct = jnp.concatenate([conv_weight[0][:, groups * share :], point_weight[0], spread], axis=1)
-    direct = lax.dynamic_slice_in_dim(direct, band * part, part, 0)
+    )(slots, init_state[0], land_mask, direct)
     relayed, direct = (all_along(piece, "segment")[1:] for piece in (relayed, direct))
     fields = all_along(field, "rows")
     group = pl.pallas_call(

time: 30.5 us -> 27.8 us (0.911)
  local copies, waits for them, and re-layouts: 5.12 us -> 2.51 us
    unnamed x27, local copies, waits for them, and re-layouts: 3.07 us -> 0.35 us
    ppermute x7, waiting for transfers between devices: 0.82 us -> 0.38 us  [passed_along(): lax.ppermute(block, axis, [(i, (i + distance) % size) for i in range(size)])]
  transfers between devices with their start and end apart: 9 -> 9, of which waited for: 4 -> 3; matrix products, arithmetic and copies ran while one was open for 5% -> 6% of each run, Pallas kernels for 7% -> 7%
where the time goes in v9:
time: 27.8 us; the launch traced here: 27.6 us
  starting transfers between devices  10.4 us (37%)
  Pallas kernels  10.3 us (37%)
  waiting for transfers between devices  2.6 us (9%)
  local copies, waits for them, and re-layouts  2.51 us (9%)
  between operations  1.66 us (6%)
    pallas_call x1, Pallas kernels, per_device(): pl.pallas_call(functools.partial(window_kernel, dims + (groups,)), out_sh...  8.27 us
    ppermute x7, starting transfers between devices, passed_along(): lax.ppermute(block, axis, [(i, (i + distance) % size) for i in range(size)])  5.25 us
    ppermute x2, starting transfers between devices, by_doubling(): partner = lax.ppermute(block, axis, [(i, i ^ reach) for i in range(size)])  5.17 us
    ppermute x2, waiting for transfers between devices, by_doubling(): partner = lax.ppermute(block, axis, [(i, i ^ reach) for i in range(size)])  2.21 us
    pallas_call x1, Pallas kernels, per_device(): pl.pallas_call(functools.partial(first_kernel, dims), out_shape=(jax.Shap...  1.43 us
    slice x1, local copies, waits for them, and re-layouts, per_device(): conv[:, groups * share:]  1.08 us
    dynamic_slice x1, local copies, waits for them, and re-layouts, per_device(): lax.dynamic_slice(conv, (band * part, places[3] * share), (part, share))  0.98 us
  transfers between devices with their start and end apart: 9, of which 3 were waited for; matrix products, arithmetic and copies ran while one was open for 6% of the time, Pallas kernels for 7%

profile of v9, /device:TPU:0, one launch (start us, length us, event | category | flops | bytes accessed | tf_op | source)
XLA Modules:
  0.0 27.6 jit_solution(1875572398911173004)
XLA Ops:
  0.6 0.0 copy-start.11
  0.6 0.0 copy-start.1
  0.7 1.0 %dynamic-slice_bitcast_fusion = bf16[128,640]{1,0:T(8,128)(2,1)S(1)} fusion(bf16[1,256,2304]{2,1,0:T(8,128)(2,1)} %param.22, s32[]{:T(128)S(6)} %select_n.7, s32[]{:T(128)S(6)} %select_n.8), kind=kLoop, calls=%fused_computation.5 | loop fusion | bytes 327688 | tf_op jit(solution)/shard_map/dynamic_slice | solution.py:323
  1.6 0.0 copy-start.4
  1.7 0.0 copy-start.5
  1.7 0.0 copy-start.6
  1.7 3.0 %collective-permute-start.3 = (bf16[128,640]{1,0:T(8,128)(2,1)S(1)}, bf16[128,640]{1,0:T(8,128)(2,1)S(1)}, u32[]{:S(2)}, u32[]{:S(2)}) collective-permute-start(bf16[128,640]{1,0:T(8,128)(2,1)S(1)} %dynamic-slice_bitcast_fusion), channel_id=1, source_target_pairs={{0,2},{2,0},{1,3},{3,1},{4,6},{6,4},{5,7},{7,5},{8,10},{10,8},{9,1... | collective-permute-start | bytes 491528 | tf_op jit(solution)/shard_map/ppermute | solution.py:21
  4.7 1.1 %slice.4 = bf16[256,1024]{1,0:T(8,128)(2,1)S(1)} slice(bf16[256,2304]{1,0:T(8,128)(2,1)} %bitcast.18), slice={[0:256], [1280:2304]} | slice | bytes 1048576 | tf_op jit(solution)/shard_map/slice | solution.py:325
  5.8 0.0 copy-done.11
  5.8 0.1 broadcast_in_dim.11.rest_4_
  5.9 0.0 copy-done.1
  5.9 0.0 copy-start.8
  6.0 0.0 copy-start.9
  6.0 0.0 copy-start.10
  6.0 0.0 copy-start.2
  6.0 0.0 copy-start.3
  6.0 0.0 copy-start.7
  6.0 0.1 collective-permute-start.7
  6.1 0.0 copy-done.4
  6.1 0.0 copy-done.5
  6.1 0.0 copy-done.6
  6.2 0.0 copy-start
  6.2 0.1 collective-permute-start
  6.2 0.1 pad_add_fusion.place_ref.scalar_ref
  7.1 0.4 %collective-permute-done.rest_1_ = bf16[1,128,128]{2,1,0:T(8,128)(2,1)S(1)} collective-permute-done((bf16[1,128,128]{2,1,0:T(8,128)(2,1)S(1)}, bf16[1,128,128]{2,1,0:T(8,128)(2,1)S(1)}, u32[]{:S(2)}, u32[]{:S(2)}) %collective-permute-start) | collective-permute-done | bytes 32800 | tf_op jit(solution)/shard_map/ppermute | solution.py:21
  7.4 0.6 %shard_map.141 = f32[24,128]{1,0:T(8,128)S(1)} custom-call(s32[4]{0:T(128)S(1)} %pad_add_fusion.place_ref.scalar_ref, s32[1]{0:T(128)S(6)} %copy.21.index_ref, bf16[1,128,128]{2,1,0:T(8,128)(2,1)S(1)} %shard_map.140.rest_0_, bf16[1,128,128]{2,1,0:T(8,128)(2,1)S(1)} %collective-permute-done.rest_1_), custom_call_target="tpu_custom_call" | custom-call | tf_op jit(solution)/shard_map/pallas_call | solution.py:337
  8.0 2.1 %collective-permute-start.1 = (f32[24,128]{1,0:T(8,128)S(1)}, f32[24,128]{1,0:T(8,128)S(1)}, u32[]{:S(2)}, u32[]{:S(2)}) collective-permute-start(f32[24,128]{1,0:T(8,128)S(1)} %shard_map.141), channel_id=1, source_target_pairs={{0,4},{4,0},{8,12},{12,8},{1,5},{5,1},{9,13},{13,9},{2,6},{6,2},{1... | collective-permute-start | bytes 36872 | tf_op jit(solution)/shard_map/ppermute | solution.py:31
  10.1 0.0 collective-permute-done.3.rest_5_
  10.1 1.5 %collective-permute-start.5 = (bf16[128,640]{1,0:T(8,128)(2,1)S(1)}, bf16[128,640]{1,0:T(8,128)(2,1)S(1)}, u32[]{:S(2)}, u32[]{:S(2)}) collective-permute-start(bf16[128,640]{1,0:T(8,128)(2,1)S(1)} %collective-permute-done.3.rest_5_), channel_id=1, source_target_pairs={{0,16},{16,0},{1,17},{17,1},{2,18},{18,2},{3,19},{19,3},{4,20},{20... | collective-permute-start | bytes 491528 | tf_op jit(solution)/shard_map/ppermute | solution.py:21
  11.7 0.0 collective-permute-start.4
  11.7 0.1 collective-permute-done.1
  11.8 3.0 %collective-permute-start.2 = (f32[48,128]{1,0:T(8,128)S(1)}, f32[48,128]{1,0:T(8,128)S(1)}, u32[]{:S(2)}, u32[]{:S(2)}) collective-permute-start(f32[48,128]{1,0:T(8,128)S(1)} %pad_maximum_fusion.1), channel_id=1, source_target_pairs={{0,8},{4,12},{8,0},{12,4},{1,9},{5,13},{9,1},{13,5},{2,10},{6,14},... | collective-permute-start | bytes 73736 | tf_op jit(solution)/shard_map/ppermute | solution.py:31
  14.8 2.1 %collective-permute-done.2 = f32[48,128]{1,0:T(8,128)S(1)} collective-permute-done((f32[48,128]{1,0:T(8,128)S(1)}, f32[48,128]{1,0:T(8,128)S(1)}, u32[]{:S(2)}, u32[]{:S(2)}) %collective-permute-start.2) | collective-permute-done | bytes 24608 | tf_op jit(solution)/shard_map/ppermute | solution.py:31
  16.9 0.0 collective-permute-done.5.refs_2_.rest_7_
  16.9 0.0 collective-permute-done.4.refs_3_.rest_6_
  16.9 0.0 collective-permute-done.7.refs_0_
  17.0 0.1 collective-permute-start.8
  17.0 0.5 %collective-permute-start.6 = (bf16[128,640]{1,0:T(8,128)(2,1)S(1)}, bf16[128,640]{1,0:T(8,128)(2,1)S(1)}, u32[]{:S(2)}, u32[]{:S(2)}) collective-permute-start(bf16[128,640]{1,0:T(8,128)(2,1)S(1)} %collective-permute-done.5.refs_2_.rest_7_), channel_id=1, source_target_pairs={{0,1},{1,0},{2,3},{3,2},{4,5},{5,4},{6,7},{7,6},{8,9},{9,8},{10,11... | collective-permute-start | bytes 491528 | tf_op jit(solution)/shard_map/ppermute | solution.py:21
  17.5 0.0 copy-done.8
  17.5 0.1 copy.16
  17.6 0.0 copy-done.9
  17.6 0.1 copy.17
  17.7 0.1 copy.18.settings_ref
  17.8 0.0 copy-done.2
  17.9 1.4 %shard_map.142 = (bf16[2,128,128]{2,1,0:T(8,128)(2,1)S(1)}, f32[1,256,512]{2,1,0:T(8,128)S(1)}, f32[1,256,512]{2,1,0:T(8,128)S(1)}, bf16[256,96]{1,0:T(8,128)(2,...) custom-call(s32[4]{0:T(128)S(1)} %pad_add_fusion.place_ref.scalar_ref, ...), custom_call_target="tpu_custom_call" | custom-call | tf_op jit(solution)/shard_map/pallas_call | solution.py:348
  19.3 0.0 collective-permute-done.6.rest_8_
  19.3 0.0 collective-permute-done.8.rest_10_
  19.3 8.3 %shard_map.144 = (bf16[1,77,128]{2,1,0:T(8,128)(2,1)}, f32[77,1,128]{2,1,0:T(1,128)}) custom-call(s32[4]{0:T(128)S(1)} %pad_add_fusion.place_ref.scalar_ref, bf16[2,128,128]{2,1,0:T(8,128)(2,1)S(1)} %get-tuple-element.11.field_ref, f32[1,256,512]{2,1,0:T(8,128)S(1)} %get-tuple-element.12.scale_ref, f32[1,256,512]{2,1,0:T(8,128)S(1)} %get-tuple-element.13.shift_ref, ...), custom_call_target="tpu_custom_call" | custom-call | tf_op jit(solution)/shard_map/pallas_call | solution.py:385
  (10 shorter events, 0.1 us)
Async XLA Ops:
  0.6 5.1 %copy-start.11 = (bf16[1,256]{1,0:T(2,128)(2,1)S(1)}, bf16[1,256]{1,0:T(2,128)(2,1)}, u32[]{:S(2)}) copy-start(bf16[1,256]{1,0:T(2,128)(2,1)} %param.24) | copy-start | bytes 1540
  0.6 5.3 %copy-start.1 = (bf16[1,256,256]{2,1,0:T(8,128)(2,1)S(1)}, bf16[1,256,256]{2,1,0:T(8,128)(2,1)}, u32[]{:S(2)}) copy-start(bf16[1,256,256]{2,1,0:T(8,128)(2,1)} %param.23) | copy-start | bytes 393220
  1.6 4.5 %copy-start.4 = (bf16[1,1,77,128]{3,2,1,0:T(8,128)(2,1)S(1)}, bf16[1,1,77,128]{3,2,1,0:T(8,128)(2,1)}, u32[]{:S(2)}) copy-start(bf16[1,1,77,128]{3,2,1,0:T(8,128)(2,1)} %param.13) | copy-start | bytes 59140
  1.7 4.5 %copy-start.5 = (bf16[1,1,2,1,4,128]{5,4,3,2,1,0:T(4,128)(2,1)S(1)}, bf16[1,1,2,1,4,128]{5,4,3,2,1,0:T(4,128)(2,1)}, u32[]{:S(2)}) copy-start(bf16[1,1,2,1,4,128]{5,4,3,2,1,0:T(4,128)(2,1)} %param.14) | copy-start | bytes 6148
  1.7 4.5 %copy-start.6 = (s32[1,128]{1,0:T(1,128)S(1)}, s32[1,128]{1,0:T(1,128)}, u32[]{:S(2)}) copy-start(s32[1,128]{1,0:T(1,128)} %land_ref.1) | copy-start | bytes 1540
  1.7 8.5 %collective-permute-start.3 = (bf16[128,640]{1,0:T(8,128)(2,1)S(1)}, bf16[128,640]{1,0:T(8,128)(2,1)S(1)}, u32[]{:S(2)}, u32[]{:S(2)}) collective-permute-start(bf16[128,640]{1,0:T(8,128)(2,1)S(1)} %dynamic-slice_bitcast_fusion), channel_id=1, source_target_pairs={{0,2},{2,0},{1,3},{3,1},{4,6},{6,4},{5,7},{7,5},{8,10},{10,8},{9,1... | collective-permute-start | bytes 491528 | tf_op jit(solution)/shard_map/ppermute | solution.py:21
  5.9 11.6 %copy-start.8 = (f32[16,256]{1,0:T(8,128)S(1)}, f32[16,256]{1,0:T(8,128)}, u32[]{:S(2)}) copy-start(f32[16,256]{1,0:T(8,128)} %param.19) | copy-start | bytes 49156
  6.0 11.7 %copy-start.9 = (f32[16,256]{1,0:T(8,128)S(1)}, f32[16,256]{1,0:T(8,128)}, u32[]{:S(2)}) copy-start(f32[16,256]{1,0:T(8,128)} %param.20) | copy-start | bytes 49156
  6.0 11.8 %copy-start.10 = (f32[64,16]{0,1:T(8,128)S(1)}, f32[64,16]{0,1:T(8,128)}, u32[]{:S(2)}) copy-start(f32[64,16]{0,1:T(8,128)} %param.18) | copy-start | bytes 12292
  6.0 11.8 %copy-start.2 = (bf16[256,81]{0,1:T(8,128)(2,1)S(1)}, bf16[256,81]{0,1:T(8,128)(2,1)}, u32[]{:S(2)}) copy-start(bf16[256,81]{0,1:T(8,128)(2,1)} %param.21) | copy-start | bytes 124420
  6.0 11.8 %copy-start.3 = (bf16[77,256]{1,0:T(8,128)(2,1)S(1)}, bf16[77,256]{1,0:T(8,128)(2,1)}, u32[]{:S(2)}) copy-start(bf16[77,256]{1,0:T(8,128)(2,1)} %dec_w_ref.1) | copy-start | bytes 118276
  6.0 11.8 %copy-start.7 = (s32[1,2]{1,0:T(1,128)S(1)}, s32[1,2]{1,0:T(1,128)}, u32[]{:S(2)}) copy-start(s32[1,2]{1,0:T(1,128)} %param.15) | copy-start | bytes 28
  6.0 10.9 %collective-permute-start.7 = (bf16[128,1408]{1,0:T(8,128)(2,1)S(1)}, bf16[128,1408]{1,0:T(8,128)(2,1)S(1)}, u32[]{:S(2)}, u32[]{:S(2)}) collective-permute-start(bf16[128,1408]{1,0:T(8,128)(2,1)S(1)} %fusion.1.earlier_ref), channel_id=1, source_target_pairs={{0,2},{2,0},{1,3},{3,1},{4,6},{6,4},{5,7},{7,5},{8,10},{10,8},{9,1... | collective-permute-start | bytes 1081352 | tf_op jit(solution)/shard_map/ppermute | solution.py:21
  6.2 13.2 %copy-start = (bf16[1,256,2304]{2,1,0:T(8,128)(2,1)S(1)}, bf16[1,256,2304]{2,1,0:T(8,128)(2,1)}, u32[]{:S(2)}) copy-start(bf16[1,256,2304]{2,1,0:T(8,128)(2,1)} %param.22) | copy-start | bytes 3538948
  6.2 1.3 %collective-permute-start = (bf16[1,128,128]{2,1,0:T(8,128)(2,1)S(1)}, bf16[1,128,128]{2,1,0:T(8,128)(2,1)S(1)}, u32[]{:S(2)}, u32[]{:S(2)}) collective-permute-start(bf16[1,128,128]{2,1,0:T(8,128)(2,1)S(1)} %shard_map.140.rest_0_), channel_id=1, source_target_pairs={{0,1},{1,0},{2,3},{3,2},{4,5},{5,4},{6,7},{7,6},{8,9},{9,8},{10,11... | collective-permute-start | bytes 98312 | tf_op jit(solution)/shard_map/ppermute | solution.py:21
  8.0 3.8 %collective-permute-start.1 = (f32[24,128]{1,0:T(8,128)S(1)}, f32[24,128]{1,0:T(8,128)S(1)}, u32[]{:S(2)}, u32[]{:S(2)}) collective-permute-start(f32[24,128]{1,0:T(8,128)S(1)} %shard_map.141), channel_id=1, source_target_pairs={{0,4},{4,0},{8,12},{12,8},{1,5},{5,1},{9,13},{13,9},{2,6},{6,2},{1... | collective-permute-start | bytes 36872 | tf_op jit(solution)/shard_map/ppermute | solution.py:31
  10.1 6.8 %collective-permute-start.5 = (bf16[128,640]{1,0:T(8,128)(2,1)S(1)}, bf16[128,640]{1,0:T(8,128)(2,1)S(1)}, u32[]{:S(2)}, u32[]{:S(2)}) collective-permute-start(bf16[128,640]{1,0:T(8,128)(2,1)S(1)} %collective-permute-done.3.rest_5_), channel_id=1, source_target_pairs={{0,16},{16,0},{1,17},{17,1},{2,18},{18,2},{3,19},{19,3},{4,20},{20... | collective-permute-start | bytes 491528 | tf_op jit(solution)/shard_map/ppermute | solution.py:21
  11.7 5.3 %collective-permute-start.4 = (bf16[128,640]{1,0:T(8,128)(2,1)S(1)}, bf16[128,640]{1,0:T(8,128)(2,1)S(1)}, u32[]{:S(2)}, u32[]{:S(2)}) collective-permute-start(bf16[128,640]{1,0:T(8,128)(2,1)S(1)} %collective-permute-done.3.rest_5_), channel_id=1, source_target_pairs={{0,1},{1,0},{2,3},{3,2},{4,5},{5,4},{6,7},{7,6},{8,9},{9,8},{10,11... | collective-permute-start | bytes 491528 | tf_op jit(solution)/shard_map/ppermute | solution.py:21
  11.8 5.1 %collective-permute-start.2 = (f32[48,128]{1,0:T(8,128)S(1)}, f32[48,128]{1,0:T(8,128)S(1)}, u32[]{:S(2)}, u32[]{:S(2)}) collective-permute-start(f32[48,128]{1,0:T(8,128)S(1)} %pad_maximum_fusion.1), channel_id=1, source_target_pairs={{0,8},{4,12},{8,0},{12,4},{1,9},{5,13},{9,1},{13,5},{2,10},{6,14},... | collective-permute-start | bytes 73736 | tf_op jit(solution)/shard_map/ppermute | solution.py:31
  17.0 2.3 %collective-permute-start.8 = (bf16[128,1408]{1,0:T(8,128)(2,1)S(1)}, bf16[128,1408]{1,0:T(8,128)(2,1)S(1)}, u32[]{:S(2)}, u32[]{:S(2)}) collective-permute-start(bf16[128,1408]{1,0:T(8,128)(2,1)S(1)} %shard_map.143.rest_9_), channel_id=1, source_target_pairs={{0,1},{1,0},{2,3},{3,2},{4,5},{5,4},{6,7},{7,6},{8,9},{9,8},{10,11... | collective-permute-start | bytes 1081352 | tf_op jit(solution)/shard_map/ppermute | solution.py:21
  17.0 2.3 %collective-permute-start.6 = (bf16[128,640]{1,0:T(8,128)(2,1)S(1)}, bf16[128,640]{1,0:T(8,128)(2,1)S(1)}, u32[]{:S(2)}, u32[]{:S(2)}) collective-permute-start(bf16[128,640]{1,0:T(8,128)(2,1)S(1)} %collective-permute-done.5.refs_2_.rest_7_), channel_id=1, source_target_pairs={{0,1},{1,0},{2,3},{3,2},{4,5},{5,4},{6,7},{7,6},{8,9},{9,8},{10,11... | collective-permute-start | bytes 491528 | tf_op jit(solution)/shard_map/ppermute | solution.py:21

commit v10 on v9

--- a/solution.py
+++ b/solution.py
@@ -41,7 +41,7 @@
     return chosen
 
 
-def pack_kernel(dims, slots_ref, state_ref, land_ref, earlier_ref, field_ref):
+def pack_kernel(dims, slots_ref, state_ref, land_ref, index_ref, earlier_ref, field_ref):
     steps, local, forced, vp, fp = dims
     field_ref[...] = jnp.zeros(field_ref.shape, field_ref.dtype)
     for i in range(local):
@@ -49,10 +49,14 @@
         for t in range(steps):
             first = (t * local + i) * forced
             field_ref[i, vp + fp * t : vp + fp * t + forced] = slots_ref[first : first + forced]
-        field_ref[i, vp + fp * steps : vp + fp * steps + 1] = land_ref[i : i + 1].astype(jnp.bfloat16)
-
-
-def group_kernel(dims, place_ref, index_ref, *rest):
+        last = vp + fp * steps
+        field_ref[i, last : last + 1] = land_ref[i : i + 1].astype(jnp.bfloat16)
+        index = jnp.broadcast_to(index_ref[...], land_ref[i : i + 1].shape)
+        field_ref[i, last + 1 : last + 2] = (index & 255).astype(jnp.float32).astype(jnp.bfloat16)
+        field_ref[i, last + 2 : last + 3] = (index >> 8).astype(jnp.float32).astype(jnp.bfloat16)
+
+
+def group_kernel(dims, place_ref, *rest):
     steps, bands, local, forced, vp, fp = dims
     fields, group_ref = rest[:bands], rest[bands]
     for b in range(bands):
@@ -62,7 +66,9 @@
                 first = ((b * local + i) * steps + t) * forced
                 group_ref[first : first + forced] = field[i, vp + fp * t : vp + fp * t + forced].astype(jnp.float32)
     last = bands * local * steps * forced
-    group_ref[last : last + 1] = jnp.full((1, group_ref.shape[1]), index_ref[0], jnp.int32).astype(jnp.float32)
+    row = vp + fp * steps + 1
+    low, high = (fields[0][0, r : r + 1].astype(jnp.float32) for r in (row, row + 1))
+    group_ref[last : last + 1] = low + 256.0 * high
 
 
 def put_taps(taps, value, row, cols, spacing):
@@ -155,9 +161,12 @@
     taps_wide, wide = 9 * chans, 3 * chans
     part = chans // bands
 
-    pltpu.make_async_copy(blocks[0], weights.at[here, :, pl.ds(0, taps_wide)], sems.at[here]).start()
-    pltpu.make_async_copy(blocks[1], weights.at[here, :, pl.ds(taps_wide, chans)], sems.at[here]).start()
-    pltpu.make_async_copy(blocks[2], weights.at[here, :, pl.ds(10 * chans, LANES)], sems.at[here]).start()
+    def own_block():
+        pltpu.make_async_copy(blocks[0], weights.at[here, :, pl.ds(0, taps_wide)], sems.at[here]).start()
+        pltpu.make_async_copy(blocks[1], weights.at[here, :, pl.ds(taps_wide, chans)], sems.at[here]).start()
+        pltpu.make_async_copy(blocks[2], weights.at[here, :, pl.ds(10 * chans, LANES)], sems.at[here]).start()
+
+    pl.when(here == 0)(own_block)
     share = 5 * chans // groups
     for k in range(1, layers):
         slot = lax.rem(here - k + layers, layers)
@@ -172,6 +181,7 @@
                 block = blocks[3 + ((k - 1) * (groups + 1) + g) * bands + j]
                 pltpu.make_async_copy(block, weights.at[slot, rows, cols], sems.at[slot]).start()
 
+    pl.when(here != 0)(own_block)
     if turns > 1:
         hidden, taps = rest[8:]
 
@@ -327,21 +337,21 @@
     field = pl.pallas_call(
         functools.partial(pack_kernel, (steps, local, forced, vp, fp)),
         out_shape=jax.ShapeDtypeStruct((local, vp + fp * steps + BF16_ROWS, lon), jnp.bfloat16),
-        in_specs=[vmem] * 3 + [whole],
+        in_specs=[vmem] * 4 + [whole],
         out_specs=vmem,
         compiler_params=small,
         cost_estimate=free,
-    )(slots, init_state[0], land_mask, direct)
+    )(slots, init_state[0], land_mask, param_index[None], direct)
     relayed, direct = (all_along(piece, "segment")[1:] for piece in (relayed, direct))
     fields = all_along(field, "rows")
     group = pl.pallas_call(
         functools.partial(group_kernel, (steps, bands, local, forced, vp, fp)),
         out_shape=jax.ShapeDtypeStruct((lat * steps * forced + 8, lon), jnp.float32),
-        in_specs=[smem, smem] + [vmem] * bands,
+        in_specs=[smem] + [vmem] * bands,
         out_specs=vmem,
         compiler_params=small,
         cost_estimate=free,
-    )(scalars, param_index, *fields)
+    )(scalars, *fields)
     group = by_doubling(group, "members")
 
     dims = (steps, layers, bands, local, at_once, lon, chans, vp, fp, turns)

time: 27.8 us -> 28.3 us (1.018)
  waiting for transfers between devices: 2.6 us -> 3.08 us
    ppermute x7, waiting for transfers between devices: 0.38 us -> 1.13 us  [passed_along(): lax.ppermute(block, axis, [(i, (i + distance) % size) for i in range(size)])]
where the time goes in v10:
time: 28.3 us; the launch traced here: 28 us
  starting transfers between devices  10.4 us (37%)
  Pallas kernels  10.4 us (37%)
  waiting for transfers between devices  3.08 us (11%)
  local copies, waits for them, and re-layouts  2.5 us (9%)
  between operations  1.55 us (5%)
    pallas_call x1, Pallas kernels, per_device(): pl.pallas_call(functools.partial(window_kernel, dims + (groups,)), out_sh...  8.29 us
    ppermute x7, starting transfers between devices, passed_along(): lax.ppermute(block, axis, [(i, (i + distance) % size) for i in range(size)])  5.19 us
    ppermute x2, starting transfers between devices, by_doubling(): partner = lax.ppermute(block, axis, [(i, i ^ reach) for i in range(size)])  5.19 us
    ppermute x2, waiting for transfers between devices, by_doubling(): partner = lax.ppermute(block, axis, [(i, i ^ reach) for i in range(size)])  1.95 us
    pallas_call x1, Pallas kernels, per_device(): pl.pallas_call(functools.partial(first_kernel, dims), out_shape=(jax.Shap...  1.43 us
    ppermute x7, waiting for transfers between devices, passed_along(): lax.ppermute(block, axis, [(i, (i + distance) % size) for i in range(size)])  1.13 us
    slice x1, local copies, waits for them, and re-layouts, per_device(): conv[:, groups * share:]  1.08 us
    dynamic_slice x1, local copies, waits for them, and re-layouts, per_device(): lax.dynamic_slice(conv, (band * part, places[3] * share), (part, share))  0.98 us
  transfers between devices with their start and end apart: 9, of which 3 were waited for; matrix products, arithmetic and copies ran while one was open for 6% of the time, Pallas kernels for 7%

profile of v10, /device:TPU:0, one launch (start us, length us, event | category | flops | bytes accessed | tf_op | source)
XLA Modules:
  0.0 28.0 jit_solution(18113308127875923244)
XLA Ops:
  0.6 0.0 copy-start.11
  0.6 0.0 copy-start.1
  0.7 1.0 %dynamic-slice_bitcast_fusion = bf16[128,640]{1,0:T(8,128)(2,1)S(1)} fusion(bf16[1,256,2304]{2,1,0:T(8,128)(2,1)} %param.22, s32[]{:T(128)S(6)} %select_n.7, s32[]{:T(128)S(6)} %select_n.8), kind=kLoop, calls=%fused_computation.5 | loop fusion | bytes 327688 | tf_op jit(solution)/shard_map/dynamic_slice | solution.py:333
  1.6 0.0 copy-start.4
  1.7 0.0 copy-start.5
  1.7 0.0 copy-start.6
  1.7 3.0 %collective-permute-start.3 = (bf16[128,640]{1,0:T(8,128)(2,1)S(1)}, bf16[128,640]{1,0:T(8,128)(2,1)S(1)}, u32[]{:S(2)}, u32[]{:S(2)}) collective-permute-start(bf16[128,640]{1,0:T(8,128)(2,1)S(1)} %dynamic-slice_bitcast_fusion), channel_id=1, source_target_pairs={{0,2},{2,0},{1,3},{3,1},{4,6},{6,4},{5,7},{7,5},{8,10},{10,8},{9,1... | collective-permute-start | bytes 491528 | tf_op jit(solution)/shard_map/ppermute | solution.py:21
  4.7 1.1 %slice.4 = bf16[256,1024]{1,0:T(8,128)(2,1)S(1)} slice(bf16[256,2304]{1,0:T(8,128)(2,1)} %bitcast.20), slice={[0:256], [1280:2304]} | slice | bytes 1048576 | tf_op jit(solution)/shard_map/slice | solution.py:335
  5.8 0.0 copy-done.11
  5.8 0.1 broadcast_in_dim.15.rest_4_
  5.9 0.0 copy-done.1
  5.9 0.0 copy-start.8
  6.0 0.0 copy-start.9
  6.0 0.0 copy-start.10
  6.0 0.0 copy-start.2
  6.0 0.0 copy-start.3
  6.0 0.0 copy-start.7
  6.0 0.1 collective-permute-start.7
  6.8 0.0 copy-done.4
  6.8 0.0 copy-done.5
  6.8 0.0 copy-done.6
  6.8 0.1 shard_map.140.rest_0_
  6.9 0.0 collective-permute-start
  6.9 0.1 pad_add_fusion.place_ref.scalar_ref
  7.0 1.1 %collective-permute-done.rest_1_ = bf16[1,128,128]{2,1,0:T(8,128)(2,1)S(1)} collective-permute-done((bf16[1,128,128]{2,1,0:T(8,128)(2,1)S(1)}, bf16[1,128,128]{2,1,0:T(8,128)(2,1)S(1)}, u32[]{:S(2)}, u32[]{:S(2)}) %collective-permute-start) | collective-permute-done | bytes 32800 | tf_op jit(solution)/shard_map/ppermute | solution.py:21
  8.1 0.6 %shard_map.141 = f32[24,128]{1,0:T(8,128)S(1)} custom-call(s32[4]{0:T(128)S(1)} %pad_add_fusion.place_ref.scalar_ref, bf16[1,128,128]{2,1,0:T(8,128)(2,1)S(1)} %shard_map.140.rest_0_, bf16[1,128,128]{2,1,0:T(8,128)(2,1)S(1)} %collective-permute-done.rest_1_), custom_call_target="tpu_custom_call" | custom-call | tf_op jit(solution)/shard_map/pallas_call | solution.py:347
  8.7 2.2 %collective-permute-start.1 = (f32[24,128]{1,0:T(8,128)S(1)}, f32[24,128]{1,0:T(8,128)S(1)}, u32[]{:S(2)}, u32[]{:S(2)}) collective-permute-start(f32[24,128]{1,0:T(8,128)S(1)} %shard_map.141), channel_id=1, source_target_pairs={{0,4},{4,0},{8,12},{12,8},{1,5},{5,1},{9,13},{13,9},{2,6},{6,2},{1... | collective-permute-start | bytes 36872 | tf_op jit(solution)/shard_map/ppermute | solution.py:31
  10.8 0.0 collective-permute-done.3.rest_5_
  10.8 1.5 %collective-permute-start.5 = (bf16[128,640]{1,0:T(8,128)(2,1)S(1)}, bf16[128,640]{1,0:T(8,128)(2,1)S(1)}, u32[]{:S(2)}, u32[]{:S(2)}) collective-permute-start(bf16[128,640]{1,0:T(8,128)(2,1)S(1)} %collective-permute-done.3.rest_5_), channel_id=1, source_target_pairs={{0,16},{16,0},{1,17},{17,1},{2,18},{18,2},{3,19},{19,3},{4,20},{20... | collective-permute-start | bytes 491528 | tf_op jit(solution)/shard_map/ppermute | solution.py:21
  12.3 0.0 collective-permute-start.4
  12.3 0.1 collective-permute-done.1
  12.5 3.0 %collective-permute-start.2 = (f32[48,128]{1,0:T(8,128)S(1)}, f32[48,128]{1,0:T(8,128)S(1)}, u32[]{:S(2)}, u32[]{:S(2)}) collective-permute-start(f32[48,128]{1,0:T(8,128)S(1)} %pad_maximum_fusion.1), channel_id=1, source_target_pairs={{0,8},{4,12},{8,0},{12,4},{1,9},{5,13},{9,1},{13,5},{2,10},{6,14},... | collective-permute-start | bytes 73736 | tf_op jit(solution)/shard_map/ppermute | solution.py:31
  15.5 1.8 %collective-permute-done.2 = f32[48,128]{1,0:T(8,128)S(1)} collective-permute-done((f32[48,128]{1,0:T(8,128)S(1)}, f32[48,128]{1,0:T(8,128)S(1)}, u32[]{:S(2)}, u32[]{:S(2)}) %collective-permute-start.2) | collective-permute-done | bytes 24608 | tf_op jit(solution)/shard_map/ppermute | solution.py:31
  17.3 0.0 collective-permute-done.5.refs_2_.rest_7_
  17.3 0.0 collective-permute-done.4.refs_3_.rest_6_
  17.4 0.0 collective-permute-done.7.refs_0_
  17.4 0.1 collective-permute-start.8
  17.5 0.5 %collective-permute-start.6 = (bf16[128,640]{1,0:T(8,128)(2,1)S(1)}, bf16[128,640]{1,0:T(8,128)(2,1)S(1)}, u32[]{:S(2)}, u32[]{:S(2)}) collective-permute-start(bf16[128,640]{1,0:T(8,128)(2,1)S(1)} %collective-permute-done.5.refs_2_.rest_7_), channel_id=1, source_target_pairs={{0,1},{1,0},{2,3},{3,2},{4,5},{5,4},{6,7},{7,6},{8,9},{9,8},{10,11... | collective-permute-start | bytes 491528 | tf_op jit(solution)/shard_map/ppermute | solution.py:21
  18.0 0.0 copy-done.8
  18.0 0.1 copy.16
  18.1 0.0 copy-done.9
  18.1 0.1 copy.17
  18.2 0.1 copy.18.settings_ref
  18.3 0.0 copy-done.2
  18.3 1.4 %shard_map.142 = (bf16[2,128,128]{2,1,0:T(8,128)(2,1)S(1)}, f32[1,256,512]{2,1,0:T(8,128)S(1)}, f32[1,256,512]{2,1,0:T(8,128)S(1)}, bf16[256,96]{1,0:T(8,128)(2,...) custom-call(s32[4]{0:T(128)S(1)} %pad_add_fusion.place_ref.scalar_ref, ...), custom_call_target="tpu_custom_call" | custom-call | tf_op jit(solution)/shard_map/pallas_call | solution.py:358
  19.7 0.0 collective-permute-done.6.rest_8_
  19.7 0.0 collective-permute-done.8.rest_10_
  19.7 8.3 %shard_map.144 = (bf16[1,77,128]{2,1,0:T(8,128)(2,1)}, f32[77,1,128]{2,1,0:T(1,128)}) custom-call(s32[4]{0:T(128)S(1)} %pad_add_fusion.place_ref.scalar_ref, bf16[2,128,128]{2,1,0:T(8,128)(2,1)S(1)} %get-tuple-element.11.field_ref, f32[1,256,512]{2,1,0:T(8,128)S(1)} %get-tuple-element.12.scale_ref, f32[1,256,512]{2,1,0:T(8,128)S(1)} %get-tuple-element.13.shift_ref, ...), custom_call_target="tpu_custom_call" | custom-call | tf_op jit(solution)/shard_map/pallas_call | solution.py:395
  (10 shorter events, 0.1 us)
Async XLA Ops:
  0.6 5.1 %copy-start.11 = (bf16[1,256]{1,0:T(2,128)(2,1)S(1)}, bf16[1,256]{1,0:T(2,128)(2,1)}, u32[]{:S(2)}) copy-start(bf16[1,256]{1,0:T(2,128)(2,1)} %param.24) | copy-start | bytes 1540
  0.6 5.3 %copy-start.1 = (bf16[1,256,256]{2,1,0:T(8,128)(2,1)S(1)}, bf16[1,256,256]{2,1,0:T(8,128)(2,1)}, u32[]{:S(2)}) copy-start(bf16[1,256,256]{2,1,0:T(8,128)(2,1)} %param.23) | copy-start | bytes 393220
  1.6 5.1 %copy-start.4 = (bf16[1,1,77,128]{3,2,1,0:T(8,128)(2,1)S(1)}, bf16[1,1,77,128]{3,2,1,0:T(8,128)(2,1)}, u32[]{:S(2)}) copy-start(bf16[1,1,77,128]{3,2,1,0:T(8,128)(2,1)} %param.13) | copy-start | bytes 59140
  1.7 5.1 %copy-start.5 = (bf16[1,1,2,1,4,128]{5,4,3,2,1,0:T(4,128)(2,1)S(1)}, bf16[1,1,2,1,4,128]{5,4,3,2,1,0:T(4,128)(2,1)}, u32[]{:S(2)}) copy-start(bf16[1,1,2,1,4,128]{5,4,3,2,1,0:T(4,128)(2,1)} %param.14) | copy-start | bytes 6148
  1.7 5.1 %copy-start.6 = (s32[1,128]{1,0:T(1,128)S(1)}, s32[1,128]{1,0:T(1,128)}, u32[]{:S(2)}) copy-start(s32[1,128]{1,0:T(1,128)} %land_ref.1) | copy-start | bytes 1540
  1.7 9.1 %collective-permute-start.3 = (bf16[128,640]{1,0:T(8,128)(2,1)S(1)}, bf16[128,640]{1,0:T(8,128)(2,1)S(1)}, u32[]{:S(2)}, u32[]{:S(2)}) collective-permute-start(bf16[128,640]{1,0:T(8,128)(2,1)S(1)} %dynamic-slice_bitcast_fusion), channel_id=1, source_target_pairs={{0,2},{2,0},{1,3},{3,1},{4,6},{6,4},{5,7},{7,5},{8,10},{10,8},{9,1... | collective-permute-start | bytes 491528 | tf_op jit(solution)/shard_map/ppermute | solution.py:21
  5.9 12.1 %copy-start.8 = (f32[16,256]{1,0:T(8,128)S(1)}, f32[16,256]{1,0:T(8,128)}, u32[]{:S(2)}) copy-start(f32[16,256]{1,0:T(8,128)} %param.19) | copy-start | bytes 49156
  6.0 12.1 %copy-start.9 = (f32[16,256]{1,0:T(8,128)S(1)}, f32[16,256]{1,0:T(8,128)}, u32[]{:S(2)}) copy-start(f32[16,256]{1,0:T(8,128)} %param.20) | copy-start | bytes 49156
  6.0 12.2 %copy-start.10 = (f32[64,16]{0,1:T(8,128)S(1)}, f32[64,16]{0,1:T(8,128)}, u32[]{:S(2)}) copy-start(f32[64,16]{0,1:T(8,128)} %param.18) | copy-start | bytes 12292
  6.0 12.3 %copy-start.2 = (bf16[256,81]{0,1:T(8,128)(2,1)S(1)}, bf16[256,81]{0,1:T(8,128)(2,1)}, u32[]{:S(2)}) copy-start(bf16[256,81]{0,1:T(8,128)(2,1)} %param.21) | copy-start | bytes 124420
  6.0 12.3 %copy-start.3 = (bf16[77,256]{1,0:T(8,128)(2,1)S(1)}, bf16[77,256]{1,0:T(8,128)(2,1)}, u32[]{:S(2)}) copy-start(bf16[77,256]{1,0:T(8,128)(2,1)} %dec_w_ref.1) | copy-start | bytes 118276
  6.0 12.3 %copy-start.7 = (s32[1,2]{1,0:T(1,128)S(1)}, s32[1,2]{1,0:T(1,128)}, u32[]{:S(2)}) copy-start(s32[1,2]{1,0:T(1,128)} %param.15) | copy-start | bytes 28
  6.0 11.3 %collective-permute-start.7 = (bf16[128,1408]{1,0:T(8,128)(2,1)S(1)}, bf16[128,1408]{1,0:T(8,128)(2,1)S(1)}, u32[]{:S(2)}, u32[]{:S(2)}) collective-permute-start(bf16[128,1408]{1,0:T(8,128)(2,1)S(1)} %fusion.1.earlier_ref), channel_id=1, source_target_pairs={{0,2},{2,0},{1,3},{3,1},{4,6},{6,4},{5,7},{7,5},{8,10},{10,8},{9,1... | collective-permute-start | bytes 1081352 | tf_op jit(solution)/shard_map/ppermute | solution.py:21
  6.9 12.9 %copy-start = (bf16[1,256,2304]{2,1,0:T(8,128)(2,1)S(1)}, bf16[1,256,2304]{2,1,0:T(8,128)(2,1)}, u32[]{:S(2)}) copy-start(bf16[1,256,2304]{2,1,0:T(8,128)(2,1)} %param.22) | copy-start | bytes 3538948
  6.9 1.2 %collective-permute-start = (bf16[1,128,128]{2,1,0:T(8,128)(2,1)S(1)}, bf16[1,128,128]{2,1,0:T(8,128)(2,1)S(1)}, u32[]{:S(2)}, u32[]{:S(2)}) collective-permute-start(bf16[1,128,128]{2,1,0:T(8,128)(2,1)S(1)} %shard_map.140.rest_0_), channel_id=1, source_target_pairs={{0,1},{1,0},{2,3},{3,2},{4,5},{5,4},{6,7},{7,6},{8,9},{9,8},{10,11... | collective-permute-start | bytes 98312 | tf_op jit(solution)/shard_map/ppermute | solution.py:21
  8.7 3.8 %collective-permute-start.1 = (f32[24,128]{1,0:T(8,128)S(1)}, f32[24,128]{1,0:T(8,128)S(1)}, u32[]{:S(2)}, u32[]{:S(2)}) collective-permute-start(f32[24,128]{1,0:T(8,128)S(1)} %shard_map.141), channel_id=1, source_target_pairs={{0,4},{4,0},{8,12},{12,8},{1,5},{5,1},{9,13},{13,9},{2,6},{6,2},{1... | collective-permute-start | bytes 36872 | tf_op jit(solution)/shard_map/ppermute | solution.py:31
  10.8 6.5 %collective-permute-start.5 = (bf16[128,640]{1,0:T(8,128)(2,1)S(1)}, bf16[128,640]{1,0:T(8,128)(2,1)S(1)}, u32[]{:S(2)}, u32[]{:S(2)}) collective-permute-start(bf16[128,640]{1,0:T(8,128)(2,1)S(1)} %collective-permute-done.3.rest_5_), channel_id=1, source_target_pairs={{0,16},{16,0},{1,17},{17,1},{2,18},{18,2},{3,19},{19,3},{4,20},{20... | collective-permute-start | bytes 491528 | tf_op jit(solution)/shard_map/ppermute | solution.py:21
  12.3 5.0 %collective-permute-start.4 = (bf16[128,640]{1,0:T(8,128)(2,1)S(1)}, bf16[128,640]{1,0:T(8,128)(2,1)S(1)}, u32[]{:S(2)}, u32[]{:S(2)}) collective-permute-start(bf16[128,640]{1,0:T(8,128)(2,1)S(1)} %collective-permute-done.3.rest_5_), channel_id=1, source_target_pairs={{0,1},{1,0},{2,3},{3,2},{4,5},{5,4},{6,7},{7,6},{8,9},{9,8},{10,11... | collective-permute-start | bytes 491528 | tf_op jit(solution)/shard_map/ppermute | solution.py:21
  12.5 4.8 %collective-permute-start.2 = (f32[48,128]{1,0:T(8,128)S(1)}, f32[48,128]{1,0:T(8,128)S(1)}, u32[]{:S(2)}, u32[]{:S(2)}) collective-permute-start(f32[48,128]{1,0:T(8,128)S(1)} %pad_maximum_fusion.1), channel_id=1, source_target_pairs={{0,8},{4,12},{8,0},{12,4},{1,9},{5,13},{9,1},{13,5},{2,10},{6,14},... | collective-permute-start | bytes 73736 | tf_op jit(solution)/shard_map/ppermute | solution.py:31
  17.4 2.3 %collective-permute-start.8 = (bf16[128,1408]{1,0:T(8,128)(2,1)S(1)}, bf16[128,1408]{1,0:T(8,128)(2,1)S(1)}, u32[]{:S(2)}, u32[]{:S(2)}) collective-permute-start(bf16[128,1408]{1,0:T(8,128)(2,1)S(1)} %shard_map.143.rest_9_), channel_id=1, source_target_pairs={{0,1},{1,0},{2,3},{3,2},{4,5},{5,4},{6,7},{7,6},{8,9},{9,8},{10,11... | collective-permute-start | bytes 1081352 | tf_op jit(solution)/shard_map/ppermute | solution.py:21
  17.5 2.3 %collective-permute-start.6 = (bf16[128,640]{1,0:T(8,128)(2,1)S(1)}, bf16[128,640]{1,0:T(8,128)(2,1)S(1)}, u32[]{:S(2)}, u32[]{:S(2)}) collective-permute-start(bf16[128,640]{1,0:T(8,128)(2,1)S(1)} %collective-permute-done.5.refs_2_.rest_7_), channel_id=1, source_target_pairs={{0,1},{1,0},{2,3},{3,2},{4,5},{5,4},{6,7},{7,6},{8,9},{9,8},{10,11... | collective-permute-start | bytes 491528 | tf_op jit(solution)/shard_map/ppermute | solution.py:21

commit v11 on v9

--- a/solution.py
+++ b/solution.py
@@ -84,7 +84,7 @@
     forced = enc_w_ref.shape[0] - dec_w_ref.shape[0]
     used = bands * local * steps * forced
     group = [everyone.at[k * (used + 8) : (k + 1) * (used + 8)] for k in range(members * turns)]
-    field_ref, scale_ref, shift_ref, enc_ref, dec_ref, hidden_ref, taps_ref, turned = rest
+    field_ref, scale_ref, shift_ref, enc_ref, dec_ref, hidden_ref, taps_ref, turned, lines = rest
     varied = dec_w_ref.shape[0]
     turned[...] = jnp.zeros(turned.shape, turned.dtype)
     turned[0:varied] = enc_w_ref[0:varied].astype(jnp.float32)
@@ -105,15 +105,17 @@
             field_ref[i, vp + fp * t : vp + fp * t + forced, :] = force.astype(jnp.bfloat16)
 
     settings = settings_ref[...]
-    numbers = lax.broadcasted_iota(jnp.int32, settings.shape, 0).astype(jnp.float32)
+    numbers = lax.broadcasted_iota(jnp.int32, settings.shape, 1).astype(jnp.float32)
     for m, entry in enumerate(group):
         chosen = entry[used : used + 1, 0 : settings.shape[1]]
-        row = jnp.sum(jnp.where(numbers == chosen, settings, 0.0), axis=0, keepdims=True)
+        column = jnp.sum(jnp.where(numbers == chosen, settings, 0.0), axis=1, keepdims=True)
+        lines[2 * m : 2 * m + 1] = 1.0 + jnp.sum(scale_w_ref[...] * column, axis=0, keepdims=True)
+        lines[2 * m + 1 : 2 * m + 2] = jnp.sum(shift_w_ref[...] * column, axis=0, keepdims=True)
+    columns = lines[...].T
+    for m in range(len(group)):
         cols = slice((m % members) * lon, (m % members + 1) * lon)
-        scale = 1.0 + jnp.sum(scale_w_ref[...] * row, axis=1, keepdims=True)
-        shift = jnp.sum(shift_w_ref[...] * row, axis=1, keepdims=True)
-        scale_ref[m // members, :, cols] = jnp.broadcast_to(scale, (chans, lon))
-        shift_ref[m // members, :, cols] = jnp.broadcast_to(shift, (chans, lon))
+        scale_ref[m // members, :, cols] = jnp.broadcast_to(columns[:, 2 * m : 2 * m + 1], (chans, lon))
+        shift_ref[m // members, :, cols] = jnp.broadcast_to(columns[:, 2 * m + 1 : 2 * m + 2], (chans, lon))
 
     if turns == 1:
         for i in range(bands * local):
@@ -201,9 +203,8 @@
     def activate(value, layer):
         centred = value - jnp.sum(value, axis=0, keepdims=True) * (1.0 / chans)
         spread = jnp.sum(centred * centred, axis=0, keepdims=True) * (1.0 / chans)
-        normed = (centred * lax.rsqrt(spread + 1e-05)).astype(jnp.bfloat16) * weights[layer, :, 10 * chans :]
-        inner = normed * (normed * normed * 0.0356774081 + 0.7978845608)
-        half = normed * 0.5
+        half = (centred * lax.rsqrt(spread + 1e-05)).astype(jnp.bfloat16) * weights[layer, :, 10 * chans :]
+        inner = half * (half * half * 0.2854192648 + 1.5957691216)
         return half + half * jnp.tanh(inner)
 
     def block(layer, not_yet):
@@ -321,7 +322,7 @@
     slots = forcing_slots[0, 0].reshape(-1, lon)
     conv = conv_weight[0]
     relayed = lax.dynamic_slice(conv, (band * part, places[3] * share), (part, share))
-    spread = jnp.broadcast_to(norm_gain[0][:, None], (chans, LANES))
+    spread = jnp.broadcast_to((norm_gain[0] * 0.5)[:, None], (chans, LANES))
     direct = jnp.concatenate([conv[:, groups * share :], point_weight[0], spread], axis=1)
     direct = lax.dynamic_slice_in_dim(direct, band * part, part, 0)
     field = pl.pallas_call(
@@ -358,10 +359,13 @@
         ),
         in_specs=[smem, smem] + [vmem] * (6 + bands),
         out_specs=(vmem,) * 7,
-        scratch_shapes=[pltpu.VMEM((vp + fp, chans), jnp.float32)],
+        scratch_shapes=[
+            pltpu.VMEM((vp + fp, chans), jnp.float32),
+            pltpu.VMEM((-(-2 * members // 8) * 8, chans), jnp.float32),
+        ],
         compiler_params=small,
         cost_estimate=free,
-    )(scalars, atmos_owner[0], encode_weight.T, decode_weight, settings, scale_weight.T, shift_weight.T, *fields, group)
+    )(scalars, atmos_owner[0], encode_weight.T, decode_weight, settings.T, scale_weight, shift_weight, *fields, group)
 
     blocks = [conv_weight[0], point_weight[0], spread]
     for k in range(layers - 1):

time: 27.8 us -> 27.6 us (level)
  local copies, waits for them, and re-layouts: 2.51 us -> 2.22 us
    unnamed x27 -> x24, local copies, waits for them, and re-layouts: 0.35 us -> 0.07 us
  transfers between devices with their start and end apart: 9 -> 9, of which waited for: 3 -> 3; matrix products, arithmetic and copies ran while one was open for 6% -> 5% of each run, Pallas kernels for 7% -> 8%
where the time goes in v11:
time: 27.6 us; the launch traced here: 27.4 us
  starting transfers between devices  10.4 us (38%)
  Pallas kernels  10.4 us (38%)
  waiting for transfers between devices  2.64 us (10%)
  local copies, waits for them, and re-layouts  2.22 us (8%)
  between operations  1.61 us (6%)
    pallas_call x1, Pallas kernels, per_device(): pl.pallas_call(functools.partial(window_kernel, dims + (groups,)), out_sh...  8.19 us
    ppermute x7, starting transfers between devices, passed_along(): lax.ppermute(block, axis, [(i, (i + distance) % size) for i in range(size)])  5.25 us
    ppermute x2, starting transfers between devices, by_doubling(): partner = lax.ppermute(block, axis, [(i, i ^ reach) for i in range(size)])  5.17 us
    ppermute x2, waiting for transfers between devices, by_doubling(): partner = lax.ppermute(block, axis, [(i, i ^ reach) for i in range(size)])  2.21 us
    pallas_call x1, Pallas kernels, per_device(): pl.pallas_call(functools.partial(first_kernel, dims), out_shape=(jax.Shap...  1.61 us
    slice x1, local copies, waits for them, and re-layouts, per_device(): conv[:, groups * share:]  1.08 us
    dynamic_slice x1, local copies, waits for them, and re-layouts, per_device(): lax.dynamic_slice(conv, (band * part, places[3] * share), (part, share))  0.98 us
    pallas_call x1, Pallas kernels, per_device(): pl.pallas_call(functools.partial(group_kernel, (steps, bands, local, forc...  0.55 us
  transfers between devices with their start and end apart: 9, of which 3 were waited for; matrix products, arithmetic and copies ran while one was open for 5% of the time, Pallas kernels for 8%

profile of v11, /device:TPU:0, one launch (start us, length us, event | category | flops | bytes accessed | tf_op | source)
XLA Modules:
  0.0 27.4 jit_solution(1812526159931956549)
XLA Ops:
  0.6 0.0 copy-start.11
  0.6 0.0 copy-start.1
  0.7 1.0 %dynamic-slice_bitcast_fusion = bf16[128,640]{1,0:T(8,128)(2,1)S(1)} fusion(bf16[1,256,2304]{2,1,0:T(8,128)(2,1)} %param.22, s32[]{:T(128)S(6)} %select_n.7, s32[]{:T(128)S(6)} %select_n.8), kind=kLoop, calls=%fused_computation.5 | loop fusion | bytes 327688 | tf_op jit(solution)/shard_map/dynamic_slice | solution.py:324
  1.6 0.0 copy-start.4
  1.7 0.0 copy-start.8
  1.7 0.0 copy-start.9
  1.7 3.0 %collective-permute-start.3 = (bf16[128,640]{1,0:T(8,128)(2,1)S(1)}, bf16[128,640]{1,0:T(8,128)(2,1)S(1)}, u32[]{:S(2)}, u32[]{:S(2)}) collective-permute-start(bf16[128,640]{1,0:T(8,128)(2,1)S(1)} %dynamic-slice_bitcast_fusion), channel_id=1, source_target_pairs={{0,2},{2,0},{1,3},{3,1},{4,6},{6,4},{5,7},{7,5},{8,10},{10,8},{9,1... | collective-permute-start | bytes 491528 | tf_op jit(solution)/shard_map/ppermute | solution.py:21
  4.7 1.1 %slice.4 = bf16[256,1024]{1,0:T(8,128)(2,1)S(1)} slice(bf16[256,2304]{1,0:T(8,128)(2,1)} %bitcast.17), slice={[0:256], [1280:2304]} | slice | bytes 1048576 | tf_op jit(solution)/shard_map/slice | solution.py:326
  5.8 0.0 copy-done.11
  5.8 0.1 broadcast_in_dim.4.rest_4_
  5.9 0.0 copy-done.1
  5.9 0.0 copy-start.2
  5.9 0.0 copy-start.3
  5.9 0.0 copy-start.5
  5.9 0.0 copy-start.6
  6.0 0.0 copy-start.7
  6.0 0.0 copy-start.10
  6.0 0.0 copy-start
  6.0 0.1 collective-permute-start.7
  6.1 0.0 copy-done.4
  6.1 0.0 copy-done.8
  6.1 0.0 copy-done.9
  6.2 0.1 collective-permute-start
  6.3 0.1 pad_add_fusion.place_ref.scalar_ref
  7.0 0.4 %collective-permute-done.rest_1_ = bf16[1,128,128]{2,1,0:T(8,128)(2,1)S(1)} collective-permute-done((bf16[1,128,128]{2,1,0:T(8,128)(2,1)S(1)}, bf16[1,128,128]{2,1,0:T(8,128)(2,1)S(1)}, u32[]{:S(2)}, u32[]{:S(2)}) %collective-permute-start) | collective-permute-done | bytes 32800 | tf_op jit(solution)/shard_map/ppermute | solution.py:21
  7.4 0.6 %shard_map.141 = f32[24,128]{1,0:T(8,128)S(1)} custom-call(s32[4]{0:T(128)S(1)} %pad_add_fusion.place_ref.scalar_ref, s32[1]{0:T(128)S(6)} %copy.18.index_ref, bf16[1,128,128]{2,1,0:T(8,128)(2,1)S(1)} %shard_map.140.rest_0_, bf16[1,128,128]{2,1,0:T(8,128)(2,1)S(1)} %collective-permute-done.rest_1_), custom_call_target="tpu_custom_call" | custom-call | tf_op jit(solution)/shard_map/pallas_call | solution.py:338
  8.0 2.1 %collective-permute-start.1 = (f32[24,128]{1,0:T(8,128)S(1)}, f32[24,128]{1,0:T(8,128)S(1)}, u32[]{:S(2)}, u32[]{:S(2)}) collective-permute-start(f32[24,128]{1,0:T(8,128)S(1)} %shard_map.141), channel_id=1, source_target_pairs={{0,4},{4,0},{8,12},{12,8},{1,5},{5,1},{9,13},{13,9},{2,6},{6,2},{1... | collective-permute-start | bytes 36872 | tf_op jit(solution)/shard_map/ppermute | solution.py:31
  10.1 0.0 collective-permute-done.3.rest_5_
  10.1 1.5 %collective-permute-start.5 = (bf16[128,640]{1,0:T(8,128)(2,1)S(1)}, bf16[128,640]{1,0:T(8,128)(2,1)S(1)}, u32[]{:S(2)}, u32[]{:S(2)}) collective-permute-start(bf16[128,640]{1,0:T(8,128)(2,1)S(1)} %collective-permute-done.3.rest_5_), channel_id=1, source_target_pairs={{0,16},{16,0},{1,17},{17,1},{2,18},{18,2},{3,19},{19,3},{4,20},{20... | collective-permute-start | bytes 491528 | tf_op jit(solution)/shard_map/ppermute | solution.py:21
  11.7 0.0 collective-permute-start.4
  11.7 0.1 collective-permute-done.1
  11.8 3.0 %collective-permute-start.2 = (f32[48,128]{1,0:T(8,128)S(1)}, f32[48,128]{1,0:T(8,128)S(1)}, u32[]{:S(2)}, u32[]{:S(2)}) collective-permute-start(f32[48,128]{1,0:T(8,128)S(1)} %pad_maximum_fusion.1), channel_id=1, source_target_pairs={{0,8},{4,12},{8,0},{12,4},{1,9},{5,13},{9,1},{13,5},{2,10},{6,14},... | collective-permute-start | bytes 73736 | tf_op jit(solution)/shard_map/ppermute | solution.py:31
  14.8 2.1 %collective-permute-done.2 = f32[48,128]{1,0:T(8,128)S(1)} collective-permute-done((f32[48,128]{1,0:T(8,128)S(1)}, f32[48,128]{1,0:T(8,128)S(1)}, u32[]{:S(2)}, u32[]{:S(2)}) %collective-permute-start.2) | collective-permute-done | bytes 24608 | tf_op jit(solution)/shard_map/ppermute | solution.py:31
  16.9 0.0 collective-permute-done.5.refs_2_.rest_7_
  16.9 0.0 collective-permute-done.4.refs_3_.rest_6_
  16.9 0.0 collective-permute-done.7.refs_0_
  17.0 0.1 collective-permute-start.8
  17.0 0.5 %collective-permute-start.6 = (bf16[128,640]{1,0:T(8,128)(2,1)S(1)}, bf16[128,640]{1,0:T(8,128)(2,1)S(1)}, u32[]{:S(2)}, u32[]{:S(2)}) collective-permute-start(bf16[128,640]{1,0:T(8,128)(2,1)S(1)} %collective-permute-done.5.refs_2_.rest_7_), channel_id=1, source_target_pairs={{0,1},{1,0},{2,3},{3,2},{4,5},{5,4},{6,7},{7,6},{8,9},{9,8},{10,11... | collective-permute-start | bytes 491528 | tf_op jit(solution)/shard_map/ppermute | solution.py:21
  17.5 0.0 copy-done.2
  17.5 0.0 copy-done.3
  17.5 0.0 copy-done.5
  17.5 0.0 copy-done.6
  17.5 0.0 copy-done.7
  17.6 0.0 copy-done.10
  17.6 1.6 %shard_map.142 = (bf16[2,128,128]{2,1,0:T(8,128)(2,1)S(1)}, f32[1,256,512]{2,1,0:T(8,128)S(1)}, f32[1,256,512]{2,1,0:T(8,128)S(1)}, bf16[256,96]{1,0:T(8,128)(2,...) custom-call(s32[4]{0:T(128)S(1)} %pad_add_fusion.place_ref.scalar_ref, ...), custom_call_target="tpu_custom_call" | custom-call | tf_op jit(solution)/shard_map/pallas_call | solution.py:349
  19.2 0.0 collective-permute-done.6.rest_8_
  19.2 0.0 collective-permute-done.8.rest_10_
  19.2 8.2 %shard_map.144 = (bf16[1,77,128]{2,1,0:T(8,128)(2,1)}, f32[77,1,128]{2,1,0:T(1,128)}) custom-call(s32[4]{0:T(128)S(1)} %pad_add_fusion.place_ref.scalar_ref, bf16[2,128,128]{2,1,0:T(8,128)(2,1)S(1)} %get-tuple-element.11.field_ref, f32[1,256,512]{2,1,0:T(8,128)S(1)} %get-tuple-element.12.scale_ref, f32[1,256,512]{2,1,0:T(8,128)S(1)} %get-tuple-element.13.shift_ref, ...), custom_call_target="tpu_custom_call" | custom-call | tf_op jit(solution)/shard_map/pallas_call | solution.py:389
  (7 shorter events, 0.1 us)
Async XLA Ops:
  0.6 5.1 %copy-start.11 = (bf16[1,256]{1,0:T(2,128)(2,1)S(1)}, bf16[1,256]{1,0:T(2,128)(2,1)}, u32[]{:S(2)}) copy-start(bf16[1,256]{1,0:T(2,128)(2,1)} %param.24) | copy-start | bytes 1540
  0.6 5.3 %copy-start.1 = (bf16[1,256,256]{2,1,0:T(8,128)(2,1)S(1)}, bf16[1,256,256]{2,1,0:T(8,128)(2,1)}, u32[]{:S(2)}) copy-start(bf16[1,256,256]{2,1,0:T(8,128)(2,1)} %param.23) | copy-start | bytes 393220
  1.6 4.5 %copy-start.4 = (bf16[1,1,77,128]{3,2,1,0:T(8,128)(2,1)S(1)}, bf16[1,1,77,128]{3,2,1,0:T(8,128)(2,1)}, u32[]{:S(2)}) copy-start(bf16[1,1,77,128]{3,2,1,0:T(8,128)(2,1)} %param.13) | copy-start | bytes 59140
  1.7 4.5 %copy-start.8 = (bf16[1,1,2,1,4,128]{5,4,3,2,1,0:T(4,128)(2,1)S(1)}, bf16[1,1,2,1,4,128]{5,4,3,2,1,0:T(4,128)(2,1)}, u32[]{:S(2)}) copy-start(bf16[1,1,2,1,4,128]{5,4,3,2,1,0:T(4,128)(2,1)} %param.14) | copy-start | bytes 6148
  1.7 4.5 %copy-start.9 = (s32[1,128]{1,0:T(1,128)S(1)}, s32[1,128]{1,0:T(1,128)}, u32[]{:S(2)}) copy-start(s32[1,128]{1,0:T(1,128)} %land_ref.1) | copy-start | bytes 1540
  1.7 8.5 %collective-permute-start.3 = (bf16[128,640]{1,0:T(8,128)(2,1)S(1)}, bf16[128,640]{1,0:T(8,128)(2,1)S(1)}, u32[]{:S(2)}, u32[]{:S(2)}) collective-permute-start(bf16[128,640]{1,0:T(8,128)(2,1)S(1)} %dynamic-slice_bitcast_fusion), channel_id=1, source_target_pairs={{0,2},{2,0},{1,3},{3,1},{4,6},{6,4},{5,7},{7,5},{8,10},{10,8},{9,1... | collective-permute-start | bytes 491528 | tf_op jit(solution)/shard_map/ppermute | solution.py:21
  5.9 11.6 %copy-start.2 = (bf16[256,81]{0,1:T(8,128)(2,1)S(1)}, bf16[256,81]{0,1:T(8,128)(2,1)}, u32[]{:S(2)}) copy-start(bf16[256,81]{0,1:T(8,128)(2,1)} %param.21) | copy-start | bytes 124420
  5.9 11.6 %copy-start.3 = (bf16[77,256]{1,0:T(8,128)(2,1)S(1)}, bf16[77,256]{1,0:T(8,128)(2,1)}, u32[]{:S(2)}) copy-start(bf16[77,256]{1,0:T(8,128)(2,1)} %dec_w_ref.1) | copy-start | bytes 118276
  5.9 11.6 %copy-start.5 = (f32[16,256]{1,0:T(8,128)S(1)}, f32[16,256]{1,0:T(8,128)}, u32[]{:S(2)}) copy-start(f32[16,256]{1,0:T(8,128)} %scale_w_ref.1) | copy-start | bytes 49156
  5.9 11.6 %copy-start.6 = (f32[16,256]{1,0:T(8,128)S(1)}, f32[16,256]{1,0:T(8,128)}, u32[]{:S(2)}) copy-start(f32[16,256]{1,0:T(8,128)} %shift_w_ref.1) | copy-start | bytes 49156
  6.0 11.6 %copy-start.7 = (f32[64,16]{0,1:T(8,128)S(1)}, f32[64,16]{0,1:T(8,128)}, u32[]{:S(2)}) copy-start(f32[64,16]{0,1:T(8,128)} %param.18) | copy-start | bytes 12292
  6.0 11.6 %copy-start.10 = (s32[1,2]{1,0:T(1,128)S(1)}, s32[1,2]{1,0:T(1,128)}, u32[]{:S(2)}) copy-start(s32[1,2]{1,0:T(1,128)} %param.15) | copy-start | bytes 28
  6.0 13.2 %copy-start = (bf16[1,256,2304]{2,1,0:T(8,128)(2,1)S(1)}, bf16[1,256,2304]{2,1,0:T(8,128)(2,1)}, u32[]{:S(2)}) copy-start(bf16[1,256,2304]{2,1,0:T(8,128)(2,1)} %param.22) | copy-start | bytes 3538948
  6.0 10.9 %collective-permute-start.7 = (bf16[128,1408]{1,0:T(8,128)(2,1)S(1)}, bf16[128,1408]{1,0:T(8,128)(2,1)S(1)}, u32[]{:S(2)}, u32[]{:S(2)}) collective-permute-start(bf16[128,1408]{1,0:T(8,128)(2,1)S(1)} %fusion.1.earlier_ref), channel_id=1, source_target_pairs={{0,2},{2,0},{1,3},{3,1},{4,6},{6,4},{5,7},{7,5},{8,10},{10,8},{9,1... | collective-permute-start | bytes 1081352 | tf_op jit(solution)/shard_map/ppermute | solution.py:21
  6.2 1.3 %collective-permute-start = (bf16[1,128,128]{2,1,0:T(8,128)(2,1)S(1)}, bf16[1,128,128]{2,1,0:T(8,128)(2,1)S(1)}, u32[]{:S(2)}, u32[]{:S(2)}) collective-permute-start(bf16[1,128,128]{2,1,0:T(8,128)(2,1)S(1)} %shard_map.140.rest_0_), channel_id=1, source_target_pairs={{0,1},{1,0},{2,3},{3,2},{4,5},{5,4},{6,7},{7,6},{8,9},{9,8},{10,11... | collective-permute-start | bytes 98312 | tf_op jit(solution)/shard_map/ppermute | solution.py:21
  8.0 3.8 %collective-permute-start.1 = (f32[24,128]{1,0:T(8,128)S(1)}, f32[24,128]{1,0:T(8,128)S(1)}, u32[]{:S(2)}, u32[]{:S(2)}) collective-permute-start(f32[24,128]{1,0:T(8,128)S(1)} %shard_map.141), channel_id=1, source_target_pairs={{0,4},{4,0},{8,12},{12,8},{1,5},{5,1},{9,13},{13,9},{2,6},{6,2},{1... | collective-permute-start | bytes 36872 | tf_op jit(solution)/shard_map/ppermute | solution.py:31
  10.1 6.8 %collective-permute-start.5 = (bf16[128,640]{1,0:T(8,128)(2,1)S(1)}, bf16[128,640]{1,0:T(8,128)(2,1)S(1)}, u32[]{:S(2)}, u32[]{:S(2)}) collective-permute-start(bf16[128,640]{1,0:T(8,128)(2,1)S(1)} %collective-permute-done.3.rest_5_), channel_id=1, source_target_pairs={{0,16},{16,0},{1,17},{17,1},{2,18},{18,2},{3,19},{19,3},{4,20},{20... | collective-permute-start | bytes 491528 | tf_op jit(solution)/shard_map/ppermute | solution.py:21
  11.7 5.3 %collective-permute-start.4 = (bf16[128,640]{1,0:T(8,128)(2,1)S(1)}, bf16[128,640]{1,0:T(8,128)(2,1)S(1)}, u32[]{:S(2)}, u32[]{:S(2)}) collective-permute-start(bf16[128,640]{1,0:T(8,128)(2,1)S(1)} %collective-permute-done.3.rest_5_), channel_id=1, source_target_pairs={{0,1},{1,0},{2,3},{3,2},{4,5},{5,4},{6,7},{7,6},{8,9},{9,8},{10,11... | collective-permute-start | bytes 491528 | tf_op jit(solution)/shard_map/ppermute | solution.py:21
  11.8 5.1 %collective-permute-start.2 = (f32[48,128]{1,0:T(8,128)S(1)}, f32[48,128]{1,0:T(8,128)S(1)}, u32[]{:S(2)}, u32[]{:S(2)}) collective-permute-start(f32[48,128]{1,0:T(8,128)S(1)} %pad_maximum_fusion.1), channel_id=1, source_target_pairs={{0,8},{4,12},{8,0},{12,4},{1,9},{5,13},{9,1},{13,5},{2,10},{6,14},... | collective-permute-start | bytes 73736 | tf_op jit(solution)/shard_map/ppermute | solution.py:31
  17.0 2.2 %collective-permute-start.8 = (bf16[128,1408]{1,0:T(8,128)(2,1)S(1)}, bf16[128,1408]{1,0:T(8,128)(2,1)S(1)}, u32[]{:S(2)}, u32[]{:S(2)}) collective-permute-start(bf16[128,1408]{1,0:T(8,128)(2,1)S(1)} %shard_map.143.rest_9_), channel_id=1, source_target_pairs={{0,1},{1,0},{2,3},{3,2},{4,5},{5,4},{6,7},{7,6},{8,9},{9,8},{10,11... | collective-permute-start | bytes 1081352 | tf_op jit(solution)/shard_map/ppermute | solution.py:21
  17.0 2.1 %collective-permute-start.6 = (bf16[128,640]{1,0:T(8,128)(2,1)S(1)}, bf16[128,640]{1,0:T(8,128)(2,1)S(1)}, u32[]{:S(2)}, u32[]{:S(2)}) collective-permute-start(bf16[128,640]{1,0:T(8,128)(2,1)S(1)} %collective-permute-done.5.refs_2_.rest_7_), channel_id=1, source_target_pairs={{0,1},{1,0},{2,3},{3,2},{4,5},{5,4},{6,7},{7,6},{8,9},{9,8},{10,11... | collective-permute-start | bytes 491528 | tf_op jit(solution)/shard_map/ppermute | solution.py:21

commit v12 on v11

--- a/solution.py
+++ b/solution.py
@@ -77,24 +77,29 @@
     )
 
 
-def first_kernel(dims, scalar_ref, owner_ref, enc_w_ref, dec_w_ref, settings_ref, scale_w_ref, shift_w_ref, *rest):
-    steps, layers, bands, local, members, lon, chans, vp, fp, turns = dims
-    fields, rest = rest[:bands], rest[bands:]
-    everyone, rest = rest[0], rest[1:]
-    forced = enc_w_ref.shape[0] - dec_w_ref.shape[0]
-    used = bands * local * steps * forced
-    group = [everyone.at[k * (used + 8) : (k + 1) * (used + 8)] for k in range(members * turns)]
-    field_ref, scale_ref, shift_ref, enc_ref, dec_ref, hidden_ref, taps_ref, turned, lines = rest
+def prepare_kernel(dims, scalar_ref, enc_w_ref, dec_w_ref, *rest):
+    steps, bands, local, vp, fp = dims
+    fields, (field_ref, enc_ref, dec_ref, lifted_ref, turned) = rest[:bands], rest[bands:]
+    for b in range(bands):
+        field_ref[b * local : (b + 1) * local] = from_place([f[...] for f in fields], scalar_ref[1], b)
     varied = dec_w_ref.shape[0]
+    forced = enc_w_ref.shape[0] - varied
     turned[...] = jnp.zeros(turned.shape, turned.dtype)
     turned[0:varied] = enc_w_ref[0:varied].astype(jnp.float32)
     turned[vp : vp + forced] = enc_w_ref[varied : varied + forced].astype(jnp.float32)
     enc_ref[...] = turned[...].T.astype(jnp.bfloat16)
     dec_ref[...] = jnp.zeros(dec_ref.shape, dec_ref.dtype)
     dec_ref[0:varied, :] = dec_w_ref[...]
-    band = scalar_ref[1]
-    for b in range(bands):
-        field_ref[b * local : (b + 1) * local] = from_place([f[...] for f in fields], band, b)
+    for i in range(bands * local):
+        lifted_ref[i] = jnp.dot(enc_ref[:, 0:vp], field_ref[i, 0:vp, :], preferred_element_type=jnp.float32)
+
+
+def first_kernel(dims, scalar_ref, owner_ref, enc_ref, settings_ref, scale_w_ref, shift_w_ref, *rest):
+    steps, layers, bands, local, members, lon, chans, vp, fp, turns, forced = dims
+    field_ref, lifted_ref, everyone, force_ref, scale_ref, shift_ref, hidden_ref, taps_ref, lines = rest
+    used = bands * local * steps * forced
+    group = [everyone.at[k * (used + 8) : (k + 1) * (used + 8)] for k in range(members * turns)]
+    force_ref[...] = jnp.zeros(force_ref.shape, force_ref.dtype)
     for i in range(bands * local):
         for t in range(steps):
             rows = slice((i * steps + t) * forced, (i * steps + t + 1) * forced)
@@ -102,7 +107,7 @@
             force = group[0][rows, :]
             for k in range(1, members * turns):
                 force = jnp.where(place == k, group[k][rows, :], force)
-            field_ref[i, vp + fp * t : vp + fp * t + forced, :] = force.astype(jnp.bfloat16)
+            force_ref[i, fp * t : fp * t + forced, :] = force.astype(jnp.bfloat16)
 
     settings = settings_ref[...]
     numbers = lax.broadcasted_iota(jnp.int32, settings.shape, 1).astype(jnp.float32)
@@ -120,7 +125,9 @@
     if turns == 1:
         for i in range(bands * local):
             land = field_ref[i, vp + fp * steps : vp + fp * steps + 1, :].astype(jnp.float32)
-            lifted = jnp.dot(enc_ref[...], field_ref[i, 0 : vp + fp, :], preferred_element_type=jnp.float32)
+            lifted = lifted_ref[i] + jnp.dot(
+                enc_ref[:, vp : vp + fp], force_ref[i, 0:fp, :], preferred_element_type=jnp.float32
+            )
             for m in range(members):
                 cols = slice(m * lon, (m + 1) * lon)
                 value = land * (lifted * scale_ref[0, :, cols] + shift_ref[0, :, cols])
@@ -146,7 +153,7 @@
     )(section, *earlier)
 
 
-def window_kernel(dims, scalar_ref, field_ref, scale_ref, shift_ref, enc_ref, dec_ref, *rest):
+def window_kernel(dims, scalar_ref, field_ref, force_ref, scale_ref, shift_ref, enc_ref, dec_ref, *rest):
     steps, layers, bands, local, members, lon, chans, vp, fp, turns, groups = dims
     lat = bands * local
     hidden, taps = rest[:2]
@@ -190,7 +197,7 @@
 
     def encode(step, turn):
         for i in range(lat):
-            force = field_ref[i, vp + fp * step : vp + fp * (step + 1), :]
+            force = force_ref[i, fp * step : fp * (step + 1), :]
             for m in range(members):
                 inputs[i, vp : vp + fp, columns(m)] = force
                 if step == 0:
@@ -346,26 +353,35 @@
     group = by_doubling(group, "members")
 
     dims = (steps, layers, bands, local, at_once, lon, chans, vp, fp, turns)
-    field, scale, shift, enc, dec, hidden, taps = pl.pallas_call(
-        functools.partial(first_kernel, dims),
+    field, enc, dec, lifted = pl.pallas_call(
+        functools.partial(prepare_kernel, (steps, bands, local, vp, fp)),
         out_shape=(
             jax.ShapeDtypeStruct((lat, vp + fp * steps + BF16_ROWS, lon), jnp.bfloat16),
+            jax.ShapeDtypeStruct((chans, vp + fp), jnp.bfloat16),
+            jax.ShapeDtypeStruct((vp, chans), jnp.bfloat16),
+            jax.ShapeDtypeStruct((lat, chans, lon), jnp.float32),
+        ),
+        in_specs=[smem] + [vmem] * (2 + bands),
+        out_specs=(vmem,) * 4,
+        scratch_shapes=[pltpu.VMEM((vp + fp, chans), jnp.float32)],
+        compiler_params=small,
+        cost_estimate=free,
+    )(scalars, encode_weight.T, decode_weight, *fields)
+    force, scale, shift, hidden, taps = pl.pallas_call(
+        functools.partial(first_kernel, dims + (forced,)),
+        out_shape=(
+            jax.ShapeDtypeStruct((lat, fp * steps, lon), jnp.bfloat16),
             jax.ShapeDtypeStruct((turns, chans, wide), jnp.float32),
             jax.ShapeDtypeStruct((turns, chans, wide), jnp.float32),
-            jax.ShapeDtypeStruct((chans, vp + fp), jnp.bfloat16),
-            jax.ShapeDtypeStruct((vp, chans), jnp.bfloat16),
             jax.ShapeDtypeStruct((lat, chans, wide), jnp.bfloat16),
             jax.ShapeDtypeStruct((lat * 3 * chans, wide), jnp.bfloat16),
         ),
-        in_specs=[smem, smem] + [vmem] * (6 + bands),
-        out_specs=(vmem,) * 7,
-        scratch_shapes=[
-            pltpu.VMEM((vp + fp, chans), jnp.float32),
-            pltpu.VMEM((-(-2 * members // 8) * 8, chans), jnp.float32),
-        ],
+        in_specs=[smem, smem] + [vmem] * 7,
+        out_specs=(vmem,) * 5,
+        scratch_shapes=[pltpu.VMEM((-(-2 * members // 8) * 8, chans), jnp.float32)],
         compiler_params=small,
         cost_estimate=free,
-    )(scalars, atmos_owner[0], encode_weight.T, decode_weight, settings.T, scale_weight, shift_weight, *fields, group)
+    )(scalars, atmos_owner[0], enc, settings.T, scale_weight, shift_weight, field, lifted, group)
 
     blocks = [conv_weight[0], point_weight[0], spread]
     for k in range(layers - 1):
@@ -374,7 +390,7 @@
         blocks += early
         for shared in shares[1:]:
             blocks += all_along(shared, "rows")
-        blocks += all_along(after(direct[k], group, *shares[1:], *early[1:]), "rows")
+        blocks += all_along(after(direct[k], group, lifted, *shares[1:], *early[1:]), "rows")
 
     scratch = [
         pltpu.VMEM((layers, chans, 10 * chans + LANES), jnp.bfloat16),
@@ -392,12 +408,12 @@
             jax.ShapeDtypeStruct((local, varied, lon), jnp.bfloat16),
             jax.ShapeDtypeStruct((varied, local, lon), jnp.float32),
         ),
-        in_specs=[smem] + [vmem] * 7 + [whole] * len(blocks),
+        in_specs=[smem] + [vmem] * 8 + [whole] * len(blocks),
         out_specs=(vmem, vmem),
         scratch_shapes=scratch,
         compiler_params=large,
         cost_estimate=free,
-    )(scalars, field, scale, shift, enc, dec, hidden, taps, *blocks)
+    )(scalars, field, force, scale, shift, enc, dec, hidden, taps, *blocks)
     return final[None, None], jnp.swapaxes(mean, 0, 1)[None]
 def solution(mesh):
     in_specs = (

time: 27.6 us -> 27.7 us (level)
  Pallas kernels: 10.4 us -> 11.3 us
  waiting for transfers between devices: 2.64 us -> 1.79 us
    pallas_call x1 -> x2, Pallas kernels: 1.61 us -> 2.57 us  [the longest x1 1.77 us: per_device(): pl.pallas_call(functools.partial(first_kernel, dims + (forced,)), out_sha...]
    ppermute x2, waiting for transfers between devices: 2.21 us -> 1.41 us  [by_doubling(): partner = lax.ppermute(block, axis, [(i, i ^ reach) for i in range(size)])]
  transfers between devices with their start and end apart: 9 -> 9, of which waited for: 3 -> 3; matrix products, arithmetic and copies ran while one was open for 5% -> 5% of each run, Pallas kernels for 8% -> 11%
where the time goes in v12:
time: 27.7 us; the launch traced here: 27.5 us
  Pallas kernels  11.3 us (41%)
  starting transfers between devices  10.4 us (38%)
  local copies, waits for them, and re-layouts  2.23 us (8%)
  waiting for transfers between devices  1.79 us (6%)
  between operations  1.61 us (6%)
    pallas_call x1, Pallas kernels, per_device(): pl.pallas_call(functools.partial(window_kernel, dims + (groups,)), out_sh...  8.19 us
    ppermute x7, starting transfers between devices, passed_along(): lax.ppermute(block, axis, [(i, (i + distance) % size) for i in range(size)])  5.28 us
    ppermute x2, starting transfers between devices, by_doubling(): partner = lax.ppermute(block, axis, [(i, i ^ reach) for i in range(size)])  5.16 us
    pallas_call x1, Pallas kernels, per_device(): pl.pallas_call(functools.partial(first_kernel, dims + (forced,)), out_sha...  1.77 us
    ppermute x2, waiting for transfers between devices, by_doubling(): partner = lax.ppermute(block, axis, [(i, i ^ reach) for i in range(size)])  1.41 us
    slice x1, local copies, waits for them, and re-layouts, per_device(): conv[:, groups * share:]  1.08 us
    dynamic_slice x1, local copies, waits for them, and re-layouts, per_device(): lax.dynamic_slice(conv, (band * part, places[3] * share), (part, share))  0.98 us
    pallas_call x1, Pallas kernels, per_device(): pl.pallas_call(functools.partial(prepare_kernel, (steps, bands, local, vp...  0.8 us
  transfers between devices with their start and end apart: 9, of which 3 were waited for; matrix products, arithmetic and copies ran while one was open for 5% of the time, Pallas kernels for 11%

profile of v12, /device:TPU:0, one launch (start us, length us, event | category | flops | bytes accessed | tf_op | source)
XLA Modules:
  0.0 27.5 jit_solution(11533224320692932577)
XLA Ops:
  0.6 0.0 copy-start.11
  0.6 0.0 copy-start.1
  0.7 1.0 %dynamic-slice_bitcast_fusion = bf16[128,640]{1,0:T(8,128)(2,1)S(1)} fusion(bf16[1,256,2304]{2,1,0:T(8,128)(2,1)} %param.22, s32[]{:T(128)S(6)} %select_n.7, s32[]{:T(128)S(6)} %select_n.8), kind=kLoop, calls=%fused_computation.5 | loop fusion | bytes 327688 | tf_op jit(solution)/shard_map/dynamic_slice | solution.py:331
  1.6 0.0 copy-start.4
  1.7 0.0 copy-start.8
  1.7 0.0 copy-start.9
  1.7 3.0 %collective-permute-start.3 = (bf16[128,640]{1,0:T(8,128)(2,1)S(1)}, bf16[128,640]{1,0:T(8,128)(2,1)S(1)}, u32[]{:S(2)}, u32[]{:S(2)}) collective-permute-start(bf16[128,640]{1,0:T(8,128)(2,1)S(1)} %dynamic-slice_bitcast_fusion), channel_id=1, source_target_pairs={{0,2},{2,0},{1,3},{3,1},{4,6},{6,4},{5,7},{7,5},{8,10},{10,8},{9,1... | collective-permute-start | bytes 491528 | tf_op jit(solution)/shard_map/ppermute | solution.py:21
  4.7 1.1 %slice.4 = bf16[256,1024]{1,0:T(8,128)(2,1)S(1)} slice(bf16[256,2304]{1,0:T(8,128)(2,1)} %bitcast.17), slice={[0:256], [1280:2304]} | slice | bytes 1048576 | tf_op jit(solution)/shard_map/slice | solution.py:333
  5.8 0.0 copy-done.11
  5.8 0.1 broadcast_in_dim.4.rest_4_
  5.9 0.0 copy-done.1
  6.0 0.0 copy-start.5
  6.0 0.0 copy-start.6
  6.0 0.0 copy-start.7
  6.0 0.0 copy-start.10
  6.0 0.1 collective-permute-start.7
  6.1 0.0 copy-done.4
  6.1 0.0 copy-done.8
  6.1 0.0 copy-done.9
  6.1 0.0 copy-start
  6.2 0.1 collective-permute-start
  6.2 0.1 pad_add_fusion.scalar_ref.place_ref
  7.1 0.4 %collective-permute-done.rest_1_ = bf16[1,128,128]{2,1,0:T(8,128)(2,1)S(1)} collective-permute-done((bf16[1,128,128]{2,1,0:T(8,128)(2,1)S(1)}, bf16[1,128,128]{2,1,0:T(8,128)(2,1)S(1)}, u32[]{:S(2)}, u32[]{:S(2)}) %collective-permute-start) | collective-permute-done | bytes 32800 | tf_op jit(solution)/shard_map/ppermute | solution.py:21
  7.4 0.6 %shard_map.142 = f32[24,128]{1,0:T(8,128)S(1)} custom-call(s32[4]{0:T(128)S(1)} %pad_add_fusion.scalar_ref.place_ref, s32[1]{0:T(128)S(6)} %copy.18.index_ref, bf16[1,128,128]{2,1,0:T(8,128)(2,1)S(1)} %shard_map.140.rest_0_, bf16[1,128,128]{2,1,0:T(8,128)(2,1)S(1)} %collective-permute-done.rest_1_), custom_call_target="tpu_custom_call" | custom-call | tf_op jit(solution)/shard_map/pallas_call | solution.py:345
  8.0 2.1 %collective-permute-start.1 = (f32[24,128]{1,0:T(8,128)S(1)}, f32[24,128]{1,0:T(8,128)S(1)}, u32[]{:S(2)}, u32[]{:S(2)}) collective-permute-start(f32[24,128]{1,0:T(8,128)S(1)} %shard_map.142), channel_id=1, source_target_pairs={{0,4},{4,0},{8,12},{12,8},{1,5},{5,1},{9,13},{13,9},{2,6},{6,2},{1... | collective-permute-start | bytes 36872 | tf_op jit(solution)/shard_map/ppermute | solution.py:31
  10.1 0.0 collective-permute-done.3.rest_5_
  10.1 1.5 %collective-permute-start.5 = (bf16[128,640]{1,0:T(8,128)(2,1)S(1)}, bf16[128,640]{1,0:T(8,128)(2,1)S(1)}, u32[]{:S(2)}, u32[]{:S(2)}) collective-permute-start(bf16[128,640]{1,0:T(8,128)(2,1)S(1)} %collective-permute-done.3.rest_5_), channel_id=1, source_target_pairs={{0,16},{16,0},{1,17},{17,1},{2,18},{18,2},{3,19},{19,3},{4,20},{20... | collective-permute-start | bytes 491528 | tf_op jit(solution)/shard_map/ppermute | solution.py:21
  11.6 0.0 collective-permute-start.4
  11.7 0.1 collective-permute-done.1
  11.8 3.0 %collective-permute-start.2 = (f32[48,128]{1,0:T(8,128)S(1)}, f32[48,128]{1,0:T(8,128)S(1)}, u32[]{:S(2)}, u32[]{:S(2)}) collective-permute-start(f32[48,128]{1,0:T(8,128)S(1)} %pad_maximum_fusion.1), channel_id=1, source_target_pairs={{0,8},{4,12},{8,0},{12,4},{1,9},{5,13},{9,1},{13,5},{2,10},{6,14},... | collective-permute-start | bytes 73736 | tf_op jit(solution)/shard_map/ppermute | solution.py:31
  14.8 0.0 copy-done.2
  14.8 0.0 copy-done.3
  14.8 0.8 %shard_map.141 = (bf16[2,128,128]{2,1,0:T(8,128)(2,1)S(1)}, bf16[256,96]{1,0:T(8,128)(2,1)S(1)}, bf16[80,256]{1,0:T(8,128)(2,1)S(1)}, f32[2,256,128]{2,1,0:T(8,128)S(1)}) custom-call(s32[4]{0:T(128)S(1)} %pad_add_fusion.scalar_ref.place_ref, bf16[81,256]{1,0:T(8,128)(2,1)S(1)} %bitcast.21, bf16[77,256]{1,0:T(8,128)(2,1)S(1)} %copy-done.3, ...), custom_call_target="tpu_custom_call" | custom-call | tf_op jit(solution)/shard_map/pallas_call | solution.py:356
  15.6 1.3 %collective-permute-done.2 = f32[48,128]{1,0:T(8,128)S(1)} collective-permute-done((f32[48,128]{1,0:T(8,128)S(1)}, f32[48,128]{1,0:T(8,128)S(1)}, u32[]{:S(2)}, u32[]{:S(2)}) %collective-permute-start.2) | collective-permute-done | bytes 24608 | tf_op jit(solution)/shard_map/ppermute | solution.py:31
  16.9 0.0 collective-permute-done.5.refs_3_.rest_7_
  16.9 0.0 collective-permute-done.4.refs_4_.rest_6_
  16.9 0.0 collective-permute-done.7.refs_0_
  16.9 0.1 collective-permute-start.8
  17.0 0.5 %collective-permute-start.6 = (bf16[128,640]{1,0:T(8,128)(2,1)S(1)}, bf16[128,640]{1,0:T(8,128)(2,1)S(1)}, u32[]{:S(2)}, u32[]{:S(2)}) collective-permute-start(bf16[128,640]{1,0:T(8,128)(2,1)S(1)} %collective-permute-done.5.refs_3_.rest_7_), channel_id=1, source_target_pairs={{0,1},{1,0},{2,3},{3,2},{4,5},{5,4},{6,7},{7,6},{8,9},{9,8},{10,11... | collective-permute-start | bytes 491528 | tf_op jit(solution)/shard_map/ppermute | solution.py:21
  17.5 0.0 copy-done.5
  17.5 0.0 copy-done.6
  17.5 0.0 copy-done.7
  17.5 0.0 copy-done.10
  17.5 1.8 %shard_map.143 = (bf16[2,32,128]{2,1,0:T(8,128)(2,1)S(1)}, f32[1,256,512]{2,1,0:T(8,128)S(1)}, f32[1,256,512]{2,1,0:T(8,128)S(1)}, bf16[2,256,512]{2,1,0:T(8,128)(2,1)S(1)}, bf16[1536,512]{1,0:T(8,128)(2,1)S(1)}) custom-call(s32[4]{0:T(128)S(1)} %pad_add_fusion.scalar_ref.place_ref, s32[2]{0:T(128)S(1)} %bitcast.25, ...), custom_call_target="tpu_custom_call" | custom-call | tf_op jit(solution)/shard_map/pallas_call | solution.py:370
  19.3 0.0 collective-permute-done.6.rest_8_
  19.3 0.0 collective-permute-done.8.rest_10_
  19.3 0.0 copy-done
  19.3 8.2 %shard_map.145 = (bf16[1,77,128]{2,1,0:T(8,128)(2,1)}, f32[77,1,128]{2,1,0:T(1,128)}) custom-call(s32[4]{0:T(128)S(1)} %pad_add_fusion.scalar_ref.place_ref, bf16[2,128,128]{2,1,0:T(8,128)(2,1)S(1)} %get-tuple-element.13.rest_0_.field_ref, bf16[2,32,128]{2,1,0:T(8,128)(2,1)S(1)} %get-tuple-element.16.force_ref, ...), custom_call_target="tpu_custom_call" | custom-call | tf_op jit(solution)/shard_map/pallas_call | solution.py:405
  (8 shorter events, 0.1 us)
Async XLA Ops:
  0.6 5.1 %copy-start.11 = (bf16[1,256]{1,0:T(2,128)(2,1)S(1)}, bf16[1,256]{1,0:T(2,128)(2,1)}, u32[]{:S(2)}) copy-start(bf16[1,256]{1,0:T(2,128)(2,1)} %param.24) | copy-start | bytes 1540
  0.6 5.3 %copy-start.1 = (bf16[1,256,256]{2,1,0:T(8,128)(2,1)S(1)}, bf16[1,256,256]{2,1,0:T(8,128)(2,1)}, u32[]{:S(2)}) copy-start(bf16[1,256,256]{2,1,0:T(8,128)(2,1)} %param.23) | copy-start | bytes 393220
  1.6 4.5 %copy-start.4 = (bf16[1,1,77,128]{3,2,1,0:T(8,128)(2,1)S(1)}, bf16[1,1,77,128]{3,2,1,0:T(8,128)(2,1)}, u32[]{:S(2)}) copy-start(bf16[1,1,77,128]{3,2,1,0:T(8,128)(2,1)} %param.13) | copy-start | bytes 59140
  1.7 4.5 %copy-start.8 = (bf16[1,1,2,1,4,128]{5,4,3,2,1,0:T(4,128)(2,1)S(1)}, bf16[1,1,2,1,4,128]{5,4,3,2,1,0:T(4,128)(2,1)}, u32[]{:S(2)}) copy-start(bf16[1,1,2,1,4,128]{5,4,3,2,1,0:T(4,128)(2,1)} %param.14) | copy-start | bytes 6148
  1.7 4.5 %copy-start.9 = (s32[1,128]{1,0:T(1,128)S(1)}, s32[1,128]{1,0:T(1,128)}, u32[]{:S(2)}) copy-start(s32[1,128]{1,0:T(1,128)} %land_ref.1) | copy-start | bytes 1540
  1.7 8.5 %collective-permute-start.3 = (bf16[128,640]{1,0:T(8,128)(2,1)S(1)}, bf16[128,640]{1,0:T(8,128)(2,1)S(1)}, u32[]{:S(2)}, u32[]{:S(2)}) collective-permute-start(bf16[128,640]{1,0:T(8,128)(2,1)S(1)} %dynamic-slice_bitcast_fusion), channel_id=1, source_target_pairs={{0,2},{2,0},{1,3},{3,1},{4,6},{6,4},{5,7},{7,5},{8,10},{10,8},{9,1... | collective-permute-start | bytes 491528 | tf_op jit(solution)/shard_map/ppermute | solution.py:21
  4.7 10.2 %copy-start.2 = (bf16[256,81]{0,1:T(8,128)(2,1)S(1)}, bf16[256,81]{0,1:T(8,128)(2,1)}, u32[]{:S(2)}) copy-start(bf16[256,81]{0,1:T(8,128)(2,1)} %param.21) | copy-start | bytes 124420
  4.7 10.2 %copy-start.3 = (bf16[77,256]{1,0:T(8,128)(2,1)S(1)}, bf16[77,256]{1,0:T(8,128)(2,1)}, u32[]{:S(2)}) copy-start(bf16[77,256]{1,0:T(8,128)(2,1)} %dec_w_ref.1) | copy-start | bytes 118276
  6.0 11.6 %copy-start.5 = (f32[16,256]{1,0:T(8,128)S(1)}, f32[16,256]{1,0:T(8,128)}, u32[]{:S(2)}) copy-start(f32[16,256]{1,0:T(8,128)} %scale_w_ref.1) | copy-start | bytes 49156
  6.0 11.6 %copy-start.6 = (f32[16,256]{1,0:T(8,128)S(1)}, f32[16,256]{1,0:T(8,128)}, u32[]{:S(2)}) copy-start(f32[16,256]{1,0:T(8,128)} %shift_w_ref.1) | copy-start | bytes 49156
  6.0 11.5 %copy-start.7 = (f32[64,16]{0,1:T(8,128)S(1)}, f32[64,16]{0,1:T(8,128)}, u32[]{:S(2)}) copy-start(f32[64,16]{0,1:T(8,128)} %param.18) | copy-start | bytes 12292
  6.0 11.5 %copy-start.10 = (s32[1,2]{1,0:T(1,128)S(1)}, s32[1,2]{1,0:T(1,128)}, u32[]{:S(2)}) copy-start(s32[1,2]{1,0:T(1,128)} %param.15) | copy-start | bytes 28
  6.0 10.9 %collective-permute-start.7 = (bf16[128,1408]{1,0:T(8,128)(2,1)S(1)}, bf16[128,1408]{1,0:T(8,128)(2,1)S(1)}, u32[]{:S(2)}, u32[]{:S(2)}) collective-permute-start(bf16[128,1408]{1,0:T(8,128)(2,1)S(1)} %fusion.1.earlier_ref), channel_id=1, source_target_pairs={{0,2},{2,0},{1,3},{3,1},{4,6},{6,4},{5,7},{7,5},{8,10},{10,8},{9,1... | collective-permute-start | bytes 1081352 | tf_op jit(solution)/shard_map/ppermute | solution.py:21
  6.1 13.2 %copy-start = (bf16[1,256,2304]{2,1,0:T(8,128)(2,1)S(1)}, bf16[1,256,2304]{2,1,0:T(8,128)(2,1)}, u32[]{:S(2)}) copy-start(bf16[1,256,2304]{2,1,0:T(8,128)(2,1)} %param.22) | copy-start | bytes 3538948
  6.2 1.3 %collective-permute-start = (bf16[1,128,128]{2,1,0:T(8,128)(2,1)S(1)}, bf16[1,128,128]{2,1,0:T(8,128)(2,1)S(1)}, u32[]{:S(2)}, u32[]{:S(2)}) collective-permute-start(bf16[1,128,128]{2,1,0:T(8,128)(2,1)S(1)} %shard_map.140.rest_0_), channel_id=1, source_target_pairs={{0,1},{1,0},{2,3},{3,2},{4,5},{5,4},{6,7},{7,6},{8,9},{9,8},{10,11... | collective-permute-start | bytes 98312 | tf_op jit(solution)/shard_map/ppermute | solution.py:21
  8.0 3.8 %collective-permute-start.1 = (f32[24,128]{1,0:T(8,128)S(1)}, f32[24,128]{1,0:T(8,128)S(1)}, u32[]{:S(2)}, u32[]{:S(2)}) collective-permute-start(f32[24,128]{1,0:T(8,128)S(1)} %shard_map.142), channel_id=1, source_target_pairs={{0,4},{4,0},{8,12},{12,8},{1,5},{5,1},{9,13},{13,9},{2,6},{6,2},{1... | collective-permute-start | bytes 36872 | tf_op jit(solution)/shard_map/ppermute | solution.py:31
  10.1 6.8 %collective-permute-start.5 = (bf16[128,640]{1,0:T(8,128)(2,1)S(1)}, bf16[128,640]{1,0:T(8,128)(2,1)S(1)}, u32[]{:S(2)}, u32[]{:S(2)}) collective-permute-start(bf16[128,640]{1,0:T(8,128)(2,1)S(1)} %collective-permute-done.3.rest_5_), channel_id=1, source_target_pairs={{0,16},{16,0},{1,17},{17,1},{2,18},{18,2},{3,19},{19,3},{4,20},{20... | collective-permute-start | bytes 491528 | tf_op jit(solution)/shard_map/ppermute | solution.py:21
  11.6 5.3 %collective-permute-start.4 = (bf16[128,640]{1,0:T(8,128)(2,1)S(1)}, bf16[128,640]{1,0:T(8,128)(2,1)S(1)}, u32[]{:S(2)}, u32[]{:S(2)}) collective-permute-start(bf16[128,640]{1,0:T(8,128)(2,1)S(1)} %collective-permute-done.3.rest_5_), channel_id=1, source_target_pairs={{0,1},{1,0},{2,3},{3,2},{4,5},{5,4},{6,7},{7,6},{8,9},{9,8},{10,11... | collective-permute-start | bytes 491528 | tf_op jit(solution)/shard_map/ppermute | solution.py:21
  11.8 5.1 %collective-permute-start.2 = (f32[48,128]{1,0:T(8,128)S(1)}, f32[48,128]{1,0:T(8,128)S(1)}, u32[]{:S(2)}, u32[]{:S(2)}) collective-permute-start(f32[48,128]{1,0:T(8,128)S(1)} %pad_maximum_fusion.1), channel_id=1, source_target_pairs={{0,8},{4,12},{8,0},{12,4},{1,9},{5,13},{9,1},{13,5},{2,10},{6,14},... | collective-permute-start | bytes 73736 | tf_op jit(solution)/shard_map/ppermute | solution.py:31
  16.9 2.4 %collective-permute-start.8 = (bf16[128,1408]{1,0:T(8,128)(2,1)S(1)}, bf16[128,1408]{1,0:T(8,128)(2,1)S(1)}, u32[]{:S(2)}, u32[]{:S(2)}) collective-permute-start(bf16[128,1408]{1,0:T(8,128)(2,1)S(1)} %shard_map.144.rest_9_), channel_id=1, source_target_pairs={{0,1},{1,0},{2,3},{3,2},{4,5},{5,4},{6,7},{7,6},{8,9},{9,8},{10,11... | collective-permute-start | bytes 1081352 | tf_op jit(solution)/shard_map/ppermute | solution.py:21
  17.0 2.3 %collective-permute-start.6 = (bf16[128,640]{1,0:T(8,128)(2,1)S(1)}, bf16[128,640]{1,0:T(8,128)(2,1)S(1)}, u32[]{:S(2)}, u32[]{:S(2)}) collective-permute-start(bf16[128,640]{1,0:T(8,128)(2,1)S(1)} %collective-permute-done.5.refs_3_.rest_7_), channel_id=1, source_target_pairs={{0,1},{1,0},{2,3},{3,2},{4,5},{5,4},{6,7},{7,6},{8,9},{9,8},{10,11... | collective-permute-start | bytes 491528 | tf_op jit(solution)/shard_map/ppermute | solution.py:21

commit v13 on v11

--- a/solution.py
+++ b/solution.py
@@ -52,11 +52,11 @@
         field_ref[i, vp + fp * steps : vp + fp * steps + 1] = land_ref[i : i + 1].astype(jnp.bfloat16)
 
 
-def group_kernel(dims, place_ref, index_ref, *rest):
+def group_kernel(dims, index_ref, *rest):
     steps, bands, local, forced, vp, fp = dims
     fields, group_ref = rest[:bands], rest[bands]
     for b in range(bands):
-        field = from_place([f[...] for f in fields], place_ref[1], b)
+        field = from_place([f[...] for f in fields], lax.axis_index("rows"), b)
         for i in range(local):
             for t in range(steps):
                 first = ((b * local + i) * steps + t) * forced
@@ -77,7 +77,7 @@
     )
 
 
-def first_kernel(dims, scalar_ref, owner_ref, enc_w_ref, dec_w_ref, settings_ref, scale_w_ref, shift_w_ref, *rest):
+def first_kernel(dims, owner_ref, enc_w_ref, dec_w_ref, settings_ref, scale_w_ref, shift_w_ref, *rest):
     steps, layers, bands, local, members, lon, chans, vp, fp, turns = dims
     fields, rest = rest[:bands], rest[bands:]
     everyone, rest = rest[0], rest[1:]
@@ -92,13 +92,13 @@
     enc_ref[...] = turned[...].T.astype(jnp.bfloat16)
     dec_ref[...] = jnp.zeros(dec_ref.shape, dec_ref.dtype)
     dec_ref[0:varied, :] = dec_w_ref[...]
-    band = scalar_ref[1]
+    band = lax.axis_index("rows")
     for b in range(bands):
         field_ref[b * local : (b + 1) * local] = from_place([f[...] for f in fields], band, b)
     for i in range(bands * local):
         for t in range(steps):
             rows = slice((i * steps + t) * forced, (i * steps + t + 1) * forced)
-            place = scalar_ref[2] ^ owner_ref[t]
+            place = lax.axis_index("members") ^ owner_ref[0:1, t : t + 1]
             force = group[0][rows, :]
             for k in range(1, members * turns):
                 force = jnp.where(place == k, group[k][rows, :], force)
@@ -146,14 +146,14 @@
     )(section, *earlier)
 
 
-def window_kernel(dims, scalar_ref, field_ref, scale_ref, shift_ref, enc_ref, dec_ref, *rest):
+def window_kernel(dims, field_ref, scale_ref, shift_ref, enc_ref, dec_ref, *rest):
     steps, layers, bands, local, members, lon, chans, vp, fp, turns, groups = dims
     lat = bands * local
     hidden, taps = rest[:2]
     pieces = 3 + (layers - 1) * (groups + 1) * bands
     blocks, rest = rest[2 : 2 + pieces], rest[2 + pieces :]
     final_ref, mean_ref, weights, conv, act, inputs, total, sems = rest[:8]
-    here, band = scalar_ref[0], scalar_ref[1]
+    here, band = lax.axis_index("segment"), lax.axis_index("rows")
     taps_wide, wide = 9 * chans, 3 * chans
     part = chans // bands
 
@@ -165,7 +165,7 @@
         slot = lax.rem(here - k + layers, layers)
         for g in range(groups + 1):
             if g < groups:
-                place = lax.rem(scalar_ref[3] - g + groups, groups)
+                place = lax.rem(lax.axis_index("groups") - g + groups, groups)
                 cols = pl.ds(pl.multiple_of(place * share, LANES), share)
             else:
                 cols = pl.ds(groups * share, 10 * chans + LANES - groups * share)
@@ -302,7 +302,7 @@
     decode_weight,
 ):
     members, layers, bands = (lax.axis_size(a) for a in ("members", "segment", "rows"))
-    here, band = lax.axis_index("segment"), lax.axis_index("rows")
+    band = lax.axis_index("rows")
     _, local, varied, lon = init_state.shape
     steps, forced = forcing_slots.shape[2], forcing_slots.shape[4]
     chans = conv_weight.shape[1]
@@ -317,11 +317,9 @@
 
     groups = lax.axis_size("groups")
     share = 5 * chans // groups
-    places = [here, band, lax.axis_index("members"), lax.axis_index("groups")]
-    scalars = jnp.stack(places).astype(jnp.int32)
     slots = forcing_slots[0, 0].reshape(-1, lon)
     conv = conv_weight[0]
-    relayed = lax.dynamic_slice(conv, (band * part, places[3] * share), (part, share))
+    relayed = lax.dynamic_slice(conv, (band * part, lax.axis_index("groups") * share), (part, share))
     spread = jnp.broadcast_to((norm_gain[0] * 0.5)[:, None], (chans, LANES))
     direct = jnp.concatenate([conv[:, groups * share :], point_weight[0], spread], axis=1)
     direct = lax.dynamic_slice_in_dim(direct, band * part, part, 0)
@@ -338,11 +336,11 @@
     group = pl.pallas_call(
         functools.partial(group_kernel, (steps, bands, local, forced, vp, fp)),
         out_shape=jax.ShapeDtypeStruct((lat * steps * forced + 8, lon), jnp.float32),
-        in_specs=[smem, smem] + [vmem] * bands,
+        in_specs=[smem] + [vmem] * bands,
         out_specs=vmem,
         compiler_params=small,
         cost_estimate=free,
-    )(scalars, param_index, *fields)
+    )(param_index, *fields)
     group = by_doubling(group, "members")
 
     dims = (steps, layers, bands, local, at_once, lon, chans, vp, fp, turns)
@@ -357,7 +355,7 @@
             jax.ShapeDtypeStruct((lat, chans, wide), jnp.bfloat16),
             jax.ShapeDtypeStruct((lat * 3 * chans, wide), jnp.bfloat16),
         ),
-        in_specs=[smem, smem] + [vmem] * (6 + bands),
+        in_specs=[vmem] * (7 + bands),
         out_specs=(vmem,) * 7,
         scratch_shapes=[
             pltpu.VMEM((vp + fp, chans), jnp.float32),
@@ -365,7 +363,7 @@
         ],
         compiler_params=small,
         cost_estimate=free,
-    )(scalars, atmos_owner[0], encode_weight.T, decode_weight, settings.T, scale_weight, shift_weight, *fields, group)
+    )(atmos_owner, encode_weight.T, decode_weight, settings.T, scale_weight, shift_weight, *fields, group)
 
     blocks = [conv_weight[0], point_weight[0], spread]
     for k in range(layers - 1):
@@ -392,12 +390,12 @@
             jax.ShapeDtypeStruct((local, varied, lon), jnp.bfloat16),
             jax.ShapeDtypeStruct((varied, local, lon), jnp.float32),
         ),
-        in_specs=[smem] + [vmem] * 7 + [whole] * len(blocks),
+        in_specs=[vmem] * 7 + [whole] * len(blocks),
         out_specs=(vmem, vmem),
         scratch_shapes=scratch,
         compiler_params=large,
         cost_estimate=free,
-    )(scalars, field, scale, shift, enc, dec, hidden, taps, *blocks)
+    )(field, scale, shift, enc, dec, hidden, taps, *blocks)
     return final[None, None], jnp.swapaxes(mean, 0, 1)[None]
 def solution(mesh):
     in_specs = (

time: 27.6 us -> 26.1 us (0.946)
  Pallas kernels: 10.4 us -> 8.51 us
  waiting for transfers between devices: 2.64 us -> 3.01 us
    pallas_call x1, Pallas kernels: 8.19 us -> 7.4 us  [per_device(): pl.pallas_call(functools.partial(window_kernel, dims + (groups,)), out_sh...]
    ppermute x7, waiting for transfers between devices: 0.42 us -> 1.05 us  [passed_along(): lax.ppermute(block, axis, [(i, (i + distance) % size) for i in range(size)])]
    pallas_call x1, Pallas kernels: 0.55 us -> 0.01 us  [per_device(): pl.pallas_call(functools.partial(group_kernel, (steps, bands, local, forc...]
    pallas_call x1, Pallas kernels: 1.61 us -> 1.09 us  [per_device(): pl.pallas_call(functools.partial(first_kernel, dims), out_shape=(jax.Shap...]
    ppermute x7, starting transfers between devices: 5.25 us -> 5.53 us  [passed_along(): lax.ppermute(block, axis, [(i, (i + distance) % size) for i in range(size)])]
  transfers between devices with their start and end apart: 9 -> 9, of which waited for: 3 -> 4; matrix products, arithmetic and copies ran while one was open for 5% -> 5% of each run, Pallas kernels for 8% -> 4%
where the time goes in v13:
time: 26.1 us; the launch traced here: 25.9 us
  starting transfers between devices  10.5 us (40%)
  Pallas kernels  8.51 us (33%)
  waiting for transfers between devices  3.01 us (12%)
  local copies, waits for them, and re-layouts  2.23 us (9%)
  between operations  1.61 us (6%)
    pallas_call x1, Pallas kernels, per_device(): pl.pallas_call(functools.partial(window_kernel, dims + (groups,)), out_sh...  7.4 us
    ppermute x7, starting transfers between devices, passed_along(): lax.ppermute(block, axis, [(i, (i + distance) % size) for i in range(size)])  5.53 us
    ppermute x2, starting transfers between devices, by_doubling(): partner = lax.ppermute(block, axis, [(i, i ^ reach) for i in range(size)])  4.97 us
    ppermute x2, waiting for transfers between devices, by_doubling(): partner = lax.ppermute(block, axis, [(i, i ^ reach) for i in range(size)])  1.96 us
    pallas_call x1, Pallas kernels, per_device(): pl.pallas_call(functools.partial(first_kernel, dims), out_shape=(jax.Shap...  1.09 us
    slice x1, local copies, waits for them, and re-layouts, per_device(): conv[:, groups * share:]  1.08 us
    ppermute x7, waiting for transfers between devices, passed_along(): lax.ppermute(block, axis, [(i, (i + distance) % size) for i in range(size)])  1.05 us
    dynamic_slice x1, local copies, waits for them, and re-layouts, per_device(): lax.dynamic_slice(conv, (band * part, lax.axis_index('groups') * share),...  0.98 us
  transfers between devices with their start and end apart: 9, of which 4 were waited for; matrix products, arithmetic and copies ran while one was open for 5% of the time, Pallas kernels for 4%

profile of v13, /device:TPU:0, one launch (start us, length us, event | category | flops | bytes accessed | tf_op | source)
XLA Modules:
  0.0 25.9 jit_solution(10561924917734389397)
XLA Ops:
  0.6 0.0 copy-start.11
  0.6 0.0 copy-start.1
  0.7 1.0 %dynamic-slice_bitcast_fusion = bf16[128,640]{1,0:T(8,128)(2,1)S(1)} fusion(bf16[1,256,2304]{2,1,0:T(8,128)(2,1)} %param.22, s32[]{:T(128)S(6)} %select_n.7, s32[]{:T(128)S(6)} %select_n.8), kind=kLoop, calls=%fused_computation.5 | loop fusion | bytes 327688 | tf_op jit(solution)/shard_map/dynamic_slice | solution.py:322
  1.6 0.0 copy-start.4
  1.7 0.0 copy-start.8
  1.7 0.0 copy-start.9
  1.7 3.0 %collective-permute-start.3 = (bf16[128,640]{1,0:T(8,128)(2,1)S(1)}, bf16[128,640]{1,0:T(8,128)(2,1)S(1)}, u32[]{:S(2)}, u32[]{:S(2)}) collective-permute-start(bf16[128,640]{1,0:T(8,128)(2,1)S(1)} %dynamic-slice_bitcast_fusion), channel_id=1, source_target_pairs={{0,2},{2,0},{1,3},{3,1},{4,6},{6,4},{5,7},{7,5},{8,10},{10,8},{9,1... | collective-permute-start | bytes 491528 | tf_op jit(solution)/shard_map/ppermute | solution.py:21
  4.7 1.1 %slice.4 = bf16[256,1024]{1,0:T(8,128)(2,1)S(1)} slice(bf16[256,2304]{1,0:T(8,128)(2,1)} %bitcast.12), slice={[0:256], [1280:2304]} | slice | bytes 1048576 | tf_op jit(solution)/shard_map/slice | solution.py:324
  5.8 0.0 copy-done.11
  5.8 0.1 broadcast_in_dim.4.rest_4_
  5.9 0.0 copy-done.1
  5.9 0.0 copy-start.2
  5.9 0.0 copy-start.3
  5.9 0.0 copy-start.5
  5.9 0.0 copy-start.6
  6.0 0.0 copy-start.7
  6.0 0.0 copy-start.10
  6.0 0.0 copy-start
  6.0 0.1 collective-permute-start.7
  6.1 0.0 copy-done.4
  6.1 0.0 copy-done.8
  6.1 0.0 copy-done.9
  6.2 0.1 collective-permute-start
  7.0 0.4 %collective-permute-done.rest_1_ = bf16[1,128,128]{2,1,0:T(8,128)(2,1)S(1)} collective-permute-done((bf16[1,128,128]{2,1,0:T(8,128)(2,1)S(1)}, bf16[1,128,128]{2,1,0:T(8,128)(2,1)S(1)}, u32[]{:S(2)}, u32[]{:S(2)}) %collective-permute-start) | collective-permute-done | bytes 32800 | tf_op jit(solution)/shard_map/ppermute | solution.py:21
  7.5 2.1 %collective-permute-start.1 = (f32[24,128]{1,0:T(8,128)S(1)}, f32[24,128]{1,0:T(8,128)S(1)}, u32[]{:S(2)}, u32[]{:S(2)}) collective-permute-start(f32[24,128]{1,0:T(8,128)S(1)} %shard_map.141), channel_id=1, source_target_pairs={{0,4},{4,0},{8,12},{12,8},{1,5},{5,1},{9,13},{13,9},{2,6},{6,2},{1... | collective-permute-start | bytes 36872 | tf_op jit(solution)/shard_map/ppermute | solution.py:31
  9.6 0.0 collective-permute-done.3.rest_5_
  9.6 1.9 %collective-permute-start.5 = (bf16[128,640]{1,0:T(8,128)(2,1)S(1)}, bf16[128,640]{1,0:T(8,128)(2,1)S(1)}, u32[]{:S(2)}, u32[]{:S(2)}) collective-permute-start(bf16[128,640]{1,0:T(8,128)(2,1)S(1)} %collective-permute-done.3.rest_5_), channel_id=1, source_target_pairs={{0,16},{16,0},{1,17},{17,1},{2,18},{18,2},{3,19},{19,3},{4,20},{20... | collective-permute-start | bytes 491528 | tf_op jit(solution)/shard_map/ppermute | solution.py:21
  11.5 0.0 collective-permute-start.4
  11.5 0.0 collective-permute-done.1
  11.5 2.8 %collective-permute-start.2 = (f32[48,128]{1,0:T(8,128)S(1)}, f32[48,128]{1,0:T(8,128)S(1)}, u32[]{:S(2)}, u32[]{:S(2)}) collective-permute-start(f32[48,128]{1,0:T(8,128)S(1)} %pad_maximum_fusion.1), channel_id=1, source_target_pairs={{0,8},{4,12},{8,0},{12,4},{1,9},{5,13},{9,1},{13,5},{2,10},{6,14},... | collective-permute-start | bytes 73736 | tf_op jit(solution)/shard_map/ppermute | solution.py:31
  14.3 2.0 %collective-permute-done.2 = f32[48,128]{1,0:T(8,128)S(1)} collective-permute-done((f32[48,128]{1,0:T(8,128)S(1)}, f32[48,128]{1,0:T(8,128)S(1)}, u32[]{:S(2)}, u32[]{:S(2)}) %collective-permute-start.2) | collective-permute-done | bytes 24608 | tf_op jit(solution)/shard_map/ppermute | solution.py:31
  16.3 0.0 collective-permute-done.5.refs_2_.rest_7_
  16.3 0.0 collective-permute-done.4.refs_3_.rest_6_
  16.3 0.3 %collective-permute-done.7.refs_0_ = bf16[128,1408]{1,0:T(8,128)(2,1)S(1)} collective-permute-done((bf16[128,1408]{1,0:T(8,128)(2,1)S(1)}, bf16[128,1408]{1,0:T(8,128)(2,1)S(1)}, u32[]{:S(2)}, u32[]{:S(2)}) %collective-permute-start.7) | collective-permute-done | bytes 360480 | tf_op jit(solution)/shard_map/ppermute | solution.py:21
  16.6 0.0 collective-permute-start.8
  16.6 0.5 %collective-permute-start.6 = (bf16[128,640]{1,0:T(8,128)(2,1)S(1)}, bf16[128,640]{1,0:T(8,128)(2,1)S(1)}, u32[]{:S(2)}, u32[]{:S(2)}) collective-permute-start(bf16[128,640]{1,0:T(8,128)(2,1)S(1)} %collective-permute-done.5.refs_2_.rest_7_), channel_id=1, source_target_pairs={{0,1},{1,0},{2,3},{3,2},{4,5},{5,4},{6,7},{7,6},{8,9},{9,8},{10,11... | collective-permute-start | bytes 491528 | tf_op jit(solution)/shard_map/ppermute | solution.py:21
  17.1 0.0 copy-done.2
  17.1 0.0 copy-done.3
  17.1 0.0 copy-done.5
  17.1 0.0 copy-done.6
  17.1 0.0 copy-done.7
  17.1 0.0 copy-done.10
  17.1 1.1 %shard_map.142 = (bf16[2,128,128]{2,1,0:T(8,128)(2,1)S(1)}, f32[1,256,512]{2,1,0:T(8,128)S(1)}, f32[1,256,512]{2,1,0:T(8,128)S(1)}, bf16[256,96]{1,0:T(8,128)(2,...) custom-call(s32[1,2]{1,0:T(1,128)S(1)} %copy-done.10, ...), custom_call_target="tpu_custom_call" | custom-call | tf_op jit(solution)/shard_map/pallas_call | solution.py:347
  18.2 0.3 %collective-permute-done.6.rest_8_ = bf16[128,640]{1,0:T(8,128)(2,1)S(1)} collective-permute-done((bf16[128,640]{1,0:T(8,128)(2,1)S(1)}, bf16[128,640]{1,0:T(8,128)(2,1)S(1)}, u32[]{:S(2)}, u32[]{:S(2)}) %collective-permute-start.6) | collective-permute-done | bytes 163872 | tf_op jit(solution)/shard_map/ppermute | solution.py:21
  18.5 0.0 collective-permute-done.8.rest_10_
  18.5 0.0 copy-done
  18.5 7.4 %shard_map.144 = (bf16[1,77,128]{2,1,0:T(8,128)(2,1)}, f32[77,1,128]{2,1,0:T(1,128)}) custom-call(bf16[2,128,128]{2,1,0:T(8,128)(2,1)S(1)} %get-tuple-element.11.field_ref, f32[1,256,512]{2,1,0:T(8,128)S(1)} %get-tuple-element.12.scale_ref, f32[1,256,512]{2,1,0:T(8,128)S(1)} %get-tuple-element.13.shift_ref, bf16[256,96]{1,0:T(8,128)(2,1)S(1)} %get-tuple-element.14.enc_ref, ...), custom_call_target="tpu_custom_call" | custom-call | tf_op jit(solution)/shard_map/pallas_call | solution.py:387
  (7 shorter events, 0.1 us)
Async XLA Ops:
  0.6 5.1 %copy-start.11 = (bf16[1,256]{1,0:T(2,128)(2,1)S(1)}, bf16[1,256]{1,0:T(2,128)(2,1)}, u32[]{:S(2)}) copy-start(bf16[1,256]{1,0:T(2,128)(2,1)} %param.24) | copy-start | bytes 1540
  0.6 5.3 %copy-start.1 = (bf16[1,256,256]{2,1,0:T(8,128)(2,1)S(1)}, bf16[1,256,256]{2,1,0:T(8,128)(2,1)}, u32[]{:S(2)}) copy-start(bf16[1,256,256]{2,1,0:T(8,128)(2,1)} %param.23) | copy-start | bytes 393220
  1.6 4.5 %copy-start.4 = (bf16[1,1,77,128]{3,2,1,0:T(8,128)(2,1)S(1)}, bf16[1,1,77,128]{3,2,1,0:T(8,128)(2,1)}, u32[]{:S(2)}) copy-start(bf16[1,1,77,128]{3,2,1,0:T(8,128)(2,1)} %param.13) | copy-start | bytes 59140
  1.7 4.5 %copy-start.8 = (bf16[1,1,2,1,4,128]{5,4,3,2,1,0:T(4,128)(2,1)S(1)}, bf16[1,1,2,1,4,128]{5,4,3,2,1,0:T(4,128)(2,1)}, u32[]{:S(2)}) copy-start(bf16[1,1,2,1,4,128]{5,4,3,2,1,0:T(4,128)(2,1)} %param.14) | copy-start | bytes 6148
  1.7 4.5 %copy-start.9 = (s32[1,128]{1,0:T(1,128)S(1)}, s32[1,128]{1,0:T(1,128)}, u32[]{:S(2)}) copy-start(s32[1,128]{1,0:T(1,128)} %land_ref.1) | copy-start | bytes 1540
  1.7 7.9 %collective-permute-start.3 = (bf16[128,640]{1,0:T(8,128)(2,1)S(1)}, bf16[128,640]{1,0:T(8,128)(2,1)S(1)}, u32[]{:S(2)}, u32[]{:S(2)}) collective-permute-start(bf16[128,640]{1,0:T(8,128)(2,1)S(1)} %dynamic-slice_bitcast_fusion), channel_id=1, source_target_pairs={{0,2},{2,0},{1,3},{3,1},{4,6},{6,4},{5,7},{7,5},{8,10},{10,8},{9,1... | collective-permute-start | bytes 491528 | tf_op jit(solution)/shard_map/ppermute | solution.py:21
  5.9 11.2 %copy-start.2 = (bf16[256,81]{0,1:T(8,128)(2,1)S(1)}, bf16[256,81]{0,1:T(8,128)(2,1)}, u32[]{:S(2)}) copy-start(bf16[256,81]{0,1:T(8,128)(2,1)} %param.21) | copy-start | bytes 124420
  5.9 11.2 %copy-start.3 = (bf16[77,256]{1,0:T(8,128)(2,1)S(1)}, bf16[77,256]{1,0:T(8,128)(2,1)}, u32[]{:S(2)}) copy-start(bf16[77,256]{1,0:T(8,128)(2,1)} %dec_w_ref.1) | copy-start | bytes 118276
  5.9 11.2 %copy-start.5 = (f32[16,256]{1,0:T(8,128)S(1)}, f32[16,256]{1,0:T(8,128)}, u32[]{:S(2)}) copy-start(f32[16,256]{1,0:T(8,128)} %scale_w_ref.1) | copy-start | bytes 49156
  5.9 11.2 %copy-start.6 = (f32[16,256]{1,0:T(8,128)S(1)}, f32[16,256]{1,0:T(8,128)}, u32[]{:S(2)}) copy-start(f32[16,256]{1,0:T(8,128)} %shift_w_ref.1) | copy-start | bytes 49156
  6.0 11.2 %copy-start.7 = (f32[64,16]{0,1:T(8,128)S(1)}, f32[64,16]{0,1:T(8,128)}, u32[]{:S(2)}) copy-start(f32[64,16]{0,1:T(8,128)} %param.18) | copy-start | bytes 12292
  6.0 11.2 %copy-start.10 = (s32[1,2]{1,0:T(1,128)S(1)}, s32[1,2]{1,0:T(1,128)}, u32[]{:S(2)}) copy-start(s32[1,2]{1,0:T(1,128)} %owner_ref.1) | copy-start | bytes 28
  6.0 12.5 %copy-start = (bf16[1,256,2304]{2,1,0:T(8,128)(2,1)S(1)}, bf16[1,256,2304]{2,1,0:T(8,128)(2,1)}, u32[]{:S(2)}) copy-start(bf16[1,256,2304]{2,1,0:T(8,128)(2,1)} %param.22) | copy-start | bytes 3538948
  6.0 10.6 %collective-permute-start.7 = (bf16[128,1408]{1,0:T(8,128)(2,1)S(1)}, bf16[128,1408]{1,0:T(8,128)(2,1)S(1)}, u32[]{:S(2)}, u32[]{:S(2)}) collective-permute-start(bf16[128,1408]{1,0:T(8,128)(2,1)S(1)} %fusion.1.earlier_ref), channel_id=1, source_target_pairs={{0,2},{2,0},{1,3},{3,1},{4,6},{6,4},{5,7},{7,5},{8,10},{10,8},{9,1... | collective-permute-start | bytes 1081352 | tf_op jit(solution)/shard_map/ppermute | solution.py:21
  6.2 1.3 %collective-permute-start = (bf16[1,128,128]{2,1,0:T(8,128)(2,1)S(1)}, bf16[1,128,128]{2,1,0:T(8,128)(2,1)S(1)}, u32[]{:S(2)}, u32[]{:S(2)}) collective-permute-start(bf16[1,128,128]{2,1,0:T(8,128)(2,1)S(1)} %shard_map.140.rest_0_), channel_id=1, source_target_pairs={{0,1},{1,0},{2,3},{3,2},{4,5},{5,4},{6,7},{7,6},{8,9},{9,8},{10,11... | collective-permute-start | bytes 98312 | tf_op jit(solution)/shard_map/ppermute | solution.py:21
  7.5 4.0 %collective-permute-start.1 = (f32[24,128]{1,0:T(8,128)S(1)}, f32[24,128]{1,0:T(8,128)S(1)}, u32[]{:S(2)}, u32[]{:S(2)}) collective-permute-start(f32[24,128]{1,0:T(8,128)S(1)} %shard_map.141), channel_id=1, source_target_pairs={{0,4},{4,0},{8,12},{12,8},{1,5},{5,1},{9,13},{13,9},{2,6},{6,2},{1... | collective-permute-start | bytes 36872 | tf_op jit(solution)/shard_map/ppermute | solution.py:31
  9.6 6.7 %collective-permute-start.5 = (bf16[128,640]{1,0:T(8,128)(2,1)S(1)}, bf16[128,640]{1,0:T(8,128)(2,1)S(1)}, u32[]{:S(2)}, u32[]{:S(2)}) collective-permute-start(bf16[128,640]{1,0:T(8,128)(2,1)S(1)} %collective-permute-done.3.rest_5_), channel_id=1, source_target_pairs={{0,16},{16,0},{1,17},{17,1},{2,18},{18,2},{3,19},{19,3},{4,20},{20... | collective-permute-start | bytes 491528 | tf_op jit(solution)/shard_map/ppermute | solution.py:21
  11.5 4.8 %collective-permute-start.4 = (bf16[128,640]{1,0:T(8,128)(2,1)S(1)}, bf16[128,640]{1,0:T(8,128)(2,1)S(1)}, u32[]{:S(2)}, u32[]{:S(2)}) collective-permute-start(bf16[128,640]{1,0:T(8,128)(2,1)S(1)} %collective-permute-done.3.rest_5_), channel_id=1, source_target_pairs={{0,1},{1,0},{2,3},{3,2},{4,5},{5,4},{6,7},{7,6},{8,9},{9,8},{10,11... | collective-permute-start | bytes 491528 | tf_op jit(solution)/shard_map/ppermute | solution.py:21
  11.5 4.8 %collective-permute-start.2 = (f32[48,128]{1,0:T(8,128)S(1)}, f32[48,128]{1,0:T(8,128)S(1)}, u32[]{:S(2)}, u32[]{:S(2)}) collective-permute-start(f32[48,128]{1,0:T(8,128)S(1)} %pad_maximum_fusion.1), channel_id=1, source_target_pairs={{0,8},{4,12},{8,0},{12,4},{1,9},{5,13},{9,1},{13,5},{2,10},{6,14},... | collective-permute-start | bytes 73736 | tf_op jit(solution)/shard_map/ppermute | solution.py:31
  16.6 1.9 %collective-permute-start.8 = (bf16[128,1408]{1,0:T(8,128)(2,1)S(1)}, bf16[128,1408]{1,0:T(8,128)(2,1)S(1)}, u32[]{:S(2)}, u32[]{:S(2)}) collective-permute-start(bf16[128,1408]{1,0:T(8,128)(2,1)S(1)} %shard_map.143.rest_9_), channel_id=1, source_target_pairs={{0,1},{1,0},{2,3},{3,2},{4,5},{5,4},{6,7},{7,6},{8,9},{9,8},{10,11... | collective-permute-start | bytes 1081352 | tf_op jit(solution)/shard_map/ppermute | solution.py:21
  16.6 1.9 %collective-permute-start.6 = (bf16[128,640]{1,0:T(8,128)(2,1)S(1)}, bf16[128,640]{1,0:T(8,128)(2,1)S(1)}, u32[]{:S(2)}, u32[]{:S(2)}) collective-permute-start(bf16[128,640]{1,0:T(8,128)(2,1)S(1)} %collective-permute-done.5.refs_2_.rest_7_), channel_id=1, source_target_pairs={{0,1},{1,0},{2,3},{3,2},{4,5},{5,4},{6,7},{7,6},{8,9},{9,8},{10,11... | collective-permute-start | bytes 491528 | tf_op jit(solution)/shard_map/ppermute | solution.py:21

commit v14 on v13

--- a/solution.py
+++ b/solution.py
@@ -150,7 +150,7 @@
     steps, layers, bands, local, members, lon, chans, vp, fp, turns, groups = dims
     lat = bands * local
     hidden, taps = rest[:2]
-    pieces = 3 + (layers - 1) * (groups + 1) * bands
+    pieces = 3 + (layers - 1) * (groups + 2) * bands
     blocks, rest = rest[2 : 2 + pieces], rest[2 + pieces :]
     final_ref, mean_ref, weights, conv, act, inputs, total, sems = rest[:8]
     here, band = lax.axis_index("segment"), lax.axis_index("rows")
@@ -163,15 +163,17 @@
     share = 5 * chans // groups
     for k in range(1, layers):
         slot = lax.rem(here - k + layers, layers)
-        for g in range(groups + 1):
+        for g in range(groups + 2):
             if g < groups:
                 place = lax.rem(lax.axis_index("groups") - g + groups, groups)
                 cols = pl.ds(pl.multiple_of(place * share, LANES), share)
+            elif g == groups:
+                cols = pl.ds(groups * share, 6 * LANES)
             else:
-                cols = pl.ds(groups * share, 10 * chans + LANES - groups * share)
+                cols = pl.ds(groups * share + 6 * LANES, 10 * chans - groups * share - 5 * LANES)
             for j in range(bands):
                 rows = pl.ds(pl.multiple_of(lax.rem(band - j + bands, bands) * part, part), part)
-                block = blocks[3 + ((k - 1) * (groups + 1) + g) * bands + j]
+                block = blocks[3 + ((k - 1) * (groups + 2) + g) * bands + j]
                 pltpu.make_async_copy(block, weights.at[slot, rows, cols], sems.at[slot]).start()
 
     if turns > 1:
@@ -321,7 +323,9 @@
     conv = conv_weight[0]
     relayed = lax.dynamic_slice(conv, (band * part, lax.axis_index("groups") * share), (part, share))
     spread = jnp.broadcast_to((norm_gain[0] * 0.5)[:, None], (chans, LANES))
-    direct = jnp.concatenate([conv[:, groups * share :], point_weight[0], spread], axis=1)
+    middle = groups * share + 6 * LANES
+    between = lax.dynamic_slice(conv, (band * part, groups * share), (part, middle - groups * share))
+    direct = jnp.concatenate([conv[:, middle:], point_weight[0], spread], axis=1)
     direct = lax.dynamic_slice_in_dim(direct, band * part, part, 0)
     field = pl.pallas_call(
         functools.partial(pack_kernel, (steps, local, forced, vp, fp)),
@@ -331,7 +335,7 @@
         compiler_params=small,
         cost_estimate=free,
     )(slots, init_state[0], land_mask, direct)
-    relayed, direct = (all_along(piece, "segment")[1:] for piece in (relayed, direct))
+    relayed, between, direct = (all_along(piece, "segment")[1:] for piece in (relayed, between, direct))
     fields = all_along(field, "rows")
     group = pl.pallas_call(
         functools.partial(group_kernel, (steps, bands, local, forced, vp, fp)),
@@ -372,6 +376,7 @@
         blocks += early
         for shared in shares[1:]:
             blocks += all_along(shared, "rows")
+        blocks += all_along(after(between[k], *fields[1:]), "rows")
         blocks += all_along(after(direct[k], group, *shares[1:], *early[1:]), "rows")
 
     scratch = [

time: 26.1 us -> 29.5 us (1.13)
  other arithmetic: 0.07 us -> 1.67 us
  starting transfers between devices: 10.5 us -> 11.7 us
  local copies, waits for them, and re-layouts: 2.23 us -> 2.99 us
    ppermute x7 -> x9, starting transfers between devices: 5.53 us -> 6.9 us  [passed_along(): lax.ppermute(block, axis, [(i, (i + distance) % size) for i in range(size)])]
    dynamic_slice x0 -> x1, local copies, waits for them, and re-layouts: none -> 0.94 us  [per_device(): lax.dynamic_slice(conv, (band * part, groups * share), (part, middle - gr...]
    concatenate x1, other arithmetic: 0.04 us -> 0.96 us  [per_device(): jnp.concatenate([conv[:, middle:], point_weight[0], spread], axis=1)]
    mul x1, other arithmetic: 0.02 us -> 0.7 us  [per_device(): spread = jnp.broadcast_to((norm_gain[0] * 0.5)[:, None], (chans, LANES))]
    ppermute x7 -> x9, waiting for transfers between devices: 1.05 us -> 0.57 us  [passed_along(): lax.ppermute(block, axis, [(i, (i + distance) % size) for i in range(size)])]
  transfers between devices with their start and end apart: 9 -> 11, of which waited for: 4 -> 2; matrix products, arithmetic and copies ran while one was open for 5% -> 12% of each run, Pallas kernels for 4% -> 4%
where the time goes in v14:
time: 29.5 us; the launch traced here: 29.3 us
  starting transfers between devices  11.7 us (40%)
  Pallas kernels  8.57 us (29%)
  local copies, waits for them, and re-layouts  2.99 us (10%)
  waiting for transfers between devices  2.81 us (10%)
  other arithmetic  1.67 us (6%)
  between operations  1.54 us (5%)
    pallas_call x1, Pallas kernels, per_device(): pl.pallas_call(functools.partial(window_kernel, dims + (groups,)), out_sh...  7.45 us
    ppermute x9, starting transfers between devices, passed_along(): lax.ppermute(block, axis, [(i, (i + distance) % size) for i in range(size)])  6.9 us
    ppermute x2, starting transfers between devices, by_doubling(): partner = lax.ppermute(block, axis, [(i, i ^ reach) for i in range(size)])  4.81 us
    ppermute x2, waiting for transfers between devices, by_doubling(): partner = lax.ppermute(block, axis, [(i, i ^ reach) for i in range(size)])  2.24 us
    pallas_call x1, Pallas kernels, per_device(): pl.pallas_call(functools.partial(first_kernel, dims), out_shape=(jax.Shap...  1.09 us
    concatenate x1, other arithmetic, per_device(): jnp.concatenate([conv[:, middle:], point_weight[0], spread], axis=1)  0.96 us
    slice x1, local copies, waits for them, and re-layouts, per_device(): conv[:, middle:]  0.95 us
    dynamic_slice x1, local copies, waits for them, and re-layouts, per_device(): lax.dynamic_slice(conv, (band * part, lax.axis_index('groups') * share),...  0.94 us
  transfers between devices with their start and end apart: 11, of which 2 were waited for; matrix products, arithmetic and copies ran while one was open for 12% of the time, Pallas kernels for 4%

profile of v14, /device:TPU:0, one launch (start us, length us, event | category | flops | bytes accessed | tf_op | source)
XLA Modules:
  0.0 29.3 jit_solution(12335194663953256573)
XLA Ops:
  0.6 0.0 copy-start.8
  0.6 0.0 copy-start.4
  0.6 0.0 copy-start.9
  0.7 0.9 %dynamic-slice_bitcast_fusion.1 = bf16[128,640]{1,0:T(8,128)(2,1)S(1)} fusion(bf16[1,256,2304]{2,1,0:T(8,128)(2,1)} %param.22, s32[]{:T(128)S(6)} %select_n.8, s32[]{:T(128)S(6)} %select_n.9), kind=kLoop, calls=%fused_computation.6 | loop fusion | bytes 327688 | tf_op jit(solution)/shard_map/dynamic_slice | solution.py:324
  1.6 3.0 %collective-permute-start.3 = (bf16[128,640]{1,0:T(8,128)(2,1)S(1)}, bf16[128,640]{1,0:T(8,128)(2,1)S(1)}, u32[]{:S(2)}, u32[]{:S(2)}) collective-permute-start(bf16[128,640]{1,0:T(8,128)(2,1)S(1)} %dynamic-slice_bitcast_fusion.1), channel_id=1, source_target_pairs={{0,2},{2,0},{1,3},{3,1},{4,6},{6,4},{5,7},{7,5},{8,10},{10,8},{9,1... | collective-permute-start | bytes 491528 | tf_op jit(solution)/shard_map/ppermute | solution.py:21
  4.6 0.9 %dynamic-slice_bitcast_fusion = bf16[128,768]{1,0:T(8,128)(2,1)S(1)} fusion(bf16[1,256,2304]{2,1,0:T(8,128)(2,1)} %param.22, s32[]{:T(128)S(6)} %select_n.8), kind=kLoop, calls=%fused_computation.3 | loop fusion | bytes 393220 | tf_op jit(solution)/shard_map/dynamic_slice | solution.py:327
  5.6 0.1 collective-permute-start.7
  5.6 0.7 %multiply_reduce_fusion = bf16[256]{0:T(256)(128)(2,1)S(1)} fusion(bf16[1,256]{1,0:T(2,128)(2,1)} %param.24), kind=kLoop, calls=%fused_computation.9 | loop fusion | flops 256 | bytes 1024 | tf_op jit(solution)/shard_map/mul | solution.py:325
  6.3 0.0 copy-start.2
  6.4 0.0 copy-start.3
  6.4 0.0 copy-start.5
  6.4 0.0 copy-start.6
  6.4 0.0 copy-start.7
  6.4 0.0 copy-start.10
  6.4 0.9 %slice.4 = bf16[256,256]{1,0:T(8,128)(2,1)S(1)} slice(bf16[256,2304]{1,0:T(8,128)(2,1)} %bitcast.14), slice={[0:256], [2048:2304]} | slice | bytes 262144 | tf_op jit(solution)/shard_map/slice | solution.py:328
  7.4 0.1 broadcast_in_dim.4.rest_4_
  7.5 0.0 copy-start
  7.5 0.0 copy-start.1
  7.5 1.0 %fusion.1.earlier_ref = bf16[128,640]{1,0:T(8,128)(2,1)S(1)} fusion(s32[]{:T(128)S(6)} %select_n.8, bf16[256,256]{1,0:T(8,128)(2,1)S(1)} %slice.4, bf16[256,256]{1,0:T(8,128)(2,1)} %bitcast.16, bf16[256,128]{1,0:T(8,128)(2,1)S(1)} %broadcast_in_dim.4.rest_4_), kind=kLoop, calls=%fused_computation.5 | loop fusion | flops 491520 | bytes 491524 | tf_op jit(solution)/shard_map/concatenate | solution.py:328
  8.5 0.0 copy-done.8
  8.5 0.0 copy-done.4
  8.5 0.0 copy-done.9
  8.5 0.1 collective-permute-start
  9.2 0.5 %collective-permute-done.rest_1_.refs_1_ = bf16[1,128,128]{2,1,0:T(8,128)(2,1)S(1)} collective-permute-done((bf16[1,128,128]{2,1,0:T(8,128)(2,1)S(1)}, bf16[1,128,128]{2,1,0:T(8,128)(2,1)S(1)}, u32[]{:S(2)}, u32[]{:S(2)}) %collective-permute-start) | collective-permute-done | bytes 32800 | tf_op jit(solution)/shard_map/ppermute | solution.py:21
  9.8 2.2 %collective-permute-start.1 = (f32[24,128]{1,0:T(8,128)S(1)}, f32[24,128]{1,0:T(8,128)S(1)}, u32[]{:S(2)}, u32[]{:S(2)}) collective-permute-start(f32[24,128]{1,0:T(8,128)S(1)} %shard_map.141), channel_id=1, source_target_pairs={{0,4},{4,0},{8,12},{12,8},{1,5},{5,1},{9,13},{13,9},{2,6},{6,2},{1... | collective-permute-start | bytes 36872 | tf_op jit(solution)/shard_map/ppermute | solution.py:31
  11.9 1.5 %collective-permute-start.9 = (bf16[128,640]{1,0:T(8,128)(2,1)S(1)}, bf16[128,640]{1,0:T(8,128)(2,1)S(1)}, u32[]{:S(2)}, u32[]{:S(2)}) collective-permute-start(bf16[128,640]{1,0:T(8,128)(2,1)S(1)} %fusion.1.earlier_ref), channel_id=1, source_target_pairs={{0,2},{2,0},{1,3},{3,1},{4,6},{6,4},{5,7},{7,5},{8,10},{10,8},{9,1... | collective-permute-start | bytes 491528 | tf_op jit(solution)/shard_map/ppermute | solution.py:21
  13.4 0.0 collective-permute-done.3.rest_5_
  13.4 1.5 %collective-permute-start.5 = (bf16[128,640]{1,0:T(8,128)(2,1)S(1)}, bf16[128,640]{1,0:T(8,128)(2,1)S(1)}, u32[]{:S(2)}, u32[]{:S(2)}) collective-permute-start(bf16[128,640]{1,0:T(8,128)(2,1)S(1)} %collective-permute-done.3.rest_5_), channel_id=1, source_target_pairs={{0,16},{16,0},{1,17},{17,1},{2,18},{18,2},{3,19},{19,3},{4,20},{20... | collective-permute-start | bytes 491528 | tf_op jit(solution)/shard_map/ppermute | solution.py:21
  15.0 0.0 collective-permute-start.4
  15.0 0.0 collective-permute-done.1
  15.0 2.7 %collective-permute-start.2 = (f32[48,128]{1,0:T(8,128)S(1)}, f32[48,128]{1,0:T(8,128)S(1)}, u32[]{:S(2)}, u32[]{:S(2)}) collective-permute-start(f32[48,128]{1,0:T(8,128)S(1)} %pad_maximum_fusion.1), channel_id=1, source_target_pairs={{0,8},{4,12},{8,0},{12,4},{1,9},{5,13},{9,1},{13,5},{2,10},{6,14},... | collective-permute-start | bytes 73736 | tf_op jit(solution)/shard_map/ppermute | solution.py:31
  17.6 0.0 collective-permute-done.7.refs_0_
  17.6 0.2 collective-permute-start.8
  17.8 2.2 %collective-permute-done.2 = f32[48,128]{1,0:T(8,128)S(1)} collective-permute-done((f32[48,128]{1,0:T(8,128)S(1)}, f32[48,128]{1,0:T(8,128)S(1)}, u32[]{:S(2)}, u32[]{:S(2)}) %collective-permute-start.2) | collective-permute-done | bytes 24608 | tf_op jit(solution)/shard_map/ppermute | solution.py:31
  20.0 0.0 collective-permute-done.9.refs_0_
  20.0 0.0 collective-permute-done.5.refs_2_.rest_7_
  20.0 0.0 collective-permute-done.4.refs_3_.rest_6_
  20.1 0.1 collective-permute-start.10
  20.1 0.5 %collective-permute-start.6 = (bf16[128,640]{1,0:T(8,128)(2,1)S(1)}, bf16[128,640]{1,0:T(8,128)(2,1)S(1)}, u32[]{:S(2)}, u32[]{:S(2)}) collective-permute-start(bf16[128,640]{1,0:T(8,128)(2,1)S(1)} %collective-permute-done.5.refs_2_.rest_7_), channel_id=1, source_target_pairs={{0,1},{1,0},{2,3},{3,2},{4,5},{5,4},{6,7},{7,6},{8,9},{9,8},{10,11... | collective-permute-start | bytes 491528 | tf_op jit(solution)/shard_map/ppermute | solution.py:21
  20.6 0.0 copy-done.2
  20.6 0.0 copy-done.3
  20.7 0.0 copy-done.5
  20.7 0.0 copy-done.6
  20.7 1.1 %shard_map.142 = (bf16[2,128,128]{2,1,0:T(8,128)(2,1)S(1)}, f32[1,256,512]{2,1,0:T(8,128)S(1)}, f32[1,256,512]{2,1,0:T(8,128)S(1)}, bf16[256,96]{1,0:T(8,128)(2,...) custom-call(s32[1,2]{1,0:T(1,128)S(1)} %copy-done.10, ...), custom_call_target="tpu_custom_call" | custom-call | tf_op jit(solution)/shard_map/pallas_call | solution.py:351
  21.8 0.0 collective-permute-done.8.rest_10_
  21.8 0.0 collective-permute-done.10.rest_12_
  21.8 0.0 collective-permute-done.6.rest_8_
  21.8 7.5 %shard_map.145 = (bf16[1,77,128]{2,1,0:T(8,128)(2,1)}, f32[77,1,128]{2,1,0:T(1,128)}) custom-call(bf16[2,128,128]{2,1,0:T(8,128)(2,1)S(1)} %get-tuple-element.11.field_ref, f32[1,256,512]{2,1,0:T(8,128)S(1)} %get-tuple-element.12.scale_ref, f32[1,256,512]{2,1,0:T(8,128)S(1)} %get-tuple-element.13.shift_ref, bf16[256,96]{1,0:T(8,128)(2,1)S(1)} %get-tuple-element.14.enc_ref, ...), custom_call_target="tpu_custom_call" | custom-call | tf_op jit(solution)/shard_map/pallas_call | solution.py:392
  (10 shorter events, 0.0 us)
Async XLA Ops:
  0.6 7.8 %copy-start.8 = (bf16[1,1,2,1,4,128]{5,4,3,2,1,0:T(4,128)(2,1)S(1)}, bf16[1,1,2,1,4,128]{5,4,3,2,1,0:T(4,128)(2,1)}, u32[]{:S(2)}) copy-start(bf16[1,1,2,1,4,128]{5,4,3,2,1,0:T(4,128)(2,1)} %param.14) | copy-start | bytes 6148
  0.6 7.8 %copy-start.4 = (bf16[1,1,77,128]{3,2,1,0:T(8,128)(2,1)S(1)}, bf16[1,1,77,128]{3,2,1,0:T(8,128)(2,1)}, u32[]{:S(2)}) copy-start(bf16[1,1,77,128]{3,2,1,0:T(8,128)(2,1)} %param.13) | copy-start | bytes 59140
  0.6 7.8 %copy-start.9 = (s32[1,128]{1,0:T(1,128)S(1)}, s32[1,128]{1,0:T(1,128)}, u32[]{:S(2)}) copy-start(s32[1,128]{1,0:T(1,128)} %land_ref.1) | copy-start | bytes 1540
  1.6 11.8 %collective-permute-start.3 = (bf16[128,640]{1,0:T(8,128)(2,1)S(1)}, bf16[128,640]{1,0:T(8,128)(2,1)S(1)}, u32[]{:S(2)}, u32[]{:S(2)}) collective-permute-start(bf16[128,640]{1,0:T(8,128)(2,1)S(1)} %dynamic-slice_bitcast_fusion.1), channel_id=1, source_target_pairs={{0,2},{2,0},{1,3},{3,1},{4,6},{6,4},{5,7},{7,5},{8,10},{10,8},{9,1... | collective-permute-start | bytes 491528 | tf_op jit(solution)/shard_map/ppermute | solution.py:21
  5.6 12.1 %collective-permute-start.7 = (bf16[128,768]{1,0:T(8,128)(2,1)S(1)}, bf16[128,768]{1,0:T(8,128)(2,1)S(1)}, u32[]{:S(2)}, u32[]{:S(2)}) collective-permute-start(bf16[128,768]{1,0:T(8,128)(2,1)S(1)} %dynamic-slice_bitcast_fusion), channel_id=1, source_target_pairs={{0,2},{2,0},{1,3},{3,1},{4,6},{6,4},{5,7},{7,5},{8,10},{10,8},{9,1... | collective-permute-start | bytes 589832 | tf_op jit(solution)/shard_map/ppermute | solution.py:21
  6.3 14.3 %copy-start.2 = (bf16[256,81]{0,1:T(8,128)(2,1)S(1)}, bf16[256,81]{0,1:T(8,128)(2,1)}, u32[]{:S(2)}) copy-start(bf16[256,81]{0,1:T(8,128)(2,1)} %param.21) | copy-start | bytes 124420
  6.4 14.3 %copy-start.3 = (bf16[77,256]{1,0:T(8,128)(2,1)S(1)}, bf16[77,256]{1,0:T(8,128)(2,1)}, u32[]{:S(2)}) copy-start(bf16[77,256]{1,0:T(8,128)(2,1)} %dec_w_ref.1) | copy-start | bytes 118276
  6.4 14.3 %copy-start.5 = (f32[16,256]{1,0:T(8,128)S(1)}, f32[16,256]{1,0:T(8,128)}, u32[]{:S(2)}) copy-start(f32[16,256]{1,0:T(8,128)} %scale_w_ref.1) | copy-start | bytes 49156
  6.4 14.3 %copy-start.6 = (f32[16,256]{1,0:T(8,128)S(1)}, f32[16,256]{1,0:T(8,128)}, u32[]{:S(2)}) copy-start(f32[16,256]{1,0:T(8,128)} %shift_w_ref.1) | copy-start | bytes 49156
  6.4 14.3 %copy-start.7 = (f32[64,16]{0,1:T(8,128)S(1)}, f32[64,16]{0,1:T(8,128)}, u32[]{:S(2)}) copy-start(f32[64,16]{0,1:T(8,128)} %param.18) | copy-start | bytes 12292
  6.4 14.3 %copy-start.10 = (s32[1,2]{1,0:T(1,128)S(1)}, s32[1,2]{1,0:T(1,128)}, u32[]{:S(2)}) copy-start(s32[1,2]{1,0:T(1,128)} %owner_ref.1) | copy-start | bytes 28
  7.5 14.3 %copy-start = (bf16[1,256,2304]{2,1,0:T(8,128)(2,1)S(1)}, bf16[1,256,2304]{2,1,0:T(8,128)(2,1)}, u32[]{:S(2)}) copy-start(bf16[1,256,2304]{2,1,0:T(8,128)(2,1)} %param.22) | copy-start | bytes 3538948
  7.5 14.3 %copy-start.1 = (bf16[1,256,256]{2,1,0:T(8,128)(2,1)S(1)}, bf16[1,256,256]{2,1,0:T(8,128)(2,1)}, u32[]{:S(2)}) copy-start(bf16[1,256,256]{2,1,0:T(8,128)(2,1)} %param.23) | copy-start | bytes 393220
  8.5 1.3 %collective-permute-start = (bf16[1,128,128]{2,1,0:T(8,128)(2,1)S(1)}, bf16[1,128,128]{2,1,0:T(8,128)(2,1)S(1)}, u32[]{:S(2)}, u32[]{:S(2)}) collective-permute-start(bf16[1,128,128]{2,1,0:T(8,128)(2,1)S(1)} %shard_map.140.rest_0_), channel_id=1, source_target_pairs={{0,1},{1,0},{2,3},{3,2},{4,5},{5,4},{6,7},{7,6},{8,9},{9,8},{10,11... | collective-permute-start | bytes 98312 | tf_op jit(solution)/shard_map/ppermute | solution.py:21
  9.8 5.2 %collective-permute-start.1 = (f32[24,128]{1,0:T(8,128)S(1)}, f32[24,128]{1,0:T(8,128)S(1)}, u32[]{:S(2)}, u32[]{:S(2)}) collective-permute-start(f32[24,128]{1,0:T(8,128)S(1)} %shard_map.141), channel_id=1, source_target_pairs={{0,4},{4,0},{8,12},{12,8},{1,5},{5,1},{9,13},{13,9},{2,6},{6,2},{1... | collective-permute-start | bytes 36872 | tf_op jit(solution)/shard_map/ppermute | solution.py:31
  11.9 8.1 %collective-permute-start.9 = (bf16[128,640]{1,0:T(8,128)(2,1)S(1)}, bf16[128,640]{1,0:T(8,128)(2,1)S(1)}, u32[]{:S(2)}, u32[]{:S(2)}) collective-permute-start(bf16[128,640]{1,0:T(8,128)(2,1)S(1)} %fusion.1.earlier_ref), channel_id=1, source_target_pairs={{0,2},{2,0},{1,3},{3,1},{4,6},{6,4},{5,7},{7,5},{8,10},{10,8},{9,1... | collective-permute-start | bytes 491528 | tf_op jit(solution)/shard_map/ppermute | solution.py:21
  13.4 6.6 %collective-permute-start.5 = (bf16[128,640]{1,0:T(8,128)(2,1)S(1)}, bf16[128,640]{1,0:T(8,128)(2,1)S(1)}, u32[]{:S(2)}, u32[]{:S(2)}) collective-permute-start(bf16[128,640]{1,0:T(8,128)(2,1)S(1)} %collective-permute-done.3.rest_5_), channel_id=1, source_target_pairs={{0,16},{16,0},{1,17},{17,1},{2,18},{18,2},{3,19},{19,3},{4,20},{20... | collective-permute-start | bytes 491528 | tf_op jit(solution)/shard_map/ppermute | solution.py:21
  15.0 5.1 %collective-permute-start.4 = (bf16[128,640]{1,0:T(8,128)(2,1)S(1)}, bf16[128,640]{1,0:T(8,128)(2,1)S(1)}, u32[]{:S(2)}, u32[]{:S(2)}) collective-permute-start(bf16[128,640]{1,0:T(8,128)(2,1)S(1)} %collective-permute-done.3.rest_5_), channel_id=1, source_target_pairs={{0,1},{1,0},{2,3},{3,2},{4,5},{5,4},{6,7},{7,6},{8,9},{9,8},{10,11... | collective-permute-start | bytes 491528 | tf_op jit(solution)/shard_map/ppermute | solution.py:21
  15.0 5.1 %collective-permute-start.2 = (f32[48,128]{1,0:T(8,128)S(1)}, f32[48,128]{1,0:T(8,128)S(1)}, u32[]{:S(2)}, u32[]{:S(2)}) collective-permute-start(f32[48,128]{1,0:T(8,128)S(1)} %pad_maximum_fusion.1), channel_id=1, source_target_pairs={{0,8},{4,12},{8,0},{12,4},{1,9},{5,13},{9,1},{13,5},{2,10},{6,14},... | collective-permute-start | bytes 73736 | tf_op jit(solution)/shard_map/ppermute | solution.py:31
  17.6 4.1 %collective-permute-start.8 = (bf16[128,768]{1,0:T(8,128)(2,1)S(1)}, bf16[128,768]{1,0:T(8,128)(2,1)S(1)}, u32[]{:S(2)}, u32[]{:S(2)}) collective-permute-start(bf16[128,768]{1,0:T(8,128)(2,1)S(1)} %shard_map.143.rest_9_), channel_id=1, source_target_pairs={{0,1},{1,0},{2,3},{3,2},{4,5},{5,4},{6,7},{7,6},{8,9},{9,8},{10,11... | collective-permute-start | bytes 589832 | tf_op jit(solution)/shard_map/ppermute | solution.py:21
  20.1 1.7 %collective-permute-start.10 = (bf16[128,640]{1,0:T(8,128)(2,1)S(1)}, bf16[128,640]{1,0:T(8,128)(2,1)S(1)}, u32[]{:S(2)}, u32[]{:S(2)}) collective-permute-start(bf16[128,640]{1,0:T(8,128)(2,1)S(1)} %shard_map.144.rest_11_), channel_id=1, source_target_pairs={{0,1},{1,0},{2,3},{3,2},{4,5},{5,4},{6,7},{7,6},{8,9},{9,8},{10,11... | collective-permute-start | bytes 491528 | tf_op jit(solution)/shard_map/ppermute | solution.py:21
  20.1 1.6 %collective-permute-start.6 = (bf16[128,640]{1,0:T(8,128)(2,1)S(1)}, bf16[128,640]{1,0:T(8,128)(2,1)S(1)}, u32[]{:S(2)}, u32[]{:S(2)}) collective-permute-start(bf16[128,640]{1,0:T(8,128)(2,1)S(1)} %collective-permute-done.5.refs_2_.rest_7_), channel_id=1, source_target_pairs={{0,1},{1,0},{2,3},{3,2},{4,5},{5,4},{6,7},{7,6},{8,9},{9,8},{10,11... | collective-permute-start | bytes 491528 | tf_op jit(solution)/shard_map/ppermute | solution.py:21

commit v15 on v13

--- a/solution.py
+++ b/solution.py
@@ -223,13 +223,21 @@
                 taps[low * wide : (high + 1) * wide, :],
                 preferred_element_type=jnp.float32,
             )
+        activate_row(0, layer)
         for i in range(lat):
-            mix(i, i, land[i], layer)
-
-    def mix(i, row, sea, layer):
+            conv[i] = mixed_row(i, layer)
+            if i + 1 < lat:
+                activate_row(i + 1, layer)
+            add_row(conv[i], i, land[i], layer)
+
+    def activate_row(i, layer):
         for m in range(members):
             act[i, :, columns(m)] = activate(conv[i, :, columns(m)], layer)
-        mixed = jnp.dot(weights[layer, :, taps_wide : 10 * chans], act[i], preferred_element_type=jnp.float32)
+
+    def mixed_row(i, layer):
+        return jnp.dot(weights[layer, :, taps_wide : 10 * chans], act[i], preferred_element_type=jnp.float32)
+
+    def add_row(mixed, row, sea, layer):
         for m in range(members):
             kept = hidden[row, :, columns(m)].astype(jnp.float32)
             later = layer + 1 if layer + 1 < layers else None
@@ -246,7 +254,8 @@
         first = pl.multiple_of((1 - band) * wide, wide)
         conv[0] = jnp.dot(weights[layer, :, pl.ds(first, 2 * wide)], taps[...], preferred_element_type=jnp.float32)
         sea = field_ref[band, vp + fp * steps : vp + fp * steps + 1, :].astype(jnp.float32)
-        mix(0, band, sea, layer)
+        activate_row(0, layer)
+        add_row(mixed_row(0, layer), band, sea, layer)
         decode(band, sea, steps - 1)
 
     varied = final_ref.shape[1]

time: 26.1 us -> 26.1 us (level)
  no operation moved by 1% of the time
where the time goes in v15:
time: 26.1 us; the launch traced here: 25.9 us
  starting transfers between devices  10.5 us (40%)
  Pallas kernels  8.51 us (33%)
  waiting for transfers between devices  3.01 us (12%)
  local copies, waits for them, and re-layouts  2.23 us (9%)
  between operations  1.61 us (6%)
    pallas_call x1, Pallas kernels, per_device(): pl.pallas_call(functools.partial(window_kernel, dims + (groups,)), out_sh...  7.4 us
    ppermute x7, starting transfers between devices, passed_along(): lax.ppermute(block, axis, [(i, (i + distance) % size) for i in range(size)])  5.53 us
    ppermute x2, starting transfers between devices, by_doubling(): partner = lax.ppermute(block, axis, [(i, i ^ reach) for i in range(size)])  4.97 us
    ppermute x2, waiting for transfers between devices, by_doubling(): partner = lax.ppermute(block, axis, [(i, i ^ reach) for i in range(size)])  1.96 us
    pallas_call x1, Pallas kernels, per_device(): pl.pallas_call(functools.partial(first_kernel, dims), out_shape=(jax.Shap...  1.09 us
    slice x1, local copies, waits for them, and re-layouts, per_device(): conv[:, groups * share:]  1.08 us
    ppermute x7, waiting for transfers between devices, passed_along(): lax.ppermute(block, axis, [(i, (i + distance) % size) for i in range(size)])  1.05 us
    dynamic_slice x1, local copies, waits for them, and re-layouts, per_device(): lax.dynamic_slice(conv, (band * part, lax.axis_index('groups') * share),...  0.98 us
  transfers between devices with their start and end apart: 9, of which 4 were waited for; matrix products, arithmetic and copies ran while one was open for 5% of the time, Pallas kernels for 4%

profile of v15, /device:TPU:0, one launch (start us, length us, event | category | flops | bytes accessed | tf_op | source)
XLA Modules:
  0.0 25.9 jit_solution(10561924917734389397)
XLA Ops:
  0.6 0.0 copy-start.11
  0.6 0.0 copy-start.1
  0.7 1.0 %dynamic-slice_bitcast_fusion = bf16[128,640]{1,0:T(8,128)(2,1)S(1)} fusion(bf16[1,256,2304]{2,1,0:T(8,128)(2,1)} %param.22, s32[]{:T(128)S(6)} %select_n.7, s32[]{:T(128)S(6)} %select_n.8), kind=kLoop, calls=%fused_computation.5 | loop fusion | bytes 327688 | tf_op jit(solution)/shard_map/dynamic_slice | solution.py:331
  1.6 0.0 copy-start.4
  1.7 0.0 copy-start.8
  1.7 0.0 copy-start.9
  1.7 3.0 %collective-permute-start.3 = (bf16[128,640]{1,0:T(8,128)(2,1)S(1)}, bf16[128,640]{1,0:T(8,128)(2,1)S(1)}, u32[]{:S(2)}, u32[]{:S(2)}) collective-permute-start(bf16[128,640]{1,0:T(8,128)(2,1)S(1)} %dynamic-slice_bitcast_fusion), channel_id=1, source_target_pairs={{0,2},{2,0},{1,3},{3,1},{4,6},{6,4},{5,7},{7,5},{8,10},{10,8},{9,1... | collective-permute-start | bytes 491528 | tf_op jit(solution)/shard_map/ppermute | solution.py:21
  4.7 1.1 %slice.4 = bf16[256,1024]{1,0:T(8,128)(2,1)S(1)} slice(bf16[256,2304]{1,0:T(8,128)(2,1)} %bitcast.12), slice={[0:256], [1280:2304]} | slice | bytes 1048576 | tf_op jit(solution)/shard_map/slice | solution.py:333
  5.8 0.0 copy-done.11
  5.8 0.1 broadcast_in_dim.4.rest_4_
  5.9 0.0 copy-done.1
  5.9 0.0 copy-start.2
  5.9 0.0 copy-start.3
  5.9 0.0 copy-start.5
  5.9 0.0 copy-start.6
  6.0 0.0 copy-start.7
  6.0 0.0 copy-start.10
  6.0 0.0 copy-start
  6.0 0.1 collective-permute-start.7
  6.1 0.0 copy-done.4
  6.1 0.0 copy-done.8
  6.1 0.0 copy-done.9
  6.2 0.1 collective-permute-start
  7.0 0.4 %collective-permute-done.rest_1_ = bf16[1,128,128]{2,1,0:T(8,128)(2,1)S(1)} collective-permute-done((bf16[1,128,128]{2,1,0:T(8,128)(2,1)S(1)}, bf16[1,128,128]{2,1,0:T(8,128)(2,1)S(1)}, u32[]{:S(2)}, u32[]{:S(2)}) %collective-permute-start) | collective-permute-done | bytes 32800 | tf_op jit(solution)/shard_map/ppermute | solution.py:21
  7.5 2.1 %collective-permute-start.1 = (f32[24,128]{1,0:T(8,128)S(1)}, f32[24,128]{1,0:T(8,128)S(1)}, u32[]{:S(2)}, u32[]{:S(2)}) collective-permute-start(f32[24,128]{1,0:T(8,128)S(1)} %shard_map.141), channel_id=1, source_target_pairs={{0,4},{4,0},{8,12},{12,8},{1,5},{5,1},{9,13},{13,9},{2,6},{6,2},{1... | collective-permute-start | bytes 36872 | tf_op jit(solution)/shard_map/ppermute | solution.py:31
  9.6 0.0 collective-permute-done.3.rest_5_
  9.6 1.9 %collective-permute-start.5 = (bf16[128,640]{1,0:T(8,128)(2,1)S(1)}, bf16[128,640]{1,0:T(8,128)(2,1)S(1)}, u32[]{:S(2)}, u32[]{:S(2)}) collective-permute-start(bf16[128,640]{1,0:T(8,128)(2,1)S(1)} %collective-permute-done.3.rest_5_), channel_id=1, source_target_pairs={{0,16},{16,0},{1,17},{17,1},{2,18},{18,2},{3,19},{19,3},{4,20},{20... | collective-permute-start | bytes 491528 | tf_op jit(solution)/shard_map/ppermute | solution.py:21
  11.5 0.0 collective-permute-start.4
  11.5 0.0 collective-permute-done.1
  11.5 2.8 %collective-permute-start.2 = (f32[48,128]{1,0:T(8,128)S(1)}, f32[48,128]{1,0:T(8,128)S(1)}, u32[]{:S(2)}, u32[]{:S(2)}) collective-permute-start(f32[48,128]{1,0:T(8,128)S(1)} %pad_maximum_fusion.1), channel_id=1, source_target_pairs={{0,8},{4,12},{8,0},{12,4},{1,9},{5,13},{9,1},{13,5},{2,10},{6,14},... | collective-permute-start | bytes 73736 | tf_op jit(solution)/shard_map/ppermute | solution.py:31
  14.3 2.0 %collective-permute-done.2 = f32[48,128]{1,0:T(8,128)S(1)} collective-permute-done((f32[48,128]{1,0:T(8,128)S(1)}, f32[48,128]{1,0:T(8,128)S(1)}, u32[]{:S(2)}, u32[]{:S(2)}) %collective-permute-start.2) | collective-permute-done | bytes 24608 | tf_op jit(solution)/shard_map/ppermute | solution.py:31
  16.3 0.0 collective-permute-done.5.refs_2_.rest_7_
  16.3 0.0 collective-permute-done.4.refs_3_.rest_6_
  16.3 0.3 %collective-permute-done.7.refs_0_ = bf16[128,1408]{1,0:T(8,128)(2,1)S(1)} collective-permute-done((bf16[128,1408]{1,0:T(8,128)(2,1)S(1)}, bf16[128,1408]{1,0:T(8,128)(2,1)S(1)}, u32[]{:S(2)}, u32[]{:S(2)}) %collective-permute-start.7) | collective-permute-done | bytes 360480 | tf_op jit(solution)/shard_map/ppermute | solution.py:21
  16.6 0.0 collective-permute-start.8
  16.6 0.5 %collective-permute-start.6 = (bf16[128,640]{1,0:T(8,128)(2,1)S(1)}, bf16[128,640]{1,0:T(8,128)(2,1)S(1)}, u32[]{:S(2)}, u32[]{:S(2)}) collective-permute-start(bf16[128,640]{1,0:T(8,128)(2,1)S(1)} %collective-permute-done.5.refs_2_.rest_7_), channel_id=1, source_target_pairs={{0,1},{1,0},{2,3},{3,2},{4,5},{5,4},{6,7},{7,6},{8,9},{9,8},{10,11... | collective-permute-start | bytes 491528 | tf_op jit(solution)/shard_map/ppermute | solution.py:21
  17.1 0.0 copy-done.2
  17.1 0.0 copy-done.3
  17.1 0.0 copy-done.5
  17.1 0.0 copy-done.6
  17.1 0.0 copy-done.7
  17.1 0.0 copy-done.10
  17.1 1.1 %shard_map.142 = (bf16[2,128,128]{2,1,0:T(8,128)(2,1)S(1)}, f32[1,256,512]{2,1,0:T(8,128)S(1)}, f32[1,256,512]{2,1,0:T(8,128)S(1)}, bf16[256,96]{1,0:T(8,128)(2,...) custom-call(s32[1,2]{1,0:T(1,128)S(1)} %copy-done.10, ...), custom_call_target="tpu_custom_call" | custom-call | tf_op jit(solution)/shard_map/pallas_call | solution.py:356
  18.2 0.3 %collective-permute-done.6.rest_8_ = bf16[128,640]{1,0:T(8,128)(2,1)S(1)} collective-permute-done((bf16[128,640]{1,0:T(8,128)(2,1)S(1)}, bf16[128,640]{1,0:T(8,128)(2,1)S(1)}, u32[]{:S(2)}, u32[]{:S(2)}) %collective-permute-start.6) | collective-permute-done | bytes 163872 | tf_op jit(solution)/shard_map/ppermute | solution.py:21
  18.5 0.0 collective-permute-done.8.rest_10_
  18.5 0.0 copy-done
  18.5 7.4 %shard_map.144 = (bf16[1,77,128]{2,1,0:T(8,128)(2,1)}, f32[77,1,128]{2,1,0:T(1,128)}) custom-call(bf16[2,128,128]{2,1,0:T(8,128)(2,1)S(1)} %get-tuple-element.11.field_ref, f32[1,256,512]{2,1,0:T(8,128)S(1)} %get-tuple-element.12.scale_ref, f32[1,256,512]{2,1,0:T(8,128)S(1)} %get-tuple-element.13.shift_ref, bf16[256,96]{1,0:T(8,128)(2,1)S(1)} %get-tuple-element.14.enc_ref, ...), custom_call_target="tpu_custom_call" | custom-call | tf_op jit(solution)/shard_map/pallas_call | solution.py:396
  (7 shorter events, 0.1 us)
Async XLA Ops:
  0.6 5.1 %copy-start.11 = (bf16[1,256]{1,0:T(2,128)(2,1)S(1)}, bf16[1,256]{1,0:T(2,128)(2,1)}, u32[]{:S(2)}) copy-start(bf16[1,256]{1,0:T(2,128)(2,1)} %param.24) | copy-start | bytes 1540
  0.6 5.3 %copy-start.1 = (bf16[1,256,256]{2,1,0:T(8,128)(2,1)S(1)}, bf16[1,256,256]{2,1,0:T(8,128)(2,1)}, u32[]{:S(2)}) copy-start(bf16[1,256,256]{2,1,0:T(8,128)(2,1)} %param.23) | copy-start | bytes 393220
  1.6 4.5 %copy-start.4 = (bf16[1,1,77,128]{3,2,1,0:T(8,128)(2,1)S(1)}, bf16[1,1,77,128]{3,2,1,0:T(8,128)(2,1)}, u32[]{:S(2)}) copy-start(bf16[1,1,77,128]{3,2,1,0:T(8,128)(2,1)} %param.13) | copy-start | bytes 59140
  1.7 4.5 %copy-start.8 = (bf16[1,1,2,1,4,128]{5,4,3,2,1,0:T(4,128)(2,1)S(1)}, bf16[1,1,2,1,4,128]{5,4,3,2,1,0:T(4,128)(2,1)}, u32[]{:S(2)}) copy-start(bf16[1,1,2,1,4,128]{5,4,3,2,1,0:T(4,128)(2,1)} %param.14) | copy-start | bytes 6148
  1.7 4.5 %copy-start.9 = (s32[1,128]{1,0:T(1,128)S(1)}, s32[1,128]{1,0:T(1,128)}, u32[]{:S(2)}) copy-start(s32[1,128]{1,0:T(1,128)} %land_ref.1) | copy-start | bytes 1540
  1.7 7.9 %collective-permute-start.3 = (bf16[128,640]{1,0:T(8,128)(2,1)S(1)}, bf16[128,640]{1,0:T(8,128)(2,1)S(1)}, u32[]{:S(2)}, u32[]{:S(2)}) collective-permute-start(bf16[128,640]{1,0:T(8,128)(2,1)S(1)} %dynamic-slice_bitcast_fusion), channel_id=1, source_target_pairs={{0,2},{2,0},{1,3},{3,1},{4,6},{6,4},{5,7},{7,5},{8,10},{10,8},{9,1... | collective-permute-start | bytes 491528 | tf_op jit(solution)/shard_map/ppermute | solution.py:21
  5.9 11.2 %copy-start.2 = (bf16[256,81]{0,1:T(8,128)(2,1)S(1)}, bf16[256,81]{0,1:T(8,128)(2,1)}, u32[]{:S(2)}) copy-start(bf16[256,81]{0,1:T(8,128)(2,1)} %param.21) | copy-start | bytes 124420
  5.9 11.2 %copy-start.3 = (bf16[77,256]{1,0:T(8,128)(2,1)S(1)}, bf16[77,256]{1,0:T(8,128)(2,1)}, u32[]{:S(2)}) copy-start(bf16[77,256]{1,0:T(8,128)(2,1)} %dec_w_ref.1) | copy-start | bytes 118276
  5.9 11.2 %copy-start.5 = (f32[16,256]{1,0:T(8,128)S(1)}, f32[16,256]{1,0:T(8,128)}, u32[]{:S(2)}) copy-start(f32[16,256]{1,0:T(8,128)} %scale_w_ref.1) | copy-start | bytes 49156
  5.9 11.2 %copy-start.6 = (f32[16,256]{1,0:T(8,128)S(1)}, f32[16,256]{1,0:T(8,128)}, u32[]{:S(2)}) copy-start(f32[16,256]{1,0:T(8,128)} %shift_w_ref.1) | copy-start | bytes 49156
  6.0 11.2 %copy-start.7 = (f32[64,16]{0,1:T(8,128)S(1)}, f32[64,16]{0,1:T(8,128)}, u32[]{:S(2)}) copy-start(f32[64,16]{0,1:T(8,128)} %param.18) | copy-start | bytes 12292
  6.0 11.2 %copy-start.10 = (s32[1,2]{1,0:T(1,128)S(1)}, s32[1,2]{1,0:T(1,128)}, u32[]{:S(2)}) copy-start(s32[1,2]{1,0:T(1,128)} %owner_ref.1) | copy-start | bytes 28
  6.0 12.5 %copy-start = (bf16[1,256,2304]{2,1,0:T(8,128)(2,1)S(1)}, bf16[1,256,2304]{2,1,0:T(8,128)(2,1)}, u32[]{:S(2)}) copy-start(bf16[1,256,2304]{2,1,0:T(8,128)(2,1)} %param.22) | copy-start | bytes 3538948
  6.0 10.6 %collective-permute-start.7 = (bf16[128,1408]{1,0:T(8,128)(2,1)S(1)}, bf16[128,1408]{1,0:T(8,128)(2,1)S(1)}, u32[]{:S(2)}, u32[]{:S(2)}) collective-permute-start(bf16[128,1408]{1,0:T(8,128)(2,1)S(1)} %fusion.1.earlier_ref), channel_id=1, source_target_pairs={{0,2},{2,0},{1,3},{3,1},{4,6},{6,4},{5,7},{7,5},{8,10},{10,8},{9,1... | collective-permute-start | bytes 1081352 | tf_op jit(solution)/shard_map/ppermute | solution.py:21
  6.2 1.3 %collective-permute-start = (bf16[1,128,128]{2,1,0:T(8,128)(2,1)S(1)}, bf16[1,128,128]{2,1,0:T(8,128)(2,1)S(1)}, u32[]{:S(2)}, u32[]{:S(2)}) collective-permute-start(bf16[1,128,128]{2,1,0:T(8,128)(2,1)S(1)} %shard_map.140.rest_0_), channel_id=1, source_target_pairs={{0,1},{1,0},{2,3},{3,2},{4,5},{5,4},{6,7},{7,6},{8,9},{9,8},{10,11... | collective-permute-start | bytes 98312 | tf_op jit(solution)/shard_map/ppermute | solution.py:21
  7.5 4.0 %collective-permute-start.1 = (f32[24,128]{1,0:T(8,128)S(1)}, f32[24,128]{1,0:T(8,128)S(1)}, u32[]{:S(2)}, u32[]{:S(2)}) collective-permute-start(f32[24,128]{1,0:T(8,128)S(1)} %shard_map.141), channel_id=1, source_target_pairs={{0,4},{4,0},{8,12},{12,8},{1,5},{5,1},{9,13},{13,9},{2,6},{6,2},{1... | collective-permute-start | bytes 36872 | tf_op jit(solution)/shard_map/ppermute | solution.py:31
  9.6 6.7 %collective-permute-start.5 = (bf16[128,640]{1,0:T(8,128)(2,1)S(1)}, bf16[128,640]{1,0:T(8,128)(2,1)S(1)}, u32[]{:S(2)}, u32[]{:S(2)}) collective-permute-start(bf16[128,640]{1,0:T(8,128)(2,1)S(1)} %collective-permute-done.3.rest_5_), channel_id=1, source_target_pairs={{0,16},{16,0},{1,17},{17,1},{2,18},{18,2},{3,19},{19,3},{4,20},{20... | collective-permute-start | bytes 491528 | tf_op jit(solution)/shard_map/ppermute | solution.py:21
  11.5 4.8 %collective-permute-start.4 = (bf16[128,640]{1,0:T(8,128)(2,1)S(1)}, bf16[128,640]{1,0:T(8,128)(2,1)S(1)}, u32[]{:S(2)}, u32[]{:S(2)}) collective-permute-start(bf16[128,640]{1,0:T(8,128)(2,1)S(1)} %collective-permute-done.3.rest_5_), channel_id=1, source_target_pairs={{0,1},{1,0},{2,3},{3,2},{4,5},{5,4},{6,7},{7,6},{8,9},{9,8},{10,11... | collective-permute-start | bytes 491528 | tf_op jit(solution)/shard_map/ppermute | solution.py:21
  11.5 4.8 %collective-permute-start.2 = (f32[48,128]{1,0:T(8,128)S(1)}, f32[48,128]{1,0:T(8,128)S(1)}, u32[]{:S(2)}, u32[]{:S(2)}) collective-permute-start(f32[48,128]{1,0:T(8,128)S(1)} %pad_maximum_fusion.1), channel_id=1, source_target_pairs={{0,8},{4,12},{8,0},{12,4},{1,9},{5,13},{9,1},{13,5},{2,10},{6,14},... | collective-permute-start | bytes 73736 | tf_op jit(solution)/shard_map/ppermute | solution.py:31
  16.6 1.9 %collective-permute-start.8 = (bf16[128,1408]{1,0:T(8,128)(2,1)S(1)}, bf16[128,1408]{1,0:T(8,128)(2,1)S(1)}, u32[]{:S(2)}, u32[]{:S(2)}) collective-permute-start(bf16[128,1408]{1,0:T(8,128)(2,1)S(1)} %shard_map.143.rest_9_), channel_id=1, source_target_pairs={{0,1},{1,0},{2,3},{3,2},{4,5},{5,4},{6,7},{7,6},{8,9},{9,8},{10,11... | collective-permute-start | bytes 1081352 | tf_op jit(solution)/shard_map/ppermute | solution.py:21
  16.6 1.9 %collective-permute-start.6 = (bf16[128,640]{1,0:T(8,128)(2,1)S(1)}, bf16[128,640]{1,0:T(8,128)(2,1)S(1)}, u32[]{:S(2)}, u32[]{:S(2)}) collective-permute-start(bf16[128,640]{1,0:T(8,128)(2,1)S(1)} %collective-permute-done.5.refs_2_.rest_7_), channel_id=1, source_target_pairs={{0,1},{1,0},{2,3},{3,2},{4,5},{5,4},{6,7},{7,6},{8,9},{9,8},{10,11... | collective-permute-start | bytes 491528 | tf_op jit(solution)/shard_map/ppermute | solution.py:21
